TPU v7x, 32 devices: a whole 2x2x4 slice. The times are simulated.
32 devices in a mesh: gx: 8 (over z, x), gy: 4 (over y, core).
Axes of the slice: x: 2, y: 2, z: 4, core: 2. Of those that a mesh axis runs over, the one named last changes fastest.
Arguments:
- state: float32 [4, 256, 512, 128], P(None, 'gx', 'gy'), may hold values from -6 to 6
- velocity: float32 [3, 256, 512, 128], P(None, 'gx', 'gy'), may hold values from -6 to 6
- threshold: float32 [8, 512], P('gx', 'gy'), may hold values from 0.5 to 3
- tile_owner: int32 [4, 256, 1], P('gy', 'gx'), may hold values from 0 to 7; in each aligned block of 32 rows (0 to 31, 32 to 63, ..., all dimensions but the last counted through in order) at most 8 rows name the same one
- parcel_owner: int32 [4, 256, 1], P('gy', 'gx'), may hold values from 0 to 7; in each aligned block of 32 rows (0 to 31, 32 to 63, ..., all dimensions but the last counted through in order) at most 8 rows name the same one
- parcel_count: int32 [4, 256], P('gy', 'gx'), may hold values from 1 to 128, as said below
- parcel_share: float32 [4, 256, 128], P('gy', 'gx'), may hold values from 0.2 to 1
Outputs:
- fields: float32 [4, 256, 512, 128], P(None, 'gx', 'gy')
- ground_flux: float32 [8, 512], P('gx', 'gy')
Inputs may be any that keep to these rules, and one draw needn't show every extreme that they name: `tile_owner`: among the 32 tiles of one device no owner is named more than 8 times, and that count is reached. `parcel_owner`: among the 32 rows of one owner no destination is named more than 8 times, and that count is reached. `parcel_count`: the first row of every owner has 128 live parcels.
All inputs are finite; a program needn't handle non-finite values.
Results may differ from a plain program's by a relative error of at most 0.0003.
Values sent between devices are 32-bit elements; how exact they have to be, the bound alone decides.
No kernel may reach another device: no remote copies, remote signals or barrier semaphores. Data moves between devices by JAX's collectives and lax.ppermute only.
A program may use at most 256 MiB of HBM per device.

v0:
```python
import jax
import jax.numpy as jnp
from jax import lax
from jax.sharding import PartitionSpec as P

LEVELS = 4
STEPS = 2


profile_weights = (0.4, 0.3, 0.2, 0.1)
time_step = 0.1


def extended(block, sides, width):
    for axis, dim in sides:
        count = lax.axis_size(axis)
        forward = [(i, i + 1) for i in range(count - 1)]
        backward = [(target, source) for source, target in forward]
        low = lax.ppermute(
            lax.slice_in_dim(block, block.shape[dim] - width, None, axis=dim), axis, forward
        )
        high = lax.ppermute(lax.slice_in_dim(block, 0, width, axis=dim), axis, backward)
        block = jnp.concatenate([low, block, high], axis=dim)
    return block


def friction(east, north):
    total = profile_weights[0] * (
        east[..., 0, :] * east[..., 0, :] + north[..., 0, :] * north[..., 0, :]
    )
    for level in range(1, east.shape[-2]):
        total = total + profile_weights[level] * (
            east[..., level, :] * east[..., level, :] + north[..., level, :] * north[..., level, :]
        )
    return total


def minmod(first, second):
    return jnp.where(
        first * second > 0, jnp.sign(first) * jnp.minimum(jnp.abs(first), jnp.abs(second)), 0.0
    )


def section(array, axis, start, stop):
    return lax.slice_in_dim(array, start, stop, axis=axis)


def divergence(field, speed, axis):
    count = field.shape[axis] - 4
    behind = section(field, axis, 0, count + 1)
    here = section(field, axis, 1, count + 2)
    ahead = section(field, axis, 2, count + 3)
    beyond = section(field, axis, 3, count + 4)
    face_speed = 0.5 * (section(speed, axis, 1, count + 2) + section(speed, axis, 2, count + 3))
    upwind = face_speed * (here + 0.5 * minmod(ahead - here, here - behind))
    downwind = face_speed * (ahead - 0.5 * minmod(beyond - ahead, ahead - here))
    fluxes = jnp.where(face_speed > 0, upwind, downwind)
    return section(fluxes, axis, 1, count + 1) - section(fluxes, axis, 0, count)


def advance(padded, wind):
    inner = padded[:, 2:-2, 2:-2, 2:-2]
    along_x = divergence(padded[:, :, 2:-2, 2:-2], wind[0:1, :, 2:-2, 2:-2], 1)
    along_y = divergence(padded[:, 2:-2, :, 2:-2], wind[1:2, 2:-2, :, 2:-2], 2)
    along_z = divergence(padded[:, 2:-2, 2:-2, :], wind[2:3, 2:-2, 2:-2, :], 3)
    return inner - time_step * (along_x + along_y + along_z)


def vertical_pad(array):
    return jnp.pad(array, ((0, 0), (0, 0), (0, 0), (2, 2)))


def pack_slots(targets, payload, groups, capacity):
    count = targets.shape[0]
    same = targets[:, None] == targets[None, :]
    earlier = jnp.arange(count)[None, :] < jnp.arange(count)[:, None]
    ranking = jnp.sum((same & earlier).astype(jnp.int32), axis=1)
    slot_index = targets * capacity + ranking
    placing = (slot_index[None, :] == jnp.arange(groups * capacity)[:, None]).astype(jnp.float32)
    return jnp.dot(placing, payload, precision=lax.Precision.HIGHEST)


def transport_all(fields, wind):
    for substep in range(STEPS):
        padded = extended(fields, (("gx", 1), ("gy", 2)), 2)
        fields = advance(vertical_pad(padded), wind)
    return fields


def shards(state, velocity, threshold, tile_owner, parcel_owner, parcel_count, parcel_share):
    groups = lax.axis_size("gx")
    rows_x = state.shape[1]
    width_y = state.shape[2]
    tile_slots = max(2, 2 * rows_x // groups)
    row_slots = max(2, 2 * parcel_owner.shape[1] // groups)
    wind = vertical_pad(extended(velocity, (("gx", 1), ("gy", 2)), 2))
    east = velocity[0, :, :, 0:LEVELS].transpose(0, 2, 1)
    north = velocity[1, :, :, 0:LEVELS].transpose(0, 2, 1)
    targets = tile_owner[0, :, 0]
    payload = jnp.stack([east, north], axis=1).reshape(rows_x, 2 * LEVELS * width_y)
    packed = pack_slots(targets, payload, groups, tile_slots).reshape(
        groups, tile_slots, 2, LEVELS, width_y
    )
    arrived = lax.all_to_all(packed, "gx", split_axis=0, concat_axis=0, tiled=True)
    stress = friction(arrived[:, :, 0], arrived[:, :, 1])
    lifting = jnp.maximum(stress - threshold[0][None, None, :], 0.0)
    flux = jnp.sum(lifting, axis=(0, 1)) / rows_x
    reach = (jnp.arange(width_y)[None, :] < parcel_count[0][:, None]).astype(jnp.float32)
    masses = flux[None, :] * parcel_share[0] * reach
    packed_rows = pack_slots(parcel_owner[0, :, 0], masses, groups, row_slots).reshape(
        groups, row_slots, width_y
    )
    landed = lax.all_to_all(packed_rows, "gx", split_axis=0, concat_axis=0, tiled=True)
    per_source = jnp.sum(landed, axis=1)
    landing = (jnp.arange(groups)[None, :] % rows_x == jnp.arange(rows_x)[:, None]).astype(
        jnp.float32
    )
    deposit = jnp.dot(landing, per_source, precision=lax.Precision.HIGHEST)
    dust = state[3:4].at[0, :, :, 0].add(deposit)
    fields = transport_all(jnp.concatenate([state[0:3], dust], axis=0), wind)
    return (fields, flux[None, :])


def solution(mesh):
    return jax.shard_map(
        shards,
        mesh=mesh,
        in_specs=(
            P(None, "gx", "gy", None),
            P(None, "gx", "gy", None),
            P("gx", "gy"),
            P("gy", "gx", None),
            P("gy", "gx", None),
            P("gy", "gx"),
            P("gy", "gx", None),
        ),
        out_specs=(P(None, "gx", "gy", None), P("gx", "gy")),
        check_vma=False,
    )
```

profile of v0, /device:TPU:3, one launch (start us, length us, event | category | flops | bytes accessed | tf_op | source)
XLA Modules:
  0.0 419.5 jit_solution(12813057573070141269)
XLA Ops:
  0.7 3.9 fusion.71
  4.6 2.2 copy.74
  6.8 0.6 copy.73
  7.7 0.2 convert_reduce_fusion
  7.9 1.0 fusion.29
  8.9 5.8 %all-to-all-start = ((f32[8,8,2,4,128]{4,1,3,2,0:T(8,128)}), f32[8,8,2,4,128]{4,1,3,2,0:T(8,128)S(1)}, u32[]{:S(2)}, u32[]{:S(2)}) async-start(f32[8,8,2,4,128]{4,1,3,2,0:T(8,128)} %fusion.29), calls=%async_computation | async-start | bytes 524288 | tf_op jit(solution)/shard_map/all_to_all | solution.py:104
  14.7 1.9 fusion.70
  16.6 3.1 collective-permute-start
  19.7 2.2 collective-permute-start.1
  21.9 0.5 and_select_fusion
  22.4 3.1 slice.322
  25.5 6.2 %slice.320 = f32[3,32,128,128]{3,2,1,0:T(8,128)} slice(f32[4,32,128,128]{3,2,1,0:T(8,128)} %param.9), slice={[0:3], [0:32], [0:128], [0:128]} | slice | bytes 12582912 | tf_op jit(solution)/shard_map/slice | solution.py:120
  31.7 2.4 copy.72
  34.1 0.9 convert_reduce_fusion.1
  35.0 1.2 multiply_add_fusion.2
  36.3 1.3 collective-permute-done
  37.6 3.4 constant_dynamic-update-slice_fusion.1
  41.1 3.0 copy-done.6
  44.1 0.7 fusion.69
  44.8 3.6 collective-permute-start.5
  48.4 3.0 collective-permute-start.4
  51.5 2.1 compare_bitcast_fusion.2
  53.6 0.5 fusion.65
  54.2 0.8 fusion.49
  55.0 4.2 all-to-all-start.1
  59.2 8.0 %select_maximum_fusion.9 = f32[3,36,132,132]{3,2,1,0:T(8,128)S(1)} fusion(f32[3,36,2,128]{3,2,1,0:T(2,128)S(1)} %collective-permute-done.5, f32[3,36,128,128]{3,2,1,0:T(8,128)} %copy-done.6, f32[3,36,2,128]{3,2,1,0:T(2,128)S(1)} %collective-permute-done.4), kind=kLoop, calls=%fused_computation.26 | loop fusion | flops 15054336 | bytes 14826240 | tf_op jit(solution)/shard_map/concatenate | solution.py:23
  67.2 5.3 %copy-done.4 = f32[3,36,132,132]{3,2,1,0:T(8,128)} copy-done((f32[3,36,132,132]{3,2,1,0:T(8,128)}, f32[3,36,132,132]{3,2,1,0:T(8,128)S(1)}, u32[]{:S(2)}) %copy-start.4) | copy-done | bytes 7527192
  72.5 4.2 %fusion.26 = f32[32,128,129]{2,1,0:T(8,128)} fusion(f32[3,36,132,132]{3,2,1,0:T(8,128)S(1)} %select_maximum_fusion.9), kind=kLoop, calls=%fused_computation.101 | loop fusion | flops 1056768 | bytes 6340608 | tf_op jit(solution)/shard_map/mul | solution.py:55
  76.7 4.5 %compare_bitcast_fusion.1 = (pred[32,129,128]{2,1,0:T(8,128)(4,1)}, f32[1,32,129,128]{3,2,1,0:T(8,128)}) fusion(f32[3,36,2,128]{3,2,1,0:T(2,128)S(1)} %collective-permute-done.5, f32[3,36,128,128]{3,2,1,0:T(8,128)} %copy-done.6, f32[3,36,2,128]{3,2,1,0:T(2,128)S(1)} %collective-permute-done.4), kind=kLoop, calls=%fused_computation.93 | loop fusion | flops 2641920 | bytes 9940992 | tf_op jit(solution)/shard_map/jit(_where)/broadcast_in_dim | solution.py:57
  81.3 0.1 fusion.25
  81.4 2.0 copy.58
  83.4 5.4 %scatter-add.4 = f32[1,32,128,128]{3,2,1,0:T(8,128)S(1)} dynamic-update-slice(f32[1,32,128,128]{3,2,1,0:T(8,128)S(1)} %slice-done.4, f32[1,32,128,1]{3,2,1,0:T(8,128)} %copy.58, s32[]{:T(128)} %constant.70.clone.1, s32[]{:T(128)} %constant.70.clone.1, s32[]{:T(128)} %constant.70.clone.1, s32[]{:T(128)} %constant.70.clone.1) | dynamic-update-slice | bytes 32772 | tf_op jit(solution)/shard_map/scatter-add | solution.py:119
  88.8 1.3 copy-done.1
  90.1 1.3 fusion.27
  91.5 2.2 collective-permute-start.3
  93.7 4.4 %collective-permute-start.2 = (f32[4,2,128,128]{3,2,1,0:T(8,128)S(1)}, f32[4,2,128,128]{3,2,1,0:T(8,128)S(1)}, u32[]{:S(2)}, u32[]{:S(2)}) collective-permute-start(f32[4,2,128,128]{3,2,1,0:T(8,128)S(1)} %get-tuple-element.32), channel_id=1, source_target_pairs={{0,4},{4,8},{8,12},{12,16},{16,20},{20,24},{24,28},{1,5},{5,9},{9,... | collective-permute-start | bytes 1572872 | tf_op jit(solution)/shard_map/ppermute | solution.py:19
  98.1 6.0 %compare_bitcast_fusion = pred[32,128,129]{2,1,0:T(8,128)(4,1)S(1)} fusion(f32[3,36,132,132]{3,2,1,0:T(8,128)} %copy-done.4), kind=kLoop, calls=%fused_computation.88 | loop fusion | flops 1585152 | bytes 4755456 | tf_op jit(solution)/shard_map/jit(_where)/broadcast_in_dim | solution.py:57
  104.1 4.1 collective-permute-done.3
  108.2 11.5 %collective-permute-done.2 = f32[4,2,128,128]{3,2,1,0:T(8,128)S(1)} collective-permute-done((f32[4,2,128,128]{3,2,1,0:T(8,128)S(1)}, f32[4,2,128,128]{3,2,1,0:T(8,128)S(1)}, u32[]{:S(2)}, u32[]{:S(2)}) %collective-permute-start.2) | collective-permute-done | bytes 524320 | tf_op jit(solution)/shard_map/ppermute | solution.py:19
  119.7 0.1 pad_maximum_fusion.16
  119.8 2.3 collective-permute-start.7
  122.2 0.7 copy.59
  122.9 3.3 collective-permute-start.6
  126.2 7.1 %maximum_maximum_fusion.2 = (f32[4,34,128,128]{3,2,1,0:T(8,128)}, f32[4,34,128,128]{3,2,1,0:T(8,128)}) fusion(f32[1,32,128,128]{3,2,1,0:T(8,128)S(1)} %copy-done.2, f32[3,32,128,128]{3,2,1,0:T(8,128)S(1)} %bitcast.65, f32[4,2,128,128]{3,2,1,0:T(8,128)S(1)} %collective-permute-done.2, f32[4,2,128,128]{3,2,1,0:T(8,128)S(1)} %collective-permute-done.3), kind=kLoop, calls=%fused_computation.42 | loop fusion | flops 8912896 | bytes 27262976 | tf_op jit(solution)/shard_map/concatenate | solution.py:23
  133.3 19.6 %multiply_select_fusion.5 = f32[4,33,128,128]{3,2,1,0:T(8,128)} fusion(f32[4,34,128,128]{3,2,1,0:T(8,128)} %get-tuple-element.31, f32[4,34,128,128]{3,2,1,0:T(8,128)} %get-tuple-element.30, f32[33,128,128]{2,1,0:T(8,128)} %bitcast.70, pred[33,128,128]{2,1,0:T(8,128)(4,1)S(1)} %copy-done.14), kind=kLoop, calls=%fused_computation.68 | loop fusion | flops 54067200 | bytes 45957120 | tf_op jit(solution)/shard_map/jit(_where)/select_n | solution.py:57
  153.0 1.0 copy.60
  154.0 22.3 %select_maximum_fusion.4 = f32[4,36,132,132]{3,2,1,0:T(8,128)} fusion(f32[4,36,2,128]{3,2,1,0:T(2,128)S(1)} %copy.62, f32[4,36,2,128]{3,2,1,0:T(2,128)S(1)} %copy.60, f32[4,2,128,128]{3,2,1,0:T(8,128)S(1)} %collective-permute-done.3, f32[4,2,128,128]{3,2,1,0:T(8,128)S(1)} %collective-permute-done.2, f32[1,32,128,128]{3,2,1,0:T(8,128)S(1)} %copy-done.2, ...), kind=kLoop, calls=%fused_computation.8 | loop fusion | flops 35126784 | bytes 19768320 | tf_op jit(solution)/shard_map/concatenate | solution.py:23
  176.3 38.5 %multiply_select_fusion.1 = f32[4,32,128,129]{3,2,1,0:T(8,128)} fusion(f32[4,36,132,132]{3,2,1,0:T(8,128)} %select_maximum_fusion.4, f32[32,128,129]{2,1,0:T(8,128)} %fusion.26, pred[32,128,129]{2,1,0:T(8,128)(4,1)S(1)} %compare_bitcast_fusion), kind=kLoop, calls=%fused_computation.22 | loop fusion | flops 52838400 | bytes 44912640 | tf_op jit(solution)/shard_map/jit(_where)/select_n | solution.py:57
  214.9 11.4 %maximum_maximum_fusion = (f32[4,36,130,128]{3,2,1,0:T(8,128)}, f32[4,36,130,128]{3,2,1,0:T(8,128)}) fusion(f32[4,2,128,128]{3,2,1,0:T(8,128)S(1)} %collective-permute-done.3, f32[1,32,128,128]{3,2,1,0:T(8,128)} %copy-done.1, f32[3,32,128,128]{3,2,1,0:T(8,128)S(1)} %bitcast.65, f32[4,2,128,128]{3,2,1,0:T(8,128)} %copy-done.11, ...), kind=kLoop, calls=%fused_computation.32 | loop fusion | flops 19169280 | bytes 28901376 | tf_op jit(solution)/shard_map/concatenate | solution.py:23
  226.3 19.3 %multiply_select_fusion.3 = f32[4,32,129,128]{3,2,1,0:T(8,128)} fusion(f32[4,36,130,128]{3,2,1,0:T(8,128)} %get-tuple-element.25, f32[4,36,130,128]{3,2,1,0:T(8,128)} %get-tuple-element.24, f32[32,129,128]{2,1,0:T(8,128)S(1)} %bitcast.68, pred[32,129,128]{2,1,0:T(8,128)(4,1)S(1)} %copy-done.12), kind=kLoop, calls=%fused_computation.52 | loop fusion | flops 52838400 | bytes 44912640 | tf_op jit(solution)/shard_map/jit(_where)/select_n | solution.py:57
  245.6 19.9 %fusion.12 = f32[4,32,128,128]{3,2,1,0:T(8,128)S(1)} fusion(f32[1,32,128,128]{3,2,1,0:T(8,128)S(1)} %copy-done.3, f32[3,32,128,128]{3,2,1,0:T(8,128)S(1)} %bitcast.65, f32[4,32,128,129]{3,2,1,0:T(8,128)} %multiply_select_fusion.1, f32[4,32,129,128]{3,2,1,0:T(8,128)} %multiply_select_fusion.3, f32[4,33,128,128]{3,2,1,0:T(8,128)} %multiply_select_fusion.5), kind=kLoop, calls=%fused_computation.72 | loop fusion | flops 16777216 | bytes 67108864 | tf_op jit(solution)/shard_map/sub | solution.py:66
  265.6 2.3 collective-permute-start.9
  267.9 4.2 collective-permute-start.8
  272.1 10.3 %collective-permute-done.9 = f32[4,2,128,128]{3,2,1,0:T(8,128)S(1)} collective-permute-done((f32[4,2,128,128]{3,2,1,0:T(8,128)S(1)}, f32[4,2,128,128]{3,2,1,0:T(8,128)S(1)}, u32[]{:S(2)}, u32[]{:S(2)}) %collective-permute-start.9) | collective-permute-done | bytes 524320 | tf_op jit(solution)/shard_map/ppermute | solution.py:22
  282.4 11.5 %collective-permute-done.8 = f32[4,2,128,128]{3,2,1,0:T(8,128)S(1)} collective-permute-done((f32[4,2,128,128]{3,2,1,0:T(8,128)S(1)}, f32[4,2,128,128]{3,2,1,0:T(8,128)S(1)}, u32[]{:S(2)}, u32[]{:S(2)}) %collective-permute-start.8) | collective-permute-done | bytes 524320 | tf_op jit(solution)/shard_map/ppermute | solution.py:19
  293.8 0.1 pad_maximum_fusion.12
  294.0 2.3 collective-permute-start.11
  296.3 3.2 collective-permute-start.10
  299.6 11.8 %multiply_select_fusion.4 = f32[4,33,128,128]{3,2,1,0:T(8,128)} fusion(f32[4,2,128,128]{3,2,1,0:T(8,128)S(1)} %collective-permute-done.9, f32[4,32,128,128]{3,2,1,0:T(8,128)S(1)} %fusion.12, f32[4,2,128,128]{3,2,1,0:T(8,128)S(1)} %collective-permute-done.8, f32[33,128,128]{2,1,0:T(8,128)S(1)} %bitcast.71, pred[33,128,128]{2,1,0:T(8,128)(4,1)S(1)} %copy-done.15), kind=kLoop, calls=%fused_computation.64 | loop fusion | flops 62717952 | bytes 20791296 | tf_op jit(solution)/shard_map/jit(_where)/select_n | solution.py:57
  311.6 18.0 %select_maximum_fusion = f32[4,36,132,132]{3,2,1,0:T(8,128)} fusion(f32[4,36,2,128]{3,2,1,0:T(2,128)S(1)} %copy.68, f32[4,36,2,128]{3,2,1,0:T(2,128)S(1)} %copy.66, f32[4,2,128,128]{3,2,1,0:T(8,128)S(1)} %collective-permute-done.9, f32[4,32,128,128]{3,2,1,0:T(8,128)S(1)} %fusion.12, f32[4,2,128,128]{3,2,1,0:T(8,128)S(1)} %collective-permute-done.8), kind=kLoop, calls=%fused_computation.4 | loop fusion | flops 30108672 | bytes 19768320 | tf_op jit(solution)/shard_map/concatenate | solution.py:23
  329.6 37.5 %multiply_select_fusion = f32[4,32,128,129]{3,2,1,0:T(8,128)} fusion(f32[4,36,132,132]{3,2,1,0:T(8,128)} %select_maximum_fusion, f32[32,128,129]{2,1,0:T(8,128)S(1)} %copy-done.5, pred[32,128,129]{2,1,0:T(8,128)(4,1)S(1)} %compare_bitcast_fusion), kind=kLoop, calls=%fused_computation.18 | loop fusion | flops 52838400 | bytes 44912640 | tf_op jit(solution)/shard_map/jit(_where)/select_n | solution.py:57
  367.1 11.9 %maximum_maximum_fusion.1 = (f32[4,36,130,128]{3,2,1,0:T(8,128)S(1)}, f32[4,36,130,128]{3,2,1,0:T(8,128)}) fusion(f32[4,2,128,128]{3,2,1,0:T(8,128)S(1)} %collective-permute-done.9, f32[4,32,128,128]{3,2,1,0:T(8,128)} %copy-done, f32[4,2,128,128]{3,2,1,0:T(8,128)} %copy-done.10, f32[4,36,2,128]{3,2,1,0:T(2,128)S(1)} %copy.66, f32[4,36,2,128]{3,2,1,0:T(2,128)S(1)} %copy.68), kind=kLoop, calls=%fused_computation.34 | loop fusion | flops 14376960 | bytes 28901376 | tf_op jit(solution)/shard_map/concatenate | solution.py:23
  379.0 17.0 %multiply_select_fusion.2 = f32[4,32,129,128]{3,2,1,0:T(8,128)} fusion(f32[4,36,130,128]{3,2,1,0:T(8,128)} %get-tuple-element.21, f32[4,36,130,128]{3,2,1,0:T(8,128)S(1)} %get-tuple-element.20, f32[32,129,128]{2,1,0:T(8,128)S(1)} %bitcast.69, pred[32,129,128]{2,1,0:T(8,128)(4,1)S(1)} %copy-done.13), kind=kLoop, calls=%fused_computation.48 | loop fusion | flops 52838400 | bytes 44912640 | tf_op jit(solution)/shard_map/jit(_where)/select_n | solution.py:57
  396.0 23.3 %fusion.15 = f32[4,32,128,128]{3,2,1,0:T(8,128)} fusion(f32[4,32,128,128]{3,2,1,0:T(8,128)S(1)} %bitcast.63, f32[4,32,128,129]{3,2,1,0:T(8,128)} %multiply_select_fusion, f32[4,32,129,128]{3,2,1,0:T(8,128)} %multiply_select_fusion.2, f32[4,33,128,128]{3,2,1,0:T(8,128)} %multiply_select_fusion.4), kind=kLoop, calls=%fused_computation.76 | loop fusion | flops 14680064 | bytes 67108864 | tf_op jit(solution)/shard_map/sub | solution.py:66
  (89 shorter events, 0.9 us)
Async XLA Ops:
  0.6 7.1 %copy-start.21 = (s32[1,32,1]{1,2,0:T(1,128)S(1)}, s32[1,32,1]{1,2,0:T(1,128)}, u32[]{:S(2)}) copy-start(s32[1,32,1]{1,2,0:T(1,128)} %param.12) | copy-start | bytes 388
  0.7 16.0 %copy-start.16 = (s32[8,8]{1,0:T(8,128)}, s32[8,8]{1,0:T(8,128)S(1)}, u32[]{:S(2)}) copy-start(s32[8,8]{1,0:T(8,128)S(1)} %multiply_add_fusion) | copy-start | bytes 772
  8.9 44.7 %all-to-all-start = ((f32[8,8,2,4,128]{4,1,3,2,0:T(8,128)}), f32[8,8,2,4,128]{4,1,3,2,0:T(8,128)S(1)}, u32[]{:S(2)}, u32[]{:S(2)}) async-start(f32[8,8,2,4,128]{4,1,3,2,0:T(8,128)} %fusion.29), calls=%async_computation | async-start | bytes 524288 | tf_op jit(solution)/shard_map/all_to_all | solution.py:104
  16.6 21.0 %collective-permute-start = (f32[3,2,128,128]{3,2,1,0:T(8,128)}, f32[3,2,128,128]{3,2,1,0:T(8,128)S(1)}, u32[]{:S(2)}, u32[]{:S(2)}) collective-permute-start(f32[3,2,128,128]{3,2,1,0:T(8,128)} %get-tuple-element.37), channel_id=1, source_target_pairs={{0,4},{4,8},{8,12},{12,16},{16,20},{20,24},{24,28},{1,5},{5,9},{9,... | collective-permute-start | bytes 1179656 | tf_op jit(solution)/shard_map/ppermute | solution.py:19
  19.7 21.3 %collective-permute-start.1 = (f32[3,2,128,128]{3,2,1,0:T(8,128)S(1)}, f32[3,2,128,128]{3,2,1,0:T(8,128)S(1)}, u32[]{:S(2)}, u32[]{:S(2)}) collective-permute-start(f32[3,2,128,128]{3,2,1,0:T(8,128)S(1)} %get-tuple-element.36), channel_id=1, source_target_pairs={{4,0},{8,4},{12,8},{16,12},{20,16},{24,20},{28,24},{5,1},{9,5},{13... | collective-permute-start | bytes 1179656 | tf_op jit(solution)/shard_map/ppermute | solution.py:22
  31.7 19.7 %slice-start.5 = ((s8[6291456]{0:T(1024)(128)(4,1)}), s8[2097152]{0:T(1024)(128)(4,1)S(1)}, s32[]{:S(2)}) async-start(s8[6291456]{0:T(1024)(128)(4,1)} %bitcast.66), calls=%async_computation.7 | async-start | bytes 4194304
  37.6 13.8 %slice-start.6 = ((s8[6291456]{0:T(1024)(128)(4,1)}), s8[4194304]{0:T(1024)(128)(4,1)S(1)}, s32[]{:S(2)}) async-start(s8[6291456]{0:T(1024)(128)(4,1)} %bitcast.66), calls=%async_computation.8 | async-start | bytes 8388608
  41.0 12.6 %copy-start.18 = (f32[1,128]{1,0:T(1,128)S(1)}, f32[1,128]{1,0:T(1,128)}, u32[]{:S(2)}) copy-start(f32[1,128]{1,0:T(1,128)} %param.11) | copy-start | bytes 1540
  41.0 13.1 %copy-start.17 = (s32[8,8]{1,0:T(8,128)S(1)}, s32[8,8]{1,0:T(8,128)}, u32[]{:S(2)}) copy-start(s32[8,8]{1,0:T(8,128)} %copy-done.16) | copy-start | bytes 772
  41.0 13.1 %copy-start.20 = (f32[1,32,128]{2,1,0:T(8,128)S(1)}, f32[1,32,128]{2,1,0:T(8,128)}, u32[]{:S(2)}) copy-start(f32[1,32,128]{2,1,0:T(8,128)} %param.15) | copy-start | bytes 49156
  41.1 13.1 %copy-start.22 = (s32[1,32]{1,0:T(1,128)S(1)}, s32[1,32]{1,0:T(1,128)}, u32[]{:S(2)}) copy-start(s32[1,32]{1,0:T(1,128)} %param.14) | copy-start | bytes 388
  41.1 13.1 %copy-start.23 = (s32[32]{0:T(128)S(1)}, s32[32]{0:T(128)}, u32[]{:S(2)}) copy-start(s32[32]{0:T(128)} %multiply_add_fusion.2) | copy-start | bytes 388
  41.1 3.0 copy-start.6
  44.8 14.4 %collective-permute-start.5 = (f32[3,36,2,128]{3,2,1,0:T(2,128)}, f32[3,36,2,128]{3,2,1,0:T(2,128)S(1)}, u32[]{:S(2)}, u32[]{:S(2)}) collective-permute-start(f32[3,36,2,128]{3,2,1,0:T(2,128)} %get-tuple-element.35), channel_id=1, source_target_pairs={{1,0},{2,1},{3,2},{5,4},{6,5},{7,6},{9,8},{10,9},{11,10},{13,12},{... | collective-permute-start | bytes 331784 | tf_op jit(solution)/shard_map/ppermute | solution.py:22
  48.4 10.8 %collective-permute-start.4 = (f32[3,36,2,128]{3,2,1,0:T(2,128)S(1)}, f32[3,36,2,128]{3,2,1,0:T(2,128)S(1)}, u32[]{:S(2)}, u32[]{:S(2)}) collective-permute-start(f32[3,36,2,128]{3,2,1,0:T(2,128)S(1)} %get-tuple-element.34), channel_id=1, source_target_pairs={{0,1},{1,2},{2,3},{4,5},{5,6},{6,7},{8,9},{9,10},{10,11},{12,13},{... | collective-permute-start | bytes 331784 | tf_op jit(solution)/shard_map/ppermute | solution.py:19
  55.0 26.2 %all-to-all-start.1 = ((f32[8,8,128]{2,1,0:T(8,128)}), f32[8,8,128]{2,1,0:T(8,128)S(1)}, u32[]{:S(2)}, u32[]{:S(2)}) async-start(f32[8,8,128]{2,1,0:T(8,128)} %fusion.49), calls=%async_computation.1 | async-start | bytes 65536 | tf_op jit(solution)/shard_map/all_to_all | solution.py:113
  67.2 5.3 %copy-start.4 = (f32[3,36,132,132]{3,2,1,0:T(8,128)}, f32[3,36,132,132]{3,2,1,0:T(8,128)S(1)}, u32[]{:S(2)}) copy-start(f32[3,36,132,132]{3,2,1,0:T(8,128)S(1)} %select_maximum_fusion.9) | copy-start | bytes 22581508
  72.5 8.8 %copy-start.19 = (s32[8]{0:T(128)S(1)}, s32[8]{0:T(128)}, u32[]{:S(2)}) copy-start(s32[8]{0:T(128)} %and_select_fusion) | copy-start | bytes 100
  76.7 6.6 %slice-start.4 = ((f32[4,32,128,128]{3,2,1,0:T(8,128)}), f32[1,32,128,128]{3,2,1,0:T(8,128)S(1)}, s32[]{:S(2)}) async-start(f32[4,32,128,128]{3,2,1,0:T(8,128)} %param.9), calls=%async_computation.6 | async-start | bytes 4194304 | tf_op jit(solution)/shard_map/slice | solution.py:119
  88.8 1.3 copy-start.1
  90.1 29.6 %slice-start.2 = ((s8[6291456]{0:T(1024)(128)(4,1)}), s8[4194304]{0:T(1024)(128)(4,1)S(1)}, s32[]{:S(2)}) async-start(s8[6291456]{0:T(1024)(128)(4,1)} %bitcast.64), calls=%async_computation.4 | async-start | bytes 8388608
  91.4 28.2 %copy-start.2 = (f32[1,32,128,128]{3,2,1,0:T(8,128)S(1)}, f32[1,32,128,128]{3,2,1,0:T(8,128)}, u32[]{:S(2)}) copy-start(f32[1,32,128,128]{3,2,1,0:T(8,128)} %copy-done.1) | copy-start | bytes 6291460
  91.5 28.2 %slice-start.3 = ((s8[6291456]{0:T(1024)(128)(4,1)}), s8[2097152]{0:T(1024)(128)(4,1)S(1)}, s32[]{:S(2)}) async-start(s8[6291456]{0:T(1024)(128)(4,1)} %bitcast.64), calls=%async_computation.5 | async-start | bytes 4194304
  91.5 16.7 %collective-permute-start.3 = (f32[4,2,128,128]{3,2,1,0:T(8,128)S(1)}, f32[4,2,128,128]{3,2,1,0:T(8,128)S(1)}, u32[]{:S(2)}, u32[]{:S(2)}) collective-permute-start(f32[4,2,128,128]{3,2,1,0:T(8,128)S(1)} %get-tuple-element.33), channel_id=1, source_target_pairs={{4,0},{8,4},{12,8},{16,12},{20,16},{24,20},{28,24},{5,1},{9,5},{13... | collective-permute-start | bytes 1572872 | tf_op jit(solution)/shard_map/ppermute | solution.py:22
  93.7 26.0 %collective-permute-start.2 = (f32[4,2,128,128]{3,2,1,0:T(8,128)S(1)}, f32[4,2,128,128]{3,2,1,0:T(8,128)S(1)}, u32[]{:S(2)}, u32[]{:S(2)}) collective-permute-start(f32[4,2,128,128]{3,2,1,0:T(8,128)S(1)} %get-tuple-element.32), channel_id=1, source_target_pairs={{0,4},{4,8},{8,12},{12,16},{16,20},{20,24},{24,28},{1,5},{5,9},{9,... | collective-permute-start | bytes 1572872 | tf_op jit(solution)/shard_map/ppermute | solution.py:19
  119.7 34.3 %copy-start.11 = (f32[4,2,128,128]{3,2,1,0:T(8,128)}, f32[4,2,128,128]{3,2,1,0:T(8,128)S(1)}, u32[]{:S(2)}) copy-start(f32[4,2,128,128]{3,2,1,0:T(8,128)S(1)} %collective-permute-done.2) | copy-start | bytes 1572868
  119.8 33.1 %collective-permute-start.7 = (f32[4,36,2,128]{3,1,2,0:T(8,128)S(1)}, f32[4,36,2,128]{3,1,2,0:T(8,128)S(1)}, u32[]{:S(2)}, u32[]{:S(2)}) collective-permute-start(f32[4,36,2,128]{3,1,2,0:T(8,128)S(1)} %copy.61), channel_id=1, source_target_pairs={{1,0},{2,1},{3,2},{5,4},{6,5},{7,6},{9,8},{10,9},{11,10},{13,12},{... | collective-permute-start | bytes 442376 | tf_op jit(solution)/shard_map/ppermute | solution.py:22
  122.9 10.5 %copy-start.14 = (pred[33,128,128]{2,1,0:T(8,128)(4,1)S(1)}, pred[33,128,128]{2,1,0:T(8,128)(4,1)}, u32[]{:S(2)}) copy-start(pred[33,128,128]{2,1,0:T(8,128)(4,1)} %get-tuple-element.16) | copy-start | bytes 1622020
  122.9 30.2 %collective-permute-start.6 = (f32[4,36,2,128]{3,1,2,0:T(8,128)}, f32[4,36,2,128]{3,1,2,0:T(8,128)}, u32[]{:S(2)}, u32[]{:S(2)}) collective-permute-start(f32[4,36,2,128]{3,1,2,0:T(8,128)} %copy.59), channel_id=1, source_target_pairs={{0,1},{1,2},{2,3},{4,5},{5,6},{6,7},{8,9},{9,10},{10,11},{12,13},{... | collective-permute-start | bytes 442376 | tf_op jit(solution)/shard_map/ppermute | solution.py:19
  214.9 11.4 %copy-start.7 = (f32[1,32,129,128]{3,2,1,0:T(8,128)S(1)}, f32[1,32,129,128]{3,2,1,0:T(8,128)}, u32[]{:S(2)}) copy-start(f32[1,32,129,128]{3,2,1,0:T(8,128)} %get-tuple-element.19) | copy-start | bytes 6340612
  214.9 11.4 %copy-start.12 = (pred[32,129,128]{2,1,0:T(8,128)(4,1)S(1)}, pred[32,129,128]{2,1,0:T(8,128)(4,1)}, u32[]{:S(2)}) copy-start(pred[32,129,128]{2,1,0:T(8,128)(4,1)} %get-tuple-element.18) | copy-start | bytes 1585156
  226.2 19.3 %copy-start.3 = (f32[1,32,128,128]{3,2,1,0:T(8,128)S(1)}, f32[1,32,128,128]{3,2,1,0:T(8,128)}, u32[]{:S(2)}) copy-start(f32[1,32,128,128]{3,2,1,0:T(8,128)} %copy-done.1) | copy-start | bytes 6291460
  265.5 46.1 %copy-start = (f32[4,32,128,128]{3,2,1,0:T(8,128)}, f32[4,32,128,128]{3,2,1,0:T(8,128)S(1)}, u32[]{:S(2)}) copy-start(f32[4,32,128,128]{3,2,1,0:T(8,128)S(1)} %fusion.12) | copy-start | bytes 25165828
  265.5 34.0 %copy-start.9 = (f32[1,33,128,128]{3,2,1,0:T(8,128)S(1)}, f32[1,33,128,128]{3,2,1,0:T(8,128)}, u32[]{:S(2)}) copy-start(f32[1,33,128,128]{3,2,1,0:T(8,128)} %get-tuple-element.17) | copy-start | bytes 6488068
  265.5 34.0 %copy-start.15 = (pred[33,128,128]{2,1,0:T(8,128)(4,1)S(1)}, pred[33,128,128]{2,1,0:T(8,128)(4,1)}, u32[]{:S(2)}) copy-start(pred[33,128,128]{2,1,0:T(8,128)(4,1)} %get-tuple-element.16) | copy-start | bytes 1622020
  265.6 16.7 %collective-permute-start.9 = (f32[4,2,128,128]{3,2,1,0:T(8,128)S(1)}, f32[4,2,128,128]{3,2,1,0:T(8,128)S(1)}, u32[]{:S(2)}, u32[]{:S(2)}) collective-permute-start(f32[4,2,128,128]{3,2,1,0:T(8,128)S(1)} %get-tuple-element.29), channel_id=1, source_target_pairs={{4,0},{8,4},{12,8},{16,12},{20,16},{24,20},{28,24},{5,1},{9,5},{13... | collective-permute-start | bytes 1572872 | tf_op jit(solution)/shard_map/ppermute | solution.py:22
  267.9 25.9 %collective-permute-start.8 = (f32[4,2,128,128]{3,2,1,0:T(8,128)S(1)}, f32[4,2,128,128]{3,2,1,0:T(8,128)S(1)}, u32[]{:S(2)}, u32[]{:S(2)}) collective-permute-start(f32[4,2,128,128]{3,2,1,0:T(8,128)S(1)} %get-tuple-element.28), channel_id=1, source_target_pairs={{0,4},{4,8},{8,12},{12,16},{16,20},{20,24},{24,28},{1,5},{5,9},{9,... | collective-permute-start | bytes 1572872 | tf_op jit(solution)/shard_map/ppermute | solution.py:19
  293.8 17.7 %copy-start.10 = (f32[4,2,128,128]{3,2,1,0:T(8,128)}, f32[4,2,128,128]{3,2,1,0:T(8,128)S(1)}, u32[]{:S(2)}) copy-start(f32[4,2,128,128]{3,2,1,0:T(8,128)S(1)} %collective-permute-done.8) | copy-start | bytes 1572868
  294.0 17.4 %collective-permute-start.11 = (f32[4,36,2,128]{3,1,2,0:T(8,128)S(1)}, f32[4,36,2,128]{3,1,2,0:T(8,128)S(1)}, u32[]{:S(2)}, u32[]{:S(2)}) collective-permute-start(f32[4,36,2,128]{3,1,2,0:T(8,128)S(1)} %copy.67), channel_id=1, source_target_pairs={{1,0},{2,1},{3,2},{5,4},{6,5},{7,6},{9,8},{10,9},{11,10},{13,12},{... | collective-permute-start | bytes 442376 | tf_op jit(solution)/shard_map/ppermute | solution.py:22
  296.3 15.2 %collective-permute-start.10 = (f32[4,36,2,128]{3,1,2,0:T(8,128)S(1)}, f32[4,36,2,128]{3,1,2,0:T(8,128)S(1)}, u32[]{:S(2)}, u32[]{:S(2)}) collective-permute-start(f32[4,36,2,128]{3,1,2,0:T(8,128)S(1)} %copy.65), channel_id=1, source_target_pairs={{0,1},{1,2},{2,3},{4,5},{5,6},{6,7},{8,9},{9,10},{10,11},{12,13},{... | collective-permute-start | bytes 442376 | tf_op jit(solution)/shard_map/ppermute | solution.py:19
  311.6 18.0 %copy-start.5 = (f32[32,128,129]{2,1,0:T(8,128)S(1)}, f32[32,128,129]{2,1,0:T(8,128)}, u32[]{:S(2)}) copy-start(f32[32,128,129]{2,1,0:T(8,128)} %fusion.26) | copy-start | bytes 6340612
  367.1 11.9 %copy-start.8 = (f32[1,32,129,128]{3,2,1,0:T(8,128)S(1)}, f32[1,32,129,128]{3,2,1,0:T(8,128)}, u32[]{:S(2)}) copy-start(f32[1,32,129,128]{3,2,1,0:T(8,128)} %get-tuple-element.19) | copy-start | bytes 6340612
  367.1 11.9 %copy-start.13 = (pred[32,129,128]{2,1,0:T(8,128)(4,1)S(1)}, pred[32,129,128]{2,1,0:T(8,128)(4,1)}, u32[]{:S(2)}) copy-start(pred[32,129,128]{2,1,0:T(8,128)(4,1)} %get-tuple-element.18) | copy-start | bytes 1585156
  367.1 28.9 %slice-start = ((s8[8388608]{0:T(1024)(128)(4,1)}), s8[4194304]{0:T(1024)(128)(4,1)S(1)}, s32[]{:S(2)}) async-start(s8[8388608]{0:T(1024)(128)(4,1)} %bitcast.62), calls=%async_computation.2 | async-start | bytes 8388608
  379.0 17.0 %slice-start.1 = ((s8[8388608]{0:T(1024)(128)(4,1)}), s8[4194304]{0:T(1024)(128)(4,1)S(1)}, s32[]{:S(2)}) async-start(s8[8388608]{0:T(1024)(128)(4,1)} %bitcast.62), calls=%async_computation.3 | async-start | bytes 8388608
where the time goes:
time: 428 us; the launch traced here: 420 us
  other arithmetic  287 us (67%)
  starting transfers between devices  46.3 us (11%)
  local copies, waits for them, and re-layouts  43.8 us (10%)
  waiting for transfers between devices  38.6 us (9%)
    select_n x6, other arithmetic, divergence(): fluxes = jnp.where(face_speed > 0, upwind, downwind)  144 us
    concatenate x6, other arithmetic, extended(): block = jnp.concatenate([low, block, high], axis=dim)  78.7 us
    sub x2, other arithmetic, advance(): return inner - time_step * (along_x + along_y + along_z)  43.2 us
    ppermute x6, waiting for transfers between devices, extended(): lax.ppermute(lax.slice_in_dim(block, block.shape[dim] - width, None, axis...  24.3 us
    ppermute x6, starting transfers between devices, extended(): lax.ppermute(lax.slice_in_dim(block, block.shape[dim] - width, None, axis...  21.3 us
    unnamed x65, local copies, waits for them, and re-layouts  18.3 us
    ppermute x6, starting transfers between devices, extended(): lax.ppermute(lax.slice_in_dim(block, 0, width, axis=dim), axis, backward)  15 us
    ppermute x6, waiting for transfers between devices, extended(): lax.ppermute(lax.slice_in_dim(block, 0, width, axis=dim), axis, backward)  14.3 us
  transfers between devices with their start and end apart: 14, of which 5 were waited for; matrix products, arithmetic and copies ran while one was open for 20% of the time, Pallas kernels for 0%

commit v1 on v0

v1 whole, which is shorter than its diff:
```python
import functools

import jax
import jax.numpy as jnp
from jax import lax
from jax.experimental import pallas as pl
from jax.experimental.pallas import tpu as pltpu
from jax.sharding import PartitionSpec as P

LEVELS = 4
profile_weights = (0.4, 0.3, 0.2, 0.1)
time_step = 0.1
FACTOR = 0.25 * time_step

VMEM_LIMIT = 48 * 1024 * 1024
PAD = 8
CHUNK = 4
HIGHEST = lax.Precision.HIGHEST
ANY = pl.BlockSpec(memory_space=pl.ANY)
VMEM = pl.BlockSpec(memory_space=pltpu.VMEM)
SMEM = pl.BlockSpec(memory_space=pltpu.SMEM)


def params():
    return pltpu.CompilerParams(vmem_limit_bytes=VMEM_LIMIT)


def cost(flops, moved):
    return pl.CostEstimate(flops=int(flops), bytes_accessed=int(moved), transcendentals=0)


def minmod(a, b):
    return jnp.maximum(jnp.minimum(a, b), jnp.minimum(jnp.maximum(a, b), 0.0))


def tile_rows(row, count):
    return pl.ds(PAD + row, 8, stride=count)


class Fields:
    def __init__(self, q, u, v, w, fx, lx, block, comps, rows, u_at, v_at):
        self.q, self.u, self.v, self.w, self.fx, self.lx = q, u, v, w, fx, lx
        self.block, self.comps, self.u_at, self.v_at = block, comps, u_at, v_at
        self.tiles = rows // 8

    def field(self, c, slab, row):
        return self.q[self.block, c, slab, tile_rows(row, self.tiles), :]

    def east(self, slab, row):
        return self.u[self.block, slab + self.u_at, pl.ds(row, 8, stride=self.tiles), :]

    def north(self, slab, row):
        return self.v[self.block, slab + self.v_at, tile_rows(row, self.tiles), :]

    def up(self, slab, row):
        return self.w[self.block, slab + self.v_at, pl.ds(row, 8, stride=self.tiles), :]


def first_face(f):
    for t in range(f.tiles):
        speed = FACTOR * (f.east(0, t) + f.east(1, t))
        right = speed > 0
        for c in range(f.comps):
            a, b, q0, q1 = [f.field(c, s, t) for s in range(4)]
            middle = q0 - b
            left_state = (b + b) + minmod(middle, b - a)
            slope = minmod(q1 - q0, middle)
            twice = q0 + q0
            f.fx[t, c] = speed * jnp.where(right, left_state, twice - slope)
            f.lx[t, c] = twice + slope


def slab_step(f, k, put):
    slab = k + 2
    lane = lax.broadcasted_iota(jnp.int32, (8, f.q.shape[-1]), 1)
    top = f.q.shape[-1] - 1
    is_first, is_last = lane == 0, lane == top
    carry = []
    north_here = f.north(k, 0)
    speed = FACTOR * (f.north(k, -1) + north_here)
    for c in range(f.comps):
        a, b, q0, q1 = [f.field(c, slab, r) for r in (-2, -1, 0, 1)]
        middle, ahead = q0 - b, q1 - q0
        left_state = (b + b) + minmod(middle, b - a)
        slope = minmod(ahead, middle)
        twice = q0 + q0
        flux = speed * jnp.where(speed > 0, left_state, twice - slope)
        carry.append((q0, q1, ahead, twice, twice + slope, flux))
    for t in range(f.tiles):
        speed_x = FACTOR * (f.east(k + 1, t) + f.east(k + 2, t))
        north_next = f.north(k, t + 1)
        speed_y = FACTOR * (north_here + north_next)
        north_here = north_next
        rise = FACTOR * f.up(k, t)
        speed_z = rise + pltpu.roll(rise, top, 1)
        speed_z = jnp.where(is_last, jnp.maximum(rise, 0.0), speed_z)
        ground = jnp.minimum(rise, 0.0)
        go_x, go_y, go_z = speed_x > 0, speed_y > 0, speed_z > 0
        for c in range(f.comps):
            q0, y1, ahead, twice, left_y, flux_y = carry[c]
            y2 = f.field(c, slab, t + 2)
            beyond = y2 - y1
            slope = minmod(beyond, ahead)
            twice_y = y1 + y1
            flux_next = speed_y * jnp.where(go_y, left_y, twice_y - slope)
            total = flux_next - flux_y
            carry[c] = (y1, y2, beyond, twice_y, twice_y + slope, flux_next)
            x1, x2 = f.field(c, slab + 1, t), f.field(c, slab + 2, t)
            slope = minmod(x2 - x1, x1 - q0)
            twice_x = x1 + x1
            flux_x = speed_x * jnp.where(go_x, f.lx[t, c], twice_x - slope)
            total = total + (flux_x - f.fx[t, c])
            f.fx[t, c] = flux_x
            f.lx[t, c] = twice_x + slope
            d = jnp.where(is_last, 0.0, pltpu.roll(q0, top, 1)) - q0
            below = jnp.where(is_first, q0, pltpu.roll(d, 1, 1))
            slope = minmod(d, below)
            lower = twice - slope
            flux_z = speed_z * jnp.where(go_z, twice + slope, pltpu.roll(lower, top, 1))
            flux_below = jnp.where(is_first, ground * lower, pltpu.roll(flux_z, 1, 1))
            total = total + (flux_z - flux_below)
            put(c, t, q0 - total)


def insert_y_halo(q, v, block, slab, v_slab, x, below, above, v_below, v_above, comps, rows):
    for c in range(comps):
        for r in range(2):
            q[block, c, slab, PAD - 2 + r : PAD - 1 + r, :] = below[2 * c + r, pl.ds(x, 1), :]
            q[block, c, slab, PAD + rows + r : PAD + rows + r + 1, :] = above[2 * c + r, pl.ds(x, 1), :]
    if v_slab is not None:
        v[block, v_slab, PAD - 1 : PAD, :] = v_below[0, pl.ds(x, 1), :]
        v[block, v_slab, PAD + rows : PAD + rows + 1, :] = v_above[0, pl.ds(x, 1), :]


def add_deposit(q, block, c, slab, column, deposit, rows):
    lanes = deposit.shape[-1]
    lane = lax.broadcasted_iota(jnp.int32, (rows, lanes), 1)
    turned = pltpu.roll(deposit[...], lanes - column, 1)
    here = q[block, c, slab, PAD : PAD + rows, :]
    q[block, c, slab, PAD : PAD + rows, :] = here + jnp.where(lane == 0, turned, 0.0)


def interior_kernel(sources, dusty, pack, count, *refs):
    refs = list(refs)
    fields, velocity = refs[:count], refs[count]
    below, above, v_below, v_above = refs[count + 1 : count + 5]
    del refs[: count + 5]
    deposit = refs.pop(0) if dusty else None
    out = refs.pop(0)
    if pack:
        pack_low, pack_high = refs.pop(0), refs.pop(0)
    q, u, v, w, fx, lx, stage, in_sem, out_sem = refs
    comps = len(sources)
    slabs, rows = q.shape[2], stage.shape[2]
    chunks = slabs // CHUNK
    inner = pl.ds(PAD, rows)

    def start(source, target, sem):
        pltpu.make_async_copy(source, target, sem).start()

    for j in range(chunks):
        at = j * CHUNK
        for c, (number, part, low, high, edge_part) in enumerate(sources):
            begin, end = at, at + CHUNK
            if low is not None and j == 0:
                begin += 2
                start(fields[low].at[edge_part], q.at[0, c, pl.ds(0, 2), inner], in_sem.at[j, c])
            if high is not None and j == chunks - 1:
                end -= 2
                start(fields[high].at[edge_part], q.at[0, c, pl.ds(slabs - 2, 2), inner], in_sem.at[j, c])
            span = pl.ds(begin, end - begin)
            start(fields[number].at[part, span], q.at[0, c, span, inner], in_sem.at[j, c])
        span = pl.ds(at, CHUNK)
        start(velocity.at[0, span], u.at[0, span], in_sem.at[j, comps])
        start(velocity.at[1, span], v.at[0, span, inner], in_sem.at[j, comps + 1])
        start(velocity.at[2, span], w.at[0, span], in_sem.at[j, comps + 2])

    def arrive(j):
        span = pl.ds(j * CHUNK, CHUNK)
        spots = [q.at[0, c, span, inner] for c in range(comps)]
        spots += [u.at[0, span], v.at[0, span, inner], w.at[0, span]]
        for n, spot in enumerate(spots):
            pltpu.make_async_copy(spot, spot, in_sem.at[j, n]).wait()

        def complete(x, _):
            insert_y_halo(q, v, 0, x, x, x, below, above, v_below, v_above, comps, rows)
            if dusty:
                add_deposit(q, 0, comps - 1, x, x + 2, deposit, rows)
            return 0

        lax.fori_loop(j * CHUNK, (j + 1) * CHUNK, complete, 0)

    f = Fields(q, u, v, w, fx, lx, 0, comps, rows, 1, 2)
    arrive(0)
    first_face(f)

    def step(k, _):
        @pl.when(k % CHUNK == 0)
        def _():
            arrive(k // CHUNK + 1)

        def put(c, t, value):
            stage[c, k, pl.ds(t, 8, stride=f.tiles), :] = value

        slab_step(f, k, put)
        pltpu.make_async_copy(stage.at[:, k], out.at[:, k + 2], out_sem).start()
        if pack:
            for c in range(comps):
                for r in range(2):
                    pack_low[2 * c + r, pl.ds(k + 2, 1), :] = stage[c, k, r : r + 1, :]
                    pack_high[2 * c + r, pl.ds(k + 2, 1), :] = stage[c, k, rows - 2 + r : rows - 1 + r, :]
        return 0

    if pack:
        pack_low[...] = jnp.zeros_like(pack_low)
        pack_high[...] = jnp.zeros_like(pack_high)
    lax.fori_loop(0, slabs - 4, step, 0)
    pltpu.make_async_copy(stage, out.at[:, pl.ds(2, slabs - 4)], out_sem).wait()


def interior(fields, sources, velocity, below, above, v_below, v_above, deposit, pack):
    comps = len(sources)
    _, slabs, rows, lanes = velocity.shape
    out_shape = [jax.ShapeDtypeStruct((comps, slabs, rows, lanes), jnp.float32)]
    out_specs = [ANY]
    if pack:
        out_shape += [jax.ShapeDtypeStruct((2 * comps, slabs, lanes), jnp.float32)] * 2
        out_specs += [VMEM] * 2
    operands = list(fields) + [velocity, below, above, v_below, v_above]
    specs = [ANY] * (len(fields) + 1) + [VMEM] * 4
    if deposit is not None:
        operands.append(deposit)
        specs.append(VMEM)
    high = rows + 2 * PAD
    cells = comps * (slabs - 4) * rows * lanes
    return pl.pallas_call(
        functools.partial(interior_kernel, sources, deposit is not None, pack, len(fields)),
        out_shape=tuple(out_shape),
        in_specs=specs,
        out_specs=tuple(out_specs),
        scratch_shapes=[
            pltpu.VMEM((1, comps, slabs, high, lanes), jnp.float32),
            pltpu.VMEM((1, slabs, rows, lanes), jnp.float32),
            pltpu.VMEM((1, slabs, high, lanes), jnp.float32),
            pltpu.VMEM((1, slabs, rows, lanes), jnp.float32),
            pltpu.VMEM((rows // 8, comps, 8, lanes), jnp.float32),
            pltpu.VMEM((rows // 8, comps, 8, lanes), jnp.float32),
            pltpu.VMEM((comps, slabs - 4, rows, lanes), jnp.float32),
            pltpu.SemaphoreType.DMA((slabs // CHUNK, comps + 3)),
            pltpu.SemaphoreType.DMA,
        ],
        compiler_params=params(),
        cost_estimate=cost(45 * cells, 4 * (2 * cells + 3 * slabs * rows * lanes)),
        name="interior",
    )(*operands)


def boundary_kernel(pieces, count, last, slabs, *refs):
    refs = list(refs)
    fields, velocity, u_low, u_high = refs[:count], refs[count], refs[count + 1], refs[count + 2]
    below, above, v_below, v_above = refs[count + 3 : count + 7]
    del refs[: count + 7]
    if last:
        out = refs[1]
        del refs[:2]
    else:
        deposit, packed, ends, packs = refs[0], refs[1:5], refs[5:7], refs[7:9]
        del refs[:9]
    q, u, v, w, fx, lx, stage, in_sem, out_sem = refs
    comps, rows = q.shape[1], u.shape[2]
    inner = pl.ds(PAD, rows)

    def start(source, target, sem):
        pltpu.make_async_copy(source, target, sem).start()

    for block, c, first, number, index, size in pieces:
        start(fields[number].at[index], q.at[block, c, pl.ds(first, size), inner], in_sem.at[block, 0])
    edge = u_low.shape[0] - 1
    start(u_low.at[pl.ds(edge, 1)], u.at[0, pl.ds(0, 1)], in_sem.at[0, 1])
    start(velocity.at[0, pl.ds(0, 3)], u.at[0, pl.ds(1, 3)], in_sem.at[0, 1])
    start(velocity.at[0, pl.ds(slabs - 3, 3)], u.at[1, pl.ds(0, 3)], in_sem.at[1, 1])
    start(u_high.at[pl.ds(edge, 1)], u.at[1, pl.ds(3, 1)], in_sem.at[1, 1])
    for block in range(2):
        span = pl.ds(block * (slabs - 2), 2)
        start(velocity.at[1, span], v.at[block, :, inner], in_sem.at[block, 2])
        start(velocity.at[2, span], w.at[block], in_sem.at[block, 3])
    if not last:
        for target, parts in ((packs[0], packed[0::2]), (packs[1], packed[1::2])):
            at = 0
            for part in parts:
                target[at : at + part.shape[0]] = part[...]
                at += part.shape[0]

    def one(block, _):
        spots = [q.at[block, :, :, inner], u.at[block], v.at[block, :, inner], w.at[block]]
        for n, spot in enumerate(spots):
            pltpu.make_async_copy(spot, spot, in_sem.at[block, n]).wait()
        begin = block * (slabs - 2)

        def complete(k, _):
            insert_y_halo(q, v, block, k + 2, k, begin + k, below, above, v_below, v_above, comps, rows)
            return 0

        lax.fori_loop(0, 2, complete, 0)
        if not last:

            def dust(slab, _):
                add_deposit(q, block, comps - 1, slab, begin + slab, deposit, rows)
                return 0

            lax.fori_loop(0, 6, dust, 0)
        f = Fields(q, u, v, w, fx, lx, block, comps, rows, 0, 0)
        first_face(f)

        def step(k, _):
            def put(c, t, value):
                stage[block, c, k, pl.ds(t, 8, stride=f.tiles), :] = value

            slab_step(f, k, put)
            if not last:
                x = pl.ds(begin + k, 1)
                for c in range(comps):
                    for r in range(2):
                        packs[0][2 * c + r, x, :] = stage[block, c, k, r : r + 1, :]
                        packs[1][2 * c + r, x, :] = stage[block, c, k, rows - 2 + r : rows - 1 + r, :]
            return 0

        lax.fori_loop(0, 2, step, 0)
        return 0

    lax.fori_loop(0, 2, one, 0)
    copies = []
    for block in range(2):
        target = out.at[:, pl.ds(block * (slabs - 2), 2)] if last else ends[block]
        copies.append(pltpu.make_async_copy(stage.at[block], target, out_sem.at[block]))
    for copy in copies:
        copy.start()
    for copy in copies:
        copy.wait()


def boundary(fields, pieces, velocity, u_low, u_high, below, above, v_below, v_above, *, deposit=None, packed=None, out=None):
    last = out is not None
    _, slabs, rows, lanes = velocity.shape
    comps = 4
    operands = list(fields) + [velocity, u_low, u_high, below, above, v_below, v_above]
    specs = [ANY] * (len(fields) + 3) + [VMEM] * 4
    if last:
        aliases = {len(operands): 0}
        operands.append(out)
        specs.append(ANY)
        out_shape = jax.ShapeDtypeStruct(out.shape, out.dtype)
        out_specs = ANY
    else:
        aliases = {}
        operands += [deposit, *packed]
        specs += [VMEM] * 5
        out_shape = (jax.ShapeDtypeStruct((comps, 2, rows, lanes), jnp.float32),) * 2
        out_shape += (jax.ShapeDtypeStruct((2 * comps, slabs, lanes), jnp.float32),) * 2
        out_specs = (ANY, ANY, VMEM, VMEM)
    high = rows + 2 * PAD
    cells = comps * 4 * rows * lanes
    return pl.pallas_call(
        functools.partial(boundary_kernel, pieces, len(fields), last, slabs),
        out_shape=out_shape,
        in_specs=specs,
        out_specs=out_specs,
        scratch_shapes=[
            pltpu.VMEM((2, comps, 6, high, lanes), jnp.float32),
            pltpu.VMEM((2, 4, rows, lanes), jnp.float32),
            pltpu.VMEM((2, 2, high, lanes), jnp.float32),
            pltpu.VMEM((2, 2, rows, lanes), jnp.float32),
            pltpu.VMEM((rows // 8, comps, 8, lanes), jnp.float32),
            pltpu.VMEM((rows // 8, comps, 8, lanes), jnp.float32),
            pltpu.VMEM((2, comps, 2, rows, lanes), jnp.float32),
            pltpu.SemaphoreType.DMA((2, 4)),
            pltpu.SemaphoreType.DMA((2,)),
        ],
        input_output_aliases=aliases,
        compiler_params=params(),
        cost_estimate=cost(50 * cells, 4 * 6 * cells),
        name="boundary",
    )(*operands)


def pack_x_kernel(state, velocity, low, high, sems):
    comps, slabs = state.shape[0], state.shape[1]
    copies = []
    for n, (target, first, edge) in enumerate(((low, 0, 0), (high, slabs - 2, slabs - 1))):
        for c in range(comps):
            copies.append(
                pltpu.make_async_copy(
                    state.at[c, pl.ds(first, 2)], target.at[pl.ds(2 * c, 2)], sems.at[n, c]
                )
            )
        copies.append(
            pltpu.make_async_copy(
                velocity.at[0, pl.ds(edge, 1)], target.at[pl.ds(2 * comps, 1)], sems.at[n, comps]
            )
        )
    for copy in copies:
        copy.start()
    for copy in copies:
        copy.wait()


def pack_x(state, velocity):
    comps, _, rows, lanes = state.shape
    shape = jax.ShapeDtypeStruct((2 * comps + 1, rows, lanes), jnp.float32)
    return pl.pallas_call(
        pack_x_kernel,
        out_shape=(shape, shape),
        in_specs=[ANY, ANY],
        out_specs=(ANY, ANY),
        scratch_shapes=[pltpu.SemaphoreType.DMA((2, comps + 1))],
        compiler_params=params(),
        cost_estimate=cost(0, 4 * 4 * (2 * comps + 1) * rows * lanes),
        name="pack_x",
    )(state, velocity)


def as_row(column, width):
    shape = (column.shape[0], width)
    same = lax.broadcasted_iota(jnp.int32, shape, 0) == lax.broadcasted_iota(jnp.int32, shape, 1)
    return jnp.sum(jnp.where(same, column, 0.0), axis=0, keepdims=True)


def as_column(row):
    count = row.shape[1]
    shape = (count, count)
    same = lax.broadcasted_iota(jnp.int32, shape, 0) == lax.broadcasted_iota(jnp.int32, shape, 1)
    return jnp.sum(jnp.where(same, row, 0.0), axis=1, keepdims=True)


def survey_kernel(
    groups, low_in, high_in, v_low, v_high, wind, threshold, tile_owner, parcel_owner, count, share,
    low, high, payload, gathered,
):
    step, steps = pl.program_id(0), pl.num_programs(0)
    comps, part, rows, lanes = low_in.shape[0], wind.shape[1], wind.shape[2], wind.shape[3]
    slabs = share.shape[1]
    for x in range(part):
        for c in range(comps):
            for r in range(2):
                low[2 * c + r, x : x + 1, :] = low_in[c, x, r : r + 1, :]
                high[2 * c + r, x : x + 1, :] = high_in[c, x, 6 + r : 7 + r, :]
        low[2 * comps, x : x + 1, :] = v_low[0, x, 0:1, :]
        high[2 * comps, x : x + 1, :] = v_high[0, x, 7:8, :]
    lane = lax.broadcasted_iota(jnp.int32, (rows, lanes), 1)
    weight = jnp.zeros((rows, lanes), jnp.float32)
    for level, value in enumerate(profile_weights):
        weight = jnp.where(lane == level, value, weight)
    total = jnp.zeros((rows, lanes), jnp.float32)
    for x in range(part):
        east, north = wind[0, x], wind[1, x]
        friction = jnp.where(lane < LEVELS, weight * (east * east + north * north), 0.0)
        total = total + pltpu.roll(friction, LEVELS * x, 1) if x else friction

    @pl.when(step == 0)
    def _():
        gathered[...] = total

    @pl.when(step > 0)
    def _():
        gathered[...] += pltpu.roll(total, LEVELS * part * step, 1)

    @pl.when(step == steps - 1)
    def _():
        turned = gathered[...].T
        shape = (slabs, lanes)
        pick = (
            lax.broadcasted_iota(jnp.int32, shape, 1) // LEVELS == lax.broadcasted_iota(jnp.int32, shape, 0)
        ).astype(jnp.float32)
        payload[0:slabs] = jnp.dot(pick, turned, precision=HIGHEST, preferred_element_type=jnp.float32)
        payload[slabs : slabs + 8] = jnp.zeros((8, lanes), jnp.float32)
        payload[slabs : slabs + 1] = threshold[...]
        payload[slabs + 1 : slabs + 2] = as_row(tile_owner[0].astype(jnp.float32), lanes)
        owners = as_row(parcel_owner[0].astype(jnp.float32), slabs)
        shape = (groups, slabs)
        place = (owners == lax.broadcasted_iota(jnp.int32, shape, 0).astype(jnp.float32)).astype(jnp.float32)
        live = as_column(count[...].astype(jnp.float32))
        shape = (slabs, lanes)
        reach = lax.broadcasted_iota(jnp.int32, shape, 1).astype(jnp.float32) < live
        masses = jnp.where(reach, share[0], 0.0)
        payload[slabs + 8 : slabs + 8 + groups] = jnp.dot(
            place, masses, precision=HIGHEST, preferred_element_type=jnp.float32
        )


def survey(groups, state, velocity, threshold, tile_owner, parcel_owner, count, share):
    comps, slabs, rows, lanes = state.shape
    part = 8
    last = rows // 8 - 1

    def whole(array):
        return pl.BlockSpec(array.shape, lambda i: (0,) * array.ndim)

    packed = jax.ShapeDtypeStruct((2 * comps + 1, slabs, lanes), jnp.float32)
    packed_spec = pl.BlockSpec((2 * comps + 1, part, lanes), lambda i: (0, i, 0))
    height = slabs + 8 + groups
    return pl.pallas_call(
        functools.partial(survey_kernel, groups),
        grid=(slabs // part,),
        out_shape=(packed, packed, jax.ShapeDtypeStruct((height, lanes), jnp.float32)),
        in_specs=[
            pl.BlockSpec((comps, part, 8, lanes), lambda i: (0, i, 0, 0)),
            pl.BlockSpec((comps, part, 8, lanes), lambda i: (0, i, last, 0)),
            pl.BlockSpec((1, part, 8, lanes), lambda i: (1, i, 0, 0)),
            pl.BlockSpec((1, part, 8, lanes), lambda i: (1, i, last, 0)),
            pl.BlockSpec((2, part, rows, lanes), lambda i: (0, i, 0, 0)),
            whole(threshold),
            whole(tile_owner),
            whole(parcel_owner),
            whole(count),
            whole(share),
        ],
        out_specs=(packed_spec, packed_spec, pl.BlockSpec((height, lanes), lambda i: (0, 0))),
        scratch_shapes=[pltpu.VMEM((rows, lanes), jnp.float32)],
        compiler_params=params(),
        cost_estimate=cost(10 * slabs * rows * lanes, 10 * slabs * rows * lanes),
        name="survey",
    )(state, state, velocity, velocity, velocity, threshold, tile_owner, parcel_owner, count, share)


def deposit_kernel(slabs, me, gathered, low_in, high_in, flux_out, deposit, low, high, flux, dropped):
    groups, lanes = gathered.shape[0], gathered.shape[2]
    here = me[0]
    limits = jnp.concatenate([gathered[g, slabs : slabs + 1] for g in range(groups)], axis=0)
    total = jnp.zeros((groups, lanes), jnp.float32)
    shape = (groups, slabs)
    numbers = lax.broadcasted_iota(jnp.int32, shape, 0).astype(jnp.float32)
    for g in range(groups):
        owners = gathered[g, slabs + 1 : slabs + 2, 0:slabs]
        stress = gathered[g, 0:slabs]
        named = (owners == numbers).astype(jnp.float32)
        limit = lax.dot_general(
            named, limits, (((0,), (0,)), ((), ())), precision=HIGHEST, preferred_element_type=jnp.float32
        )
        lifting = jnp.maximum(stress - limit, 0.0)
        total = total + jnp.dot(named, lifting, precision=HIGHEST, preferred_element_type=jnp.float32)
    flux[...] = total / slabs
    flux_out[...] = flux[pl.ds(here, 1), :]
    dropped[...] = jnp.zeros_like(dropped)
    before, after = jnp.maximum(here - 1, 0), jnp.minimum(here + 1, groups - 1)
    has_before, has_after = here > 0, here < groups - 1
    base = slabs + 8
    for p in range(groups):
        x = p % slabs
        row = flux[p : p + 1, :]
        dropped[x + 2 : x + 3] += row * gathered[p, pl.ds(base + here, 1), :]
        if x >= slabs - 2:
            mass = row * gathered[p, pl.ds(base + before, 1), :]
            dropped[x - slabs + 2 : x - slabs + 3] += jnp.where(has_before, mass, 0.0)
        if x < 2:
            mass = row * gathered[p, pl.ds(base + after, 1), :]
            dropped[x + slabs + 2 : x + slabs + 3] += jnp.where(has_after, mass, 0.0)
    deposit[...] = dropped[...].T
    own = dropped[2 : 2 + slabs, :]
    lane = lax.broadcasted_iota(jnp.int32, (slabs, lanes), 1)
    rows = lanes
    for r in range(2):
        low[r] = low_in[r] + jnp.where(lane == 0, own[:, r : r + 1], 0.0)
        high[r] = high_in[r] + jnp.where(lane == 0, own[:, rows - 2 + r : rows - 1 + r], 0.0)


def settle(me, gathered, low, high, slabs):
    groups, _, lanes = gathered.shape
    edge = jax.ShapeDtypeStruct(low.shape, jnp.float32)
    return pl.pallas_call(
        functools.partial(deposit_kernel, slabs),
        out_shape=(
            jax.ShapeDtypeStruct((1, lanes), jnp.float32),
            jax.ShapeDtypeStruct((lanes, lanes), jnp.float32),
            edge,
            edge,
        ),
        in_specs=[SMEM, VMEM, VMEM, VMEM],
        out_specs=(VMEM, VMEM, VMEM, VMEM),
        scratch_shapes=[
            pltpu.VMEM((groups, lanes), jnp.float32),
            pltpu.VMEM((lanes, lanes), jnp.float32),
        ],
        compiler_params=params(),
        cost_estimate=cost(10**6, 10**6),
        name="settle",
    )(me, gathered, low, high)


def exchange(low, high, axis):
    count = lax.axis_size(axis)
    forward = [(i, i + 1) for i in range(count - 1)]
    backward = [(target, source) for source, target in forward]
    return lax.ppermute(high, axis, forward), lax.ppermute(low, axis, backward)


def shards(state, velocity, threshold, tile_owner, parcel_owner, parcel_count, parcel_share):
    groups = lax.axis_size("gx")
    slabs = state.shape[1]
    me = lax.axis_index("gx").astype(jnp.int32).reshape(1)

    x_low, x_high = exchange(*pack_x(state, velocity), "gx")
    low, high, payload = survey(
        groups, state, velocity, threshold, tile_owner, parcel_owner, parcel_count, parcel_share
    )
    v_low, v_high = low[8:9], high[8:9]
    keep = jnp.concatenate
    below, above = exchange(keep([low[0:6], v_low]), keep([high[0:6], v_high]), "gy")
    v_below, v_above = below[6:7], above[6:7]
    gathered = lax.all_gather(payload, "gx")
    flux, deposit, dust_low, dust_high = settle(me, gathered, low[6:8], high[6:8], slabs)
    dust_below, dust_above = exchange(dust_low, dust_high, "gy")

    sources = [(0, c, None, None, None) for c in range(3)]
    first, pack_low, pack_high = interior(
        [state], sources, velocity, below, above, v_below, v_above, None, True
    )
    sources = [(0, 3, None, None, None)]
    dust, dust_pack_low, dust_pack_high = interior(
        [state], sources, velocity, dust_below, dust_above, v_below, v_above, deposit, True
    )
    pieces = []
    for c in range(4):
        pieces += [
            (0, c, 0, 1, (pl.ds(2 * c, 2),), 2),
            (0, c, 2, 0, (c, pl.ds(0, 4)), 4),
            (1, c, 0, 0, (c, pl.ds(slabs - 4, 4)), 4),
            (1, c, 4, 2, (pl.ds(2 * c, 2),), 2),
        ]
    all_below, all_above = keep([below[0:6], dust_below]), keep([above[0:6], dust_above])
    end_low, end_high, y_low, y_high = boundary(
        [state, x_low, x_high], pieces, velocity, x_low, x_high, all_below, all_above, v_below, v_above,
        deposit=deposit, packed=(pack_low, pack_high, dust_pack_low, dust_pack_high),
    )
    x2_low, x2_high = exchange(end_low, end_high, "gx")
    below, above = exchange(y_low, y_high, "gy")
    sources = [(0, c, 2, 3, c) for c in range(3)] + [(1, 0, 2, 3, 3)]
    (inside,) = interior(
        [first, dust, end_low, end_high], sources, velocity, below, above, v_below, v_above, None, False
    )
    pieces = []
    for c in range(4):
        number, part = (0, c) if c < 3 else (1, 0)
        pieces += [
            (0, c, 0, 4, (c,), 2),
            (0, c, 2, 2, (c,), 2),
            (0, c, 4, number, (part, pl.ds(2, 2)), 2),
            (1, c, 0, number, (part, pl.ds(slabs - 4, 2)), 2),
            (1, c, 2, 3, (c,), 2),
            (1, c, 4, 5, (c,), 2),
        ]
    fields = boundary(
        [first, dust, end_low, end_high, x2_low, x2_high], pieces, velocity, x_low, x_high, below, above,
        v_below, v_above, out=inside,
    )
    return fields, flux


def solution(mesh):
    return jax.shard_map(
        shards,
        mesh=mesh,
        in_specs=(
            P(None, "gx", "gy", None),
            P(None, "gx", "gy", None),
            P("gx", "gy"),
            P("gy", "gx", None),
            P("gy", "gx", None),
            P("gy", "gx"),
            P("gy", "gx", None),
        ),
        out_specs=(P(None, "gx", "gy", None), P("gx", "gy")),
        check_vma=False,
    )
```

time: 428 us -> 161 us (0.38); the launches traced: 420 us -> 158 us
  other arithmetic: 287 us -> 0.04 us
  Pallas kernels: 0 us -> 84.5 us
  local copies, waits for them, and re-layouts: 43.8 us -> 0.25 us
  waiting for transfers between devices: 38.6 us -> 7.68 us
  blocking collectives: 0 us -> 29.6 us
  starting transfers between devices: 46.3 us -> 34.8 us
    select_n x7 -> x0, other arithmetic: 144 us -> none  [the longest x6 144 us: divergence(): fluxes = jnp.where(face_speed > 0, upwind, downwind)]
    pallas_call x0 -> x8, Pallas kernels: none -> 84.5 us  [the longest x3 62.1 us: interior(): pl.pallas_call(functools.partial(interior_kernel, sources, deposit is not...]
    concatenate x7 -> x4, other arithmetic: 80 us -> 0.04 us  [the longest x1 0.01 us: shards(): keep([above[0:6], dust_above])]
    sub x2 -> x0, other arithmetic: 43.2 us -> none  [advance(): return inner - time_step * (along_x + along_y + along_z)]
    ppermute x12 -> x10, waiting for transfers between devices: 38.6 us -> 7.68 us  [the longest x5 7.66 us: exchange(): lax.ppermute(low, axis, backward)]
    all_gather x0 -> x1, blocking collectives: none -> 29.6 us  [shards(): gathered = lax.all_gather(payload, 'gx')]
    unnamed x65 -> x12, local copies, waits for them, and re-layouts: 18.3 us -> 0.2 us
    slice x11 -> x10, local copies, waits for them, and re-layouts: 13.6 us -> 0.05 us  [the longest x1 0.01 us: shards(): above[0:6]]
  transfers between devices with their start and end apart: 14 -> 10, of which waited for: 5 -> 2; matrix products, arithmetic and copies ran while one was open for 20% -> 0% of each run, Pallas kernels for 0% -> 43%
where the time goes in v1:
time: 161 us; the launch traced here: 158 us
  Pallas kernels  84.5 us (52%)
  starting transfers between devices  34.8 us (22%)
  blocking collectives  29.6 us (18%)
  waiting for transfers between devices  7.68 us (5%)
    pallas_call x3, Pallas kernels, interior(): pl.pallas_call(functools.partial(interior_kernel, sources, deposit is not...  62.1 us
    all_gather x1, blocking collectives, shards(): gathered = lax.all_gather(payload, 'gx')  29.6 us
    ppermute x5, starting transfers between devices, exchange(): lax.ppermute(high, axis, forward)  19.6 us
    pallas_call x2, Pallas kernels, boundary(): pl.pallas_call(functools.partial(boundary_kernel, pieces, len(fields), la...  15.4 us
    ppermute x5, starting transfers between devices, exchange(): lax.ppermute(low, axis, backward)  15.2 us
    ppermute x5, waiting for transfers between devices, exchange(): lax.ppermute(low, axis, backward)  7.66 us
    pallas_call x1, Pallas kernels, survey(): pl.pallas_call(functools.partial(survey_kernel, groups), grid=(slabs // p...  4.27 us
  transfers between devices with their start and end apart: 10, of which 2 were waited for; matrix products, arithmetic and copies ran while one was open for 0% of the time, Pallas kernels for 43%

profile of v1, /device:TPU:3, one launch (start us, length us, event | category | flops | bytes accessed | tf_op | source)
XLA Modules:
  0.0 158.0 jit_solution(7738756849469635011)
XLA Ops:
  0.6 0.0 copy-start.3
  0.6 0.0 copy-start.4
  0.7 0.0 copy-start
  0.7 0.0 copy-start.2
  0.7 0.0 copy-start.1
  0.7 1.4 pack_x.1
  2.1 3.2 %collective-permute-start.4 = (f32[9,128,128]{2,1,0:T(8,128)S(1)}, f32[9,128,128]{2,1,0:T(8,128)S(1)}, u32[]{:S(2)}, u32[]{:S(2)}) collective-permute-start(f32[9,128,128]{2,1,0:T(8,128)S(1)} %get-tuple-element.29), channel_id=1, source_target_pairs={{0,4},{4,8},{8,12},{12,16},{16,20},{20,24},{24,28},{1,5},{5,9},{9,... | collective-permute-start | bytes 1769480 | tf_op jit(solution)/shard_map/ppermute | solution.py:593
  5.3 2.1 %collective-permute-start.5 = (f32[9,128,128]{2,1,0:T(8,128)S(1)}, f32[9,128,128]{2,1,0:T(8,128)S(1)}, u32[]{:S(2)}, u32[]{:S(2)}) collective-permute-start(f32[9,128,128]{2,1,0:T(8,128)S(1)} %get-tuple-element.30), channel_id=1, source_target_pairs={{4,0},{8,4},{12,8},{16,12},{20,16},{24,20},{28,24},{5,1},{9,5},{13... | collective-permute-start | bytes 1769480 | tf_op jit(solution)/shard_map/ppermute | solution.py:593
  7.4 0.0 copy-done.3
  7.4 0.1 copy.10.tile_owner
  7.5 0.0 copy-done.4
  7.5 0.1 copy.11.parcel_owner
  7.6 0.0 copy-done
  7.6 0.0 copy-done.2
  7.6 0.0 copy-done.1
  7.6 4.3 %survey.1 = (f32[9,32,128]{2,1,0:T(8,128)S(1)}, f32[9,32,128]{2,1,0:T(8,128)S(1)}, f32[48,128]{1,0:T(8,128)S(1)}) custom-call(f32[4,32,128,128]{3,2,1,0:T(8,128)} %refs_0_.5, f32[4,32,128,128]{3,2,1,0:T(8,128)} %refs_0_.5, f32[3,32,128,128]{3,2,1,0:T(8,128)} %refs_6_.1, f32[3,32,128,128]{3,2,1,0:T(8,128)} %refs_6_.1, f32[3,32,128,128]{3,2,1,0:T(8,128)} %refs_6_.1, ...), custom_call_target="tpu_custom_call" | custom-call | flops 5242880 | bytes 5242880 | tf_op jit(solution)/shard_map/survey/pallas_call | solution.py:501
  12.0 3.1 %collective-permute-start.1 = (f32[7,32,128]{2,1,0:T(8,128)S(1)}, f32[7,32,128]{2,1,0:T(8,128)S(1)}, u32[]{:S(2)}, u32[]{:S(2)}) collective-permute-start(f32[7,32,128]{2,1,0:T(8,128)S(1)} %pad_maximum_fusion.3), channel_id=1, source_target_pairs={{1,0},{2,1},{3,2},{5,4},{6,5},{7,6},{9,8},{10,9},{11,10},{13,12},{... | collective-permute-start | bytes 344072 | tf_op jit(solution)/shard_map/ppermute | solution.py:593
  15.2 3.0 %collective-permute-start = (f32[7,32,128]{2,1,0:T(8,128)S(1)}, f32[7,32,128]{2,1,0:T(8,128)S(1)}, u32[]{:S(2)}, u32[]{:S(2)}) collective-permute-start(f32[7,32,128]{2,1,0:T(8,128)S(1)} %pad_maximum_fusion.2), channel_id=1, source_target_pairs={{0,1},{1,2},{2,3},{4,5},{5,6},{6,7},{8,9},{9,10},{10,11},{12,13},{... | collective-permute-start | bytes 344072 | tf_op jit(solution)/shard_map/ppermute | solution.py:593
  18.2 29.6 %all-gather = f32[384,128]{1,0:T(8,128)S(1)} all-gather(f32[48,128]{1,0:T(8,128)S(1)} %get-tuple-element.24), channel_id=2, replica_groups=mesh['gx'=8,'gy'=4] {'gx'}, dimensions={0}, use_global_device_ids=true | all-gather | bytes 221184 | tf_op jit(solution)/shard_map/all_gather | solution.py:609
  47.9 1.3 settle.1
  49.2 9.2 %collective-permute-start.2 = (f32[2,32,128]{2,1,0:T(8,128)S(1)}, f32[2,32,128]{2,1,0:T(8,128)S(1)}, u32[]{:S(2)}, u32[]{:S(2)}) collective-permute-start(f32[2,32,128]{2,1,0:T(8,128)S(1)} %get-tuple-element.25), channel_id=1, source_target_pairs={{0,1},{1,2},{2,3},{4,5},{5,6},{6,7},{8,9},{9,10},{10,11},{12,13},{... | collective-permute-start | bytes 98312 | tf_op jit(solution)/shard_map/ppermute | solution.py:593
  58.5 0.0 collective-permute-done.1.refs_3_
  58.5 1.9 %collective-permute-start.3 = (f32[2,32,128]{2,1,0:T(8,128)S(1)}, f32[2,32,128]{2,1,0:T(8,128)S(1)}, u32[]{:S(2)}, u32[]{:S(2)}) collective-permute-start(f32[2,32,128]{2,1,0:T(8,128)S(1)} %get-tuple-element.26), channel_id=1, source_target_pairs={{1,0},{2,1},{3,2},{5,4},{6,5},{7,6},{9,8},{10,9},{11,10},{13,12},{... | collective-permute-start | bytes 98312 | tf_op jit(solution)/shard_map/ppermute | solution.py:593
  60.4 0.0 collective-permute-done.refs_2_
  60.5 0.0 collective-permute-done.2.refs_2_
  60.5 3.2 %collective-permute-done.3.refs_3_ = f32[2,32,128]{2,1,0:T(8,128)S(1)} collective-permute-done((f32[2,32,128]{2,1,0:T(8,128)S(1)}, f32[2,32,128]{2,1,0:T(8,128)S(1)}, u32[]{:S(2)}, u32[]{:S(2)}) %collective-permute-start.3) | collective-permute-done | bytes 32800 | tf_op jit(solution)/shard_map/ppermute | solution.py:593
  63.7 16.9 %interior.4 = (f32[1,32,128,128]{3,2,1,0:T(8,128)S(1)}, f32[2,32,128]{2,1,0:T(8,128)S(1)}, f32[2,32,128]{2,1,0:T(8,128)S(1)}) custom-call(f32[4,32,128,128]{3,2,1,0:T(8,128)} %refs_0_.5, f32[3,32,128,128]{3,2,1,0:T(8,128)} %refs_6_.1, f32[2,32,128]{2,1,0:T(8,128)S(1)} %collective-permute-done.2.refs_2_, f32[2,32,128]{2,1,0:T(8,128)S(1)} %collective-permute-done.3.refs_3_, ...), custom_call_target="tpu_custom_call" | custom-call | flops 20643840 | bytes 9961472 | tf_op jit(solution)/shard_map/interior/pallas_call | solution.py:236
  80.6 19.9 %interior.3 = (f32[3,32,128,128]{3,2,1,0:T(8,128)}, f32[6,32,128]{2,1,0:T(8,128)S(1)}, f32[6,32,128]{2,1,0:T(8,128)S(1)}) custom-call(f32[4,32,128,128]{3,2,1,0:T(8,128)} %refs_0_.5, f32[3,32,128,128]{3,2,1,0:T(8,128)} %refs_6_.1, f32[7,32,128]{2,1,0:T(8,128)S(1)} %collective-permute-done.refs_2_, f32[7,32,128]{2,1,0:T(8,128)S(1)} %collective-permute-done.1.refs_3_, ...), custom_call_target="tpu_custom_call" | custom-call | flops 61931520 | bytes 17301504 | tf_op jit(solution)/shard_map/interior/pallas_call | solution.py:236
  100.6 0.0 collective-permute-done.4.refs_1_.refs_4_.refs_7_
  100.6 0.0 collective-permute-done.5.refs_2_.refs_5_.refs_8_
  100.6 7.5 %boundary.2 = (f32[4,2,128,128]{3,2,1,0:T(8,128)S(1)}, f32[4,2,128,128]{3,2,1,0:T(8,128)S(1)}, f32[8,32,128]{2,1,0:T(8,128)S(1)}, f32[8,32,128]{2,1,0:T(8,128)S(1)}) custom-call(f32[4,32,128,128]{3,2,1,0:T(8,128)} %refs_0_.5, f32[9,128,128]{2,1,0:T(8,128)S(1)} %collective-permute-done.4.refs_1_.refs_4_.refs_7_, ...), custom_call_target="tpu_custom_call" | custom-call | flops 13107200 | bytes 6291456 | tf_op jit(solution)/shard_map/boundary/pallas_call | solution.py:363
  108.1 5.9 %collective-permute-start.7 = (f32[4,2,128,128]{3,2,1,0:T(8,128)S(1)}, f32[4,2,128,128]{3,2,1,0:T(8,128)S(1)}, u32[]{:S(2)}, u32[]{:S(2)}) collective-permute-start(f32[4,2,128,128]{3,2,1,0:T(8,128)S(1)} %get-tuple-element.35.refs_2_), channel_id=1, source_target_pairs={{4,0},{8,4},{12,8},{16,12},{20,16},{24,20},{28,24},{5,1},{9,5},{13... | collective-permute-start | bytes 1572872 | tf_op jit(solution)/shard_map/ppermute | solution.py:593
  114.0 1.9 %collective-permute-start.6 = (f32[4,2,128,128]{3,2,1,0:T(8,128)S(1)}, f32[4,2,128,128]{3,2,1,0:T(8,128)S(1)}, u32[]{:S(2)}, u32[]{:S(2)}) collective-permute-start(f32[4,2,128,128]{3,2,1,0:T(8,128)S(1)} %get-tuple-element.36.refs_3_), channel_id=1, source_target_pairs={{0,4},{4,8},{8,12},{12,16},{16,20},{20,24},{24,28},{1,5},{5,9},{9,... | collective-permute-start | bytes 1572872 | tf_op jit(solution)/shard_map/ppermute | solution.py:593
  115.9 2.2 %collective-permute-start.8 = (f32[8,32,128]{2,1,0:T(8,128)S(1)}, f32[8,32,128]{2,1,0:T(8,128)S(1)}, u32[]{:S(2)}, u32[]{:S(2)}) collective-permute-start(f32[8,32,128]{2,1,0:T(8,128)S(1)} %get-tuple-element.37), channel_id=1, source_target_pairs={{0,1},{1,2},{2,3},{4,5},{5,6},{6,7},{8,9},{9,10},{10,11},{12,13},{... | collective-permute-start | bytes 393224 | tf_op jit(solution)/shard_map/ppermute | solution.py:593
  118.1 2.1 %collective-permute-start.9 = (f32[8,32,128]{2,1,0:T(8,128)S(1)}, f32[8,32,128]{2,1,0:T(8,128)S(1)}, u32[]{:S(2)}, u32[]{:S(2)}) collective-permute-start(f32[8,32,128]{2,1,0:T(8,128)S(1)} %get-tuple-element.38), channel_id=1, source_target_pairs={{1,0},{2,1},{3,2},{5,4},{6,5},{7,6},{9,8},{10,9},{11,10},{13,12},{... | collective-permute-start | bytes 393224 | tf_op jit(solution)/shard_map/ppermute | solution.py:593
  120.3 0.0 collective-permute-done.8.refs_5_.refs_9_
  120.3 4.4 %collective-permute-done.9.refs_6_.refs_10_ = f32[8,32,128]{2,1,0:T(8,128)S(1)} collective-permute-done((f32[8,32,128]{2,1,0:T(8,128)S(1)}, f32[8,32,128]{2,1,0:T(8,128)S(1)}, u32[]{:S(2)}, u32[]{:S(2)}) %collective-permute-start.9) | collective-permute-done | bytes 131104 | tf_op jit(solution)/shard_map/ppermute | solution.py:593
  124.7 25.3 %interior.5.refs_13_ = f32[4,32,128,128]{3,2,1,0:T(8,128)} custom-call(f32[3,32,128,128]{3,2,1,0:T(8,128)} %get-tuple-element.23.refs_0_, f32[1,32,128,128]{3,2,1,0:T(8,128)S(1)} %get-tuple-element.28.refs_1_, f32[4,2,128,128]{3,2,1,0:T(8,128)S(1)} %get-tuple-element.35.refs_2_, f32[4,2,128,128]{3,2,1,0:T(8,128)S(1)} %get-tuple-element.36.refs_3_, ...), custom_call_target="tpu_custom_call" | custom-call | flops 82575360 | bytes 20971520 | tf_op jit(solution)/shard_map/interior/pallas_call | solution.py:236
  150.0 0.0 collective-permute-done.7.refs_5_
  150.0 0.0 collective-permute-done.6.refs_4_
  150.0 7.9 %boundary.3 = f32[4,32,128,128]{3,2,1,0:T(8,128)} custom-call(f32[3,32,128,128]{3,2,1,0:T(8,128)} %get-tuple-element.23.refs_0_, f32[1,32,128,128]{3,2,1,0:T(8,128)S(1)} %get-tuple-element.28.refs_1_, f32[4,2,128,128]{3,2,1,0:T(8,128)S(1)} %get-tuple-element.35.refs_2_, ...), custom_call_target="tpu_custom_call", output_to_operand_aliasing={{}: (13, {})} | custom-call | flops 13107200 | bytes 6291456 | tf_op jit(solution)/shard_map/boundary/pallas_call | solution.py:363
  (14 shorter events, 0.1 us)
Async XLA Ops:
  0.6 6.8 %copy-start.3 = (s32[1,32,1]{1,2,0:T(1,128)S(1)}, s32[1,32,1]{1,2,0:T(1,128)}, u32[]{:S(2)}) copy-start(s32[1,32,1]{1,2,0:T(1,128)} %param.10) | copy-start | bytes 388
  0.6 6.9 %copy-start.4 = (s32[1,32,1]{1,2,0:T(1,128)S(1)}, s32[1,32,1]{1,2,0:T(1,128)}, u32[]{:S(2)}) copy-start(s32[1,32,1]{1,2,0:T(1,128)} %param.11) | copy-start | bytes 388
  0.7 7.0 %copy-start = (f32[1,32,128]{2,1,0:T(8,128)S(1)}, f32[1,32,128]{2,1,0:T(8,128)}, u32[]{:S(2)}) copy-start(f32[1,32,128]{2,1,0:T(8,128)} %share.1) | copy-start | bytes 49156
  0.7 7.0 %copy-start.2 = (s32[1,32]{1,0:T(1,128)S(1)}, s32[1,32]{1,0:T(1,128)}, u32[]{:S(2)}) copy-start(s32[1,32]{1,0:T(1,128)} %count.1) | copy-start | bytes 388
  0.7 7.0 %copy-start.1 = (f32[1,128]{1,0:T(1,128)S(1)}, f32[1,128]{1,0:T(1,128)}, u32[]{:S(2)}) copy-start(f32[1,128]{1,0:T(1,128)} %threshold.1) | copy-start | bytes 1540
  2.1 98.5 %collective-permute-start.4 = (f32[9,128,128]{2,1,0:T(8,128)S(1)}, f32[9,128,128]{2,1,0:T(8,128)S(1)}, u32[]{:S(2)}, u32[]{:S(2)}) collective-permute-start(f32[9,128,128]{2,1,0:T(8,128)S(1)} %get-tuple-element.29), channel_id=1, source_target_pairs={{0,4},{4,8},{8,12},{12,16},{16,20},{20,24},{24,28},{1,5},{5,9},{9,... | collective-permute-start | bytes 1769480 | tf_op jit(solution)/shard_map/ppermute | solution.py:593
  5.3 95.3 %collective-permute-start.5 = (f32[9,128,128]{2,1,0:T(8,128)S(1)}, f32[9,128,128]{2,1,0:T(8,128)S(1)}, u32[]{:S(2)}, u32[]{:S(2)}) collective-permute-start(f32[9,128,128]{2,1,0:T(8,128)S(1)} %get-tuple-element.30), channel_id=1, source_target_pairs={{4,0},{8,4},{12,8},{16,12},{20,16},{24,20},{28,24},{5,1},{9,5},{13... | collective-permute-start | bytes 1769480 | tf_op jit(solution)/shard_map/ppermute | solution.py:593
  12.0 46.5 %collective-permute-start.1 = (f32[7,32,128]{2,1,0:T(8,128)S(1)}, f32[7,32,128]{2,1,0:T(8,128)S(1)}, u32[]{:S(2)}, u32[]{:S(2)}) collective-permute-start(f32[7,32,128]{2,1,0:T(8,128)S(1)} %pad_maximum_fusion.3), channel_id=1, source_target_pairs={{1,0},{2,1},{3,2},{5,4},{6,5},{7,6},{9,8},{10,9},{11,10},{13,12},{... | collective-permute-start | bytes 344072 | tf_op jit(solution)/shard_map/ppermute | solution.py:593
  15.2 45.3 %collective-permute-start = (f32[7,32,128]{2,1,0:T(8,128)S(1)}, f32[7,32,128]{2,1,0:T(8,128)S(1)}, u32[]{:S(2)}, u32[]{:S(2)}) collective-permute-start(f32[7,32,128]{2,1,0:T(8,128)S(1)} %pad_maximum_fusion.2), channel_id=1, source_target_pairs={{0,1},{1,2},{2,3},{4,5},{5,6},{6,7},{8,9},{9,10},{10,11},{12,13},{... | collective-permute-start | bytes 344072 | tf_op jit(solution)/shard_map/ppermute | solution.py:593
  49.2 11.3 %collective-permute-start.2 = (f32[2,32,128]{2,1,0:T(8,128)S(1)}, f32[2,32,128]{2,1,0:T(8,128)S(1)}, u32[]{:S(2)}, u32[]{:S(2)}) collective-permute-start(f32[2,32,128]{2,1,0:T(8,128)S(1)} %get-tuple-element.25), channel_id=1, source_target_pairs={{0,1},{1,2},{2,3},{4,5},{5,6},{6,7},{8,9},{9,10},{10,11},{12,13},{... | collective-permute-start | bytes 98312 | tf_op jit(solution)/shard_map/ppermute | solution.py:593
  58.5 5.2 %collective-permute-start.3 = (f32[2,32,128]{2,1,0:T(8,128)S(1)}, f32[2,32,128]{2,1,0:T(8,128)S(1)}, u32[]{:S(2)}, u32[]{:S(2)}) collective-permute-start(f32[2,32,128]{2,1,0:T(8,128)S(1)} %get-tuple-element.26), channel_id=1, source_target_pairs={{1,0},{2,1},{3,2},{5,4},{6,5},{7,6},{9,8},{10,9},{11,10},{13,12},{... | collective-permute-start | bytes 98312 | tf_op jit(solution)/shard_map/ppermute | solution.py:593
  108.1 41.9 %collective-permute-start.7 = (f32[4,2,128,128]{3,2,1,0:T(8,128)S(1)}, f32[4,2,128,128]{3,2,1,0:T(8,128)S(1)}, u32[]{:S(2)}, u32[]{:S(2)}) collective-permute-start(f32[4,2,128,128]{3,2,1,0:T(8,128)S(1)} %get-tuple-element.35.refs_2_), channel_id=1, source_target_pairs={{4,0},{8,4},{12,8},{16,12},{20,16},{24,20},{28,24},{5,1},{9,5},{13... | collective-permute-start | bytes 1572872 | tf_op jit(solution)/shard_map/ppermute | solution.py:593
  114.0 36.0 %collective-permute-start.6 = (f32[4,2,128,128]{3,2,1,0:T(8,128)S(1)}, f32[4,2,128,128]{3,2,1,0:T(8,128)S(1)}, u32[]{:S(2)}, u32[]{:S(2)}) collective-permute-start(f32[4,2,128,128]{3,2,1,0:T(8,128)S(1)} %get-tuple-element.36.refs_3_), channel_id=1, source_target_pairs={{0,4},{4,8},{8,12},{12,16},{16,20},{20,24},{24,28},{1,5},{5,9},{9,... | collective-permute-start | bytes 1572872 | tf_op jit(solution)/shard_map/ppermute | solution.py:593
  115.9 4.3 %collective-permute-start.8 = (f32[8,32,128]{2,1,0:T(8,128)S(1)}, f32[8,32,128]{2,1,0:T(8,128)S(1)}, u32[]{:S(2)}, u32[]{:S(2)}) collective-permute-start(f32[8,32,128]{2,1,0:T(8,128)S(1)} %get-tuple-element.37), channel_id=1, source_target_pairs={{0,1},{1,2},{2,3},{4,5},{5,6},{6,7},{8,9},{9,10},{10,11},{12,13},{... | collective-permute-start | bytes 393224 | tf_op jit(solution)/shard_map/ppermute | solution.py:593
  118.1 6.6 %collective-permute-start.9 = (f32[8,32,128]{2,1,0:T(8,128)S(1)}, f32[8,32,128]{2,1,0:T(8,128)S(1)}, u32[]{:S(2)}, u32[]{:S(2)}) collective-permute-start(f32[8,32,128]{2,1,0:T(8,128)S(1)} %get-tuple-element.38), channel_id=1, source_target_pairs={{1,0},{2,1},{3,2},{5,4},{6,5},{7,6},{9,8},{10,9},{11,10},{13,12},{... | collective-permute-start | bytes 393224 | tf_op jit(solution)/shard_map/ppermute | solution.py:593

commit v2 on v1

v2 whole, which is shorter than its diff:
```python
import functools

import jax
import jax.numpy as jnp
from jax import lax
from jax.experimental import pallas as pl
from jax.experimental.pallas import tpu as pltpu
from jax.sharding import PartitionSpec as P

LEVELS = 4
profile_weights = (0.4, 0.3, 0.2, 0.1)
time_step = 0.1
FACTOR = 0.25 * time_step

VMEM_LIMIT = 48 * 1024 * 1024
PAIR = 2
GROUP = 8
CHUNK = 4
AHEAD = 3
HIGHEST = lax.Precision.HIGHEST
ANY = pl.BlockSpec(memory_space=pl.ANY)
VMEM = pl.BlockSpec(memory_space=pltpu.VMEM)
SMEM = pl.BlockSpec(memory_space=pltpu.SMEM)


def params():
    return pltpu.CompilerParams(vmem_limit_bytes=VMEM_LIMIT)


def cost(flops, moved):
    return pl.CostEstimate(flops=int(flops), bytes_accessed=int(moved), transcendentals=0)


def minmod(a, b):
    return jnp.maximum(jnp.minimum(a, b), jnp.minimum(jnp.maximum(a, b), 0.0))


def tile_of(ref, t, tiles):
    return ref[pl.ds(t, 8, stride=tiles), :]


class Slabs:
    def __init__(self, q, u, v, w, fx, lx, block, u_at, v_at):
        self.q, self.u, self.v, self.w, self.fx, self.lx = q, u, v, w, fx, lx
        self.block, self.u_at, self.v_at = block, u_at, v_at
        self.comps, self.tiles, self.lanes = q.shape[1], w.shape[2], q.shape[-1]

    def field(self, c, slab, t):
        return self.q[self.block, c, slab, t + 2]

    def east(self, slab, t):
        return self.u[self.block, slab + self.u_at, t]

    def north(self, slab, t):
        return self.v[self.block, slab + self.v_at, t + 1]

    def up(self, slab, t):
        return self.w[self.block, slab + self.v_at, t]


def each(function, *lists):
    return [function(*items) for items in zip(*lists)]


def minmods(a, b):
    low, high = each(jnp.minimum, a, b), each(jnp.maximum, a, b)
    high = each(lambda x: jnp.minimum(x, 0.0), high)
    return each(jnp.maximum, low, high)


def difference(a, b):
    return each(lambda x, y: x - y, a, b)


def total_of(a, b):
    return each(lambda x, y: x + y, a, b)


def face_flux(speeds, masks, low_side, high_side):
    picked = each(jnp.where, masks, low_side, high_side)
    return each(lambda x, y: x * y, speeds, picked)


def staged(jobs):
    waiting = []
    for job in jobs:
        stores = job()
        for ref, index, value in waiting:
            ref[index] = value
        waiting = stores
    for ref, index, value in waiting:
        ref[index] = value


def first_face(f):
    def job(ts):
        spots = [(t, c) for t in ts for c in range(f.comps)]
        speeds = {t: FACTOR * (f.east(0, t) + f.east(1, t)) for t in ts}
        masks = {t: speeds[t] > 0 for t in ts}
        a, b, q0, q1 = [[f.field(c, slab, t) for t, c in spots] for slab in range(4)]
        middle = difference(q0, b)
        left = total_of(total_of(b, b), minmods(middle, difference(b, a)))
        slope = minmods(difference(q1, q0), middle)
        twice = total_of(q0, q0)
        flux = face_flux([speeds[t] for t, _ in spots], [masks[t] for t, _ in spots], left, difference(twice, slope))
        stores = [(f.fx, spot, x) for spot, x in zip(spots, flux)]
        return stores + [(f.lx, spot, x) for spot, x in zip(spots, total_of(twice, slope))]

    staged([functools.partial(job, range(t, t + PAIR)) for t in range(0, f.tiles, PAIR)])


def slab_step(f, k, put):
    slab = k + 2
    lane = lax.broadcasted_iota(jnp.int32, (8, f.lanes), 1)
    top = f.lanes - 1
    is_first, is_last = lane == 0, lane == top
    carry = []
    north_here = f.north(k, 0)
    speed = FACTOR * (f.north(k, -1) + north_here)
    for c in range(f.comps):
        a, b, q0, q1 = [f.field(c, slab, t) for t in (-2, -1, 0, 1)]
        middle, ahead = q0 - b, q1 - q0
        left_state = (b + b) + minmod(middle, b - a)
        slope = minmod(ahead, middle)
        twice = q0 + q0
        flux = speed * jnp.where(speed > 0, left_state, twice - slope)
        carry.append((q0, q1, ahead, twice, twice + slope, flux))
    states = {}

    def vertical(t):
        for c in range(f.comps):
            q0 = f.field(c, slab, t)
            over = jnp.where(is_last, 0.0, pltpu.roll(q0, top, 1))
            under = jnp.where(is_first, 0.0, pltpu.roll(q0, 1, 1))
            slope = minmod(over - q0, q0 - under)
            twice = q0 + q0
            states[t, c] = (twice - slope, twice + slope)

    held = []
    for t in range(GROUP):
        vertical(t)
    for begin in range(0, f.tiles, GROUP):
        group = range(begin, min(begin + GROUP, f.tiles))
        for t in range(begin + GROUP, min(begin + 2 * GROUP, f.tiles)):
            vertical(t)
        loaded = {}
        for t in group:
            loaded[t] = (f.east(k + 1, t), f.east(k + 2, t), f.north(k, t + 1), f.up(k, t))
            for c in range(f.comps):
                loaded[t, c] = (
                    f.field(c, slab, t + 2), f.field(c, slab + 1, t), f.field(c, slab + 2, t),
                    f.fx[t, c], f.lx[t, c],
                )
        for c, t, flux_x, left_x, value in held:
            f.fx[t, c], f.lx[t, c] = flux_x, left_x
            put(c, t, value)
        held = []
        for t in group:
            east_here, east_next, north_next, rise = loaded[t]
            speed_x = FACTOR * (east_here + east_next)
            speed_y = FACTOR * (north_here + north_next)
            north_here = north_next
            rise = FACTOR * rise
            speed_z = rise + pltpu.roll(rise, top, 1)
            fall = jnp.where(is_first, jnp.minimum(rise, 0.0), pltpu.roll(speed_z, 1, 1))
            speed_z = jnp.where(is_last, jnp.maximum(rise, 0.0), speed_z)
            go_x, go_y, go_z, go_fall = speed_x > 0, speed_y > 0, speed_z > 0, fall > 0
            for c in range(f.comps):
                y2, x1, x2, flux_w, left_w = loaded[t, c]
                q0, y1, ahead, twice, left_y, flux_y = carry[c]
                beyond = y2 - y1
                slope = minmod(beyond, ahead)
                twice_y = y1 + y1
                flux_next = speed_y * jnp.where(go_y, left_y, twice_y - slope)
                total = flux_next - flux_y
                carry[c] = (y1, y2, beyond, twice_y, twice_y + slope, flux_next)
                slope = minmod(x2 - x1, x1 - q0)
                twice_x = x1 + x1
                flux_x = speed_x * jnp.where(go_x, left_w, twice_x - slope)
                left_x = twice_x + slope
                total = total + (flux_x - flux_w)
                lower, upper = states[t, c]
                flux_z = speed_z * jnp.where(go_z, upper, pltpu.roll(lower, top, 1))
                flux_below = fall * jnp.where(go_fall, pltpu.roll(upper, 1, 1), lower)
                total = total + (flux_z - flux_below)
                held.append((c, t, flux_x, left_x, q0 - total))
    for c, t, flux_x, left_x, value in held:
        f.fx[t, c], f.lx[t, c] = flux_x, left_x
        put(c, t, value)


def rotated_edges(tiles, lows, highs):
    row = lax.broadcasted_iota(jnp.int32, tiles[0].shape, 0)
    ahead = [pltpu.roll(tile, 1, 0) for tile in tiles[-len(lows) :]]
    after = [pltpu.roll(tile, 7, 0) for tile in tiles[: len(highs)]]
    ahead = [jnp.where(row == 0, low, tile) for low, tile in zip(lows, ahead)]
    after = [jnp.where(row == 7, high, tile) for high, tile in zip(highs, after)]
    return ahead, after


def field_job(q, block, c, slab, source, dust, below, above, x):
    count = q.shape[3] - 4
    spots = range(count) if source is not None else (0, 1, count - 2, count - 1)
    if source is None:
        tiles = [q[block, c, slab, 2 + t] for t in spots]
    else:
        tiles = [tile_of(source, t, count) for t in spots]
    if below is not None:
        x = pl.ds(x, 1)
        lows = [below[2 * c + r, x, :] for r in range(2)]
        highs = [above[2 * c + r, x, :] for r in range(2)]
    if dust is not None:
        tiles = total_of(tiles, dust(spots))
    stores = []
    if source is not None:
        stores += [(q, (block, c, slab, t + 2), tile) for t, tile in zip(spots, tiles)]
    if below is not None:
        ahead, after = rotated_edges(tiles, lows, highs)
        stores += [(q, (block, c, slab, r), tile) for r, tile in enumerate(ahead)]
        stores += [(q, (block, c, slab, count + 2 + r), tile) for r, tile in enumerate(after)]
    return stores


def north_job(v, block, slab, source, below, above, x):
    count = v.shape[2] - 2
    tiles = [tile_of(source, t, count) for t in range(count)]
    x = pl.ds(x, 1)
    ahead, after = rotated_edges(tiles, [below[8, x, :]], [above[8, x, :]])
    return [(v, (block, slab, t), tile) for t, tile in enumerate(ahead + tiles + after)]


def plain_job(target, block, slab, source):
    count = target.shape[2]
    return [(target, (block, slab, t), tile_of(source, t, count)) for t in range(count)]


def falling(deposit, column, tiles):
    lanes = deposit.shape[-1]

    def dust(spots):
        parts = [pltpu.roll(tile_of(deposit, t, tiles), lanes - column, 1) for t in spots]
        lane = lax.broadcasted_iota(jnp.int32, parts[0].shape, 1)
        return [jnp.where(lane == 0, part, 0.0) for part in parts]

    return dust


def pack_edges(packs, stage_slab, comps, x):
    x = pl.ds(x, 1)
    stores = []
    for c in range(comps):
        tiles = stage_slab(c)
        count = tiles.shape[0]
        for r in range(2):
            stores.append((packs[0], (2 * c + r, x), tiles[r, 0:1, :]))
            stores.append((packs[1], (2 * c + r, x), tiles[count - 2 + r, 7:8, :]))
    staged([lambda: stores])


def start(source, target, sem):
    pltpu.make_async_copy(source, target, sem).start()


def arrived(spot, sem):
    pltpu.make_async_copy(spot, spot, sem).wait()


def interior_kernel(last, count, *refs):
    refs = list(refs)
    fields, velocity = refs[:count], refs[count]
    below, above, v_below, v_above = refs[count + 1 : count + 5]
    del refs[: count + 5]
    deposit = None if last else refs.pop(0)
    out = refs.pop(0)
    packs = None if last else (refs.pop(0), refs.pop(0))
    q, u, v, w, fx, lx, wind, stage, in_sem, out_sem = refs[:10]
    natural = None if last else refs[10]
    comps, slabs, tiles = q.shape[1], q.shape[2], w.shape[2]
    chunks = slabs // CHUNK
    inner = pl.ds(2, tiles)

    def fetch(j, first, final):
        begin, size = j * CHUNK, CHUNK
        span = pl.ds(begin, CHUNK)
        if last:
            middle, low, high = fields
            if first:
                begin, size = begin + 2, size - 2
                start(low, q.at[0, :, pl.ds(0, 2), inner], in_sem.at[j, 0])
            if final:
                size -= 2
                start(high, q.at[0, :, pl.ds(slabs - 2, 2), inner], in_sem.at[j, 0])
            part = pl.ds(begin, size)
            start(middle.at[:, part], q.at[0, :, part, inner], in_sem.at[j, 0])
        else:
            start(fields[0].at[:, span], natural.at[:, span], in_sem.at[j, 0])
        start(velocity.at[:, span], wind.at[:, span], in_sem.at[j, 1])

    for j in range(AHEAD):
        fetch(j, j == 0, False)

    def arrive(j):
        span = pl.ds(j * CHUNK, CHUNK)
        arrived(q.at[0, :, span, inner] if last else natural.at[:, span], in_sem.at[j, 0])
        arrived(wind.at[:, span], in_sem.at[j, 1])
        later = j + AHEAD

        @pl.when(later < chunks - 1)
        def _():
            fetch(later, False, False)

        @pl.when(later == chunks - 1)
        def _():
            fetch(chunks - 1, False, True)

        def complete(x, _):
            jobs = []
            for c in range(comps):
                dust = falling(deposit, x + 2, tiles) if not last and c == comps - 1 else None
                source = None if last else natural.at[c, x]
                jobs.append(functools.partial(field_job, q, 0, c, x, source, dust, below, above, x))
            jobs.append(functools.partial(plain_job, u, 0, x, wind.at[0, x]))
            jobs.append(functools.partial(north_job, v, 0, x, wind.at[1, x], v_below, v_above, x))
            jobs.append(functools.partial(plain_job, w, 0, x, wind.at[2, x]))
            staged(jobs)
            return 0

        lax.fori_loop(j * CHUNK, (j + 1) * CHUNK, complete, 0)

    f = Slabs(q, u, v, w, fx, lx, 0, 1, 2)
    arrive(jnp.int32(0))
    first_face(f)

    def step(k, _):
        @pl.when(k % CHUNK == 0)
        def _():
            arrive(k // CHUNK + 1)

        def put(c, t, value):
            if last:
                stage[c, k, pl.ds(t, 8, stride=tiles), :] = value
            else:
                stage[c, k, t] = value

        slab_step(f, k, put)
        start(stage.at[:, k], out.at[:, k + 2], out_sem)
        if not last:
            pack_edges(packs, lambda c: stage.at[c, k], comps, k + 2)
        return 0

    if not last:
        for pack in packs:
            pack[...] = jnp.zeros_like(pack)
    lax.fori_loop(0, slabs - 4, step, 0)
    pltpu.make_async_copy(stage, out.at[:, pl.ds(2, slabs - 4)], out_sem).wait()


def interior(fields, velocity, below, above, v_below, v_above, deposit=None):
    last = deposit is None
    _, slabs, rows, lanes = velocity.shape
    tiles, comps = rows // 8, fields[0].shape[0]
    operands = list(fields) + [velocity, below, above, v_below, v_above]
    specs = [ANY] * (len(fields) + 1) + [VMEM] * 4
    form = (rows, lanes) if last else (tiles, 8, lanes)
    out_shape = [jax.ShapeDtypeStruct((comps, slabs, *form), jnp.float32)]
    out_specs = [ANY]
    scratch = [
        pltpu.VMEM((1, comps, slabs, tiles + 4, 8, lanes), jnp.float32),
        pltpu.VMEM((1, slabs, tiles, 8, lanes), jnp.float32),
        pltpu.VMEM((1, slabs, tiles + 2, 8, lanes), jnp.float32),
        pltpu.VMEM((1, slabs, tiles, 8, lanes), jnp.float32),
        pltpu.VMEM((tiles, comps, 8, lanes), jnp.float32),
        pltpu.VMEM((tiles, comps, 8, lanes), jnp.float32),
        pltpu.VMEM(velocity.shape, jnp.float32),
        pltpu.VMEM((comps, slabs - 4, *form), jnp.float32),
        pltpu.SemaphoreType.DMA((slabs // CHUNK, 2)),
        pltpu.SemaphoreType.DMA,
    ]
    if not last:
        out_shape += [jax.ShapeDtypeStruct((2 * comps, slabs, lanes), jnp.float32)] * 2
        out_specs += [VMEM] * 2
        operands.append(deposit)
        specs.append(VMEM)
        scratch.append(pltpu.VMEM((comps, slabs, rows, lanes), jnp.float32))
    cells = comps * (slabs - 4) * rows * lanes
    return pl.pallas_call(
        functools.partial(interior_kernel, last, len(fields)),
        out_shape=tuple(out_shape),
        in_specs=specs,
        out_specs=tuple(out_specs),
        scratch_shapes=scratch,
        compiler_params=params(),
        cost_estimate=cost(45 * cells, 4 * (2 * cells + 3 * slabs * rows * lanes)),
        name="interior",
    )(*operands)


def boundary_kernel(last, slabs, *refs):
    refs = list(refs)
    count = 5 if last else 3
    fields, velocity, u_low, u_high = refs[:count], refs[count], refs[count + 1], refs[count + 2]
    below, above, v_below, v_above = refs[count + 3 : count + 7]
    del refs[: count + 7]
    if last:
        out = refs[1]
        del refs[:2]
    else:
        deposit, packed, ends, packs = refs[0], refs[1:3], refs[3:5], refs[5:7]
        del refs[:7]
    q, u, v, w, fx, lx, wind, stage, in_sem, out_sem = refs[:10]
    natural = None if last else refs[10]
    comps, tiles = q.shape[1], w.shape[2]
    inner = pl.ds(2, tiles)

    if last:
        middle, end_low, end_high, x_low, x_high = fields
        for block, at, source in (
            (0, 0, x_low), (0, 2, end_low), (0, 4, middle.at[:, pl.ds(2, 2)]),
            (1, 0, middle.at[:, pl.ds(slabs - 4, 2)]), (1, 2, end_high), (1, 4, x_high),
        ):
            start(source, q.at[block, :, pl.ds(at, 2), inner], in_sem.at[block, 0])
    else:
        state, x_low, x_high = fields
        start(state.at[:, pl.ds(0, 4)], natural.at[0, :, pl.ds(2, 4)], in_sem.at[0, 0])
        start(state.at[:, pl.ds(slabs - 4, 4)], natural.at[1, :, pl.ds(0, 4)], in_sem.at[1, 0])
        for c in range(comps):
            pair = pl.ds(2 * c, 2)
            start(x_low.at[pair], natural.at[0, c, pl.ds(0, 2)], in_sem.at[0, 0])
            start(x_high.at[pair], natural.at[1, c, pl.ds(4, 2)], in_sem.at[1, 0])
    edge = pl.ds(2 * comps, 1)
    start(u_low.at[edge], wind.at[0, 0, pl.ds(0, 1)], in_sem.at[0, 1])
    start(velocity.at[:, pl.ds(0, 3)], wind.at[0, :, pl.ds(1, 3)], in_sem.at[0, 2])
    start(velocity.at[:, pl.ds(slabs - 3, 3)], wind.at[1, :, pl.ds(0, 3)], in_sem.at[1, 2])
    start(u_high.at[edge], wind.at[1, 0, pl.ds(3, 1)], in_sem.at[1, 1])
    if not last:
        packs[0][...] = packed[0][...]
        packs[1][...] = packed[1][...]

    def one(block, _):
        begin = block * (slabs - 2)
        arrived(q.at[block, :, :, inner] if last else natural.at[block], in_sem.at[block, 0])
        arrived(wind.at[0, 0, pl.ds(0, 1)], in_sem.at[block, 1])
        arrived(wind.at[0, :, pl.ds(0, 3)], in_sem.at[block, 2])

        def complete(slab, _):
            jobs = []
            for c in range(comps):
                dust = falling(deposit, begin + slab, tiles) if c == comps - 1 else None
                source = natural.at[block, c, slab]
                jobs.append(functools.partial(field_job, q, block, c, slab, source, dust, None, None, None))
            staged(jobs)
            return 0

        if not last:
            lax.fori_loop(0, 6, complete, 0)

        def edges(k, _):
            x = begin + k
            jobs = [
                functools.partial(field_job, q, block, c, k + 2, None, None, below, above, x) for c in range(comps)
            ]
            jobs.append(functools.partial(north_job, v, block, k, wind.at[block, 1, k + 1], v_below, v_above, x))
            jobs.append(functools.partial(plain_job, w, block, k, wind.at[block, 2, k + 1]))
            staged(jobs)
            return 0

        lax.fori_loop(0, 2, edges, 0)
        staged([functools.partial(plain_job, u, block, k, wind.at[block, 0, k]) for k in range(4)])
        f = Slabs(q, u, v, w, fx, lx, block, 0, 0)
        first_face(f)

        def step(k, _):
            def put(c, t, value):
                if last:
                    stage[block, c, k, pl.ds(t, 8, stride=tiles), :] = value
                else:
                    stage[block, c, k, t] = value

            slab_step(f, k, put)
            if not last:
                pack_edges(packs, lambda c: stage.at[block, c, k], comps, begin + k)
            return 0

        lax.fori_loop(0, 2, step, 0)
        return 0

    lax.fori_loop(0, 2, one, 0)
    copies = []
    for block in range(2):
        target = out.at[:, pl.ds(block * (slabs - 2), 2)] if last else ends[block]
        copies.append(pltpu.make_async_copy(stage.at[block], target, out_sem.at[block]))
    for copy in copies:
        copy.start()
    for copy in copies:
        copy.wait()


def boundary(fields, velocity, u_low, u_high, below, above, v_below, v_above, *, deposit=None, packed=None, out=None):
    last = out is not None
    _, slabs, rows, lanes = velocity.shape
    tiles, comps = rows // 8, fields[0].shape[0]
    operands = list(fields) + [velocity, u_low, u_high, below, above, v_below, v_above]
    specs = [ANY] * (len(fields) + 3) + [VMEM] * 4
    form = (rows, lanes) if last else (tiles, 8, lanes)
    scratch = [
        pltpu.VMEM((2, comps, 6, tiles + 4, 8, lanes), jnp.float32),
        pltpu.VMEM((2, 4, tiles, 8, lanes), jnp.float32),
        pltpu.VMEM((2, 2, tiles + 2, 8, lanes), jnp.float32),
        pltpu.VMEM((2, 2, tiles, 8, lanes), jnp.float32),
        pltpu.VMEM((tiles, comps, 8, lanes), jnp.float32),
        pltpu.VMEM((tiles, comps, 8, lanes), jnp.float32),
        pltpu.VMEM((2, 3, 4, rows, lanes), jnp.float32),
        pltpu.VMEM((2, comps, 2, *form), jnp.float32),
        pltpu.SemaphoreType.DMA((2, 3)),
        pltpu.SemaphoreType.DMA((2,)),
    ]
    if last:
        aliases = {len(operands): 0}
        operands.append(out)
        specs.append(ANY)
        out_shape = jax.ShapeDtypeStruct(out.shape, out.dtype)
        out_specs = ANY
    else:
        aliases = {}
        operands += [deposit, *packed]
        specs += [VMEM] * 3
        out_shape = (jax.ShapeDtypeStruct((comps, 2, *form), jnp.float32),) * 2
        out_shape += (jax.ShapeDtypeStruct((2 * comps, slabs, lanes), jnp.float32),) * 2
        out_specs = (ANY, ANY, VMEM, VMEM)
        scratch.append(pltpu.VMEM((2, comps, 6, rows, lanes), jnp.float32))
    cells = comps * 4 * rows * lanes
    return pl.pallas_call(
        functools.partial(boundary_kernel, last, slabs),
        out_shape=out_shape,
        in_specs=specs,
        out_specs=out_specs,
        scratch_shapes=scratch,
        input_output_aliases=aliases,
        compiler_params=params(),
        cost_estimate=cost(50 * cells, 4 * 6 * cells),
        name="boundary",
    )(*operands)


def x_copies(state, velocity, low, high, sems):
    comps, slabs = state.shape[0], state.shape[1]
    copies = []
    for n, (target, first, edge) in enumerate(((low, 0, 0), (high, slabs - 2, slabs - 1))):
        pairs = [(state.at[c, pl.ds(first, 2)], target.at[pl.ds(2 * c, 2)]) for c in range(comps)]
        pairs.append((velocity.at[0, pl.ds(edge, 1)], target.at[pl.ds(2 * comps, 1)]))
        copies += [pltpu.make_async_copy(*pair, sems.at[n, i]) for i, pair in enumerate(pairs)]
    return copies


def as_column(row):
    count = row.shape[1]
    shape = (count, count)
    same = lax.broadcasted_iota(jnp.int32, shape, 0) == lax.broadcasted_iota(jnp.int32, shape, 1)
    return jnp.sum(jnp.where(same, row, 0.0), axis=1, keepdims=True)


def survey_kernel(
    groups, low_in, high_in, v_low, v_high, wind, threshold_in, tile_owner_in, parcel_owner_in, count_in, share_in,
    state, velocity, low, high, payload, x_low, x_high,
    gathered, threshold, tile_owner, parcel_owner, count, share, sems, small_sems,
):
    small = [
        pltpu.make_async_copy(source, target, small_sems.at[n])
        for n, (source, target) in enumerate(
            (
                (threshold_in, threshold), (tile_owner_in, tile_owner), (parcel_owner_in, parcel_owner),
                (count_in, count), (share_in, share),
            )
        )
    ]
    step, steps = pl.program_id(0), pl.num_programs(0)

    @pl.when(step == 0)
    def _():
        for copy in small + x_copies(state, velocity, x_low, x_high, sems):
            copy.start()

    comps, part, rows, lanes = low_in.shape[0], wind.shape[1], wind.shape[2], wind.shape[3]
    slabs = share.shape[1]
    for x in range(part):
        for c in range(comps):
            for r in range(2):
                low[2 * c + r, x : x + 1, :] = low_in[c, x, r : r + 1, :]
                high[2 * c + r, x : x + 1, :] = high_in[c, x, 6 + r : 7 + r, :]
        low[2 * comps, x : x + 1, :] = v_low[0, x, 0:1, :]
        high[2 * comps, x : x + 1, :] = v_high[0, x, 7:8, :]
    lane = lax.broadcasted_iota(jnp.int32, (rows, lanes), 1)
    weight = jnp.zeros((rows, lanes), jnp.float32)
    for level, value in enumerate(profile_weights):
        weight = jnp.where(lane == level, value, weight)
    total = jnp.zeros((rows, lanes), jnp.float32)
    for x in range(part):
        east, north = wind[0, x], wind[1, x]
        friction = jnp.where(lane < LEVELS, weight * (east * east + north * north), 0.0)
        total = total + pltpu.roll(friction, LEVELS * x, 1) if x else friction

    @pl.when(step == 0)
    def _():
        gathered[...] = total

    @pl.when(step == steps // 2)
    def _():
        for copy in small:
            copy.wait()
        payload[slabs : slabs + 8] = jnp.zeros((8, lanes), jnp.float32)
        payload[slabs : slabs + 1] = threshold[...]
        payload[slabs + 1 : slabs + 2, 0:slabs] = tile_owner[...].astype(jnp.float32)
        owners = parcel_owner[...].astype(jnp.float32)
        shape = (groups, slabs)
        place = (owners == lax.broadcasted_iota(jnp.int32, shape, 0).astype(jnp.float32)).astype(jnp.float32)
        live = as_column(count[...].astype(jnp.float32))
        shape = (slabs, lanes)
        reach = lax.broadcasted_iota(jnp.int32, shape, 1).astype(jnp.float32) < live
        masses = jnp.where(reach, share[0], 0.0)
        payload[slabs + 8 : slabs + 8 + groups] = jnp.dot(
            place, masses, precision=HIGHEST, preferred_element_type=jnp.float32
        )

    @pl.when(step > 0)
    def _():
        gathered[...] += pltpu.roll(total, LEVELS * part * step, 1)

    @pl.when(step == steps - 1)
    def _():
        gathered[...] = gathered[...].T
        stress = gathered[pl.ds(0, slabs, stride=LEVELS), :]
        for level in range(1, LEVELS):
            stress = stress + gathered[pl.ds(level, slabs, stride=LEVELS), :]
        payload[0:slabs] = stress
        for copy in x_copies(state, velocity, x_low, x_high, sems):
            copy.wait()


def survey(groups, state, velocity, threshold, tile_owner, parcel_owner, count, share):
    comps, slabs, rows, lanes = state.shape
    part = 8
    last = rows // 8 - 1

    small = (threshold, tile_owner, parcel_owner, count, share)
    packed = jax.ShapeDtypeStruct((2 * comps + 1, slabs, lanes), jnp.float32)
    packed_spec = pl.BlockSpec((2 * comps + 1, part, lanes), lambda i: (0, i, 0))
    x_packed = jax.ShapeDtypeStruct((2 * comps + 1, rows, lanes), jnp.float32)
    height = slabs + 8 + groups
    return pl.pallas_call(
        functools.partial(survey_kernel, groups),
        grid=(slabs // part,),
        out_shape=(packed, packed, jax.ShapeDtypeStruct((height, lanes), jnp.float32), x_packed, x_packed),
        in_specs=[
            pl.BlockSpec((comps, part, 8, lanes), lambda i: (0, i, 0, 0)),
            pl.BlockSpec((comps, part, 8, lanes), lambda i: (0, i, last, 0)),
            pl.BlockSpec((1, part, 8, lanes), lambda i: (1, i, 0, 0)),
            pl.BlockSpec((1, part, 8, lanes), lambda i: (1, i, last, 0)),
            pl.BlockSpec((2, part, rows, lanes), lambda i: (0, i, 0, 0)),
            *[pl.BlockSpec(memory_space=pltpu.HBM)] * 7,
        ],
        out_specs=(packed_spec, packed_spec, pl.BlockSpec((height, lanes), lambda i: (0, 0)), ANY, ANY),
        scratch_shapes=[
            pltpu.VMEM((rows, lanes), jnp.float32),
            *[pltpu.VMEM(array.shape, array.dtype) for array in small],
            pltpu.SemaphoreType.DMA((2, comps + 1)),
            pltpu.SemaphoreType.DMA((len(small),)),
        ],
        compiler_params=params(),
        cost_estimate=cost(10 * slabs * rows * lanes, 10 * slabs * rows * lanes),
        name="survey",
    )(state, state, velocity, velocity, velocity, *small, state, velocity)


def deposit_kernel(slabs, me, gathered, low_in, high_in, flux_out, deposit, low, high, flux, dropped):
    groups, lanes = gathered.shape[0], gathered.shape[2]
    here = me[0]
    limits = jnp.concatenate([gathered[g, slabs : slabs + 1] for g in range(groups)], axis=0)
    total = jnp.zeros((groups, lanes), jnp.float32)
    shape = (groups, slabs)
    numbers = lax.broadcasted_iota(jnp.int32, shape, 0).astype(jnp.float32)
    for g in range(groups):
        owners = gathered[g, slabs + 1 : slabs + 2, 0:slabs]
        stress = gathered[g, 0:slabs]
        named = (owners == numbers).astype(jnp.float32)
        limit = lax.dot_general(
            named, limits, (((0,), (0,)), ((), ())), precision=HIGHEST, preferred_element_type=jnp.float32
        )
        lifting = jnp.maximum(stress - limit, 0.0)
        total = total + jnp.dot(named, lifting, precision=HIGHEST, preferred_element_type=jnp.float32)
    flux[...] = total / slabs
    flux_out[...] = flux[pl.ds(here, 1), :]
    dropped[...] = jnp.zeros_like(dropped)
    before, after = jnp.maximum(here - 1, 0), jnp.minimum(here + 1, groups - 1)
    has_before, has_after = here > 0, here < groups - 1
    base = slabs + 8
    for p in range(groups):
        x = p % slabs
        row = flux[p : p + 1, :]
        dropped[x + 2 : x + 3] += row * gathered[p, pl.ds(base + here, 1), :]
        if x >= slabs - 2:
            mass = row * gathered[p, pl.ds(base + before, 1), :]
            dropped[x - slabs + 2 : x - slabs + 3] += jnp.where(has_before, mass, 0.0)
        if x < 2:
            mass = row * gathered[p, pl.ds(base + after, 1), :]
            dropped[x + slabs + 2 : x + slabs + 3] += jnp.where(has_after, mass, 0.0)
    deposit[...] = dropped[...].T
    own = dropped[2 : 2 + slabs, :]
    lane = lax.broadcasted_iota(jnp.int32, (slabs, lanes), 1)
    rows = lanes
    dust = low.shape[0] - 3
    low[...] = low_in[...]
    high[...] = high_in[...]
    for r in range(2):
        low[dust + r] += jnp.where(lane == 0, own[:, r : r + 1], 0.0)
        high[dust + r] += jnp.where(lane == 0, own[:, rows - 2 + r : rows - 1 + r], 0.0)


def settle(me, gathered, low, high, slabs):
    groups, _, lanes = gathered.shape
    edge = jax.ShapeDtypeStruct(low.shape, jnp.float32)
    return pl.pallas_call(
        functools.partial(deposit_kernel, slabs),
        out_shape=(
            jax.ShapeDtypeStruct((1, lanes), jnp.float32),
            jax.ShapeDtypeStruct((lanes, lanes), jnp.float32),
            edge,
            edge,
        ),
        in_specs=[SMEM, VMEM, VMEM, VMEM],
        out_specs=(VMEM, VMEM, VMEM, VMEM),
        scratch_shapes=[
            pltpu.VMEM((groups, lanes), jnp.float32),
            pltpu.VMEM((lanes, lanes), jnp.float32),
        ],
        compiler_params=params(),
        cost_estimate=cost(10**6, 10**6),
        name="settle",
    )(me, gathered, low, high)


def exchange(low, high, axis):
    count = lax.axis_size(axis)
    forward = [(i, i + 1) for i in range(count - 1)]
    backward = [(target, source) for source, target in forward]
    return lax.ppermute(high, axis, forward), lax.ppermute(low, axis, backward)


def shards(state, velocity, threshold, tile_owner, parcel_owner, parcel_count, parcel_share):
    groups = lax.axis_size("gx")
    slabs = state.shape[1]
    me = lax.axis_index("gx").astype(jnp.int32).reshape(1)

    low, high, payload, x_low, x_high = survey(
        groups, state, velocity, threshold, tile_owner[:, :, 0], parcel_owner[:, :, 0], parcel_count, parcel_share
    )
    copies = jnp.broadcast_to(payload[None], (groups, *payload.shape))
    gathered = lax.all_to_all(copies, "gx", split_axis=0, concat_axis=0, tiled=True)
    flux, deposit, low, high = settle(me, gathered, low, high, slabs)
    below, above = exchange(low, high, "gy")
    x_low, x_high, _ = lax.optimization_barrier((x_low, x_high, gathered))
    x_low, x_high = exchange(x_low, x_high, "gx")
    middle, pack_low, pack_high = interior([state], velocity, below, above, below, above, deposit)
    end_low, end_high, y_low, y_high = boundary(
        [state, x_low, x_high], velocity, x_low, x_high, below, above, below, above,
        deposit=deposit, packed=(pack_low, pack_high),
    )
    x2_low, x2_high = exchange(end_low, end_high, "gx")
    below2, above2 = exchange(y_low, y_high, "gy")
    (inside,) = interior([middle, end_low, end_high], velocity, below2, above2, below, above)
    fields = boundary(
        [middle, end_low, end_high, x2_low, x2_high], velocity, x_low, x_high, below2, above2, below, above,
        out=inside,
    )
    return fields, flux


def solution(mesh):
    return jax.shard_map(
        shards,
        mesh=mesh,
        in_specs=(
            P(None, "gx", "gy", None),
            P(None, "gx", "gy", None),
            P("gx", "gy"),
            P("gy", "gx", None),
            P("gy", "gx", None),
            P("gy", "gx"),
            P("gy", "gx", None),
        ),
        out_specs=(P(None, "gx", "gy", None), P("gx", "gy")),
        check_vma=False,
    )
```

time: 161 us -> 112 us (0.70); the launches traced: 158 us -> 112 us
  Pallas kernels: 84.5 us -> 63.3 us
  blocking collectives: 29.6 us -> 10.5 us
  starting transfers between devices: 34.8 us -> 24.6 us
  local copies, waits for them, and re-layouts: 0.25 us -> 3.34 us
    all_gather x1 -> x0, blocking collectives: 29.6 us -> none  [shards(): gathered = lax.all_gather(payload, 'gx')]
    pallas_call x6 -> x4, Pallas kernels: 78.9 us -> 57.6 us  [the longest x2 44.7 us: interior(): pl.pallas_call(functools.partial(interior_kernel, last, len(fields)), out...]
    all_to_all x0 -> x1, blocking collectives: none -> 10.5 us  [shards(): lax.all_to_all(copies, 'gx', split_axis=0, concat_axis=0, tiled=True)]
    ppermute x5 -> x4, starting transfers between devices: 15.2 us -> 8.37 us  [exchange(): lax.ppermute(low, axis, backward)]
    ppermute x5 -> x4, starting transfers between devices: 19.6 us -> 16.2 us  [exchange(): lax.ppermute(high, axis, forward)]
    unnamed x12 -> x10, local copies, waits for them, and re-layouts: 0.2 us -> 3.33 us
    ppermute x5 -> x4, waiting for transfers between devices: 7.66 us -> 8.94 us  [exchange(): lax.ppermute(low, axis, backward)]
  transfers between devices with their start and end apart: 10 -> 8, of which waited for: 2 -> 3; matrix products, arithmetic and copies ran while one was open for 0% -> 0% of each run, Pallas kernels for 43% -> 41%
where the time goes in v2:
time: 112 us
  Pallas kernels  63.3 us (57%)
  starting transfers between devices  24.6 us (22%)
  blocking collectives  10.5 us (9%)
  waiting for transfers between devices  9.1 us (8%)
  local copies, waits for them, and re-layouts  3.34 us (3%)
    pallas_call x2, Pallas kernels, interior(): pl.pallas_call(functools.partial(interior_kernel, last, len(fields)), out...  44.7 us
    ppermute x4, starting transfers between devices, exchange(): lax.ppermute(high, axis, forward)  16.2 us
    pallas_call x2, Pallas kernels, boundary(): pl.pallas_call(functools.partial(boundary_kernel, last, slabs), out_shape...  12.9 us
    all_to_all x1, blocking collectives, shards(): lax.all_to_all(copies, 'gx', split_axis=0, concat_axis=0, tiled=True)  10.5 us
    ppermute x4, waiting for transfers between devices, exchange(): lax.ppermute(low, axis, backward)  8.94 us
    ppermute x4, starting transfers between devices, exchange(): lax.ppermute(low, axis, backward)  8.37 us
    pallas_call x1, Pallas kernels, survey(): pl.pallas_call(functools.partial(survey_kernel, groups), grid=(slabs // p...  4.32 us
    unnamed x10, local copies, waits for them, and re-layouts  3.33 us
  transfers between devices with their start and end apart: 8, of which 3 were waited for; matrix products, arithmetic and copies ran while one was open for 0% of the time, Pallas kernels for 41%

profile of v2, /device:TPU:3, one launch (start us, length us, event | category | flops | bytes accessed | tf_op | source)
XLA Modules:
  0.0 111.6 jit_solution(13825803487204520573)
XLA Ops:
  0.6 0.0 copy-start
  0.6 0.7 copy-done
  1.4 0.0 copy-start.1
  1.4 0.7 copy-done.1
  2.0 0.0 copy-start.2
  2.0 0.7 copy-done.2
  2.7 0.0 copy-start.3
  2.7 0.7 copy-done.3
  3.3 0.0 copy-start.4
  3.3 0.7 copy-done.4
  4.0 4.3 %survey.1 = (f32[9,32,128]{2,1,0:T(8,128)S(1)}, f32[9,32,128]{2,1,0:T(8,128)S(1)}, f32[48,128]{1,0:T(8,128)S(1)}, f32[9,128,128]{2,1,0:T(8,128)S(1)}, f32[9,128,128]{2,1,0:T(8,128)S(1)}) custom-call(f32[4,32,128,128]{3,2,1,0:T(8,128)} %refs_0_.3, f32[4,32,128,128]{3,2,1,0:T(8,128)} %refs_0_.3, f32[3,32,128,128]{3,2,1,0:T(8,128)} %refs_5_.1, ...), custom_call_target="tpu_custom_call" | custom-call | flops 5242880 | bytes 5242880 | tf_op jit(solution)/shard_map/survey/pallas_call | solution.py:649
  8.3 10.5 %all_to_all.5.gathered = f32[8,48,128]{2,1,0:T(8,128)S(1)} all-to-all(f32[8,48,128]{2,1,0:T(8,128)S(1)} %broadcast_in_dim.2), channel_id=1, replica_groups=mesh['gx'=8,'gy'=4] {'gx'}, dimensions={0} | all-to-all | bytes 393216 | tf_op jit(solution)/shard_map/all_to_all | solution.py:757
  18.8 3.1 %collective-permute-start.2 = (f32[9,128,128]{2,1,0:T(8,128)S(1)}, f32[9,128,128]{2,1,0:T(8,128)S(1)}, u32[]{:S(2)}, u32[]{:S(2)}) collective-permute-start(f32[9,128,128]{2,1,0:T(8,128)S(1)} %get-tuple-element.29), channel_id=1, source_target_pairs={{0,4},{4,8},{8,12},{12,16},{16,20},{20,24},{24,28},{1,5},{5,9},{9,... | collective-permute-start | bytes 1769480 | tf_op jit(solution)/shard_map/ppermute | solution.py:745
  21.9 2.2 %collective-permute-start.3 = (f32[9,128,128]{2,1,0:T(8,128)S(1)}, f32[9,128,128]{2,1,0:T(8,128)S(1)}, u32[]{:S(2)}, u32[]{:S(2)}) collective-permute-start(f32[9,128,128]{2,1,0:T(8,128)S(1)} %get-tuple-element.30), channel_id=1, source_target_pairs={{4,0},{8,4},{12,8},{16,12},{20,16},{24,20},{28,24},{5,1},{9,5},{13... | collective-permute-start | bytes 1769480 | tf_op jit(solution)/shard_map/ppermute | solution.py:745
  24.2 1.3 %settle.1 = (f32[1,128]{1,0:T(1,128)}, f32[128,128]{1,0:T(8,128)S(1)}, f32[9,32,128]{2,1,0:T(8,128)S(1)}, f32[9,32,128]{2,1,0:T(8,128)S(1)}) custom-call(s32[1]{0:T(128)} %bitcast.me, f32[8,48,128]{2,1,0:T(8,128)S(1)} %all_to_all.5.gathered, f32[9,32,128]{2,1,0:T(8,128)S(1)} %get-tuple-element.21.low_in, f32[9,32,128]{2,1,0:T(8,128)S(1)} %get-tuple-element.22.high_in), custom_call_target="tpu_custom_call" | custom-call | flops 1000000 | bytes 1000000 | tf_op jit(solution)/shard_map/settle/pallas_call | solution.py:721
  25.5 6.9 %collective-permute-start = (f32[9,32,128]{2,1,0:T(8,128)S(1)}, f32[9,32,128]{2,1,0:T(8,128)S(1)}, u32[]{:S(2)}, u32[]{:S(2)}) collective-permute-start(f32[9,32,128]{2,1,0:T(8,128)S(1)} %get-tuple-element.23), channel_id=1, source_target_pairs={{0,1},{1,2},{2,3},{4,5},{5,6},{6,7},{8,9},{9,10},{10,11},{12,13},{... | collective-permute-start | bytes 442376 | tf_op jit(solution)/shard_map/ppermute | solution.py:745
  32.4 1.9 %collective-permute-start.1 = (f32[9,32,128]{2,1,0:T(8,128)S(1)}, f32[9,32,128]{2,1,0:T(8,128)S(1)}, u32[]{:S(2)}, u32[]{:S(2)}) collective-permute-start(f32[9,32,128]{2,1,0:T(8,128)S(1)} %get-tuple-element.24), channel_id=1, source_target_pairs={{1,0},{2,1},{3,2},{5,4},{6,5},{7,6},{9,8},{10,9},{11,10},{13,12},{... | collective-permute-start | bytes 442376 | tf_op jit(solution)/shard_map/ppermute | solution.py:745
  34.3 0.2 collective-permute-done.refs_2_.refs_4_.refs_6_.refs_8_.refs_10_
  34.5 4.7 %collective-permute-done.1.refs_3_.refs_5_.refs_7_.refs_9_.refs_11_ = f32[9,32,128]{2,1,0:T(8,128)S(1)} collective-permute-done((f32[9,32,128]{2,1,0:T(8,128)S(1)}, f32[9,32,128]{2,1,0:T(8,128)S(1)}, u32[]{:S(2)}, u32[]{:S(2)}) %collective-permute-start.1) | collective-permute-done | bytes 147488 | tf_op jit(solution)/shard_map/ppermute | solution.py:745
  39.2 23.4 %interior.2 = (f32[4,32,16,8,128]{4,3,2,1,0:T(8,128)}, f32[8,32,128]{2,1,0:T(8,128)S(1)}, f32[8,32,128]{2,1,0:T(8,128)S(1)}) custom-call(f32[4,32,128,128]{3,2,1,0:T(8,128)} %refs_0_.3, f32[3,32,128,128]{3,2,1,0:T(8,128)} %refs_5_.1, f32[9,32,128]{2,1,0:T(8,128)S(1)} %collective-permute-done.refs_2_.refs_4_.refs_6_.refs_8_.refs_10_, ...), custom_call_target="tpu_custom_call" | custom-call | flops 82575360 | bytes 20971520 | tf_op jit(solution)/shard_map/interior/pallas_call | solution.py:386
  62.5 0.0 collective-permute-done.2.refs_1_.refs_4_.refs_6_
  62.6 0.0 collective-permute-done.3.refs_2_.refs_5_.refs_7_
  62.6 7.3 %boundary.2 = (f32[4,2,16,8,128]{4,3,2,1,0:T(8,128)S(1)}, f32[4,2,16,8,128]{4,3,2,1,0:T(8,128)S(1)}, f32[8,32,128]{2,1,0:T(8,128)S(1)}, f32[8,32,128]{2,1,0:T(8,128)S(1)}) custom-call(f32[4,32,128,128]{3,2,1,0:T(8,128)} %refs_0_.3, f32[9,128,128]{2,1,0:T(8,128)S(1)} %collective-permute-done.2.refs_1_.refs_4_.refs_6_, ...), custom_call_target="tpu_custom_call" | custom-call | flops 13107200 | bytes 6291456 | tf_op jit(solution)/shard_map/boundary/pallas_call | solution.py:532
  69.9 1.9 %collective-permute-start.5 = (f32[4,2,16,8,128]{4,3,2,1,0:T(8,128)S(1)}, f32[4,2,16,8,128]{4,3,2,1,0:T(8,128)S(1)}, u32[]{:S(2)}, u32[]{:S(2)}) collective-permute-start(f32[4,2,16,8,128]{4,3,2,1,0:T(8,128)S(1)} %get-tuple-element.33.refs_1_), channel_id=1, source_target_pairs={{4,0},{8,4},{12,8},{16,12},{20,16},{24,20},{28,24},{5,1},{9,5},{13... | collective-permute-start | bytes 1572872 | tf_op jit(solution)/shard_map/ppermute | solution.py:745
  71.8 4.3 %collective-permute-start.4 = (f32[4,2,16,8,128]{4,3,2,1,0:T(8,128)S(1)}, f32[4,2,16,8,128]{4,3,2,1,0:T(8,128)S(1)}, u32[]{:S(2)}, u32[]{:S(2)}) collective-permute-start(f32[4,2,16,8,128]{4,3,2,1,0:T(8,128)S(1)} %get-tuple-element.34.refs_2_), channel_id=1, source_target_pairs={{0,4},{4,8},{8,12},{12,16},{16,20},{20,24},{24,28},{1,5},{5,9},{9,... | collective-permute-start | bytes 1572872 | tf_op jit(solution)/shard_map/ppermute | solution.py:745
  76.1 2.0 %collective-permute-start.6 = (f32[8,32,128]{2,1,0:T(8,128)S(1)}, f32[8,32,128]{2,1,0:T(8,128)S(1)}, u32[]{:S(2)}, u32[]{:S(2)}) collective-permute-start(f32[8,32,128]{2,1,0:T(8,128)S(1)} %get-tuple-element.35), channel_id=1, source_target_pairs={{0,1},{1,2},{2,3},{4,5},{5,6},{6,7},{8,9},{9,10},{10,11},{12,13},{... | collective-permute-start | bytes 393224 | tf_op jit(solution)/shard_map/ppermute | solution.py:745
  78.1 2.3 %collective-permute-start.7 = (f32[8,32,128]{2,1,0:T(8,128)S(1)}, f32[8,32,128]{2,1,0:T(8,128)S(1)}, u32[]{:S(2)}, u32[]{:S(2)}) collective-permute-start(f32[8,32,128]{2,1,0:T(8,128)S(1)} %get-tuple-element.36), channel_id=1, source_target_pairs={{1,0},{2,1},{3,2},{5,4},{6,5},{7,6},{9,8},{10,9},{11,10},{13,12},{... | collective-permute-start | bytes 393224 | tf_op jit(solution)/shard_map/ppermute | solution.py:745
  80.4 0.0 collective-permute-done.6.refs_4_.refs_8_
  80.5 4.3 %collective-permute-done.7.refs_5_.refs_9_ = f32[8,32,128]{2,1,0:T(8,128)S(1)} collective-permute-done((f32[8,32,128]{2,1,0:T(8,128)S(1)}, f32[8,32,128]{2,1,0:T(8,128)S(1)}, u32[]{:S(2)}, u32[]{:S(2)}) %collective-permute-start.7) | collective-permute-done | bytes 131104 | tf_op jit(solution)/shard_map/ppermute | solution.py:745
  84.7 21.4 %interior.3.refs_12_ = f32[4,32,128,128]{3,2,1,0:T(8,128)} custom-call(f32[4,32,16,8,128]{4,3,2,1,0:T(8,128)} %get-tuple-element.26.refs_0_, f32[4,2,16,8,128]{4,3,2,1,0:T(8,128)S(1)} %get-tuple-element.33.refs_1_, f32[4,2,16,8,128]{4,3,2,1,0:T(8,128)S(1)} %get-tuple-element.34.refs_2_, f32[3,32,128,128]{3,2,1,0:T(8,128)} %refs_5_.1, ...), custom_call_target="tpu_custom_call" | custom-call | flops 82575360 | bytes 20971520 | tf_op jit(solution)/shard_map/interior/pallas_call | solution.py:386
  106.1 0.0 collective-permute-done.5.refs_4_
  106.1 0.0 collective-permute-done.4.refs_3_
  106.1 5.5 %boundary.3 = f32[4,32,128,128]{3,2,1,0:T(8,128)} custom-call(f32[4,32,16,8,128]{4,3,2,1,0:T(8,128)} %get-tuple-element.26.refs_0_, f32[4,2,16,8,128]{4,3,2,1,0:T(8,128)S(1)} %get-tuple-element.33.refs_1_, f32[4,2,16,8,128]{4,3,2,1,0:T(8,128)S(1)} %get-tuple-element.34.refs_2_, ...), custom_call_target="tpu_custom_call", output_to_operand_aliasing={{}: (12, {})} | custom-call | flops 13107200 | bytes 6291456 | tf_op jit(solution)/shard_map/boundary/pallas_call | solution.py:532
  (1 shorter events, 0.0 us)
Async XLA Ops:
  0.6 0.7 copy-start
  1.4 0.7 copy-start.1
  2.0 0.7 copy-start.2
  2.7 0.7 copy-start.3
  3.3 0.7 copy-start.4
  18.8 43.7 %collective-permute-start.2 = (f32[9,128,128]{2,1,0:T(8,128)S(1)}, f32[9,128,128]{2,1,0:T(8,128)S(1)}, u32[]{:S(2)}, u32[]{:S(2)}) collective-permute-start(f32[9,128,128]{2,1,0:T(8,128)S(1)} %get-tuple-element.29), channel_id=1, source_target_pairs={{0,4},{4,8},{8,12},{12,16},{16,20},{20,24},{24,28},{1,5},{5,9},{9,... | collective-permute-start | bytes 1769480 | tf_op jit(solution)/shard_map/ppermute | solution.py:745
  21.9 40.6 %collective-permute-start.3 = (f32[9,128,128]{2,1,0:T(8,128)S(1)}, f32[9,128,128]{2,1,0:T(8,128)S(1)}, u32[]{:S(2)}, u32[]{:S(2)}) collective-permute-start(f32[9,128,128]{2,1,0:T(8,128)S(1)} %get-tuple-element.30), channel_id=1, source_target_pairs={{4,0},{8,4},{12,8},{16,12},{20,16},{24,20},{28,24},{5,1},{9,5},{13... | collective-permute-start | bytes 1769480 | tf_op jit(solution)/shard_map/ppermute | solution.py:745
  25.5 9.0 %collective-permute-start = (f32[9,32,128]{2,1,0:T(8,128)S(1)}, f32[9,32,128]{2,1,0:T(8,128)S(1)}, u32[]{:S(2)}, u32[]{:S(2)}) collective-permute-start(f32[9,32,128]{2,1,0:T(8,128)S(1)} %get-tuple-element.23), channel_id=1, source_target_pairs={{0,1},{1,2},{2,3},{4,5},{5,6},{6,7},{8,9},{9,10},{10,11},{12,13},{... | collective-permute-start | bytes 442376 | tf_op jit(solution)/shard_map/ppermute | solution.py:745
  32.4 6.8 %collective-permute-start.1 = (f32[9,32,128]{2,1,0:T(8,128)S(1)}, f32[9,32,128]{2,1,0:T(8,128)S(1)}, u32[]{:S(2)}, u32[]{:S(2)}) collective-permute-start(f32[9,32,128]{2,1,0:T(8,128)S(1)} %get-tuple-element.24), channel_id=1, source_target_pairs={{1,0},{2,1},{3,2},{5,4},{6,5},{7,6},{9,8},{10,9},{11,10},{13,12},{... | collective-permute-start | bytes 442376 | tf_op jit(solution)/shard_map/ppermute | solution.py:745
  69.9 36.2 %collective-permute-start.5 = (f32[4,2,16,8,128]{4,3,2,1,0:T(8,128)S(1)}, f32[4,2,16,8,128]{4,3,2,1,0:T(8,128)S(1)}, u32[]{:S(2)}, u32[]{:S(2)}) collective-permute-start(f32[4,2,16,8,128]{4,3,2,1,0:T(8,128)S(1)} %get-tuple-element.33.refs_1_), channel_id=1, source_target_pairs={{4,0},{8,4},{12,8},{16,12},{20,16},{24,20},{28,24},{5,1},{9,5},{13... | collective-permute-start | bytes 1572872 | tf_op jit(solution)/shard_map/ppermute | solution.py:745
  71.8 34.3 %collective-permute-start.4 = (f32[4,2,16,8,128]{4,3,2,1,0:T(8,128)S(1)}, f32[4,2,16,8,128]{4,3,2,1,0:T(8,128)S(1)}, u32[]{:S(2)}, u32[]{:S(2)}) collective-permute-start(f32[4,2,16,8,128]{4,3,2,1,0:T(8,128)S(1)} %get-tuple-element.34.refs_2_), channel_id=1, source_target_pairs={{0,4},{4,8},{8,12},{12,16},{16,20},{20,24},{24,28},{1,5},{5,9},{9,... | collective-permute-start | bytes 1572872 | tf_op jit(solution)/shard_map/ppermute | solution.py:745
  76.1 4.3 %collective-permute-start.6 = (f32[8,32,128]{2,1,0:T(8,128)S(1)}, f32[8,32,128]{2,1,0:T(8,128)S(1)}, u32[]{:S(2)}, u32[]{:S(2)}) collective-permute-start(f32[8,32,128]{2,1,0:T(8,128)S(1)} %get-tuple-element.35), channel_id=1, source_target_pairs={{0,1},{1,2},{2,3},{4,5},{5,6},{6,7},{8,9},{9,10},{10,11},{12,13},{... | collective-permute-start | bytes 393224 | tf_op jit(solution)/shard_map/ppermute | solution.py:745
  78.1 6.6 %collective-permute-start.7 = (f32[8,32,128]{2,1,0:T(8,128)S(1)}, f32[8,32,128]{2,1,0:T(8,128)S(1)}, u32[]{:S(2)}, u32[]{:S(2)}) collective-permute-start(f32[8,32,128]{2,1,0:T(8,128)S(1)} %get-tuple-element.36), channel_id=1, source_target_pairs={{1,0},{2,1},{3,2},{5,4},{6,5},{7,6},{9,8},{10,9},{11,10},{13,12},{... | collective-permute-start | bytes 393224 | tf_op jit(solution)/shard_map/ppermute | solution.py:745

commit v3 on v2

--- a/solution.py
+++ b/solution.py
@@ -33,6 +33,11 @@
 
 def minmod(a, b):
     return jnp.maximum(jnp.minimum(a, b), jnp.minimum(jnp.maximum(a, b), 0.0))
+
+
+def picked_minmod(a, b):
+    smaller = jnp.where(jnp.abs(a) < jnp.abs(b), a, b)
+    return jnp.where(a * b > 0, smaller, 0.0)
 
 
 def tile_of(ref, t, tiles):
@@ -109,7 +114,17 @@
     staged([functools.partial(job, range(t, t + PAIR)) for t in range(0, f.tiles, PAIR)])
 
 
-def slab_step(f, k, put):
+def z_shifts(lanes):
+    shape = (2 * lanes, 2 * lanes)
+    row, column = (lax.broadcasted_iota(jnp.int32, shape, axis) for axis in range(2))
+    row = jnp.where(row >= lanes, row - lanes, row)
+    later = jnp.where(column >= lanes, 0, 1)
+    column = jnp.where(column >= lanes, column - lanes, column)
+    plus, minus = row == column + later, row == column + later - 1
+    return (jnp.where(plus, 1.0, 0.0) - jnp.where(minus, 1.0, 0.0)).astype(jnp.bfloat16)
+
+
+def slab_step(f, k, put, minmod=minmod, shifts=None):
     slab = k + 2
     lane = lax.broadcasted_iota(jnp.int32, (8, f.lanes), 1)
     top = f.lanes - 1
@@ -127,7 +142,25 @@
         carry.append((q0, q1, ahead, twice, twice + slope, flux))
     states = {}
 
+    def vertical_by_product(ts):
+        spots = [(t, c) for t in ts for c in range(f.comps)]
+        tiles = [f.field(c, slab, t) for t, c in spots]
+        here = jnp.concatenate(tiles, axis=0)
+        high = here.astype(jnp.bfloat16)
+        rest = (here - high.astype(jnp.float32)).astype(jnp.bfloat16)
+        both = jnp.concatenate([high, rest], axis=1)
+        change = jnp.dot(both, shifts, preferred_element_type=jnp.float32)
+        for n, (spot, q0) in enumerate(zip(spots, tiles)):
+            part = slice(8 * n, 8 * n + 8)
+            slope = minmod(change[part, : f.lanes], change[part, f.lanes :])
+            twice = q0 + q0
+            states[spot] = (twice - slope, twice + slope)
+
     def vertical(t):
+        if shifts is not None:
+            if t % GROUP == 0:
+                vertical_by_product(range(t, t + GROUP))
+            return
         for c in range(f.comps):
             q0 = f.field(c, slab, t)
             over = jnp.where(is_last, 0.0, pltpu.roll(q0, top, 1))
@@ -275,6 +308,9 @@
     packs = None if last else (refs.pop(0), refs.pop(0))
     q, u, v, w, fx, lx, wind, stage, in_sem, out_sem = refs[:10]
     natural = None if last else refs[10]
+    if last:
+        shifts = refs[10]
+        shifts[...] = z_shifts(q.shape[-1])
     comps, slabs, tiles = q.shape[1], q.shape[2], w.shape[2]
     chunks = slabs // CHUNK
     inner = pl.ds(2, tiles)
@@ -342,7 +378,7 @@
             else:
                 stage[c, k, t] = value
 
-        slab_step(f, k, put)
+        slab_step(f, k, put, minmod if last else picked_minmod, shifts[...] if last else None)
         start(stage.at[:, k], out.at[:, k + 2], out_sem)
         if not last:
             pack_edges(packs, lambda c: stage.at[c, k], comps, k + 2)
@@ -376,7 +412,9 @@
         pltpu.SemaphoreType.DMA((slabs // CHUNK, 2)),
         pltpu.SemaphoreType.DMA,
     ]
-    if not last:
+    if last:
+        scratch.append(pltpu.VMEM((2 * lanes, 2 * lanes), jnp.bfloat16))
+    else:
         out_shape += [jax.ShapeDtypeStruct((2 * comps, slabs, lanes), jnp.float32)] * 2
         out_specs += [VMEM] * 2
         operands.append(deposit)

time: 112 us -> 113 us (level)
  transfers between devices with their start and end apart: 8 -> 8, of which waited for: 3 -> 3; matrix products, arithmetic and copies ran while one was open for 0% -> 0% of each run, Pallas kernels for 41% -> 42%
where the time goes in v3:
time: 113 us
  Pallas kernels  64.3 us (57%)
  starting transfers between devices  24.6 us (22%)
  blocking collectives  10.5 us (9%)
  waiting for transfers between devices  9.1 us (8%)
  local copies, waits for them, and re-layouts  3.34 us (3%)
    pallas_call x2, Pallas kernels, interior(): pl.pallas_call(functools.partial(interior_kernel, last, len(fields)), out...  45.8 us
    ppermute x4, starting transfers between devices, exchange(): lax.ppermute(high, axis, forward)  16.2 us
    pallas_call x2, Pallas kernels, boundary(): pl.pallas_call(functools.partial(boundary_kernel, last, slabs), out_shape...  12.9 us
    all_to_all x1, blocking collectives, shards(): lax.all_to_all(copies, 'gx', split_axis=0, concat_axis=0, tiled=True)  10.5 us
    ppermute x4, waiting for transfers between devices, exchange(): lax.ppermute(low, axis, backward)  8.94 us
    ppermute x4, starting transfers between devices, exchange(): lax.ppermute(low, axis, backward)  8.37 us
    pallas_call x1, Pallas kernels, survey(): pl.pallas_call(functools.partial(survey_kernel, groups), grid=(slabs // p...  4.32 us
    unnamed x10, local copies, waits for them, and re-layouts  3.33 us
  transfers between devices with their start and end apart: 8, of which 3 were waited for; matrix products, arithmetic and copies ran while one was open for 0% of the time, Pallas kernels for 42%

profile of v3, /device:TPU:3, one launch (start us, length us, event | category | flops | bytes accessed | tf_op | source)
XLA Modules:
  0.0 112.7 jit_solution(5499609080501496490)
XLA Ops:
  0.6 0.0 copy-start
  0.6 0.7 copy-done
  1.4 0.0 copy-start.1
  1.4 0.7 copy-done.1
  2.0 0.0 copy-start.2
  2.0 0.7 copy-done.2
  2.7 0.0 copy-start.3
  2.7 0.7 copy-done.3
  3.3 0.0 copy-start.4
  3.3 0.7 copy-done.4
  4.0 4.3 %survey.1 = (f32[9,32,128]{2,1,0:T(8,128)S(1)}, f32[9,32,128]{2,1,0:T(8,128)S(1)}, f32[48,128]{1,0:T(8,128)S(1)}, f32[9,128,128]{2,1,0:T(8,128)S(1)}, f32[9,128,128]{2,1,0:T(8,128)S(1)}) custom-call(f32[4,32,128,128]{3,2,1,0:T(8,128)} %refs_0_.3, f32[4,32,128,128]{3,2,1,0:T(8,128)} %refs_0_.3, f32[3,32,128,128]{3,2,1,0:T(8,128)} %refs_5_.1, ...), custom_call_target="tpu_custom_call" | custom-call | flops 5242880 | bytes 5242880 | tf_op jit(solution)/shard_map/survey/pallas_call | solution.py:687
  8.3 10.5 %all_to_all.5.gathered = f32[8,48,128]{2,1,0:T(8,128)S(1)} all-to-all(f32[8,48,128]{2,1,0:T(8,128)S(1)} %broadcast_in_dim.2), channel_id=1, replica_groups=mesh['gx'=8,'gy'=4] {'gx'}, dimensions={0} | all-to-all | bytes 393216 | tf_op jit(solution)/shard_map/all_to_all | solution.py:795
  18.8 3.1 %collective-permute-start.2 = (f32[9,128,128]{2,1,0:T(8,128)S(1)}, f32[9,128,128]{2,1,0:T(8,128)S(1)}, u32[]{:S(2)}, u32[]{:S(2)}) collective-permute-start(f32[9,128,128]{2,1,0:T(8,128)S(1)} %get-tuple-element.29), channel_id=1, source_target_pairs={{0,4},{4,8},{8,12},{12,16},{16,20},{20,24},{24,28},{1,5},{5,9},{9,... | collective-permute-start | bytes 1769480 | tf_op jit(solution)/shard_map/ppermute | solution.py:783
  21.9 2.2 %collective-permute-start.3 = (f32[9,128,128]{2,1,0:T(8,128)S(1)}, f32[9,128,128]{2,1,0:T(8,128)S(1)}, u32[]{:S(2)}, u32[]{:S(2)}) collective-permute-start(f32[9,128,128]{2,1,0:T(8,128)S(1)} %get-tuple-element.30), channel_id=1, source_target_pairs={{4,0},{8,4},{12,8},{16,12},{20,16},{24,20},{28,24},{5,1},{9,5},{13... | collective-permute-start | bytes 1769480 | tf_op jit(solution)/shard_map/ppermute | solution.py:783
  24.2 1.3 %settle.1 = (f32[1,128]{1,0:T(1,128)}, f32[128,128]{1,0:T(8,128)S(1)}, f32[9,32,128]{2,1,0:T(8,128)S(1)}, f32[9,32,128]{2,1,0:T(8,128)S(1)}) custom-call(s32[1]{0:T(128)} %bitcast.me, f32[8,48,128]{2,1,0:T(8,128)S(1)} %all_to_all.5.gathered, f32[9,32,128]{2,1,0:T(8,128)S(1)} %get-tuple-element.21.low_in, f32[9,32,128]{2,1,0:T(8,128)S(1)} %get-tuple-element.22.high_in), custom_call_target="tpu_custom_call" | custom-call | flops 1000000 | bytes 1000000 | tf_op jit(solution)/shard_map/settle/pallas_call | solution.py:759
  25.5 6.9 %collective-permute-start = (f32[9,32,128]{2,1,0:T(8,128)S(1)}, f32[9,32,128]{2,1,0:T(8,128)S(1)}, u32[]{:S(2)}, u32[]{:S(2)}) collective-permute-start(f32[9,32,128]{2,1,0:T(8,128)S(1)} %get-tuple-element.23), channel_id=1, source_target_pairs={{0,1},{1,2},{2,3},{4,5},{5,6},{6,7},{8,9},{9,10},{10,11},{12,13},{... | collective-permute-start | bytes 442376 | tf_op jit(solution)/shard_map/ppermute | solution.py:783
  32.4 1.9 %collective-permute-start.1 = (f32[9,32,128]{2,1,0:T(8,128)S(1)}, f32[9,32,128]{2,1,0:T(8,128)S(1)}, u32[]{:S(2)}, u32[]{:S(2)}) collective-permute-start(f32[9,32,128]{2,1,0:T(8,128)S(1)} %get-tuple-element.24), channel_id=1, source_target_pairs={{1,0},{2,1},{3,2},{5,4},{6,5},{7,6},{9,8},{10,9},{11,10},{13,12},{... | collective-permute-start | bytes 442376 | tf_op jit(solution)/shard_map/ppermute | solution.py:783
  34.3 0.2 collective-permute-done.refs_2_.refs_4_.refs_6_.refs_8_.refs_10_
  34.5 4.7 %collective-permute-done.1.refs_3_.refs_5_.refs_7_.refs_9_.refs_11_ = f32[9,32,128]{2,1,0:T(8,128)S(1)} collective-permute-done((f32[9,32,128]{2,1,0:T(8,128)S(1)}, f32[9,32,128]{2,1,0:T(8,128)S(1)}, u32[]{:S(2)}, u32[]{:S(2)}) %collective-permute-start.1) | collective-permute-done | bytes 147488 | tf_op jit(solution)/shard_map/ppermute | solution.py:783
  39.2 24.9 %interior.2 = (f32[4,32,16,8,128]{4,3,2,1,0:T(8,128)}, f32[8,32,128]{2,1,0:T(8,128)S(1)}, f32[8,32,128]{2,1,0:T(8,128)S(1)}) custom-call(f32[4,32,128,128]{3,2,1,0:T(8,128)} %refs_0_.3, f32[3,32,128,128]{3,2,1,0:T(8,128)} %refs_5_.1, f32[9,32,128]{2,1,0:T(8,128)S(1)} %collective-permute-done.refs_2_.refs_4_.refs_6_.refs_8_.refs_10_, ...), custom_call_target="tpu_custom_call" | custom-call | flops 82575360 | bytes 20971520 | tf_op jit(solution)/shard_map/interior/pallas_call | solution.py:424
  64.0 0.0 collective-permute-done.2.refs_1_.refs_4_.refs_6_
  64.0 0.0 collective-permute-done.3.refs_2_.refs_5_.refs_7_
  64.1 7.3 %boundary.2 = (f32[4,2,16,8,128]{4,3,2,1,0:T(8,128)S(1)}, f32[4,2,16,8,128]{4,3,2,1,0:T(8,128)S(1)}, f32[8,32,128]{2,1,0:T(8,128)S(1)}, f32[8,32,128]{2,1,0:T(8,128)S(1)}) custom-call(f32[4,32,128,128]{3,2,1,0:T(8,128)} %refs_0_.3, f32[9,128,128]{2,1,0:T(8,128)S(1)} %collective-permute-done.2.refs_1_.refs_4_.refs_6_, ...), custom_call_target="tpu_custom_call" | custom-call | flops 13107200 | bytes 6291456 | tf_op jit(solution)/shard_map/boundary/pallas_call | solution.py:570
  71.4 1.9 %collective-permute-start.5 = (f32[4,2,16,8,128]{4,3,2,1,0:T(8,128)S(1)}, f32[4,2,16,8,128]{4,3,2,1,0:T(8,128)S(1)}, u32[]{:S(2)}, u32[]{:S(2)}) collective-permute-start(f32[4,2,16,8,128]{4,3,2,1,0:T(8,128)S(1)} %get-tuple-element.33.refs_1_), channel_id=1, source_target_pairs={{4,0},{8,4},{12,8},{16,12},{20,16},{24,20},{28,24},{5,1},{9,5},{13... | collective-permute-start | bytes 1572872 | tf_op jit(solution)/shard_map/ppermute | solution.py:783
  73.3 4.3 %collective-permute-start.4 = (f32[4,2,16,8,128]{4,3,2,1,0:T(8,128)S(1)}, f32[4,2,16,8,128]{4,3,2,1,0:T(8,128)S(1)}, u32[]{:S(2)}, u32[]{:S(2)}) collective-permute-start(f32[4,2,16,8,128]{4,3,2,1,0:T(8,128)S(1)} %get-tuple-element.34.refs_2_), channel_id=1, source_target_pairs={{0,4},{4,8},{8,12},{12,16},{16,20},{20,24},{24,28},{1,5},{5,9},{9,... | collective-permute-start | bytes 1572872 | tf_op jit(solution)/shard_map/ppermute | solution.py:783
  77.6 2.0 %collective-permute-start.6 = (f32[8,32,128]{2,1,0:T(8,128)S(1)}, f32[8,32,128]{2,1,0:T(8,128)S(1)}, u32[]{:S(2)}, u32[]{:S(2)}) collective-permute-start(f32[8,32,128]{2,1,0:T(8,128)S(1)} %get-tuple-element.35), channel_id=1, source_target_pairs={{0,1},{1,2},{2,3},{4,5},{5,6},{6,7},{8,9},{9,10},{10,11},{12,13},{... | collective-permute-start | bytes 393224 | tf_op jit(solution)/shard_map/ppermute | solution.py:783
  79.6 2.3 %collective-permute-start.7 = (f32[8,32,128]{2,1,0:T(8,128)S(1)}, f32[8,32,128]{2,1,0:T(8,128)S(1)}, u32[]{:S(2)}, u32[]{:S(2)}) collective-permute-start(f32[8,32,128]{2,1,0:T(8,128)S(1)} %get-tuple-element.36), channel_id=1, source_target_pairs={{1,0},{2,1},{3,2},{5,4},{6,5},{7,6},{9,8},{10,9},{11,10},{13,12},{... | collective-permute-start | bytes 393224 | tf_op jit(solution)/shard_map/ppermute | solution.py:783
  81.9 0.0 collective-permute-done.6.refs_4_.refs_8_
  82.0 4.3 %collective-permute-done.7.refs_5_.refs_9_ = f32[8,32,128]{2,1,0:T(8,128)S(1)} collective-permute-done((f32[8,32,128]{2,1,0:T(8,128)S(1)}, f32[8,32,128]{2,1,0:T(8,128)S(1)}, u32[]{:S(2)}, u32[]{:S(2)}) %collective-permute-start.7) | collective-permute-done | bytes 131104 | tf_op jit(solution)/shard_map/ppermute | solution.py:783
  86.2 20.9 %interior.3.refs_12_ = f32[4,32,128,128]{3,2,1,0:T(8,128)} custom-call(f32[4,32,16,8,128]{4,3,2,1,0:T(8,128)} %get-tuple-element.26.refs_0_, f32[4,2,16,8,128]{4,3,2,1,0:T(8,128)S(1)} %get-tuple-element.33.refs_1_, f32[4,2,16,8,128]{4,3,2,1,0:T(8,128)S(1)} %get-tuple-element.34.refs_2_, f32[3,32,128,128]{3,2,1,0:T(8,128)} %refs_5_.1, ...), custom_call_target="tpu_custom_call" | custom-call | flops 82575360 | bytes 20971520 | tf_op jit(solution)/shard_map/interior/pallas_call | solution.py:424
  107.1 0.0 collective-permute-done.5.refs_4_
  107.2 0.0 collective-permute-done.4.refs_3_
  107.2 5.5 %boundary.3 = f32[4,32,128,128]{3,2,1,0:T(8,128)} custom-call(f32[4,32,16,8,128]{4,3,2,1,0:T(8,128)} %get-tuple-element.26.refs_0_, f32[4,2,16,8,128]{4,3,2,1,0:T(8,128)S(1)} %get-tuple-element.33.refs_1_, f32[4,2,16,8,128]{4,3,2,1,0:T(8,128)S(1)} %get-tuple-element.34.refs_2_, ...), custom_call_target="tpu_custom_call", output_to_operand_aliasing={{}: (12, {})} | custom-call | flops 13107200 | bytes 6291456 | tf_op jit(solution)/shard_map/boundary/pallas_call | solution.py:570
  (1 shorter events, 0.0 us)
Async XLA Ops:
  0.6 0.7 copy-start
  1.4 0.7 copy-start.1
  2.0 0.7 copy-start.2
  2.7 0.7 copy-start.3
  3.3 0.7 copy-start.4
  18.8 45.2 %collective-permute-start.2 = (f32[9,128,128]{2,1,0:T(8,128)S(1)}, f32[9,128,128]{2,1,0:T(8,128)S(1)}, u32[]{:S(2)}, u32[]{:S(2)}) collective-permute-start(f32[9,128,128]{2,1,0:T(8,128)S(1)} %get-tuple-element.29), channel_id=1, source_target_pairs={{0,4},{4,8},{8,12},{12,16},{16,20},{20,24},{24,28},{1,5},{5,9},{9,... | collective-permute-start | bytes 1769480 | tf_op jit(solution)/shard_map/ppermute | solution.py:783
  21.9 42.1 %collective-permute-start.3 = (f32[9,128,128]{2,1,0:T(8,128)S(1)}, f32[9,128,128]{2,1,0:T(8,128)S(1)}, u32[]{:S(2)}, u32[]{:S(2)}) collective-permute-start(f32[9,128,128]{2,1,0:T(8,128)S(1)} %get-tuple-element.30), channel_id=1, source_target_pairs={{4,0},{8,4},{12,8},{16,12},{20,16},{24,20},{28,24},{5,1},{9,5},{13... | collective-permute-start | bytes 1769480 | tf_op jit(solution)/shard_map/ppermute | solution.py:783
  25.5 9.0 %collective-permute-start = (f32[9,32,128]{2,1,0:T(8,128)S(1)}, f32[9,32,128]{2,1,0:T(8,128)S(1)}, u32[]{:S(2)}, u32[]{:S(2)}) collective-permute-start(f32[9,32,128]{2,1,0:T(8,128)S(1)} %get-tuple-element.23), channel_id=1, source_target_pairs={{0,1},{1,2},{2,3},{4,5},{5,6},{6,7},{8,9},{9,10},{10,11},{12,13},{... | collective-permute-start | bytes 442376 | tf_op jit(solution)/shard_map/ppermute | solution.py:783
  32.4 6.8 %collective-permute-start.1 = (f32[9,32,128]{2,1,0:T(8,128)S(1)}, f32[9,32,128]{2,1,0:T(8,128)S(1)}, u32[]{:S(2)}, u32[]{:S(2)}) collective-permute-start(f32[9,32,128]{2,1,0:T(8,128)S(1)} %get-tuple-element.24), channel_id=1, source_target_pairs={{1,0},{2,1},{3,2},{5,4},{6,5},{7,6},{9,8},{10,9},{11,10},{13,12},{... | collective-permute-start | bytes 442376 | tf_op jit(solution)/shard_map/ppermute | solution.py:783
  71.4 35.7 %collective-permute-start.5 = (f32[4,2,16,8,128]{4,3,2,1,0:T(8,128)S(1)}, f32[4,2,16,8,128]{4,3,2,1,0:T(8,128)S(1)}, u32[]{:S(2)}, u32[]{:S(2)}) collective-permute-start(f32[4,2,16,8,128]{4,3,2,1,0:T(8,128)S(1)} %get-tuple-element.33.refs_1_), channel_id=1, source_target_pairs={{4,0},{8,4},{12,8},{16,12},{20,16},{24,20},{28,24},{5,1},{9,5},{13... | collective-permute-start | bytes 1572872 | tf_op jit(solution)/shard_map/ppermute | solution.py:783
  73.3 33.8 %collective-permute-start.4 = (f32[4,2,16,8,128]{4,3,2,1,0:T(8,128)S(1)}, f32[4,2,16,8,128]{4,3,2,1,0:T(8,128)S(1)}, u32[]{:S(2)}, u32[]{:S(2)}) collective-permute-start(f32[4,2,16,8,128]{4,3,2,1,0:T(8,128)S(1)} %get-tuple-element.34.refs_2_), channel_id=1, source_target_pairs={{0,4},{4,8},{8,12},{12,16},{16,20},{20,24},{24,28},{1,5},{5,9},{9,... | collective-permute-start | bytes 1572872 | tf_op jit(solution)/shard_map/ppermute | solution.py:783
  77.6 4.3 %collective-permute-start.6 = (f32[8,32,128]{2,1,0:T(8,128)S(1)}, f32[8,32,128]{2,1,0:T(8,128)S(1)}, u32[]{:S(2)}, u32[]{:S(2)}) collective-permute-start(f32[8,32,128]{2,1,0:T(8,128)S(1)} %get-tuple-element.35), channel_id=1, source_target_pairs={{0,1},{1,2},{2,3},{4,5},{5,6},{6,7},{8,9},{9,10},{10,11},{12,13},{... | collective-permute-start | bytes 393224 | tf_op jit(solution)/shard_map/ppermute | solution.py:783
  79.6 6.6 %collective-permute-start.7 = (f32[8,32,128]{2,1,0:T(8,128)S(1)}, f32[8,32,128]{2,1,0:T(8,128)S(1)}, u32[]{:S(2)}, u32[]{:S(2)}) collective-permute-start(f32[8,32,128]{2,1,0:T(8,128)S(1)} %get-tuple-element.36), channel_id=1, source_target_pairs={{1,0},{2,1},{3,2},{5,4},{6,5},{7,6},{9,8},{10,9},{11,10},{13,12},{... | collective-permute-start | bytes 393224 | tf_op jit(solution)/shard_map/ppermute | solution.py:783

commit v4 on v2

--- a/solution.py
+++ b/solution.py
@@ -40,22 +40,25 @@
 
 
 class Slabs:
-    def __init__(self, q, u, v, w, fx, lx, block, u_at, v_at):
-        self.q, self.u, self.v, self.w, self.fx, self.lx = q, u, v, w, fx, lx
-        self.block, self.u_at, self.v_at = block, u_at, v_at
-        self.comps, self.tiles, self.lanes = q.shape[1], w.shape[2], q.shape[-1]
+    def __init__(self, q, sx, sy, sz, fall, fx, lx, block, x_at, at, kept=None):
+        self.q, self.sx, self.sy, self.sz, self.falls, self.fx, self.lx = q, sx, sy, sz, fall, fx, lx
+        self.block, self.x_at, self.at, self.kept = block, x_at, at, kept
+        self.comps, self.tiles, self.lanes = q.shape[1], sz.shape[2], q.shape[-1]
 
     def field(self, c, slab, t):
         return self.q[self.block, c, slab, t + 2]
 
-    def east(self, slab, t):
-        return self.u[self.block, slab + self.u_at, t]
-
-    def north(self, slab, t):
-        return self.v[self.block, slab + self.v_at, t + 1]
-
-    def up(self, slab, t):
-        return self.w[self.block, slab + self.v_at, t]
+    def east(self, k, t):
+        return self.sx[self.block, k + self.x_at, t]
+
+    def north(self, k, t):
+        return self.sy[self.block, k + self.at, t + 1]
+
+    def up(self, k, t):
+        return self.sz[self.block, k + self.at, t]
+
+    def down(self, k, t):
+        return self.falls[self.block, k + self.at, t]
 
 
 def each(function, *lists):
@@ -95,7 +98,7 @@
 def first_face(f):
     def job(ts):
         spots = [(t, c) for t in ts for c in range(f.comps)]
-        speeds = {t: FACTOR * (f.east(0, t) + f.east(1, t)) for t in ts}
+        speeds = {t: f.east(-1, t) for t in ts}
         masks = {t: speeds[t] > 0 for t in ts}
         a, b, q0, q1 = [[f.field(c, slab, t) for t, c in spots] for slab in range(4)]
         middle = difference(q0, b)
@@ -104,6 +107,9 @@
         twice = total_of(q0, q0)
         flux = face_flux([speeds[t] for t, _ in spots], [masks[t] for t, _ in spots], left, difference(twice, slope))
         stores = [(f.fx, spot, x) for spot, x in zip(spots, flux)]
+        if f.kept is not None:
+            stores += [(f.kept[0], spot, x) for spot, x in zip(spots, twice)]
+            stores += [(f.kept[1], spot, x) for spot, x in zip(spots, difference(q1, q0))]
         return stores + [(f.lx, spot, x) for spot, x in zip(spots, total_of(twice, slope))]
 
     staged([functools.partial(job, range(t, t + PAIR)) for t in range(0, f.tiles, PAIR)])
@@ -115,8 +121,7 @@
     top = f.lanes - 1
     is_first, is_last = lane == 0, lane == top
     carry = []
-    north_here = f.north(k, 0)
-    speed = FACTOR * (f.north(k, -1) + north_here)
+    speed = f.north(k, -1)
     for c in range(f.comps):
         a, b, q0, q1 = [f.field(c, slab, t) for t in (-2, -1, 0, 1)]
         middle, ahead = q0 - b, q1 - q0
@@ -125,7 +130,7 @@
         twice = q0 + q0
         flux = speed * jnp.where(speed > 0, left_state, twice - slope)
         carry.append((q0, q1, ahead, twice, twice + slope, flux))
-    states = {}
+    states, doubles = {}, {}
 
     def vertical(t):
         for c in range(f.comps):
@@ -133,8 +138,22 @@
             over = jnp.where(is_last, 0.0, pltpu.roll(q0, top, 1))
             under = jnp.where(is_first, 0.0, pltpu.roll(q0, 1, 1))
             slope = minmod(over - q0, q0 - under)
-            twice = q0 + q0
+            if f.kept is not None:
+                doubles[c, t] = f.kept[0][t, c]
+            twice = double(c, t, q0)
             states[t, c] = (twice - slope, twice + slope)
+
+    def flush(held):
+        for c, t, flux_x, left_x, twice_x, step_x, value in held:
+            f.fx[t, c], f.lx[t, c] = flux_x, left_x
+            if f.kept is not None:
+                f.kept[0][t, c], f.kept[1][t, c] = twice_x, step_x
+            put(c, t, value)
+
+    def double(c, t, tile):
+        if f.kept is None or not 0 <= t < f.tiles:
+            return tile + tile
+        return doubles[c, t]
 
     held = []
     for t in range(GROUP):
@@ -145,36 +164,28 @@
             vertical(t)
         loaded = {}
         for t in group:
-            loaded[t] = (f.east(k + 1, t), f.east(k + 2, t), f.north(k, t + 1), f.up(k, t))
+            loaded[t] = (f.east(k, t), f.north(k, t), f.up(k, t), f.down(k, t))
             for c in range(f.comps):
                 loaded[t, c] = (
                     f.field(c, slab, t + 2), f.field(c, slab + 1, t), f.field(c, slab + 2, t),
-                    f.fx[t, c], f.lx[t, c],
+                    f.fx[t, c], f.lx[t, c], f.kept[1][t, c] if f.kept is not None else None,
                 )
-        for c, t, flux_x, left_x, value in held:
-            f.fx[t, c], f.lx[t, c] = flux_x, left_x
-            put(c, t, value)
+        flush(held)
         held = []
         for t in group:
-            east_here, east_next, north_next, rise = loaded[t]
-            speed_x = FACTOR * (east_here + east_next)
-            speed_y = FACTOR * (north_here + north_next)
-            north_here = north_next
-            rise = FACTOR * rise
-            speed_z = rise + pltpu.roll(rise, top, 1)
-            fall = jnp.where(is_first, jnp.minimum(rise, 0.0), pltpu.roll(speed_z, 1, 1))
-            speed_z = jnp.where(is_last, jnp.maximum(rise, 0.0), speed_z)
+            speed_x, speed_y, speed_z, fall = loaded[t]
             go_x, go_y, go_z, go_fall = speed_x > 0, speed_y > 0, speed_z > 0, fall > 0
             for c in range(f.comps):
-                y2, x1, x2, flux_w, left_w = loaded[t, c]
+                y2, x1, x2, flux_w, left_w, step_w = loaded[t, c]
                 q0, y1, ahead, twice, left_y, flux_y = carry[c]
                 beyond = y2 - y1
                 slope = minmod(beyond, ahead)
-                twice_y = y1 + y1
+                twice_y = double(c, t + 1, y1)
                 flux_next = speed_y * jnp.where(go_y, left_y, twice_y - slope)
                 total = flux_next - flux_y
                 carry[c] = (y1, y2, beyond, twice_y, twice_y + slope, flux_next)
-                slope = minmod(x2 - x1, x1 - q0)
+                step_x = x2 - x1
+                slope = minmod(step_x, x1 - q0 if step_w is None else step_w)
                 twice_x = x1 + x1
                 flux_x = speed_x * jnp.where(go_x, left_w, twice_x - slope)
                 left_x = twice_x + slope
@@ -183,10 +194,8 @@
                 flux_z = speed_z * jnp.where(go_z, upper, pltpu.roll(lower, top, 1))
                 flux_below = fall * jnp.where(go_fall, pltpu.roll(upper, 1, 1), lower)
                 total = total + (flux_z - flux_below)
-                held.append((c, t, flux_x, left_x, q0 - total))
-    for c, t, flux_x, left_x, value in held:
-        f.fx[t, c], f.lx[t, c] = flux_x, left_x
-        put(c, t, value)
+                held.append((c, t, flux_x, left_x, twice_x, step_x, q0 - total))
+    flush(held)
 
 
 def rotated_edges(tiles, lows, highs):
@@ -198,21 +207,17 @@
     return ahead, after
 
 
-def field_job(q, block, c, slab, source, dust, below, above, x):
+def field_job(q, block, c, slab, dust, below, above, x):
     count = q.shape[3] - 4
-    spots = range(count) if source is not None else (0, 1, count - 2, count - 1)
-    if source is None:
-        tiles = [q[block, c, slab, 2 + t] for t in spots]
-    else:
-        tiles = [tile_of(source, t, count) for t in spots]
+    spots = range(count) if dust is not None else (0, 1, count - 2, count - 1)
+    tiles = [q[block, c, slab, 2 + t] for t in spots]
+    stores = []
     if below is not None:
         x = pl.ds(x, 1)
         lows = [below[2 * c + r, x, :] for r in range(2)]
         highs = [above[2 * c + r, x, :] for r in range(2)]
     if dust is not None:
         tiles = total_of(tiles, dust(spots))
-    stores = []
-    if source is not None:
         stores += [(q, (block, c, slab, t + 2), tile) for t, tile in zip(spots, tiles)]
     if below is not None:
         ahead, after = rotated_edges(tiles, lows, highs)
@@ -221,17 +226,14 @@
     return stores
 
 
-def north_job(v, block, slab, source, below, above, x):
-    count = v.shape[2] - 2
-    tiles = [tile_of(source, t, count) for t in range(count)]
+def north_job(sy, block, slab, below, above, x):
+    count = sy.shape[2] - 1
     x = pl.ds(x, 1)
-    ahead, after = rotated_edges(tiles, [below[8, x, :]], [above[8, x, :]])
-    return [(v, (block, slab, t), tile) for t, tile in enumerate(ahead + tiles + after)]
-
-
-def plain_job(target, block, slab, source):
-    count = target.shape[2]
-    return [(target, (block, slab, t), tile_of(source, t, count)) for t in range(count)]
+    row = lax.broadcasted_iota(jnp.int32, sy.shape[-2:], 0)
+    first, final = sy[block, slab, 0], sy[block, slab, count]
+    first = first + jnp.where(row == 0, FACTOR * below[8, x, :], 0.0)
+    final = final + jnp.where(row == 7, FACTOR * above[8, x, :], 0.0)
+    return [(sy, (block, slab, 0), first), (sy, (block, slab, count), final)]
 
 
 def falling(deposit, column, tiles):
@@ -261,21 +263,27 @@
     pltpu.make_async_copy(source, target, sem).start()
 
 
+def start_sets(pairs, sem):
+    for source, target in pairs:
+        for number in range(8):
+            start(source(number), target(number), sem)
+
+
 def arrived(spot, sem):
     pltpu.make_async_copy(spot, spot, sem).wait()
 
 
 def interior_kernel(last, count, *refs):
     refs = list(refs)
-    fields, velocity = refs[:count], refs[count]
-    below, above, v_below, v_above = refs[count + 1 : count + 5]
-    del refs[: count + 5]
+    fields, speeds = refs[:count], refs[count : count + 4]
+    below, above, v_below, v_above = refs[count + 4 : count + 8]
+    del refs[: count + 8]
     deposit = None if last else refs.pop(0)
     out = refs.pop(0)
     packs = None if last else (refs.pop(0), refs.pop(0))
-    q, u, v, w, fx, lx, wind, stage, in_sem, out_sem = refs[:10]
-    natural = None if last else refs[10]
-    comps, slabs, tiles = q.shape[1], q.shape[2], w.shape[2]
+    q, sx, sy, sz, fall, fx, lx, stage, in_sem, out_sem = refs[:10]
+    kept = refs[10:12]
+    comps, slabs, tiles = q.shape[1], q.shape[2], sz.shape[2]
     chunks = slabs // CHUNK
     inner = pl.ds(2, tiles)
 
@@ -293,16 +301,19 @@
             part = pl.ds(begin, size)
             start(middle.at[:, part], q.at[0, :, part, inner], in_sem.at[j, 0])
         else:
-            start(fields[0].at[:, span], natural.at[:, span], in_sem.at[j, 0])
-        start(velocity.at[:, span], wind.at[:, span], in_sem.at[j, 1])
+            pair = (lambda n: fields[0].at[:, span, n], lambda n: q.at[0, :, span, inner, n])
+            start_sets([pair], in_sem.at[j, 0])
+        for n, (source, target) in enumerate(zip(speeds, (sx, sy, sz, fall))):
+            start(source.at[span], target.at[0, span], in_sem.at[j, n + 1])
 
     for j in range(AHEAD):
         fetch(j, j == 0, False)
 
     def arrive(j):
         span = pl.ds(j * CHUNK, CHUNK)
-        arrived(q.at[0, :, span, inner] if last else natural.at[:, span], in_sem.at[j, 0])
-        arrived(wind.at[:, span], in_sem.at[j, 1])
+        arrived(q.at[0, :, span, inner], in_sem.at[j, 0])
+        for n, target in enumerate((sx, sy, sz, fall)):
+            arrived(target.at[0, span], in_sem.at[j, n + 1])
         later = j + AHEAD
 
         @pl.when(later < chunks - 1)
@@ -317,17 +328,14 @@
             jobs = []
             for c in range(comps):
                 dust = falling(deposit, x + 2, tiles) if not last and c == comps - 1 else None
-                source = None if last else natural.at[c, x]
-                jobs.append(functools.partial(field_job, q, 0, c, x, source, dust, below, above, x))
-            jobs.append(functools.partial(plain_job, u, 0, x, wind.at[0, x]))
-            jobs.append(functools.partial(north_job, v, 0, x, wind.at[1, x], v_below, v_above, x))
-            jobs.append(functools.partial(plain_job, w, 0, x, wind.at[2, x]))
+                jobs.append(functools.partial(field_job, q, 0, c, x, dust, below, above, x))
+            jobs.append(functools.partial(north_job, sy, 0, x, v_below, v_above, x))
             staged(jobs)
             return 0
 
         lax.fori_loop(j * CHUNK, (j + 1) * CHUNK, complete, 0)
 
-    f = Slabs(q, u, v, w, fx, lx, 0, 1, 2)
+    f = Slabs(q, sx, sy, sz, fall, fx, lx, 0, 2, 2, kept)
     arrive(jnp.int32(0))
     first_face(f)
 
@@ -337,13 +345,13 @@
             arrive(k // CHUNK + 1)
 
         def put(c, t, value):
-            if last:
-                stage[c, k, pl.ds(t, 8, stride=tiles), :] = value
-            else:
-                stage[c, k, t] = value
+            stage[c, k, t] = value
 
         slab_step(f, k, put)
-        start(stage.at[:, k], out.at[:, k + 2], out_sem)
+        if last:
+            start_sets([(lambda n: stage.at[:, k, :, n], lambda n: out.at[:, k + 2, n])], out_sem)
+        else:
+            start(stage.at[:, k], out.at[:, k + 2], out_sem)
         if not last:
             pack_edges(packs, lambda c: stage.at[c, k], comps, k + 2)
         return 0
@@ -352,36 +360,33 @@
         for pack in packs:
             pack[...] = jnp.zeros_like(pack)
     lax.fori_loop(0, slabs - 4, step, 0)
-    pltpu.make_async_copy(stage, out.at[:, pl.ds(2, slabs - 4)], out_sem).wait()
-
-
-def interior(fields, velocity, below, above, v_below, v_above, deposit=None):
+    arrived(stage, out_sem)
+
+
+def interior(fields, speeds, below, above, v_below, v_above, deposit=None):
     last = deposit is None
-    _, slabs, rows, lanes = velocity.shape
-    tiles, comps = rows // 8, fields[0].shape[0]
-    operands = list(fields) + [velocity, below, above, v_below, v_above]
-    specs = [ANY] * (len(fields) + 1) + [VMEM] * 4
-    form = (rows, lanes) if last else (tiles, 8, lanes)
+    slabs, tiles, _, lanes = speeds[0].shape
+    rows, comps = 8 * tiles, fields[0].shape[0]
+    operands = list(fields) + [*speeds, below, above, v_below, v_above]
+    specs = [ANY] * (len(fields) + 4) + [VMEM] * 4
+    form = (8, tiles, lanes) if last else (tiles, 8, lanes)
     out_shape = [jax.ShapeDtypeStruct((comps, slabs, *form), jnp.float32)]
     out_specs = [ANY]
     scratch = [
         pltpu.VMEM((1, comps, slabs, tiles + 4, 8, lanes), jnp.float32),
-        pltpu.VMEM((1, slabs, tiles, 8, lanes), jnp.float32),
-        pltpu.VMEM((1, slabs, tiles + 2, 8, lanes), jnp.float32),
-        pltpu.VMEM((1, slabs, tiles, 8, lanes), jnp.float32),
+        *[pltpu.VMEM((1, *speed.shape), jnp.float32) for speed in speeds],
         pltpu.VMEM((tiles, comps, 8, lanes), jnp.float32),
         pltpu.VMEM((tiles, comps, 8, lanes), jnp.float32),
-        pltpu.VMEM(velocity.shape, jnp.float32),
-        pltpu.VMEM((comps, slabs - 4, *form), jnp.float32),
-        pltpu.SemaphoreType.DMA((slabs // CHUNK, 2)),
+        pltpu.VMEM((comps, slabs - 4, tiles, 8, lanes), jnp.float32),
+        pltpu.SemaphoreType.DMA((slabs // CHUNK, 5)),
         pltpu.SemaphoreType.DMA,
     ]
+    scratch += [pltpu.VMEM((tiles, comps, 8, lanes), jnp.float32)] * 2
     if not last:
         out_shape += [jax.ShapeDtypeStruct((2 * comps, slabs, lanes), jnp.float32)] * 2
         out_specs += [VMEM] * 2
         operands.append(deposit)
         specs.append(VMEM)
-        scratch.append(pltpu.VMEM((comps, slabs, rows, lanes), jnp.float32))
     cells = comps * (slabs - 4) * rows * lanes
     return pl.pallas_call(
         functools.partial(interior_kernel, last, len(fields)),
@@ -390,7 +395,7 @@
         out_specs=tuple(out_specs),
         scratch_shapes=scratch,
         compiler_params=params(),
-        cost_estimate=cost(45 * cells, 4 * (2 * cells + 3 * slabs * rows * lanes)),
+        cost_estimate=cost(40 * cells, 4 * (2 * cells + 4 * slabs * rows * lanes)),
         name="interior",
     )(*operands)
 
@@ -398,18 +403,18 @@
 def boundary_kernel(last, slabs, *refs):
     refs = list(refs)
     count = 5 if last else 3
-    fields, velocity, u_low, u_high = refs[:count], refs[count], refs[count + 1], refs[count + 2]
-    below, above, v_below, v_above = refs[count + 3 : count + 7]
-    del refs[: count + 7]
+    fields, speeds = refs[:count], refs[count : count + 4]
+    u_outer, u_inner = refs[count + 4 : count + 6], refs[count + 6 : count + 8]
+    below, above, v_below, v_above = refs[count + 8 : count + 12]
+    del refs[: count + 12]
     if last:
         out = refs[1]
         del refs[:2]
     else:
         deposit, packed, ends, packs = refs[0], refs[1:3], refs[3:5], refs[5:7]
         del refs[:7]
-    q, u, v, w, fx, lx, wind, stage, in_sem, out_sem = refs[:10]
-    natural = None if last else refs[10]
-    comps, tiles = q.shape[1], w.shape[2]
+    q, sx, sy, sz, fall, fx, lx, u, stage, in_sem, out_sem = refs
+    comps, tiles = q.shape[1], sz.shape[2]
     inner = pl.ds(2, tiles)
 
     if last:
@@ -421,34 +426,45 @@
             start(source, q.at[block, :, pl.ds(at, 2), inner], in_sem.at[block, 0])
     else:
         state, x_low, x_high = fields
-        start(state.at[:, pl.ds(0, 4)], natural.at[0, :, pl.ds(2, 4)], in_sem.at[0, 0])
-        start(state.at[:, pl.ds(slabs - 4, 4)], natural.at[1, :, pl.ds(0, 4)], in_sem.at[1, 0])
-        for c in range(comps):
-            pair = pl.ds(2 * c, 2)
-            start(x_low.at[pair], natural.at[0, c, pl.ds(0, 2)], in_sem.at[0, 0])
-            start(x_high.at[pair], natural.at[1, c, pl.ds(4, 2)], in_sem.at[1, 0])
+        for block, at, first in ((0, 2, 0), (1, 0, slabs - 4)):
+            pair = (
+                lambda n: state.at[:, pl.ds(first, 4), n], lambda n: q.at[block, :, pl.ds(at, 4), inner, n]
+            )
+            start_sets([pair], in_sem.at[block, 0])
+        for block, at, halo in ((0, 0, x_low), (1, 4, x_high)):
+            pairs = [
+                (lambda n, c=c: halo.at[pl.ds(2 * c, 2), n], lambda n, c=c: q.at[block, c, pl.ds(at, 2), inner, n])
+                for c in range(comps)
+            ]
+            start_sets(pairs, in_sem.at[block, 0])
     edge = pl.ds(2 * comps, 1)
-    start(u_low.at[edge], wind.at[0, 0, pl.ds(0, 1)], in_sem.at[0, 1])
-    start(velocity.at[:, pl.ds(0, 3)], wind.at[0, :, pl.ds(1, 3)], in_sem.at[0, 2])
-    start(velocity.at[:, pl.ds(slabs - 3, 3)], wind.at[1, :, pl.ds(0, 3)], in_sem.at[1, 2])
-    start(u_high.at[edge], wind.at[1, 0, pl.ds(3, 1)], in_sem.at[1, 1])
+    for block in range(2):
+        pairs = [
+            (lambda n, r=ref: r.at[edge, n], lambda n, i=i: u.at[block, pl.ds(i, 1), :, n])
+            for i, ref in enumerate((u_outer[block], u_inner[block]))
+        ]
+        start_sets(pairs, in_sem.at[block, 1])
+    start(speeds[0].at[pl.ds(0, 2)], sx.at[0, pl.ds(1, 2)], in_sem.at[0, 2])
+    start(speeds[0].at[pl.ds(slabs - 3, 2)], sx.at[1, pl.ds(0, 2)], in_sem.at[1, 2])
+    for block in range(2):
+        span = pl.ds(block * (slabs - 2), 2)
+        for n, target in enumerate((sy, sz, fall)):
+            start(speeds[n + 1].at[span], target.at[block], in_sem.at[block, n + 3])
     if not last:
         packs[0][...] = packed[0][...]
         packs[1][...] = packed[1][...]
 
     def one(block, _):
         begin = block * (slabs - 2)
-        arrived(q.at[block, :, :, inner] if last else natural.at[block], in_sem.at[block, 0])
-        arrived(wind.at[0, 0, pl.ds(0, 1)], in_sem.at[block, 1])
-        arrived(wind.at[0, :, pl.ds(0, 3)], in_sem.at[block, 2])
+        arrived(q.at[block, :, :, inner], in_sem.at[block, 0])
+        arrived(u.at[block], in_sem.at[block, 1])
+        arrived(sx.at[block, pl.ds(0, 2)], in_sem.at[block, 2])
+        for n, target in enumerate((sy, sz, fall)):
+            arrived(target.at[block], in_sem.at[block, n + 3])
 
         def complete(slab, _):
-            jobs = []
-            for c in range(comps):
-                dust = falling(deposit, begin + slab, tiles) if c == comps - 1 else None
-                source = natural.at[block, c, slab]
-                jobs.append(functools.partial(field_job, q, block, c, slab, source, dust, None, None, None))
-            staged(jobs)
+            dust = falling(deposit, begin + slab, tiles)
+            staged([functools.partial(field_job, q, block, comps - 1, slab, dust, None, None, None)])
             return 0
 
         if not last:
@@ -457,24 +473,22 @@
         def edges(k, _):
             x = begin + k
             jobs = [
-                functools.partial(field_job, q, block, c, k + 2, None, None, below, above, x) for c in range(comps)
+                functools.partial(field_job, q, block, c, k + 2, None, below, above, x) for c in range(comps)
             ]
-            jobs.append(functools.partial(north_job, v, block, k, wind.at[block, 1, k + 1], v_below, v_above, x))
-            jobs.append(functools.partial(plain_job, w, block, k, wind.at[block, 2, k + 1]))
+            jobs.append(functools.partial(north_job, sy, block, k, v_below, v_above, x))
             staged(jobs)
             return 0
 
         lax.fori_loop(0, 2, edges, 0)
-        staged([functools.partial(plain_job, u, block, k, wind.at[block, 0, k]) for k in range(4)])
-        f = Slabs(q, u, v, w, fx, lx, block, 0, 0)
+        faces = total_of([u[block, 0, t] for t in range(tiles)], [u[block, 1, t] for t in range(tiles)])
+        for t, x in enumerate(faces):
+            sx[block, 2 * block, t] = FACTOR * x
+        f = Slabs(q, sx, sy, sz, fall, fx, lx, block, 1, 0)
         first_face(f)
 
         def step(k, _):
             def put(c, t, value):
-                if last:
-                    stage[block, c, k, pl.ds(t, 8, stride=tiles), :] = value
-                else:
-                    stage[block, c, k, t] = value
+                stage[block, c, k, t] = value
 
             slab_step(f, k, put)
             if not last:
@@ -485,33 +499,35 @@
         return 0
 
     lax.fori_loop(0, 2, one, 0)
-    copies = []
     for block in range(2):
-        target = out.at[:, pl.ds(block * (slabs - 2), 2)] if last else ends[block]
-        copies.append(pltpu.make_async_copy(stage.at[block], target, out_sem.at[block]))
-    for copy in copies:
-        copy.start()
-    for copy in copies:
-        copy.wait()
-
-
-def boundary(fields, velocity, u_low, u_high, below, above, v_below, v_above, *, deposit=None, packed=None, out=None):
+        if last:
+            span = pl.ds(block * (slabs - 2), 2)
+            pair = (lambda n: stage.at[block, :, :, :, n], lambda n: out.at[:, span, n])
+            start_sets([pair], out_sem.at[block])
+        else:
+            start(stage.at[block], ends[block], out_sem.at[block])
+    for block in range(2):
+        arrived(stage.at[block], out_sem.at[block])
+
+
+def boundary(fields, speeds, u_outer, u_inner, below, above, v_below, v_above, *, deposit=None, packed=None, out=None):
     last = out is not None
-    _, slabs, rows, lanes = velocity.shape
-    tiles, comps = rows // 8, fields[0].shape[0]
-    operands = list(fields) + [velocity, u_low, u_high, below, above, v_below, v_above]
-    specs = [ANY] * (len(fields) + 3) + [VMEM] * 4
-    form = (rows, lanes) if last else (tiles, 8, lanes)
+    slabs, tiles, _, lanes = speeds[0].shape
+    rows, comps = 8 * tiles, fields[0].shape[0]
+    operands = list(fields) + [*speeds, *u_outer, *u_inner, below, above, v_below, v_above]
+    specs = [ANY] * (len(fields) + 8) + [VMEM] * 4
+    form = (tiles, 8, lanes)
     scratch = [
         pltpu.VMEM((2, comps, 6, tiles + 4, 8, lanes), jnp.float32),
-        pltpu.VMEM((2, 4, tiles, 8, lanes), jnp.float32),
-        pltpu.VMEM((2, 2, tiles + 2, 8, lanes), jnp.float32),
+        pltpu.VMEM((2, 3, tiles, 8, lanes), jnp.float32),
+        pltpu.VMEM((2, 2, tiles + 1, 8, lanes), jnp.float32),
+        pltpu.VMEM((2, 2, tiles, 8, lanes), jnp.float32),
         pltpu.VMEM((2, 2, tiles, 8, lanes), jnp.float32),
         pltpu.VMEM((tiles, comps, 8, lanes), jnp.float32),
         pltpu.VMEM((tiles, comps, 8, lanes), jnp.float32),
-        pltpu.VMEM((2, 3, 4, rows, lanes), jnp.float32),
+        pltpu.VMEM((2, 2, tiles, 8, lanes), jnp.float32),
         pltpu.VMEM((2, comps, 2, *form), jnp.float32),
-        pltpu.SemaphoreType.DMA((2, 3)),
+        pltpu.SemaphoreType.DMA((2, 6)),
         pltpu.SemaphoreType.DMA((2,)),
     ]
     if last:
@@ -527,7 +543,6 @@
         out_shape = (jax.ShapeDtypeStruct((comps, 2, *form), jnp.float32),) * 2
         out_shape += (jax.ShapeDtypeStruct((2 * comps, slabs, lanes), jnp.float32),) * 2
         out_specs = (ANY, ANY, VMEM, VMEM)
-        scratch.append(pltpu.VMEM((2, comps, 6, rows, lanes), jnp.float32))
     cells = comps * 4 * rows * lanes
     return pl.pallas_call(
         functools.partial(boundary_kernel, last, slabs),
@@ -540,6 +555,75 @@
         cost_estimate=cost(50 * cells, 4 * 6 * cells),
         name="boundary",
     )(*operands)
+
+
+def speeds_kernel(velocity, sx, sy, sz, fall, wind, sems):
+    step, steps = pl.program_id(0), pl.num_programs(0)
+    part, count, lanes = sx.shape[0], wind.shape[2], wind.shape[4]
+    shape = (8, lanes)
+    row, lane = (lax.broadcasted_iota(jnp.int32, shape, axis) for axis in range(2))
+    is_first, is_last = lane == 0, lane == lanes - 1
+
+    @pl.when(step == 0)
+    def _():
+        for j in range(wind.shape[1] // part):
+            span = pl.ds(j * part, part)
+            start_sets([(lambda n: velocity.at[:, span, n], lambda n: wind.at[:, span, :, n])], sems.at[j])
+        arrived(wind.at[:, pl.ds(0, part)], sems.at[0])
+
+    @pl.when(step < steps - 1)
+    def _():
+        arrived(wind.at[:, pl.ds((step + 1) * part, part)], sems.at[step + 1])
+
+    def one(x, _):
+        at = step * part + x
+        after = jnp.minimum(at + 1, wind.shape[1] - 1)
+
+        def job_x():
+            here = [wind[0, at, t] for t in range(count)]
+            nearer = [wind[0, after, t] for t in range(count)]
+            return [(sx, (x, t), FACTOR * tile) for t, tile in enumerate(total_of(here, nearer))]
+
+        def job_y():
+            here = [FACTOR * wind[1, at, t] for t in range(count)]
+            inner = total_of(here[:-1], here[1:])
+            final = here[-1] + jnp.where(row == 7, 0.0, pltpu.roll(here[0], 7, 0))
+            first = here[0] + jnp.where(row == 0, 0.0, pltpu.roll(here[-1], 1, 0))
+            return [(sy, (x, t), tile) for t, tile in enumerate([first, *inner, final])]
+
+        def job_z():
+            here = [FACTOR * wind[2, at, t] for t in range(count)]
+            over = [pltpu.roll(tile, lanes - 1, 1) for tile in here]
+            under = [pltpu.roll(tile, 1, 1) for tile in here]
+            upper = [jnp.where(is_last, jnp.maximum(a, 0.0), a + b) for a, b in zip(here, over)]
+            lower = [jnp.where(is_first, jnp.minimum(a, 0.0), a + b) for a, b in zip(here, under)]
+            stores = [(sz, (x, t), tile) for t, tile in enumerate(upper)]
+            return stores + [(fall, (x, t), tile) for t, tile in enumerate(lower)]
+
+        staged([job_x, job_y, job_z])
+        return 0
+
+    lax.fori_loop(0, part, one, 0)
+
+
+def face_speeds(velocity):
+    _, slabs, _, tiles, lanes = velocity.shape
+    part = 8
+    counts = (tiles, tiles + 1, tiles, tiles)
+    return pl.pallas_call(
+        speeds_kernel,
+        grid=(slabs // part,),
+        out_shape=tuple(jax.ShapeDtypeStruct((slabs, n, 8, lanes), jnp.float32) for n in counts),
+        in_specs=[ANY],
+        out_specs=tuple(pl.BlockSpec((part, n, 8, lanes), lambda i: (i, 0, 0, 0)) for n in counts),
+        scratch_shapes=[
+            pltpu.VMEM((3, slabs, tiles, 8, lanes), jnp.float32),
+            pltpu.SemaphoreType.DMA((slabs // part,)),
+        ],
+        compiler_params=params(),
+        cost_estimate=cost(16 * slabs * 8 * tiles * lanes, 28 * slabs * 8 * tiles * lanes),
+        name="face_speeds",
+    )(velocity)
 
 
 def x_copies(state, velocity, low, high, sems):
@@ -750,28 +834,36 @@
     slabs = state.shape[1]
     me = lax.axis_index("gx").astype(jnp.int32).reshape(1)
 
-    low, high, payload, x_low, x_high = survey(
+    low, high, payload, own_low, own_high = survey(
         groups, state, velocity, threshold, tile_owner[:, :, 0], parcel_owner[:, :, 0], parcel_count, parcel_share
     )
+    rows, lanes = state.shape[2:]
+
+    def sets(array):
+        return array.reshape(*array.shape[:-2], 8, rows // 8, lanes)
+
+    speeds = face_speeds(sets(velocity))
     copies = jnp.broadcast_to(payload[None], (groups, *payload.shape))
     gathered = lax.all_to_all(copies, "gx", split_axis=0, concat_axis=0, tiled=True)
     flux, deposit, low, high = settle(me, gathered, low, high, slabs)
     below, above = exchange(low, high, "gy")
-    x_low, x_high, _ = lax.optimization_barrier((x_low, x_high, gathered))
-    x_low, x_high = exchange(x_low, x_high, "gx")
-    middle, pack_low, pack_high = interior([state], velocity, below, above, below, above, deposit)
+    own_low, own_high, _ = lax.optimization_barrier((own_low, own_high, gathered))
+    x_low, x_high = exchange(own_low, own_high, "gx")
+    x_low, x_high = sets(x_low), sets(x_high)
+    u_edges = ((x_low, x_high), (sets(own_low), sets(own_high)))
+    middle, pack_low, pack_high = interior([sets(state)], speeds, below, above, below, above, deposit)
     end_low, end_high, y_low, y_high = boundary(
-        [state, x_low, x_high], velocity, x_low, x_high, below, above, below, above,
+        [sets(state), x_low, x_high], speeds, *u_edges, below, above, below, above,
         deposit=deposit, packed=(pack_low, pack_high),
     )
     x2_low, x2_high = exchange(end_low, end_high, "gx")
     below2, above2 = exchange(y_low, y_high, "gy")
-    (inside,) = interior([middle, end_low, end_high], velocity, below2, above2, below, above)
+    (inside,) = interior([middle, end_low, end_high], speeds, below2, above2, below, above)
     fields = boundary(
-        [middle, end_low, end_high, x2_low, x2_high], velocity, x_low, x_high, below2, above2, below, above,
+        [middle, end_low, end_high, x2_low, x2_high], speeds, *u_edges, below2, above2, below, above,
         out=inside,
     )
-    return fields, flux
+    return fields.reshape(state.shape), flux
 
 
 def solution(mesh):

time: 112 us -> 109 us (0.973)
  waiting for transfers between devices: 9.1 us -> 4.66 us
  starting transfers between devices: 24.6 us -> 26.4 us
    pallas_call x0 -> x1, Pallas kernels: none -> 6.71 us  [face_speeds(): pl.pallas_call(speeds_kernel, grid=(slabs // part,), out_shape=tuple((jax...]
    pallas_call x2, Pallas kernels: 44.7 us -> 38.6 us  [interior(): pl.pallas_call(functools.partial(interior_kernel, last, len(fields)), out...]
    ppermute x4, waiting for transfers between devices: 8.94 us -> 4.65 us  [exchange(): lax.ppermute(low, axis, backward)]
    ppermute x4, starting transfers between devices: 16.2 us -> 18.4 us  [exchange(): lax.ppermute(high, axis, forward)]
    pallas_call x2, Pallas kernels: 12.9 us -> 11.5 us  [boundary(): pl.pallas_call(functools.partial(boundary_kernel, last, slabs), out_shape...]
    unnamed x10 -> x18, local copies, waits for them, and re-layouts: 3.33 us -> 3.35 us
  transfers between devices with their start and end apart: 8 -> 8, of which waited for: 3 -> 1; matrix products, arithmetic and copies ran while one was open for 0% -> 0% of each run, Pallas kernels for 41% -> 43%
where the time goes in v4:
time: 109 us; the launch traced here: 108 us
  Pallas kernels  62.4 us (57%)
  starting transfers between devices  26.4 us (24%)
  blocking collectives  10.5 us (10%)
  waiting for transfers between devices  4.66 us (4%)
  local copies, waits for them, and re-layouts  3.36 us (3%)
    pallas_call x2, Pallas kernels, interior(): pl.pallas_call(functools.partial(interior_kernel, last, len(fields)), out...  38.6 us
    ppermute x4, starting transfers between devices, exchange(): lax.ppermute(high, axis, forward)  18.4 us
    pallas_call x2, Pallas kernels, boundary(): pl.pallas_call(functools.partial(boundary_kernel, last, slabs), out_shape...  11.5 us
    all_to_all x1, blocking collectives, shards(): lax.all_to_all(copies, 'gx', split_axis=0, concat_axis=0, tiled=True)  10.5 us
    ppermute x4, starting transfers between devices, exchange(): lax.ppermute(low, axis, backward)  7.99 us
    pallas_call x1, Pallas kernels, face_speeds(): pl.pallas_call(speeds_kernel, grid=(slabs // part,), out_shape=tuple((jax...  6.71 us
    ppermute x4, waiting for transfers between devices, exchange(): lax.ppermute(low, axis, backward)  4.65 us
    pallas_call x1, Pallas kernels, survey(): pl.pallas_call(functools.partial(survey_kernel, groups), grid=(slabs // p...  4.32 us
  transfers between devices with their start and end apart: 8, of which 1 were waited for; matrix products, arithmetic and copies ran while one was open for 0% of the time, Pallas kernels for 43%

profile of v4, /device:TPU:3, one launch (start us, length us, event | category | flops | bytes accessed | tf_op | source)
XLA Modules:
  0.0 108.2 jit_solution(14088585800776254541)
XLA Ops:
  0.6 0.0 copy-start.4
  0.6 0.7 copy-done.4
  1.4 0.0 copy-start.5
  1.4 0.7 copy-done.5
  2.0 0.0 copy-start.6
  2.0 0.7 copy-done.6
  2.7 0.0 copy-start.7
  2.7 0.7 copy-done.7
  3.3 0.0 copy-start.8
  3.3 0.7 copy-done.8
  4.0 4.3 %survey.1 = (f32[9,32,128]{2,1,0:T(8,128)S(1)}, f32[9,32,128]{2,1,0:T(8,128)S(1)}, f32[48,128]{1,0:T(8,128)S(1)}, f32[9,128,128]{2,1,0:T(8,128)S(1)}, f32[9,128,128]{2,1,0:T(8,128)S(1)}) custom-call(f32[4,32,128,128]{3,2,1,0:T(8,128)} %state.1, f32[4,32,128,128]{3,2,1,0:T(8,128)} %state.1, f32[3,32,128,128]{3,2,1,0:T(8,128)} %velocity.1, ...), custom_call_target="tpu_custom_call" | custom-call | flops 5242880 | bytes 5242880 | tf_op jit(solution)/shard_map/survey/pallas_call | solution.py:733
  8.3 10.5 %all_to_all.5.gathered = f32[8,48,128]{2,1,0:T(8,128)S(1)} all-to-all(f32[8,48,128]{2,1,0:T(8,128)S(1)} %broadcast_in_dim.2), channel_id=1, replica_groups=mesh['gx'=8,'gy'=4] {'gx'}, dimensions={0} | all-to-all | bytes 393216 | tf_op jit(solution)/shard_map/all_to_all | solution.py:847
  18.8 3.1 %collective-permute-start.2 = (f32[9,128,128]{2,1,0:T(8,128)S(1)}, f32[9,128,128]{2,1,0:T(8,128)S(1)}, u32[]{:S(2)}, u32[]{:S(2)}) collective-permute-start(f32[9,128,128]{2,1,0:T(8,128)S(1)} %get-tuple-element.37), channel_id=1, source_target_pairs={{0,4},{4,8},{8,12},{12,16},{16,20},{20,24},{24,28},{1,5},{5,9},{9,... | collective-permute-start | bytes 1769480 | tf_op jit(solution)/shard_map/ppermute | solution.py:829
  21.9 2.2 %collective-permute-start.3 = (f32[9,128,128]{2,1,0:T(8,128)S(1)}, f32[9,128,128]{2,1,0:T(8,128)S(1)}, u32[]{:S(2)}, u32[]{:S(2)}) collective-permute-start(f32[9,128,128]{2,1,0:T(8,128)S(1)} %get-tuple-element.38), channel_id=1, source_target_pairs={{4,0},{8,4},{12,8},{16,12},{20,16},{24,20},{28,24},{5,1},{9,5},{13... | collective-permute-start | bytes 1769480 | tf_op jit(solution)/shard_map/ppermute | solution.py:829
  24.2 1.3 %settle.1 = (f32[1,128]{1,0:T(1,128)}, f32[128,128]{1,0:T(8,128)S(1)}, f32[9,32,128]{2,1,0:T(8,128)S(1)}, f32[9,32,128]{2,1,0:T(8,128)S(1)}) custom-call(s32[1]{0:T(128)} %bitcast.2.me, f32[8,48,128]{2,1,0:T(8,128)S(1)} %all_to_all.5.gathered, f32[9,32,128]{2,1,0:T(8,128)S(1)} %get-tuple-element.29.low_in, f32[9,32,128]{2,1,0:T(8,128)S(1)} %get-tuple-element.30.high_in), custom_call_target="tpu_custom_call" | custom-call | flops 1000000 | bytes 1000000 | tf_op jit(solution)/shard_map/settle/pallas_call | solution.py:805
  25.5 6.9 %collective-permute-start = (f32[9,32,128]{2,1,0:T(8,128)S(1)}, f32[9,32,128]{2,1,0:T(8,128)S(1)}, u32[]{:S(2)}, u32[]{:S(2)}) collective-permute-start(f32[9,32,128]{2,1,0:T(8,128)S(1)} %get-tuple-element.31), channel_id=1, source_target_pairs={{0,1},{1,2},{2,3},{4,5},{5,6},{6,7},{8,9},{9,10},{10,11},{12,13},{... | collective-permute-start | bytes 442376 | tf_op jit(solution)/shard_map/ppermute | solution.py:829
  32.4 1.9 %collective-permute-start.1 = (f32[9,32,128]{2,1,0:T(8,128)S(1)}, f32[9,32,128]{2,1,0:T(8,128)S(1)}, u32[]{:S(2)}, u32[]{:S(2)}) collective-permute-start(f32[9,32,128]{2,1,0:T(8,128)S(1)} %get-tuple-element.32), channel_id=1, source_target_pairs={{1,0},{2,1},{3,2},{5,4},{6,5},{7,6},{9,8},{10,9},{11,10},{13,12},{... | collective-permute-start | bytes 442376 | tf_op jit(solution)/shard_map/ppermute | solution.py:829
  34.3 6.7 %face_speeds.1 = (f32[32,16,8,128]{3,2,1,0:T(8,128)S(1)}, f32[32,17,8,128]{3,2,1,0:T(8,128)}, f32[32,16,8,128]{3,2,1,0:T(8,128)S(1)}, f32[32,16,8,128]{3,2,1,0:T(8,128)}) custom-call(f32[3,32,8,16,128]{4,3,2,1,0:T(8,128)} %bitcast.24), custom_call_target="tpu_custom_call" | custom-call | flops 8388608 | bytes 14680064 | tf_op jit(solution)/shard_map/face_speeds/pallas_call | solution.py:613
  41.1 0.0 copy-start
  41.1 0.0 copy-start.2
  41.1 0.0 collective-permute-done.refs_5_.refs_7_.refs_11_.refs_13_.refs_9_.refs_15_
  41.1 0.0 collective-permute-done.1.refs_6_.refs_8_.refs_12_.refs_14_.refs_10_.refs_16_
  41.1 21.2 %interior.2 = (f32[4,32,16,8,128]{4,3,2,1,0:T(8,128)}, f32[8,32,128]{2,1,0:T(8,128)S(1)}, f32[8,32,128]{2,1,0:T(8,128)S(1)}) custom-call(f32[4,32,8,16,128]{4,3,2,1,0:T(8,128)} %bitcast.22, f32[32,16,8,128]{3,2,1,0:T(8,128)S(1)} %get-tuple-element.24.refs_1_.refs_3_.refs_5_, f32[32,17,8,128]{3,2,1,0:T(8,128)} %get-tuple-element.25.refs_2_.refs_4_.refs_6_, ...), custom_call_target="tpu_custom_call" | custom-call | flops 73400320 | bytes 23068672 | tf_op jit(solution)/shard_map/interior/pallas_call | solution.py:391
  62.3 0.0 copy-done
  62.3 0.0 copy-done.2
  62.3 0.0 collective-permute-done.2
  62.3 0.0 collective-permute-done.3
  62.3 0.0 copy-start.1
  62.3 0.0 copy-start.3
  62.3 6.6 %boundary.2 = (f32[4,2,16,8,128]{4,3,2,1,0:T(8,128)S(1)}, f32[4,2,16,8,128]{4,3,2,1,0:T(8,128)S(1)}, f32[8,32,128]{2,1,0:T(8,128)S(1)}, f32[8,32,128]{2,1,0:T(8,128)S(1)}) custom-call(f32[4,32,8,16,128]{4,3,2,1,0:T(8,128)} %bitcast.23, f32[9,8,16,128]{3,2,1,0:T(8,128)S(1)} %bitcast.10, f32[9,8,16,128]{3,2,1,0:T(8,128)S(1)} %bitcast.13, ...), custom_call_target="tpu_custom_call" | custom-call | flops 13107200 | bytes 6291456 | tf_op jit(solution)/shard_map/boundary/pallas_call | solution.py:547
  68.9 1.9 %collective-permute-start.5 = (f32[4,2,16,8,128]{4,3,2,1,0:T(8,128)S(1)}, f32[4,2,16,8,128]{4,3,2,1,0:T(8,128)S(1)}, u32[]{:S(2)}, u32[]{:S(2)}) collective-permute-start(f32[4,2,16,8,128]{4,3,2,1,0:T(8,128)S(1)} %get-tuple-element.41.refs_1_), channel_id=1, source_target_pairs={{4,0},{8,4},{12,8},{16,12},{20,16},{24,20},{28,24},{5,1},{9,5},{13... | collective-permute-start | bytes 1572872 | tf_op jit(solution)/shard_map/ppermute | solution.py:829
  70.8 4.3 %collective-permute-start.4 = (f32[4,2,16,8,128]{4,3,2,1,0:T(8,128)S(1)}, f32[4,2,16,8,128]{4,3,2,1,0:T(8,128)S(1)}, u32[]{:S(2)}, u32[]{:S(2)}) collective-permute-start(f32[4,2,16,8,128]{4,3,2,1,0:T(8,128)S(1)} %get-tuple-element.42.refs_2_), channel_id=1, source_target_pairs={{0,4},{4,8},{8,12},{12,16},{16,20},{20,24},{24,28},{1,5},{5,9},{9,... | collective-permute-start | bytes 1572872 | tf_op jit(solution)/shard_map/ppermute | solution.py:829
  75.1 4.2 %collective-permute-start.6 = (f32[8,32,128]{2,1,0:T(8,128)S(1)}, f32[8,32,128]{2,1,0:T(8,128)S(1)}, u32[]{:S(2)}, u32[]{:S(2)}) collective-permute-start(f32[8,32,128]{2,1,0:T(8,128)S(1)} %get-tuple-element.43), channel_id=1, source_target_pairs={{0,1},{1,2},{2,3},{4,5},{5,6},{6,7},{8,9},{9,10},{10,11},{12,13},{... | collective-permute-start | bytes 393224 | tf_op jit(solution)/shard_map/ppermute | solution.py:829
  79.3 1.9 %collective-permute-start.7 = (f32[8,32,128]{2,1,0:T(8,128)S(1)}, f32[8,32,128]{2,1,0:T(8,128)S(1)}, u32[]{:S(2)}, u32[]{:S(2)}) collective-permute-start(f32[8,32,128]{2,1,0:T(8,128)S(1)} %get-tuple-element.44), channel_id=1, source_target_pairs={{1,0},{2,1},{3,2},{5,4},{6,5},{7,6},{9,8},{10,9},{11,10},{13,12},{... | collective-permute-start | bytes 393224 | tf_op jit(solution)/shard_map/ppermute | solution.py:829
  81.2 0.0 collective-permute-done.6.refs_7_.refs_13_
  81.3 4.6 %collective-permute-done.7.refs_8_.refs_14_ = f32[8,32,128]{2,1,0:T(8,128)S(1)} collective-permute-done((f32[8,32,128]{2,1,0:T(8,128)S(1)}, f32[8,32,128]{2,1,0:T(8,128)S(1)}, u32[]{:S(2)}, u32[]{:S(2)}) %collective-permute-start.7) | collective-permute-done | bytes 131104 | tf_op jit(solution)/shard_map/ppermute | solution.py:829
  85.9 0.0 copy-done.1
  85.9 0.0 copy-done.3
  85.9 17.4 %interior.3.refs_17_ = f32[4,32,8,16,128]{4,3,2,1,0:T(8,128)} custom-call(f32[4,32,16,8,128]{4,3,2,1,0:T(8,128)} %get-tuple-element.34.refs_0_, f32[4,2,16,8,128]{4,3,2,1,0:T(8,128)S(1)} %get-tuple-element.41.refs_1_, f32[4,2,16,8,128]{4,3,2,1,0:T(8,128)S(1)} %get-tuple-element.42.refs_2_, f32[32,16,8,128]{3,2,1,0:T(8,128)S(1)} %copy-done.1, ...), custom_call_target="tpu_custom_call" | custom-call | flops 73400320 | bytes 23068672 | tf_op jit(solution)/shard_map/interior/pallas_call | solution.py:391
  103.3 0.0 collective-permute-done.5.refs_4_
  103.3 0.0 collective-permute-done.4.refs_3_
  103.3 4.9 %boundary.3 = f32[4,32,8,16,128]{4,3,2,1,0:T(8,128)} custom-call(f32[4,32,16,8,128]{4,3,2,1,0:T(8,128)} %get-tuple-element.34.refs_0_, f32[4,2,16,8,128]{4,3,2,1,0:T(8,128)S(1)} %get-tuple-element.41.refs_1_, f32[4,2,16,8,128]{4,3,2,1,0:T(8,128)S(1)} %get-tuple-element.42.refs_2_, ...), custom_call_target="tpu_custom_call", output_to_operand_aliasing={{}: (17, {})} | custom-call | flops 13107200 | bytes 6291456 | tf_op jit(solution)/shard_map/boundary/pallas_call | solution.py:547
  (1 shorter events, 0.0 us)
Async XLA Ops:
  0.6 0.7 copy-start.4
  1.4 0.7 copy-start.5
  2.0 0.7 copy-start.6
  2.7 0.7 copy-start.7
  3.3 0.7 copy-start.8
  18.8 43.5 %collective-permute-start.2 = (f32[9,128,128]{2,1,0:T(8,128)S(1)}, f32[9,128,128]{2,1,0:T(8,128)S(1)}, u32[]{:S(2)}, u32[]{:S(2)}) collective-permute-start(f32[9,128,128]{2,1,0:T(8,128)S(1)} %get-tuple-element.37), channel_id=1, source_target_pairs={{0,4},{4,8},{8,12},{12,16},{16,20},{20,24},{24,28},{1,5},{5,9},{9,... | collective-permute-start | bytes 1769480 | tf_op jit(solution)/shard_map/ppermute | solution.py:829
  21.9 40.4 %collective-permute-start.3 = (f32[9,128,128]{2,1,0:T(8,128)S(1)}, f32[9,128,128]{2,1,0:T(8,128)S(1)}, u32[]{:S(2)}, u32[]{:S(2)}) collective-permute-start(f32[9,128,128]{2,1,0:T(8,128)S(1)} %get-tuple-element.38), channel_id=1, source_target_pairs={{4,0},{8,4},{12,8},{16,12},{20,16},{24,20},{28,24},{5,1},{9,5},{13... | collective-permute-start | bytes 1769480 | tf_op jit(solution)/shard_map/ppermute | solution.py:829
  25.5 15.6 %collective-permute-start = (f32[9,32,128]{2,1,0:T(8,128)S(1)}, f32[9,32,128]{2,1,0:T(8,128)S(1)}, u32[]{:S(2)}, u32[]{:S(2)}) collective-permute-start(f32[9,32,128]{2,1,0:T(8,128)S(1)} %get-tuple-element.31), channel_id=1, source_target_pairs={{0,1},{1,2},{2,3},{4,5},{5,6},{6,7},{8,9},{9,10},{10,11},{12,13},{... | collective-permute-start | bytes 442376 | tf_op jit(solution)/shard_map/ppermute | solution.py:829
  32.4 8.7 %collective-permute-start.1 = (f32[9,32,128]{2,1,0:T(8,128)S(1)}, f32[9,32,128]{2,1,0:T(8,128)S(1)}, u32[]{:S(2)}, u32[]{:S(2)}) collective-permute-start(f32[9,32,128]{2,1,0:T(8,128)S(1)} %get-tuple-element.32), channel_id=1, source_target_pairs={{1,0},{2,1},{3,2},{5,4},{6,5},{7,6},{9,8},{10,9},{11,10},{13,12},{... | collective-permute-start | bytes 442376 | tf_op jit(solution)/shard_map/ppermute | solution.py:829
  41.1 21.2 %copy-start = (f32[32,16,8,128]{3,2,1,0:T(8,128)}, f32[32,16,8,128]{3,2,1,0:T(8,128)S(1)}, u32[]{:S(2)}) copy-start(f32[32,16,8,128]{3,2,1,0:T(8,128)S(1)} %get-tuple-element.24.refs_1_.refs_3_.refs_5_) | copy-start | bytes 6291460
  41.1 21.2 %copy-start.2 = (f32[32,16,8,128]{3,2,1,0:T(8,128)}, f32[32,16,8,128]{3,2,1,0:T(8,128)S(1)}, u32[]{:S(2)}) copy-start(f32[32,16,8,128]{3,2,1,0:T(8,128)S(1)} %get-tuple-element.26.refs_3_.refs_5_.refs_7_) | copy-start | bytes 6291460
  62.3 23.6 %copy-start.1 = (f32[32,16,8,128]{3,2,1,0:T(8,128)S(1)}, f32[32,16,8,128]{3,2,1,0:T(8,128)}, u32[]{:S(2)}) copy-start(f32[32,16,8,128]{3,2,1,0:T(8,128)} %copy-done) | copy-start | bytes 6291460
  62.3 23.6 %copy-start.3 = (f32[32,16,8,128]{3,2,1,0:T(8,128)S(1)}, f32[32,16,8,128]{3,2,1,0:T(8,128)}, u32[]{:S(2)}) copy-start(f32[32,16,8,128]{3,2,1,0:T(8,128)} %copy-done.2) | copy-start | bytes 6291460
  68.9 34.4 %collective-permute-start.5 = (f32[4,2,16,8,128]{4,3,2,1,0:T(8,128)S(1)}, f32[4,2,16,8,128]{4,3,2,1,0:T(8,128)S(1)}, u32[]{:S(2)}, u32[]{:S(2)}) collective-permute-start(f32[4,2,16,8,128]{4,3,2,1,0:T(8,128)S(1)} %get-tuple-element.41.refs_1_), channel_id=1, source_target_pairs={{4,0},{8,4},{12,8},{16,12},{20,16},{24,20},{28,24},{5,1},{9,5},{13... | collective-permute-start | bytes 1572872 | tf_op jit(solution)/shard_map/ppermute | solution.py:829
  70.8 32.5 %collective-permute-start.4 = (f32[4,2,16,8,128]{4,3,2,1,0:T(8,128)S(1)}, f32[4,2,16,8,128]{4,3,2,1,0:T(8,128)S(1)}, u32[]{:S(2)}, u32[]{:S(2)}) collective-permute-start(f32[4,2,16,8,128]{4,3,2,1,0:T(8,128)S(1)} %get-tuple-element.42.refs_2_), channel_id=1, source_target_pairs={{0,4},{4,8},{8,12},{12,16},{16,20},{20,24},{24,28},{1,5},{5,9},{9,... | collective-permute-start | bytes 1572872 | tf_op jit(solution)/shard_map/ppermute | solution.py:829
  75.1 6.1 %collective-permute-start.6 = (f32[8,32,128]{2,1,0:T(8,128)S(1)}, f32[8,32,128]{2,1,0:T(8,128)S(1)}, u32[]{:S(2)}, u32[]{:S(2)}) collective-permute-start(f32[8,32,128]{2,1,0:T(8,128)S(1)} %get-tuple-element.43), channel_id=1, source_target_pairs={{0,1},{1,2},{2,3},{4,5},{5,6},{6,7},{8,9},{9,10},{10,11},{12,13},{... | collective-permute-start | bytes 393224 | tf_op jit(solution)/shard_map/ppermute | solution.py:829
  79.3 6.6 %collective-permute-start.7 = (f32[8,32,128]{2,1,0:T(8,128)S(1)}, f32[8,32,128]{2,1,0:T(8,128)S(1)}, u32[]{:S(2)}, u32[]{:S(2)}) collective-permute-start(f32[8,32,128]{2,1,0:T(8,128)S(1)} %get-tuple-element.44), channel_id=1, source_target_pairs={{1,0},{2,1},{3,2},{5,4},{6,5},{7,6},{9,8},{10,9},{11,10},{13,12},{... | collective-permute-start | bytes 393224 | tf_op jit(solution)/shard_map/ppermute | solution.py:829

commit v5 on v4

v5 whole, which is shorter than its diff:
```python
import functools

import jax
import jax.numpy as jnp
from jax import lax
from jax.experimental import pallas as pl
from jax.experimental.pallas import tpu as pltpu
from jax.sharding import PartitionSpec as P

LEVELS = 4
profile_weights = (0.4, 0.3, 0.2, 0.1)
time_step = 0.1
FACTOR = 0.25 * time_step

VMEM_LIMIT = 48 * 1024 * 1024
PAIR = 2
GROUP = 8
HIGHEST = lax.Precision.HIGHEST
ANY = pl.BlockSpec(memory_space=pl.ANY)
VMEM = pl.BlockSpec(memory_space=pltpu.VMEM)
SMEM = pl.BlockSpec(memory_space=pltpu.SMEM)


def params():
    return pltpu.CompilerParams(vmem_limit_bytes=VMEM_LIMIT)


def cost(flops, moved):
    return pl.CostEstimate(flops=int(flops), bytes_accessed=int(moved), transcendentals=0)


def minmod(a, b):
    return jnp.maximum(jnp.minimum(a, b), jnp.minimum(jnp.maximum(a, b), 0.0))


def tile_of(ref, t, tiles):
    return ref[pl.ds(t, 8, stride=tiles), :]


class Slabs:
    def __init__(self, q, u, v, sz, fall, fx, lx, block, x_at, at, halo, x, kept=None):
        self.q, self.u, self.v, self.sz, self.falls, self.fx, self.lx = q, u, v, sz, fall, fx, lx
        self.block, self.x_at, self.at, self.kept = block, x_at, at, kept
        self.halo, self.x = halo, x
        self.comps, self.tiles, self.lanes = q.shape[1], sz.shape[2], q.shape[-1]

    def field(self, c, slab, t):
        return self.q[self.block, c, slab, t]

    def row(self, k, which, number):
        return self.halo[which][number, pl.ds(self.x + k, 1), :]

    def centre(self, c, k, t):
        slab = k + 2
        if 0 <= t < self.tiles:
            return self.field(c, slab, t)
        row = lax.broadcasted_iota(jnp.int32, (8, self.lanes), 0)
        if t < 0:
            moved = pltpu.roll(self.field(c, slab, t + self.tiles), 1, 0)
            return jnp.where(row == 0, self.row(k, 0, 2 * c + t + 2), moved)
        t -= self.tiles
        return jnp.where(row == 7, self.row(k, 1, 2 * c + t), pltpu.roll(self.field(c, slab, t), 7, 0))

    def east(self, k, t):
        here = k + self.x_at
        return FACTOR * (self.u[self.block, here, t] + self.u[self.block, here + 1, t])

    def wind(self, k, t):
        inner = self.v[self.block, k + self.at, t % self.tiles]
        if 0 <= t < self.tiles:
            return inner
        row = lax.broadcasted_iota(jnp.int32, (8, self.lanes), 0)
        end, turn, which = (0, 1, 2) if t < 0 else (7, 7, 3)
        return jnp.where(row == end, self.row(k, which, 2 * self.comps), pltpu.roll(inner, turn, 0))

    def north(self, k, t):
        return FACTOR * (self.wind(k, t) + self.wind(k, t + 1))

    def up(self, k, t):
        return self.sz[self.block, k + self.at, t]

    def down(self, k, t):
        return self.falls[self.block, k + self.at, t]


def each(function, *lists):
    return [function(*items) for items in zip(*lists)]


def minmods(a, b):
    low, high = each(jnp.minimum, a, b), each(jnp.maximum, a, b)
    high = each(lambda x: jnp.minimum(x, 0.0), high)
    return each(jnp.maximum, low, high)


def difference(a, b):
    return each(lambda x, y: x - y, a, b)


def total_of(a, b):
    return each(lambda x, y: x + y, a, b)


def face_flux(speeds, masks, low_side, high_side):
    picked = each(jnp.where, masks, low_side, high_side)
    return each(lambda x, y: x * y, speeds, picked)


def staged(jobs):
    waiting = []
    for job in jobs:
        stores = job()
        for ref, index, value in waiting:
            ref[index] = value
        waiting = stores
    for ref, index, value in waiting:
        ref[index] = value


def first_face(f):
    def job(ts):
        spots = [(t, c) for t in ts for c in range(f.comps)]
        speeds = {t: f.east(-1, t) for t in ts}
        masks = {t: speeds[t] > 0 for t in ts}
        a, b, q0, q1 = [[f.field(c, slab, t) for t, c in spots] for slab in range(4)]
        middle = difference(q0, b)
        left = total_of(total_of(b, b), minmods(middle, difference(b, a)))
        slope = minmods(difference(q1, q0), middle)
        twice = total_of(q0, q0)
        flux = face_flux([speeds[t] for t, _ in spots], [masks[t] for t, _ in spots], left, difference(twice, slope))
        stores = [(f.fx, spot, x) for spot, x in zip(spots, flux)]
        if f.kept is not None:
            stores += [(f.kept[0], spot, x) for spot, x in zip(spots, twice)]
            stores += [(f.kept[1], spot, x) for spot, x in zip(spots, difference(q1, q0))]
        return stores + [(f.lx, spot, x) for spot, x in zip(spots, total_of(twice, slope))]

    staged([functools.partial(job, range(t, t + PAIR)) for t in range(0, f.tiles, PAIR)])


def slab_step(f, k, put):
    slab = k + 2
    lane = lax.broadcasted_iota(jnp.int32, (8, f.lanes), 1)
    top = f.lanes - 1
    is_first, is_last = lane == 0, lane == top
    carry = []
    speed = f.north(k, -1)
    for c in range(f.comps):
        a, b, q0, q1 = [f.centre(c, k, t) for t in (-2, -1, 0, 1)]
        middle, ahead = q0 - b, q1 - q0
        left_state = (b + b) + minmod(middle, b - a)
        slope = minmod(ahead, middle)
        twice = q0 + q0
        flux = speed * jnp.where(speed > 0, left_state, twice - slope)
        carry.append((q0, q1, ahead, twice, twice + slope, flux))
    states, doubles = {}, {}

    def vertical(t):
        for c in range(f.comps):
            q0 = f.field(c, slab, t)
            over = jnp.where(is_last, 0.0, pltpu.roll(q0, top, 1))
            under = jnp.where(is_first, 0.0, pltpu.roll(q0, 1, 1))
            slope = minmod(over - q0, q0 - under)
            if f.kept is not None:
                doubles[c, t] = f.kept[0][t, c]
            twice = double(c, t, q0)
            states[t, c] = (twice - slope, twice + slope)

    def flush(held):
        for c, t, flux_x, left_x, twice_x, step_x, value in held:
            f.fx[t, c], f.lx[t, c] = flux_x, left_x
            if f.kept is not None:
                f.kept[0][t, c], f.kept[1][t, c] = twice_x, step_x
            put(c, t, value)

    def double(c, t, tile):
        if f.kept is None or not 0 <= t < f.tiles:
            return tile + tile
        return doubles[c, t]

    held = []
    for t in range(GROUP):
        vertical(t)
    for begin in range(0, f.tiles, GROUP):
        group = range(begin, min(begin + GROUP, f.tiles))
        for t in range(begin + GROUP, min(begin + 2 * GROUP, f.tiles)):
            vertical(t)
        loaded = {}
        for t in group:
            loaded[t] = (f.east(k, t), f.north(k, t), f.up(k, t), f.down(k, t))
            for c in range(f.comps):
                loaded[t, c] = (
                    f.centre(c, k, t + 2), f.field(c, slab + 1, t), f.field(c, slab + 2, t),
                    f.fx[t, c], f.lx[t, c], f.kept[1][t, c] if f.kept is not None else None,
                )
        flush(held)
        held = []
        for t in group:
            speed_x, speed_y, speed_z, fall = loaded[t]
            go_x, go_y, go_z, go_fall = speed_x > 0, speed_y > 0, speed_z > 0, fall > 0
            for c in range(f.comps):
                y2, x1, x2, flux_w, left_w, step_w = loaded[t, c]
                q0, y1, ahead, twice, left_y, flux_y = carry[c]
                beyond = y2 - y1
                slope = minmod(beyond, ahead)
                twice_y = double(c, t + 1, y1)
                flux_next = speed_y * jnp.where(go_y, left_y, twice_y - slope)
                total = flux_next - flux_y
                carry[c] = (y1, y2, beyond, twice_y, twice_y + slope, flux_next)
                step_x = x2 - x1
                slope = minmod(step_x, x1 - q0 if step_w is None else step_w)
                twice_x = x1 + x1
                flux_x = speed_x * jnp.where(go_x, left_w, twice_x - slope)
                left_x = twice_x + slope
                total = total + (flux_x - flux_w)
                lower, upper = states[t, c]
                flux_z = speed_z * jnp.where(go_z, upper, pltpu.roll(lower, top, 1))
                flux_below = fall * jnp.where(go_fall, pltpu.roll(upper, 1, 1), lower)
                total = total + (flux_z - flux_below)
                held.append((c, t, flux_x, left_x, twice_x, step_x, q0 - total))
    flush(held)


def dust_job(q, block, slab, dust):
    c, spots = q.shape[1] - 1, range(q.shape[3])
    tiles = total_of([q[block, c, slab, t] for t in spots], dust(spots))
    return [(q, (block, c, slab, t), tile) for t, tile in zip(spots, tiles)]


def falling(deposit, column):
    lanes = deposit.shape[-1]

    def dust(spots):
        parts = [pltpu.roll(deposit[t], lanes - column, 1) for t in spots]
        lane = lax.broadcasted_iota(jnp.int32, parts[0].shape, 1)
        return [jnp.where(lane == 0, part, 0.0) for part in parts]

    return dust


def pack_edges(packs, stage_slab, comps, x):
    x = pl.ds(x, 1)
    stores = []
    for c in range(comps):
        tiles = stage_slab(c)
        count = tiles.shape[0]
        for r in range(2):
            stores.append((packs[0], (2 * c + r, x), tiles[r, 0:1, :]))
            stores.append((packs[1], (2 * c + r, x), tiles[count - 2 + r, 7:8, :]))
    staged([lambda: stores])


def start(source, target, sem):
    pltpu.make_async_copy(source, target, sem).start()


def start_sets(pairs, sem):
    for source, target in pairs:
        for number in range(8):
            start(source(number), target(number), sem)


def arrived(spot, sem):
    pltpu.make_async_copy(spot, spot, sem).wait()


def interior_kernel(last, groups, count, *refs):
    refs = list(refs)
    fields, velocity, speeds = refs[:count], refs[count], refs[count + 1 : count + 3]
    below, above, v_below, v_above = refs[count + 3 : count + 7]
    del refs[: count + 7]
    deposit = None if last else refs.pop(0)
    out = refs.pop(0)
    packs = None if last else (refs.pop(0), refs.pop(0))
    q, u, v, sz, fall, fx, lx, stage, in_sem, out_sem = refs[:10]
    kept = refs[10:12]
    comps, slabs, tiles = q.shape[1], q.shape[2], sz.shape[2]
    chunk, flight = (8, 3) if last else (4, 6)
    chunks = slabs // chunk

    def fetch(j, first, final):
        span = pl.ds(j * chunk, chunk)
        if last:
            middle, low, high = fields
            begin, size = j * chunk, chunk
            if first:
                begin, size = begin + 2, size - 2
                start(low, q.at[0, :, pl.ds(0, 2)], in_sem.at[j, 0])
            if final:
                size -= 2
                start(high, q.at[0, :, pl.ds(slabs - 2, 2)], in_sem.at[j, 0])
            part = pl.ds(begin, size)
            start(middle.at[:, part], q.at[0, :, part], in_sem.at[j, 0])
        else:
            pair = (lambda n: fields[0].at[:, span, n], lambda n: q.at[0, :, span, :, n])
            start_sets([pair], in_sem.at[j, 0])
        for c, target in enumerate((u, v)):
            pair = (lambda n: velocity.at[c, span, n], lambda n: target.at[0, span, :, n])
            start_sets([pair], in_sem.at[j, c + 1])
        for n, (source, target) in enumerate(zip(speeds, (sz, fall))):
            start(source.at[span], target.at[0, span], in_sem.at[j, n + 3])

    for j in range(flight):
        fetch(j, j == 0, False)

    def arrive(j):
        span = pl.ds(j * chunk, chunk)
        arrived(q.at[0, :, span], in_sem.at[j, 0])
        for n, target in enumerate((u, v, sz, fall)):
            arrived(target.at[0, span], in_sem.at[j, n + 1])
        later = j + flight

        @pl.when(later < chunks - 1)
        def _():
            fetch(later, False, False)

        @pl.when(later == chunks - 1)
        def _():
            fetch(chunks - 1, False, True)

        def complete(x, _):
            staged([functools.partial(dust_job, q, 0, x, falling(deposit, x + 2))])
            return 0

        if not last:
            lax.fori_loop(j * chunk, jnp.minimum((j + 1) * chunk, groups), complete, 0)

    f = Slabs(q, u, v, sz, fall, fx, lx, 0, 2, 2, (below, above, v_below, v_above), 2, kept)
    arrive(jnp.int32(0))
    first_face(f)

    def step(k, _):
        @pl.when((k + 4) % chunk == 0)
        def _():
            arrive((k + 4) // chunk)

        def put(c, t, value):
            stage[c, k, t] = value

        slab_step(f, k, put)
        if last:
            start_sets([(lambda n: stage.at[:, k, :, n], lambda n: out.at[:, k + 2, n])], out_sem)
        else:
            start(stage.at[:, k], out.at[:, k + 2], out_sem)
        if not last:
            pack_edges(packs, lambda c: stage.at[c, k], comps, k + 2)
        return 0

    if not last:
        for pack in packs:
            pack[...] = jnp.zeros_like(pack)
    lax.fori_loop(0, slabs - 4, step, 0)
    arrived(stage, out_sem)


def interior(groups, fields, velocity, speeds, below, above, v_below, v_above, deposit=None):
    last = deposit is None
    slabs, tiles, _, lanes = speeds[0].shape
    rows, comps = 8 * tiles, fields[0].shape[0]
    operands = list(fields) + [velocity, *speeds, below, above, v_below, v_above]
    specs = [ANY] * (len(fields) + 3) + [VMEM] * 4
    form = (8, tiles, lanes) if last else (tiles, 8, lanes)
    out_shape = [jax.ShapeDtypeStruct((comps, slabs, *form), jnp.float32)]
    out_specs = [ANY]
    scratch = [
        pltpu.VMEM((1, comps, slabs, tiles, 8, lanes), jnp.float32),
        *[pltpu.VMEM((1, slabs, tiles, 8, lanes), jnp.float32)] * 4,
        pltpu.VMEM((tiles, comps, 8, lanes), jnp.float32),
        pltpu.VMEM((tiles, comps, 8, lanes), jnp.float32),
        pltpu.VMEM((comps, slabs - 4, tiles, 8, lanes), jnp.float32),
        pltpu.SemaphoreType.DMA((slabs // 4, 5)),
        pltpu.SemaphoreType.DMA,
    ]
    scratch += [pltpu.VMEM((tiles, comps, 8, lanes), jnp.float32)] * 2
    if not last:
        out_shape += [jax.ShapeDtypeStruct((2 * comps, slabs, lanes), jnp.float32)] * 2
        out_specs += [VMEM] * 2
        operands.append(deposit)
        specs.append(VMEM)
    cells = comps * (slabs - 4) * rows * lanes
    return pl.pallas_call(
        functools.partial(interior_kernel, last, groups, len(fields)),
        out_shape=tuple(out_shape),
        in_specs=specs,
        out_specs=tuple(out_specs),
        scratch_shapes=scratch,
        compiler_params=params(),
        cost_estimate=cost(40 * cells, 4 * (2 * cells + 4 * slabs * rows * lanes)),
        name="interior",
    )(*operands)


def boundary_kernel(last, groups, slabs, *refs):
    refs = list(refs)
    count = 5 if last else 3
    fields, velocity, speeds = refs[:count], refs[count], refs[count + 1 : count + 3]
    u_outer = refs[count + 3 : count + 5]
    below, above, v_below, v_above = refs[count + 5 : count + 9]
    del refs[: count + 9]
    if last:
        out = refs[1]
        del refs[:2]
    else:
        deposit, packed, ends, packs = refs[0], refs[1:3], refs[3:5], refs[5:7]
        del refs[:7]
    q, u, v, sz, fall, fx, lx, stage, in_sem, out_sem = refs
    comps, tiles = q.shape[1], sz.shape[2]

    if last:
        middle, end_low, end_high, x_low, x_high = fields
        for block, at, source in (
            (0, 0, x_low), (0, 2, end_low), (0, 4, middle.at[:, pl.ds(2, 2)]),
            (1, 0, middle.at[:, pl.ds(slabs - 4, 2)]), (1, 2, end_high), (1, 4, x_high),
        ):
            start(source, q.at[block, :, pl.ds(at, 2)], in_sem.at[block, 0])
    else:
        state, x_low, x_high = fields
        for block, at, first in ((0, 2, 0), (1, 0, slabs - 4)):
            pair = (
                lambda n: state.at[:, pl.ds(first, 4), n], lambda n: q.at[block, :, pl.ds(at, 4), :, n]
            )
            start_sets([pair], in_sem.at[block, 0])
        for block, at, halo in ((0, 0, x_low), (1, 4, x_high)):
            pairs = [
                (lambda n, c=c: halo.at[pl.ds(2 * c, 2), n], lambda n, c=c: q.at[block, c, pl.ds(at, 2), :, n])
                for c in range(comps)
            ]
            start_sets(pairs, in_sem.at[block, 0])
    edge = pl.ds(2 * comps, 1)
    for block in range(2):
        outer, first, at = 3 * block, block * (slabs - 3), 1 - block
        pairs = [
            (lambda n: u_outer[block].at[edge, n], lambda n: u.at[block, pl.ds(outer, 1), :, n]),
            (lambda n: velocity.at[0, pl.ds(first, 3), n], lambda n: u.at[block, pl.ds(at, 3), :, n]),
        ]
        start_sets(pairs, in_sem.at[block, 1])
        span = pl.ds(block * (slabs - 2), 2)
        start_sets([(lambda n: velocity.at[1, span, n], lambda n: v.at[block, :, :, n])], in_sem.at[block, 2])
        for n, target in enumerate((sz, fall)):
            start(speeds[n].at[span], target.at[block], in_sem.at[block, n + 3])
    if not last:
        packs[0][...] = packed[0][...]
        packs[1][...] = packed[1][...]

    def one(block, _):
        begin = block * (slabs - 2)
        arrived(q.at[block], in_sem.at[block, 0])
        for n, target in enumerate((u, v, sz, fall)):
            arrived(target.at[block], in_sem.at[block, n + 1])

        def complete(slab, _):
            x = begin + slab - 2
            lands = (x >= slabs) | ((x >= 0) & (x < groups)) | (x + slabs < groups)

            @pl.when(lands)
            def _():
                staged([functools.partial(dust_job, q, block, slab, falling(deposit, x + 2))])

            return 0

        if not last:
            lax.fori_loop(0, 6, complete, 0)
        f = Slabs(q, u, v, sz, fall, fx, lx, block, 1, 0, (below, above, v_below, v_above), begin)
        first_face(f)

        def step(k, _):
            def put(c, t, value):
                stage[block, c, k, t] = value

            slab_step(f, k, put)
            if not last:
                pack_edges(packs, lambda c: stage.at[block, c, k], comps, begin + k)
            return 0

        lax.fori_loop(0, 2, step, 0)
        if last:
            span = pl.ds(begin, 2)
            pair = (lambda n: stage.at[block, :, :, :, n], lambda n: out.at[:, span, n])
            start_sets([pair], out_sem.at[block])
        else:
            for number in range(2):

                @pl.when(block == number)
                def _():
                    start(stage.at[number], ends[number], out_sem.at[number])

        return 0

    lax.fori_loop(0, 2, one, 0)
    for block in range(2):
        arrived(stage.at[block], out_sem.at[block])


def boundary(groups, fields, velocity, speeds, u_outer, below, above, v_below, v_above, *, deposit=None, packed=None, out=None):
    last = out is not None
    slabs, tiles, _, lanes = speeds[0].shape
    rows, comps = 8 * tiles, fields[0].shape[0]
    operands = list(fields) + [velocity, *speeds, *u_outer, below, above, v_below, v_above]
    specs = [ANY] * (len(fields) + 5) + [VMEM] * 4
    form = (tiles, 8, lanes)
    scratch = [
        pltpu.VMEM((2, comps, 6, tiles, 8, lanes), jnp.float32),
        pltpu.VMEM((2, 4, tiles, 8, lanes), jnp.float32),
        *[pltpu.VMEM((2, 2, tiles, 8, lanes), jnp.float32)] * 3,
        pltpu.VMEM((tiles, comps, 8, lanes), jnp.float32),
        pltpu.VMEM((tiles, comps, 8, lanes), jnp.float32),
        pltpu.VMEM((2, comps, 2, *form), jnp.float32),
        pltpu.SemaphoreType.DMA((2, 5)),
        pltpu.SemaphoreType.DMA((2,)),
    ]
    if last:
        aliases = {len(operands): 0}
        operands.append(out)
        specs.append(ANY)
        out_shape = jax.ShapeDtypeStruct(out.shape, out.dtype)
        out_specs = ANY
    else:
        aliases = {}
        operands += [deposit, *packed]
        specs += [VMEM] * 3
        out_shape = (jax.ShapeDtypeStruct((comps, 2, *form), jnp.float32),) * 2
        out_shape += (jax.ShapeDtypeStruct((2 * comps, slabs, lanes), jnp.float32),) * 2
        out_specs = (ANY, ANY, VMEM, VMEM)
    cells = comps * 4 * rows * lanes
    return pl.pallas_call(
        functools.partial(boundary_kernel, last, groups, slabs),
        out_shape=out_shape,
        in_specs=specs,
        out_specs=out_specs,
        scratch_shapes=scratch,
        input_output_aliases=aliases,
        compiler_params=params(),
        cost_estimate=cost(50 * cells, 4 * 6 * cells),
        name="boundary",
    )(*operands)


def speeds_kernel(velocity, sz, fall, wind, sems):
    step = pl.program_id(0)
    part, count, lanes = sz.shape[0], wind.shape[1], wind.shape[3]
    lane = lax.broadcasted_iota(jnp.int32, (8, lanes), 1)
    is_first, is_last = lane == 0, lane == lanes - 1

    @pl.when(step == 0)
    def _():
        for j in range(wind.shape[0] // part):
            span = pl.ds(j * part, part)
            start_sets([(lambda n: velocity.at[2, span, n], lambda n: wind.at[span, :, n])], sems.at[j])

    arrived(wind.at[pl.ds(step * part, part)], sems.at[step])

    def one(x, _):
        here = [FACTOR * wind[step * part + x, t] for t in range(count)]
        over = [pltpu.roll(tile, lanes - 1, 1) for tile in here]
        under = [pltpu.roll(tile, 1, 1) for tile in here]
        upper = [jnp.where(is_last, jnp.maximum(a, 0.0), a + b) for a, b in zip(here, over)]
        lower = [jnp.where(is_first, jnp.minimum(a, 0.0), a + b) for a, b in zip(here, under)]
        for t in range(count):
            sz[x, t] = upper[t]
            fall[x, t] = lower[t]
        return 0

    lax.fori_loop(0, part, one, 0)


def face_speeds(velocity):
    _, slabs, _, tiles, lanes = velocity.shape
    part = 8
    return pl.pallas_call(
        speeds_kernel,
        grid=(slabs // part,),
        out_shape=(jax.ShapeDtypeStruct((slabs, tiles, 8, lanes), jnp.float32),) * 2,
        in_specs=[ANY],
        out_specs=(pl.BlockSpec((part, tiles, 8, lanes), lambda i: (i, 0, 0, 0)),) * 2,
        scratch_shapes=[
            pltpu.VMEM((slabs, tiles, 8, lanes), jnp.float32),
            pltpu.SemaphoreType.DMA((slabs // part,)),
        ],
        compiler_params=params(),
        cost_estimate=cost(8 * slabs * 8 * tiles * lanes, 12 * slabs * 8 * tiles * lanes),
        name="face_speeds",
    )(velocity)


def x_copies(state, velocity, low, high, sems):
    comps, slabs = state.shape[0], state.shape[1]
    copies = []
    for n, (target, first, edge) in enumerate(((low, 0, 0), (high, slabs - 2, slabs - 1))):
        pairs = [(state.at[c, pl.ds(first, 2)], target.at[pl.ds(2 * c, 2)]) for c in range(comps)]
        pairs.append((velocity.at[0, pl.ds(edge, 1)], target.at[pl.ds(2 * comps, 1)]))
        copies += [pltpu.make_async_copy(*pair, sems.at[n, i]) for i, pair in enumerate(pairs)]
    return copies


def as_column(row):
    count = row.shape[1]
    shape = (count, count)
    same = lax.broadcasted_iota(jnp.int32, shape, 0) == lax.broadcasted_iota(jnp.int32, shape, 1)
    return jnp.sum(jnp.where(same, row, 0.0), axis=1, keepdims=True)


def survey_kernel(
    low_in, high_in, v_low, v_high, wind, state, velocity, low, high, stress, x_low, x_high, gathered, sems,
):
    step, steps = pl.program_id(0), pl.num_programs(0)

    @pl.when(step == 0)
    def _():
        for copy in x_copies(state, velocity, x_low, x_high, sems):
            copy.start()

    comps, part, rows, lanes = low_in.shape[0], wind.shape[1], wind.shape[2], wind.shape[3]
    slabs = stress.shape[0]
    for x in range(part):
        for c in range(comps):
            for r in range(2):
                low[2 * c + r, x : x + 1, :] = low_in[c, x, r : r + 1, :]
                high[2 * c + r, x : x + 1, :] = high_in[c, x, 6 + r : 7 + r, :]
        low[2 * comps, x : x + 1, :] = v_low[0, x, 0:1, :]
        high[2 * comps, x : x + 1, :] = v_high[0, x, 7:8, :]
    lane = lax.broadcasted_iota(jnp.int32, (rows, lanes), 1)
    weight = jnp.zeros((rows, lanes), jnp.float32)
    for level, value in enumerate(profile_weights):
        weight = jnp.where(lane == level, value, weight)
    total = jnp.zeros((rows, lanes), jnp.float32)
    for x in range(part):
        east, north = wind[0, x], wind[1, x]
        friction = jnp.where(lane < LEVELS, weight * (east * east + north * north), 0.0)
        total = total + pltpu.roll(friction, LEVELS * x, 1) if x else friction

    @pl.when(step == 0)
    def _():
        gathered[...] = total

    @pl.when(step > 0)
    def _():
        gathered[...] += pltpu.roll(total, LEVELS * part * step, 1)

    @pl.when(step == steps - 1)
    def _():
        gathered[...] = gathered[...].T
        total = gathered[pl.ds(0, slabs, stride=LEVELS), :]
        for level in range(1, LEVELS):
            total = total + gathered[pl.ds(level, slabs, stride=LEVELS), :]
        stress[...] = total
        for copy in x_copies(state, velocity, x_low, x_high, sems):
            copy.wait()


def survey(state, velocity):
    comps, slabs, rows, lanes = state.shape
    part = 8
    last = rows // 8 - 1
    packed = jax.ShapeDtypeStruct((2 * comps + 1, slabs, lanes), jnp.float32)
    packed_spec = pl.BlockSpec((2 * comps + 1, part, lanes), lambda i: (0, i, 0))
    x_packed = jax.ShapeDtypeStruct((2 * comps + 1, rows, lanes), jnp.float32)
    return pl.pallas_call(
        survey_kernel,
        grid=(slabs // part,),
        out_shape=(packed, packed, jax.ShapeDtypeStruct((slabs, lanes), jnp.float32), x_packed, x_packed),
        in_specs=[
            pl.BlockSpec((comps, part, 8, lanes), lambda i: (0, i, 0, 0)),
            pl.BlockSpec((comps, part, 8, lanes), lambda i: (0, i, last, 0)),
            pl.BlockSpec((1, part, 8, lanes), lambda i: (1, i, 0, 0)),
            pl.BlockSpec((1, part, 8, lanes), lambda i: (1, i, last, 0)),
            pl.BlockSpec((2, part, rows, lanes), lambda i: (0, i, 0, 0)),
            ANY,
            ANY,
        ],
        out_specs=(packed_spec, packed_spec, pl.BlockSpec((slabs, lanes), lambda i: (0, 0)), ANY, ANY),
        scratch_shapes=[pltpu.VMEM((rows, lanes), jnp.float32), pltpu.SemaphoreType.DMA((2, comps + 1))],
        compiler_params=params(),
        cost_estimate=cost(10 * slabs * rows * lanes, 10 * slabs * rows * lanes),
        name="survey",
    )(state, state, velocity, velocity, velocity, state, velocity)


def census_kernel(stress, threshold, tile_owner, parcel_owner, count, share, copies):
    groups, height, lanes = copies.shape
    slabs = stress.shape[0]
    owners = parcel_owner[...].astype(jnp.float32)
    shape = (groups, slabs)
    place = (owners == lax.broadcasted_iota(jnp.int32, shape, 0).astype(jnp.float32)).astype(jnp.float32)
    live = as_column(count[...].astype(jnp.float32))
    shape = (slabs, lanes)
    reach = lax.broadcasted_iota(jnp.int32, shape, 1).astype(jnp.float32) < live
    masses = jnp.where(reach, share[0], 0.0)
    copies[0, 0:slabs] = stress[...]
    copies[0, slabs : slabs + 8] = jnp.zeros((8, lanes), jnp.float32)
    copies[0, slabs : slabs + 1] = threshold[...]
    copies[0, slabs + 1 : slabs + 2, 0:slabs] = tile_owner[...].astype(jnp.float32)
    copies[0, slabs + 8 : height] = jnp.dot(place, masses, precision=HIGHEST, preferred_element_type=jnp.float32)
    whole = copies[0]
    for g in range(1, groups):
        copies[g] = whole


def census(groups, stress, *small):
    slabs, lanes = stress.shape
    return pl.pallas_call(
        census_kernel,
        out_shape=jax.ShapeDtypeStruct((groups, slabs + 8 + groups, lanes), jnp.float32),
        in_specs=[VMEM] * 6,
        out_specs=VMEM,
        compiler_params=params(),
        cost_estimate=cost(10**6, 10**6),
        name="census",
    )(stress, *small)


def deposit_kernel(slabs, me, gathered, low_in, high_in, flux_out, deposit, low, high, flux, dropped):
    groups, lanes = gathered.shape[0], gathered.shape[2]
    here = me[0]
    limits = jnp.concatenate([gathered[g, slabs : slabs + 1] for g in range(groups)], axis=0)
    total = jnp.zeros((groups, lanes), jnp.float32)
    shape = (groups, slabs)
    numbers = lax.broadcasted_iota(jnp.int32, shape, 0).astype(jnp.float32)
    for g in range(groups):
        owners = gathered[g, slabs + 1 : slabs + 2, 0:slabs]
        stress = gathered[g, 0:slabs]
        named = (owners == numbers).astype(jnp.float32)
        limit = lax.dot_general(
            named, limits, (((0,), (0,)), ((), ())), precision=HIGHEST, preferred_element_type=jnp.float32
        )
        lifting = jnp.maximum(stress - limit, 0.0)
        total = total + jnp.dot(named, lifting, precision=HIGHEST, preferred_element_type=jnp.float32)
    flux[...] = total / slabs
    flux_out[...] = flux[pl.ds(here, 1), :]
    dropped[...] = jnp.zeros_like(dropped)
    before, after = jnp.maximum(here - 1, 0), jnp.minimum(here + 1, groups - 1)
    has_before, has_after = here > 0, here < groups - 1
    base = slabs + 8
    for p in range(groups):
        x = p % slabs
        row = flux[p : p + 1, :]
        dropped[x + 2 : x + 3] += row * gathered[p, pl.ds(base + here, 1), :]
        if x >= slabs - 2:
            mass = row * gathered[p, pl.ds(base + before, 1), :]
            dropped[x - slabs + 2 : x - slabs + 3] += jnp.where(has_before, mass, 0.0)
        if x < 2:
            mass = row * gathered[p, pl.ds(base + after, 1), :]
            dropped[x + slabs + 2 : x + slabs + 3] += jnp.where(has_after, mass, 0.0)
    own = dropped[2 : 2 + slabs, :]
    dropped[...] = dropped[...].T
    count = deposit.shape[0]
    tiles = [tile_of(dropped, t, count) for t in range(count)]
    for t, tile in enumerate(tiles):
        deposit[t] = tile
    lane = lax.broadcasted_iota(jnp.int32, (slabs, lanes), 1)
    rows = lanes
    dust = low.shape[0] - 3
    low[...] = low_in[...]
    high[...] = high_in[...]
    for r in range(2):
        low[dust + r] += jnp.where(lane == 0, own[:, r : r + 1], 0.0)
        high[dust + r] += jnp.where(lane == 0, own[:, rows - 2 + r : rows - 1 + r], 0.0)


def settle(me, gathered, low, high, slabs):
    groups, _, lanes = gathered.shape
    edge = jax.ShapeDtypeStruct(low.shape, jnp.float32)
    return pl.pallas_call(
        functools.partial(deposit_kernel, slabs),
        out_shape=(
            jax.ShapeDtypeStruct((1, lanes), jnp.float32),
            jax.ShapeDtypeStruct((lanes // 8, 8, lanes), jnp.float32),
            edge,
            edge,
        ),
        in_specs=[SMEM, VMEM, VMEM, VMEM],
        out_specs=(VMEM, VMEM, VMEM, VMEM),
        scratch_shapes=[
            pltpu.VMEM((groups, lanes), jnp.float32),
            pltpu.VMEM((lanes, lanes), jnp.float32),
        ],
        compiler_params=params(),
        cost_estimate=cost(10**6, 10**6),
        name="settle",
    )(me, gathered, low, high)


def exchange(low, high, axis):
    count = lax.axis_size(axis)
    forward = [(i, i + 1) for i in range(count - 1)]
    backward = [(target, source) for source, target in forward]
    return lax.ppermute(high, axis, forward), lax.ppermute(low, axis, backward)


def shards(state, velocity, threshold, tile_owner, parcel_owner, parcel_count, parcel_share):
    groups = lax.axis_size("gx")
    slabs = state.shape[1]
    me = lax.axis_index("gx").astype(jnp.int32).reshape(1)

    low, high, stress, own_low, own_high = survey(state, velocity)
    copies = census(
        groups, stress, threshold, tile_owner[:, :, 0], parcel_owner[:, :, 0], parcel_count, parcel_share
    )
    rows, lanes = state.shape[2:]

    def sets(array):
        return array.reshape(*array.shape[:-2], 8, rows // 8, lanes)

    velocity = sets(velocity)
    speeds = face_speeds(velocity)
    gathered = lax.all_to_all(copies, "gx", split_axis=0, concat_axis=0, tiled=True)
    flux, deposit, low, high = settle(me, gathered, low, high, slabs)
    below, above = exchange(low, high, "gy")
    own_low, own_high, _ = lax.optimization_barrier((own_low, own_high, gathered))
    x_low, x_high = exchange(own_low, own_high, "gx")
    x_low, x_high = sets(x_low), sets(x_high)
    u_edges = (x_low, x_high)
    middle, pack_low, pack_high = interior(groups, [sets(state)], velocity, speeds, below, above, below, above, deposit)
    end_low, end_high, y_low, y_high = boundary(
        groups, [sets(state), x_low, x_high], velocity, speeds, u_edges, below, above, below, above,
        deposit=deposit, packed=(pack_low, pack_high),
    )
    x2_low, x2_high = exchange(end_low, end_high, "gx")
    below2, above2 = exchange(y_low, y_high, "gy")
    (inside,) = interior(groups, [middle, end_low, end_high], velocity, speeds, below2, above2, below, above)
    fields = boundary(
        groups, [middle, end_low, end_high, x2_low, x2_high], velocity, speeds, u_edges, below2, above2, below, above,
        out=inside,
    )
    return fields.reshape(state.shape), flux


def solution(mesh):
    return jax.shard_map(
        shards,
        mesh=mesh,
        in_specs=(
            P(None, "gx", "gy", None),
            P(None, "gx", "gy", None),
            P("gx", "gy"),
            P("gy", "gx", None),
            P("gy", "gx", None),
            P("gy", "gx"),
            P("gy", "gx", None),
        ),
        out_specs=(P(None, "gx", "gy", None), P("gx", "gy")),
        check_vma=False,
    )
```

time: 109 us -> 99.5 us (0.913)
  Pallas kernels: 62.4 us -> 56.1 us
  local copies, waits for them, and re-layouts: 3.36 us -> 0.03 us
    pallas_call x6 -> x7, Pallas kernels: 61.1 us -> 54.7 us  [the longest x2 35.6 us: interior(): pl.pallas_call(functools.partial(interior_kernel, last, groups, len(field...]
    unnamed x18 -> x14, local copies, waits for them, and re-layouts: 3.35 us -> 0.03 us
  transfers between devices with their start and end apart: 8 -> 8, of which waited for: 1 -> 2; matrix products, arithmetic and copies ran while one was open for 0% -> 0% of each run, Pallas kernels for 43% -> 42%
where the time goes in v5:
time: 99.5 us; the launch traced here: 99 us
  Pallas kernels  56.1 us (56%)
  starting transfers between devices  26.4 us (27%)
  blocking collectives  10.5 us (11%)
  waiting for transfers between devices  5.02 us (5%)
    pallas_call x2, Pallas kernels, interior(): pl.pallas_call(functools.partial(interior_kernel, last, groups, len(field...  35.6 us
    ppermute x4, starting transfers between devices, exchange(): lax.ppermute(high, axis, forward)  18.5 us
    all_to_all x1, blocking collectives, shards(): lax.all_to_all(copies, 'gx', split_axis=0, concat_axis=0, tiled=True)  10.5 us
    pallas_call x2, Pallas kernels, boundary(): pl.pallas_call(functools.partial(boundary_kernel, last, groups, slabs), o...  10.1 us
    ppermute x4, starting transfers between devices, exchange(): lax.ppermute(low, axis, backward)  7.99 us
    ppermute x4, waiting for transfers between devices, exchange(): lax.ppermute(low, axis, backward)  5.01 us
    pallas_call x1, Pallas kernels, face_speeds(): pl.pallas_call(speeds_kernel, grid=(slabs // part,), out_shape=(jax.Shape...  4.44 us
    pallas_call x1, Pallas kernels, survey(): pl.pallas_call(survey_kernel, grid=(slabs // part,), out_shape=(packed, p...  4.38 us
  transfers between devices with their start and end apart: 8, of which 2 were waited for; matrix products, arithmetic and copies ran while one was open for 0% of the time, Pallas kernels for 42%

profile of v5, /device:TPU:3, one launch (start us, length us, event | category | flops | bytes accessed | tf_op | source)
XLA Modules:
  0.0 99.0 jit_solution(14570688902461350347)
XLA Ops:
  0.6 0.0 copy-start.2
  0.6 0.0 copy-start.6
  0.7 0.0 copy-start.5
  0.7 0.0 copy-start.4
  0.7 0.0 copy-start.3
  0.7 4.4 %survey.1 = (f32[9,32,128]{2,1,0:T(8,128)S(1)}, f32[9,32,128]{2,1,0:T(8,128)S(1)}, f32[32,128]{1,0:T(8,128)S(1)}, f32[9,128,128]{2,1,0:T(8,128)S(1)}, f32[9,128,128]{2,1,0:T(8,128)S(1)}) custom-call(f32[4,32,128,128]{3,2,1,0:T(8,128)} %state.1, f32[4,32,128,128]{3,2,1,0:T(8,128)} %state.1, f32[3,32,128,128]{3,2,1,0:T(8,128)} %velocity.1, ...), custom_call_target="tpu_custom_call" | custom-call | flops 5242880 | bytes 5242880 | tf_op jit(solution)/shard_map/survey/pallas_call | solution.py:656
  5.1 0.0 copy-done.2
  5.1 0.0 copy-done.6
  5.1 0.0 copy-done.5
  5.1 0.0 copy-done.4
  5.1 0.0 copy-done.3
  5.1 0.2 census.1
  5.3 10.5 %all_to_all.5.gathered = f32[8,48,128]{2,1,0:T(8,128)S(1)} all-to-all(f32[8,48,128]{2,1,0:T(8,128)S(1)} %census.1), channel_id=1, replica_groups=mesh['gx'=8,'gy'=4] {'gx'}, dimensions={0} | all-to-all | bytes 393216 | tf_op jit(solution)/shard_map/all_to_all | solution.py:804
  15.8 3.1 %collective-permute-start.2 = (f32[9,128,128]{2,1,0:T(8,128)S(1)}, f32[9,128,128]{2,1,0:T(8,128)S(1)}, u32[]{:S(2)}, u32[]{:S(2)}) collective-permute-start(f32[9,128,128]{2,1,0:T(8,128)S(1)} %get-tuple-element.33), channel_id=1, source_target_pairs={{0,4},{4,8},{8,12},{12,16},{16,20},{20,24},{24,28},{1,5},{5,9},{9,... | collective-permute-start | bytes 1769480 | tf_op jit(solution)/shard_map/ppermute | solution.py:785
  18.9 2.2 %collective-permute-start.3 = (f32[9,128,128]{2,1,0:T(8,128)S(1)}, f32[9,128,128]{2,1,0:T(8,128)S(1)}, u32[]{:S(2)}, u32[]{:S(2)}) collective-permute-start(f32[9,128,128]{2,1,0:T(8,128)S(1)} %get-tuple-element.34), channel_id=1, source_target_pairs={{4,0},{8,4},{12,8},{16,12},{20,16},{24,20},{28,24},{5,1},{9,5},{13... | collective-permute-start | bytes 1769480 | tf_op jit(solution)/shard_map/ppermute | solution.py:785
  21.2 1.3 %settle.1 = (f32[1,128]{1,0:T(1,128)}, f32[16,8,128]{2,1,0:T(8,128)S(1)}, f32[9,32,128]{2,1,0:T(8,128)S(1)}, f32[9,32,128]{2,1,0:T(8,128)S(1)}) custom-call(s32[1]{0:T(128)} %bitcast.2.me, f32[8,48,128]{2,1,0:T(8,128)S(1)} %all_to_all.5.gathered, f32[9,32,128]{2,1,0:T(8,128)S(1)} %get-tuple-element.25.low_in, f32[9,32,128]{2,1,0:T(8,128)S(1)} %get-tuple-element.26.high_in), custom_call_target="tpu_custom_call" | custom-call | flops 1000000 | bytes 1000000 | tf_op jit(solution)/shard_map/settle/pallas_call | solution.py:761
  22.5 6.9 %collective-permute-start = (f32[9,32,128]{2,1,0:T(8,128)S(1)}, f32[9,32,128]{2,1,0:T(8,128)S(1)}, u32[]{:S(2)}, u32[]{:S(2)}) collective-permute-start(f32[9,32,128]{2,1,0:T(8,128)S(1)} %get-tuple-element.27), channel_id=1, source_target_pairs={{0,1},{1,2},{2,3},{4,5},{5,6},{6,7},{8,9},{9,10},{10,11},{12,13},{... | collective-permute-start | bytes 442376 | tf_op jit(solution)/shard_map/ppermute | solution.py:785
  29.4 1.9 %collective-permute-start.1 = (f32[9,32,128]{2,1,0:T(8,128)S(1)}, f32[9,32,128]{2,1,0:T(8,128)S(1)}, u32[]{:S(2)}, u32[]{:S(2)}) collective-permute-start(f32[9,32,128]{2,1,0:T(8,128)S(1)} %get-tuple-element.28), channel_id=1, source_target_pairs={{1,0},{2,1},{3,2},{5,4},{6,5},{7,6},{9,8},{10,9},{11,10},{13,12},{... | collective-permute-start | bytes 442376 | tf_op jit(solution)/shard_map/ppermute | solution.py:785
  31.3 4.4 %face_speeds.1 = (f32[32,16,8,128]{3,2,1,0:T(8,128)S(1)}, f32[32,16,8,128]{3,2,1,0:T(8,128)S(1)}) custom-call(f32[3,32,8,16,128]{4,3,2,1,0:T(8,128)} %bitcast.16), custom_call_target="tpu_custom_call" | custom-call | flops 4194304 | bytes 6291456 | tf_op jit(solution)/shard_map/face_speeds/pallas_call | solution.py:568
  35.8 0.0 copy-start
  35.8 0.0 collective-permute-done.refs_4_.refs_6_.refs_8_.refs_10_.refs_12_
  35.8 0.4 collective-permute-done.1.refs_5_.refs_7_.refs_9_.refs_11_.refs_13_
  36.2 18.1 %interior.2 = (f32[4,32,16,8,128]{4,3,2,1,0:T(8,128)}, f32[8,32,128]{2,1,0:T(8,128)S(1)}, f32[8,32,128]{2,1,0:T(8,128)S(1)}) custom-call(f32[4,32,8,16,128]{4,3,2,1,0:T(8,128)} %bitcast.21, f32[3,32,8,16,128]{4,3,2,1,0:T(8,128)} %bitcast.17, f32[32,16,8,128]{3,2,1,0:T(8,128)S(1)} %get-tuple-element.22.refs_2_.refs_4_.refs_6_, ...), custom_call_target="tpu_custom_call" | custom-call | flops 73400320 | bytes 23068672 | tf_op jit(solution)/shard_map/interior/pallas_call | solution.py:380
  54.3 0.0 copy-done
  54.3 0.0 collective-permute-done.2
  54.3 0.0 collective-permute-done.3
  54.3 0.0 copy-start.1
  54.3 5.4 %boundary.2 = (f32[4,2,16,8,128]{4,3,2,1,0:T(8,128)S(1)}, f32[4,2,16,8,128]{4,3,2,1,0:T(8,128)S(1)}, f32[8,32,128]{2,1,0:T(8,128)S(1)}, f32[8,32,128]{2,1,0:T(8,128)S(1)}) custom-call(f32[4,32,8,16,128]{4,3,2,1,0:T(8,128)} %bitcast.22, f32[9,8,16,128]{3,2,1,0:T(8,128)S(1)} %bitcast.8, f32[9,8,16,128]{3,2,1,0:T(8,128)S(1)} %bitcast.11, ...), custom_call_target="tpu_custom_call" | custom-call | flops 13107200 | bytes 6291456 | tf_op jit(solution)/shard_map/boundary/pallas_call | solution.py:524
  59.7 1.9 %collective-permute-start.5 = (f32[4,2,16,8,128]{4,3,2,1,0:T(8,128)S(1)}, f32[4,2,16,8,128]{4,3,2,1,0:T(8,128)S(1)}, u32[]{:S(2)}, u32[]{:S(2)}) collective-permute-start(f32[4,2,16,8,128]{4,3,2,1,0:T(8,128)S(1)} %get-tuple-element.37.refs_1_), channel_id=1, source_target_pairs={{4,0},{8,4},{12,8},{16,12},{20,16},{24,20},{28,24},{5,1},{9,5},{13... | collective-permute-start | bytes 1572872 | tf_op jit(solution)/shard_map/ppermute | solution.py:785
  61.6 4.3 %collective-permute-start.4 = (f32[4,2,16,8,128]{4,3,2,1,0:T(8,128)S(1)}, f32[4,2,16,8,128]{4,3,2,1,0:T(8,128)S(1)}, u32[]{:S(2)}, u32[]{:S(2)}) collective-permute-start(f32[4,2,16,8,128]{4,3,2,1,0:T(8,128)S(1)} %get-tuple-element.38.refs_2_), channel_id=1, source_target_pairs={{0,4},{4,8},{8,12},{12,16},{16,20},{20,24},{24,28},{1,5},{5,9},{9,... | collective-permute-start | bytes 1572872 | tf_op jit(solution)/shard_map/ppermute | solution.py:785
  65.9 4.2 %collective-permute-start.6 = (f32[8,32,128]{2,1,0:T(8,128)S(1)}, f32[8,32,128]{2,1,0:T(8,128)S(1)}, u32[]{:S(2)}, u32[]{:S(2)}) collective-permute-start(f32[8,32,128]{2,1,0:T(8,128)S(1)} %get-tuple-element.39), channel_id=1, source_target_pairs={{0,1},{1,2},{2,3},{4,5},{5,6},{6,7},{8,9},{9,10},{10,11},{12,13},{... | collective-permute-start | bytes 393224 | tf_op jit(solution)/shard_map/ppermute | solution.py:785
  70.1 1.9 %collective-permute-start.7 = (f32[8,32,128]{2,1,0:T(8,128)S(1)}, f32[8,32,128]{2,1,0:T(8,128)S(1)}, u32[]{:S(2)}, u32[]{:S(2)}) collective-permute-start(f32[8,32,128]{2,1,0:T(8,128)S(1)} %get-tuple-element.40), channel_id=1, source_target_pairs={{1,0},{2,1},{3,2},{5,4},{6,5},{7,6},{9,8},{10,9},{11,10},{13,12},{... | collective-permute-start | bytes 393224 | tf_op jit(solution)/shard_map/ppermute | solution.py:785
  72.1 0.0 collective-permute-done.6.refs_6_.refs_10_
  72.1 4.6 %collective-permute-done.7.refs_7_.refs_11_ = f32[8,32,128]{2,1,0:T(8,128)S(1)} collective-permute-done((f32[8,32,128]{2,1,0:T(8,128)S(1)}, f32[8,32,128]{2,1,0:T(8,128)S(1)}, u32[]{:S(2)}, u32[]{:S(2)}) %collective-permute-start.7) | collective-permute-done | bytes 131104 | tf_op jit(solution)/shard_map/ppermute | solution.py:785
  76.7 0.0 copy-done.1
  76.7 17.5 %interior.3.refs_14_ = f32[4,32,8,16,128]{4,3,2,1,0:T(8,128)} custom-call(f32[4,32,16,8,128]{4,3,2,1,0:T(8,128)} %get-tuple-element.30.refs_0_, f32[4,2,16,8,128]{4,3,2,1,0:T(8,128)S(1)} %get-tuple-element.37.refs_1_, f32[4,2,16,8,128]{4,3,2,1,0:T(8,128)S(1)} %get-tuple-element.38.refs_2_, f32[3,32,8,16,128]{4,3,2,1,0:T(8,128)} %bitcast.19, ...), custom_call_target="tpu_custom_call" | custom-call | flops 73400320 | bytes 23068672 | tf_op jit(solution)/shard_map/interior/pallas_call | solution.py:380
  94.2 0.0 collective-permute-done.5.refs_4_
  94.2 0.0 collective-permute-done.4.refs_3_
  94.2 4.8 %boundary.3 = f32[4,32,8,16,128]{4,3,2,1,0:T(8,128)} custom-call(f32[4,32,16,8,128]{4,3,2,1,0:T(8,128)} %get-tuple-element.30.refs_0_, f32[4,2,16,8,128]{4,3,2,1,0:T(8,128)S(1)} %get-tuple-element.37.refs_1_, f32[4,2,16,8,128]{4,3,2,1,0:T(8,128)S(1)} %get-tuple-element.38.refs_2_, ...), custom_call_target="tpu_custom_call", output_to_operand_aliasing={{}: (14, {})} | custom-call | flops 13107200 | bytes 6291456 | tf_op jit(solution)/shard_map/boundary/pallas_call | solution.py:524
Async XLA Ops:
  0.6 4.4 %copy-start.2 = (f32[1,32,128]{2,1,0:T(8,128)S(1)}, f32[1,32,128]{2,1,0:T(8,128)}, u32[]{:S(2)}) copy-start(f32[1,32,128]{2,1,0:T(8,128)} %share.1) | copy-start | bytes 49156
  0.6 4.4 %copy-start.6 = (s32[1,32]{1,0:T(1,128)S(1)}, s32[1,32]{1,0:T(1,128)}, u32[]{:S(2)}) copy-start(s32[1,32]{1,0:T(1,128)} %count.1) | copy-start | bytes 388
  0.7 4.4 %copy-start.5 = (s32[1,32,1]{1,2,0:T(1,128)S(1)}, s32[1,32,1]{1,2,0:T(1,128)}, u32[]{:S(2)}) copy-start(s32[1,32,1]{1,2,0:T(1,128)} %param.11) | copy-start | bytes 388
  0.7 4.4 %copy-start.4 = (s32[1,32,1]{1,2,0:T(1,128)S(1)}, s32[1,32,1]{1,2,0:T(1,128)}, u32[]{:S(2)}) copy-start(s32[1,32,1]{1,2,0:T(1,128)} %param.10) | copy-start | bytes 388
  0.7 4.4 %copy-start.3 = (f32[1,128]{1,0:T(1,128)S(1)}, f32[1,128]{1,0:T(1,128)}, u32[]{:S(2)}) copy-start(f32[1,128]{1,0:T(1,128)} %threshold.1) | copy-start | bytes 1540
  15.8 38.4 %collective-permute-start.2 = (f32[9,128,128]{2,1,0:T(8,128)S(1)}, f32[9,128,128]{2,1,0:T(8,128)S(1)}, u32[]{:S(2)}, u32[]{:S(2)}) collective-permute-start(f32[9,128,128]{2,1,0:T(8,128)S(1)} %get-tuple-element.33), channel_id=1, source_target_pairs={{0,4},{4,8},{8,12},{12,16},{16,20},{20,24},{24,28},{1,5},{5,9},{9,... | collective-permute-start | bytes 1769480 | tf_op jit(solution)/shard_map/ppermute | solution.py:785
  18.9 35.4 %collective-permute-start.3 = (f32[9,128,128]{2,1,0:T(8,128)S(1)}, f32[9,128,128]{2,1,0:T(8,128)S(1)}, u32[]{:S(2)}, u32[]{:S(2)}) collective-permute-start(f32[9,128,128]{2,1,0:T(8,128)S(1)} %get-tuple-element.34), channel_id=1, source_target_pairs={{4,0},{8,4},{12,8},{16,12},{20,16},{24,20},{28,24},{5,1},{9,5},{13... | collective-permute-start | bytes 1769480 | tf_op jit(solution)/shard_map/ppermute | solution.py:785
  22.5 13.3 %collective-permute-start = (f32[9,32,128]{2,1,0:T(8,128)S(1)}, f32[9,32,128]{2,1,0:T(8,128)S(1)}, u32[]{:S(2)}, u32[]{:S(2)}) collective-permute-start(f32[9,32,128]{2,1,0:T(8,128)S(1)} %get-tuple-element.27), channel_id=1, source_target_pairs={{0,1},{1,2},{2,3},{4,5},{5,6},{6,7},{8,9},{9,10},{10,11},{12,13},{... | collective-permute-start | bytes 442376 | tf_op jit(solution)/shard_map/ppermute | solution.py:785
  29.4 6.8 %collective-permute-start.1 = (f32[9,32,128]{2,1,0:T(8,128)S(1)}, f32[9,32,128]{2,1,0:T(8,128)S(1)}, u32[]{:S(2)}, u32[]{:S(2)}) collective-permute-start(f32[9,32,128]{2,1,0:T(8,128)S(1)} %get-tuple-element.28), channel_id=1, source_target_pairs={{1,0},{2,1},{3,2},{5,4},{6,5},{7,6},{9,8},{10,9},{11,10},{13,12},{... | collective-permute-start | bytes 442376 | tf_op jit(solution)/shard_map/ppermute | solution.py:785
  35.8 18.5 %copy-start = (f32[32,16,8,128]{3,2,1,0:T(8,128)}, f32[32,16,8,128]{3,2,1,0:T(8,128)S(1)}, u32[]{:S(2)}) copy-start(f32[32,16,8,128]{3,2,1,0:T(8,128)S(1)} %get-tuple-element.23.refs_3_.refs_5_.refs_7_) | copy-start | bytes 6291460
  54.3 22.4 %copy-start.1 = (f32[32,16,8,128]{3,2,1,0:T(8,128)S(1)}, f32[32,16,8,128]{3,2,1,0:T(8,128)}, u32[]{:S(2)}) copy-start(f32[32,16,8,128]{3,2,1,0:T(8,128)} %copy-done) | copy-start | bytes 6291460
  59.7 34.5 %collective-permute-start.5 = (f32[4,2,16,8,128]{4,3,2,1,0:T(8,128)S(1)}, f32[4,2,16,8,128]{4,3,2,1,0:T(8,128)S(1)}, u32[]{:S(2)}, u32[]{:S(2)}) collective-permute-start(f32[4,2,16,8,128]{4,3,2,1,0:T(8,128)S(1)} %get-tuple-element.37.refs_1_), channel_id=1, source_target_pairs={{4,0},{8,4},{12,8},{16,12},{20,16},{24,20},{28,24},{5,1},{9,5},{13... | collective-permute-start | bytes 1572872 | tf_op jit(solution)/shard_map/ppermute | solution.py:785
  61.6 32.6 %collective-permute-start.4 = (f32[4,2,16,8,128]{4,3,2,1,0:T(8,128)S(1)}, f32[4,2,16,8,128]{4,3,2,1,0:T(8,128)S(1)}, u32[]{:S(2)}, u32[]{:S(2)}) collective-permute-start(f32[4,2,16,8,128]{4,3,2,1,0:T(8,128)S(1)} %get-tuple-element.38.refs_2_), channel_id=1, source_target_pairs={{0,4},{4,8},{8,12},{12,16},{16,20},{20,24},{24,28},{1,5},{5,9},{9,... | collective-permute-start | bytes 1572872 | tf_op jit(solution)/shard_map/ppermute | solution.py:785
  65.9 6.2 %collective-permute-start.6 = (f32[8,32,128]{2,1,0:T(8,128)S(1)}, f32[8,32,128]{2,1,0:T(8,128)S(1)}, u32[]{:S(2)}, u32[]{:S(2)}) collective-permute-start(f32[8,32,128]{2,1,0:T(8,128)S(1)} %get-tuple-element.39), channel_id=1, source_target_pairs={{0,1},{1,2},{2,3},{4,5},{5,6},{6,7},{8,9},{9,10},{10,11},{12,13},{... | collective-permute-start | bytes 393224 | tf_op jit(solution)/shard_map/ppermute | solution.py:785
  70.1 6.6 %collective-permute-start.7 = (f32[8,32,128]{2,1,0:T(8,128)S(1)}, f32[8,32,128]{2,1,0:T(8,128)S(1)}, u32[]{:S(2)}, u32[]{:S(2)}) collective-permute-start(f32[8,32,128]{2,1,0:T(8,128)S(1)} %get-tuple-element.40), channel_id=1, source_target_pairs={{1,0},{2,1},{3,2},{5,4},{6,5},{7,6},{9,8},{10,9},{11,10},{13,12},{... | collective-permute-start | bytes 393224 | tf_op jit(solution)/shard_map/ppermute | solution.py:785

commit v6 on v5

--- a/solution.py
+++ b/solution.py
@@ -15,6 +15,7 @@
 VMEM_LIMIT = 48 * 1024 * 1024
 PAIR = 2
 GROUP = 8
+GATHER = 4
 HIGHEST = lax.Precision.HIGHEST
 ANY = pl.BlockSpec(memory_space=pl.ANY)
 VMEM = pl.BlockSpec(memory_space=pltpu.VMEM)
@@ -38,8 +39,8 @@
 
 
 class Slabs:
-    def __init__(self, q, u, v, sz, fall, fx, lx, block, x_at, at, halo, x, kept=None):
-        self.q, self.u, self.v, self.sz, self.falls, self.fx, self.lx = q, u, v, sz, fall, fx, lx
+    def __init__(self, q, uv, sz, fall, fx, lx, block, x_at, at, halo, x, kept=None):
+        self.q, self.uv, self.sz, self.falls, self.fx, self.lx = q, uv, sz, fall, fx, lx
         self.block, self.x_at, self.at, self.kept = block, x_at, at, kept
         self.halo, self.x = halo, x
         self.comps, self.tiles, self.lanes = q.shape[1], sz.shape[2], q.shape[-1]
@@ -63,10 +64,10 @@
 
     def east(self, k, t):
         here = k + self.x_at
-        return FACTOR * (self.u[self.block, here, t] + self.u[self.block, here + 1, t])
+        return FACTOR * (self.uv[self.block, 0, here, t] + self.uv[self.block, 0, here + 1, t])
 
     def wind(self, k, t):
-        inner = self.v[self.block, k + self.at, t % self.tiles]
+        inner = self.uv[self.block, 1, k + self.x_at, t % self.tiles]
         if 0 <= t < self.tiles:
             return inner
         row = lax.broadcasted_iota(jnp.int32, (8, self.lanes), 0)
@@ -271,10 +272,10 @@
     deposit = None if last else refs.pop(0)
     out = refs.pop(0)
     packs = None if last else (refs.pop(0), refs.pop(0))
-    q, u, v, sz, fall, fx, lx, stage, in_sem, out_sem = refs[:10]
-    kept = refs[10:12]
+    q, uv, sz, fall, fx, lx, stage, in_sem, out_sem = refs[:9]
+    kept = refs[9:11]
     comps, slabs, tiles = q.shape[1], q.shape[2], sz.shape[2]
-    chunk, flight = (8, 3) if last else (4, 6)
+    chunk, flight = 8, 3
     chunks = slabs // chunk
 
     def fetch(j, first, final):
@@ -293,11 +294,10 @@
         else:
             pair = (lambda n: fields[0].at[:, span, n], lambda n: q.at[0, :, span, :, n])
             start_sets([pair], in_sem.at[j, 0])
-        for c, target in enumerate((u, v)):
-            pair = (lambda n: velocity.at[c, span, n], lambda n: target.at[0, span, :, n])
-            start_sets([pair], in_sem.at[j, c + 1])
+        pair = (lambda n: velocity.at[pl.ds(0, 2), span, n], lambda n: uv.at[0, :, span, :, n])
+        start_sets([pair], in_sem.at[j, 1])
         for n, (source, target) in enumerate(zip(speeds, (sz, fall))):
-            start(source.at[span], target.at[0, span], in_sem.at[j, n + 3])
+            start(source.at[span], target.at[0, span], in_sem.at[j, n + 2])
 
     for j in range(flight):
         fetch(j, j == 0, False)
@@ -305,8 +305,8 @@
     def arrive(j):
         span = pl.ds(j * chunk, chunk)
         arrived(q.at[0, :, span], in_sem.at[j, 0])
-        for n, target in enumerate((u, v, sz, fall)):
-            arrived(target.at[0, span], in_sem.at[j, n + 1])
+        for n, spot in enumerate((uv.at[0, :, span], sz.at[0, span], fall.at[0, span])):
+            arrived(spot, in_sem.at[j, n + 1])
         later = j + flight
 
         @pl.when(later < chunks - 1)
@@ -324,7 +324,7 @@
         if not last:
             lax.fori_loop(j * chunk, jnp.minimum((j + 1) * chunk, groups), complete, 0)
 
-    f = Slabs(q, u, v, sz, fall, fx, lx, 0, 2, 2, (below, above, v_below, v_above), 2, kept)
+    f = Slabs(q, uv, sz, fall, fx, lx, 0, 2, 2, (below, above, v_below, v_above), 2, kept)
     arrive(jnp.int32(0))
     first_face(f)
 
@@ -338,7 +338,13 @@
 
         slab_step(f, k, put)
         if last:
-            start_sets([(lambda n: stage.at[:, k, :, n], lambda n: out.at[:, k + 2, n])], out_sem)
+
+            @pl.when((k + 1) % GATHER == 0)
+            def _():
+                first = k + 1 - GATHER
+                source, target = pl.ds(first, GATHER), pl.ds(first + 2, GATHER)
+                start_sets([(lambda n: stage.at[:, source, :, n], lambda n: out.at[:, target, n])], out_sem)
+
         else:
             start(stage.at[:, k], out.at[:, k + 2], out_sem)
         if not last:
@@ -363,7 +369,8 @@
     out_specs = [ANY]
     scratch = [
         pltpu.VMEM((1, comps, slabs, tiles, 8, lanes), jnp.float32),
-        *[pltpu.VMEM((1, slabs, tiles, 8, lanes), jnp.float32)] * 4,
+        pltpu.VMEM((1, 2, slabs, tiles, 8, lanes), jnp.float32),
+        *[pltpu.VMEM((1, slabs, tiles, 8, lanes), jnp.float32)] * 2,
         pltpu.VMEM((tiles, comps, 8, lanes), jnp.float32),
         pltpu.VMEM((tiles, comps, 8, lanes), jnp.float32),
         pltpu.VMEM((comps, slabs - 4, tiles, 8, lanes), jnp.float32),
@@ -402,7 +409,7 @@
     else:
         deposit, packed, ends, packs = refs[0], refs[1:3], refs[3:5], refs[5:7]
         del refs[:7]
-    q, u, v, sz, fall, fx, lx, stage, in_sem, out_sem = refs
+    q, uv, sz, fall, fx, lx, stage, in_sem, out_sem = refs
     comps, tiles = q.shape[1], sz.shape[2]
 
     if last:
@@ -429,12 +436,15 @@
     for block in range(2):
         outer, first, at = 3 * block, block * (slabs - 3), 1 - block
         pairs = [
-            (lambda n: u_outer[block].at[edge, n], lambda n: u.at[block, pl.ds(outer, 1), :, n]),
-            (lambda n: velocity.at[0, pl.ds(first, 3), n], lambda n: u.at[block, pl.ds(at, 3), :, n]),
+            (lambda n: u_outer[block].at[edge, n], lambda n: uv.at[block, 0, pl.ds(outer, 1), :, n]),
+            (
+                lambda n: velocity.at[pl.ds(0, 2), pl.ds(first, 3), n],
+                lambda n: uv.at[block, :, pl.ds(at, 3), :, n],
+            ),
         ]
-        start_sets(pairs, in_sem.at[block, 1])
+        for number, pair in enumerate(pairs):
+            start_sets([pair], in_sem.at[block, number + 1])
         span = pl.ds(block * (slabs - 2), 2)
-        start_sets([(lambda n: velocity.at[1, span, n], lambda n: v.at[block, :, :, n])], in_sem.at[block, 2])
         for n, target in enumerate((sz, fall)):
             start(speeds[n].at[span], target.at[block], in_sem.at[block, n + 3])
     if not last:
@@ -444,8 +454,9 @@
     def one(block, _):
         begin = block * (slabs - 2)
         arrived(q.at[block], in_sem.at[block, 0])
-        for n, target in enumerate((u, v, sz, fall)):
-            arrived(target.at[block], in_sem.at[block, n + 1])
+        spots = (uv.at[block, 0, pl.ds(0, 1)], uv.at[block, :, pl.ds(0, 3)], sz.at[block], fall.at[block])
+        for n, spot in enumerate(spots):
+            arrived(spot, in_sem.at[block, n + 1])
 
         def complete(slab, _):
             x = begin + slab - 2
@@ -459,7 +470,7 @@
 
         if not last:
             lax.fori_loop(0, 6, complete, 0)
-        f = Slabs(q, u, v, sz, fall, fx, lx, block, 1, 0, (below, above, v_below, v_above), begin)
+        f = Slabs(q, uv, sz, fall, fx, lx, block, 1, 0, (below, above, v_below, v_above), begin)
         first_face(f)
 
         def step(k, _):
@@ -499,8 +510,8 @@
     form = (tiles, 8, lanes)
     scratch = [
         pltpu.VMEM((2, comps, 6, tiles, 8, lanes), jnp.float32),
-        pltpu.VMEM((2, 4, tiles, 8, lanes), jnp.float32),
-        *[pltpu.VMEM((2, 2, tiles, 8, lanes), jnp.float32)] * 3,
+        pltpu.VMEM((2, 2, 4, tiles, 8, lanes), jnp.float32),
+        *[pltpu.VMEM((2, 2, tiles, 8, lanes), jnp.float32)] * 2,
         pltpu.VMEM((tiles, comps, 8, lanes), jnp.float32),
         pltpu.VMEM((tiles, comps, 8, lanes), jnp.float32),
         pltpu.VMEM((2, comps, 2, *form), jnp.float32),

time: 99.5 us -> 100 us (level)
  no operation moved by 1% of the time
where the time goes in v6:
time: 100 us; the launch traced here: 99.7 us
  Pallas kernels  56.8 us (57%)
  starting transfers between devices  26.4 us (26%)
  blocking collectives  10.5 us (10%)
  waiting for transfers between devices  5.02 us (5%)
    pallas_call x2, Pallas kernels, interior(): pl.pallas_call(functools.partial(interior_kernel, last, groups, len(field...  36.3 us
    ppermute x4, starting transfers between devices, exchange(): lax.ppermute(high, axis, forward)  18.5 us
    all_to_all x1, blocking collectives, shards(): lax.all_to_all(copies, 'gx', split_axis=0, concat_axis=0, tiled=True)  10.5 us
    pallas_call x2, Pallas kernels, boundary(): pl.pallas_call(functools.partial(boundary_kernel, last, groups, slabs), o...  10.1 us
    ppermute x4, starting transfers between devices, exchange(): lax.ppermute(low, axis, backward)  7.99 us
    ppermute x4, waiting for transfers between devices, exchange(): lax.ppermute(low, axis, backward)  5.01 us
    pallas_call x1, Pallas kernels, face_speeds(): pl.pallas_call(speeds_kernel, grid=(slabs // part,), out_shape=(jax.Shape...  4.44 us
    pallas_call x1, Pallas kernels, survey(): pl.pallas_call(survey_kernel, grid=(slabs // part,), out_shape=(packed, p...  4.38 us
  transfers between devices with their start and end apart: 8, of which 2 were waited for; matrix products, arithmetic and copies ran while one was open for 0% of the time, Pallas kernels for 42%

profile of v6, /device:TPU:3, one launch (start us, length us, event | category | flops | bytes accessed | tf_op | source)
XLA Modules:
  0.0 99.7 jit_solution(12000236982701170298)
XLA Ops:
  0.6 0.0 copy-start.2
  0.6 0.0 copy-start.6
  0.7 0.0 copy-start.5
  0.7 0.0 copy-start.4
  0.7 0.0 copy-start.3
  0.7 4.4 %survey.1 = (f32[9,32,128]{2,1,0:T(8,128)S(1)}, f32[9,32,128]{2,1,0:T(8,128)S(1)}, f32[32,128]{1,0:T(8,128)S(1)}, f32[9,128,128]{2,1,0:T(8,128)S(1)}, f32[9,128,128]{2,1,0:T(8,128)S(1)}) custom-call(f32[4,32,128,128]{3,2,1,0:T(8,128)} %state.1, f32[4,32,128,128]{3,2,1,0:T(8,128)} %state.1, f32[3,32,128,128]{3,2,1,0:T(8,128)} %velocity.1, ...), custom_call_target="tpu_custom_call" | custom-call | flops 5242880 | bytes 5242880 | tf_op jit(solution)/shard_map/survey/pallas_call | solution.py:667
  5.1 0.0 copy-done.2
  5.1 0.0 copy-done.6
  5.1 0.0 copy-done.5
  5.1 0.0 copy-done.4
  5.1 0.0 copy-done.3
  5.1 0.2 census.1
  5.3 10.5 %all_to_all.5.gathered = f32[8,48,128]{2,1,0:T(8,128)S(1)} all-to-all(f32[8,48,128]{2,1,0:T(8,128)S(1)} %census.1), channel_id=1, replica_groups=mesh['gx'=8,'gy'=4] {'gx'}, dimensions={0} | all-to-all | bytes 393216 | tf_op jit(solution)/shard_map/all_to_all | solution.py:815
  15.8 3.1 %collective-permute-start.2 = (f32[9,128,128]{2,1,0:T(8,128)S(1)}, f32[9,128,128]{2,1,0:T(8,128)S(1)}, u32[]{:S(2)}, u32[]{:S(2)}) collective-permute-start(f32[9,128,128]{2,1,0:T(8,128)S(1)} %get-tuple-element.33), channel_id=1, source_target_pairs={{0,4},{4,8},{8,12},{12,16},{16,20},{20,24},{24,28},{1,5},{5,9},{9,... | collective-permute-start | bytes 1769480 | tf_op jit(solution)/shard_map/ppermute | solution.py:796
  18.9 2.2 %collective-permute-start.3 = (f32[9,128,128]{2,1,0:T(8,128)S(1)}, f32[9,128,128]{2,1,0:T(8,128)S(1)}, u32[]{:S(2)}, u32[]{:S(2)}) collective-permute-start(f32[9,128,128]{2,1,0:T(8,128)S(1)} %get-tuple-element.34), channel_id=1, source_target_pairs={{4,0},{8,4},{12,8},{16,12},{20,16},{24,20},{28,24},{5,1},{9,5},{13... | collective-permute-start | bytes 1769480 | tf_op jit(solution)/shard_map/ppermute | solution.py:796
  21.2 1.3 %settle.1 = (f32[1,128]{1,0:T(1,128)}, f32[16,8,128]{2,1,0:T(8,128)S(1)}, f32[9,32,128]{2,1,0:T(8,128)S(1)}, f32[9,32,128]{2,1,0:T(8,128)S(1)}) custom-call(s32[1]{0:T(128)} %bitcast.2.me, f32[8,48,128]{2,1,0:T(8,128)S(1)} %all_to_all.5.gathered, f32[9,32,128]{2,1,0:T(8,128)S(1)} %get-tuple-element.25.low_in, f32[9,32,128]{2,1,0:T(8,128)S(1)} %get-tuple-element.26.high_in), custom_call_target="tpu_custom_call" | custom-call | flops 1000000 | bytes 1000000 | tf_op jit(solution)/shard_map/settle/pallas_call | solution.py:772
  22.5 6.9 %collective-permute-start = (f32[9,32,128]{2,1,0:T(8,128)S(1)}, f32[9,32,128]{2,1,0:T(8,128)S(1)}, u32[]{:S(2)}, u32[]{:S(2)}) collective-permute-start(f32[9,32,128]{2,1,0:T(8,128)S(1)} %get-tuple-element.27), channel_id=1, source_target_pairs={{0,1},{1,2},{2,3},{4,5},{5,6},{6,7},{8,9},{9,10},{10,11},{12,13},{... | collective-permute-start | bytes 442376 | tf_op jit(solution)/shard_map/ppermute | solution.py:796
  29.4 1.9 %collective-permute-start.1 = (f32[9,32,128]{2,1,0:T(8,128)S(1)}, f32[9,32,128]{2,1,0:T(8,128)S(1)}, u32[]{:S(2)}, u32[]{:S(2)}) collective-permute-start(f32[9,32,128]{2,1,0:T(8,128)S(1)} %get-tuple-element.28), channel_id=1, source_target_pairs={{1,0},{2,1},{3,2},{5,4},{6,5},{7,6},{9,8},{10,9},{11,10},{13,12},{... | collective-permute-start | bytes 442376 | tf_op jit(solution)/shard_map/ppermute | solution.py:796
  31.3 4.4 %face_speeds.1 = (f32[32,16,8,128]{3,2,1,0:T(8,128)S(1)}, f32[32,16,8,128]{3,2,1,0:T(8,128)S(1)}) custom-call(f32[3,32,8,16,128]{4,3,2,1,0:T(8,128)} %bitcast.16), custom_call_target="tpu_custom_call" | custom-call | flops 4194304 | bytes 6291456 | tf_op jit(solution)/shard_map/face_speeds/pallas_call | solution.py:579
  35.8 0.0 copy-start
  35.8 0.0 collective-permute-done.refs_4_.refs_6_.refs_8_.refs_10_.refs_12_
  35.8 0.4 collective-permute-done.1.refs_5_.refs_7_.refs_9_.refs_11_.refs_13_
  36.2 18.4 %interior.2 = (f32[4,32,16,8,128]{4,3,2,1,0:T(8,128)}, f32[8,32,128]{2,1,0:T(8,128)S(1)}, f32[8,32,128]{2,1,0:T(8,128)S(1)}) custom-call(f32[4,32,8,16,128]{4,3,2,1,0:T(8,128)} %bitcast.21, f32[3,32,8,16,128]{4,3,2,1,0:T(8,128)} %bitcast.17, f32[32,16,8,128]{3,2,1,0:T(8,128)S(1)} %get-tuple-element.22.refs_2_.refs_4_.refs_6_, ...), custom_call_target="tpu_custom_call" | custom-call | flops 73400320 | bytes 23068672 | tf_op jit(solution)/shard_map/interior/pallas_call | solution.py:387
  54.5 0.0 copy-done
  54.5 0.0 collective-permute-done.2
  54.5 0.0 collective-permute-done.3
  54.6 0.0 copy-start.1
  54.6 5.4 %boundary.2 = (f32[4,2,16,8,128]{4,3,2,1,0:T(8,128)S(1)}, f32[4,2,16,8,128]{4,3,2,1,0:T(8,128)S(1)}, f32[8,32,128]{2,1,0:T(8,128)S(1)}, f32[8,32,128]{2,1,0:T(8,128)S(1)}) custom-call(f32[4,32,8,16,128]{4,3,2,1,0:T(8,128)} %bitcast.22, f32[9,8,16,128]{3,2,1,0:T(8,128)S(1)} %bitcast.8, f32[9,8,16,128]{3,2,1,0:T(8,128)S(1)} %bitcast.11, ...), custom_call_target="tpu_custom_call" | custom-call | flops 13107200 | bytes 6291456 | tf_op jit(solution)/shard_map/boundary/pallas_call | solution.py:535
  59.9 1.9 %collective-permute-start.5 = (f32[4,2,16,8,128]{4,3,2,1,0:T(8,128)S(1)}, f32[4,2,16,8,128]{4,3,2,1,0:T(8,128)S(1)}, u32[]{:S(2)}, u32[]{:S(2)}) collective-permute-start(f32[4,2,16,8,128]{4,3,2,1,0:T(8,128)S(1)} %get-tuple-element.37.refs_1_), channel_id=1, source_target_pairs={{4,0},{8,4},{12,8},{16,12},{20,16},{24,20},{28,24},{5,1},{9,5},{13... | collective-permute-start | bytes 1572872 | tf_op jit(solution)/shard_map/ppermute | solution.py:796
  61.9 4.3 %collective-permute-start.4 = (f32[4,2,16,8,128]{4,3,2,1,0:T(8,128)S(1)}, f32[4,2,16,8,128]{4,3,2,1,0:T(8,128)S(1)}, u32[]{:S(2)}, u32[]{:S(2)}) collective-permute-start(f32[4,2,16,8,128]{4,3,2,1,0:T(8,128)S(1)} %get-tuple-element.38.refs_2_), channel_id=1, source_target_pairs={{0,4},{4,8},{8,12},{12,16},{16,20},{20,24},{24,28},{1,5},{5,9},{9,... | collective-permute-start | bytes 1572872 | tf_op jit(solution)/shard_map/ppermute | solution.py:796
  66.1 4.2 %collective-permute-start.6 = (f32[8,32,128]{2,1,0:T(8,128)S(1)}, f32[8,32,128]{2,1,0:T(8,128)S(1)}, u32[]{:S(2)}, u32[]{:S(2)}) collective-permute-start(f32[8,32,128]{2,1,0:T(8,128)S(1)} %get-tuple-element.39), channel_id=1, source_target_pairs={{0,1},{1,2},{2,3},{4,5},{5,6},{6,7},{8,9},{9,10},{10,11},{12,13},{... | collective-permute-start | bytes 393224 | tf_op jit(solution)/shard_map/ppermute | solution.py:796
  70.4 1.9 %collective-permute-start.7 = (f32[8,32,128]{2,1,0:T(8,128)S(1)}, f32[8,32,128]{2,1,0:T(8,128)S(1)}, u32[]{:S(2)}, u32[]{:S(2)}) collective-permute-start(f32[8,32,128]{2,1,0:T(8,128)S(1)} %get-tuple-element.40), channel_id=1, source_target_pairs={{1,0},{2,1},{3,2},{5,4},{6,5},{7,6},{9,8},{10,9},{11,10},{13,12},{... | collective-permute-start | bytes 393224 | tf_op jit(solution)/shard_map/ppermute | solution.py:796
  72.3 0.0 collective-permute-done.6.refs_6_.refs_10_
  72.3 4.6 %collective-permute-done.7.refs_7_.refs_11_ = f32[8,32,128]{2,1,0:T(8,128)S(1)} collective-permute-done((f32[8,32,128]{2,1,0:T(8,128)S(1)}, f32[8,32,128]{2,1,0:T(8,128)S(1)}, u32[]{:S(2)}, u32[]{:S(2)}) %collective-permute-start.7) | collective-permute-done | bytes 131104 | tf_op jit(solution)/shard_map/ppermute | solution.py:796
  77.0 0.0 copy-done.1
  77.0 17.9 %interior.3.refs_14_ = f32[4,32,8,16,128]{4,3,2,1,0:T(8,128)} custom-call(f32[4,32,16,8,128]{4,3,2,1,0:T(8,128)} %get-tuple-element.30.refs_0_, f32[4,2,16,8,128]{4,3,2,1,0:T(8,128)S(1)} %get-tuple-element.37.refs_1_, f32[4,2,16,8,128]{4,3,2,1,0:T(8,128)S(1)} %get-tuple-element.38.refs_2_, f32[3,32,8,16,128]{4,3,2,1,0:T(8,128)} %bitcast.19, ...), custom_call_target="tpu_custom_call" | custom-call | flops 73400320 | bytes 23068672 | tf_op jit(solution)/shard_map/interior/pallas_call | solution.py:387
  94.9 0.0 collective-permute-done.5.refs_4_
  94.9 0.0 collective-permute-done.4.refs_3_
  94.9 4.7 %boundary.3 = f32[4,32,8,16,128]{4,3,2,1,0:T(8,128)} custom-call(f32[4,32,16,8,128]{4,3,2,1,0:T(8,128)} %get-tuple-element.30.refs_0_, f32[4,2,16,8,128]{4,3,2,1,0:T(8,128)S(1)} %get-tuple-element.37.refs_1_, f32[4,2,16,8,128]{4,3,2,1,0:T(8,128)S(1)} %get-tuple-element.38.refs_2_, ...), custom_call_target="tpu_custom_call", output_to_operand_aliasing={{}: (14, {})} | custom-call | flops 13107200 | bytes 6291456 | tf_op jit(solution)/shard_map/boundary/pallas_call | solution.py:535
Async XLA Ops:
  0.6 4.4 %copy-start.2 = (f32[1,32,128]{2,1,0:T(8,128)S(1)}, f32[1,32,128]{2,1,0:T(8,128)}, u32[]{:S(2)}) copy-start(f32[1,32,128]{2,1,0:T(8,128)} %share.1) | copy-start | bytes 49156
  0.6 4.4 %copy-start.6 = (s32[1,32]{1,0:T(1,128)S(1)}, s32[1,32]{1,0:T(1,128)}, u32[]{:S(2)}) copy-start(s32[1,32]{1,0:T(1,128)} %count.1) | copy-start | bytes 388
  0.7 4.4 %copy-start.5 = (s32[1,32,1]{1,2,0:T(1,128)S(1)}, s32[1,32,1]{1,2,0:T(1,128)}, u32[]{:S(2)}) copy-start(s32[1,32,1]{1,2,0:T(1,128)} %param.11) | copy-start | bytes 388
  0.7 4.4 %copy-start.4 = (s32[1,32,1]{1,2,0:T(1,128)S(1)}, s32[1,32,1]{1,2,0:T(1,128)}, u32[]{:S(2)}) copy-start(s32[1,32,1]{1,2,0:T(1,128)} %param.10) | copy-start | bytes 388
  0.7 4.4 %copy-start.3 = (f32[1,128]{1,0:T(1,128)S(1)}, f32[1,128]{1,0:T(1,128)}, u32[]{:S(2)}) copy-start(f32[1,128]{1,0:T(1,128)} %threshold.1) | copy-start | bytes 1540
  15.8 38.7 %collective-permute-start.2 = (f32[9,128,128]{2,1,0:T(8,128)S(1)}, f32[9,128,128]{2,1,0:T(8,128)S(1)}, u32[]{:S(2)}, u32[]{:S(2)}) collective-permute-start(f32[9,128,128]{2,1,0:T(8,128)S(1)} %get-tuple-element.33), channel_id=1, source_target_pairs={{0,4},{4,8},{8,12},{12,16},{16,20},{20,24},{24,28},{1,5},{5,9},{9,... | collective-permute-start | bytes 1769480 | tf_op jit(solution)/shard_map/ppermute | solution.py:796
  18.9 35.6 %collective-permute-start.3 = (f32[9,128,128]{2,1,0:T(8,128)S(1)}, f32[9,128,128]{2,1,0:T(8,128)S(1)}, u32[]{:S(2)}, u32[]{:S(2)}) collective-permute-start(f32[9,128,128]{2,1,0:T(8,128)S(1)} %get-tuple-element.34), channel_id=1, source_target_pairs={{4,0},{8,4},{12,8},{16,12},{20,16},{24,20},{28,24},{5,1},{9,5},{13... | collective-permute-start | bytes 1769480 | tf_op jit(solution)/shard_map/ppermute | solution.py:796
  22.5 13.3 %collective-permute-start = (f32[9,32,128]{2,1,0:T(8,128)S(1)}, f32[9,32,128]{2,1,0:T(8,128)S(1)}, u32[]{:S(2)}, u32[]{:S(2)}) collective-permute-start(f32[9,32,128]{2,1,0:T(8,128)S(1)} %get-tuple-element.27), channel_id=1, source_target_pairs={{0,1},{1,2},{2,3},{4,5},{5,6},{6,7},{8,9},{9,10},{10,11},{12,13},{... | collective-permute-start | bytes 442376 | tf_op jit(solution)/shard_map/ppermute | solution.py:796
  29.4 6.8 %collective-permute-start.1 = (f32[9,32,128]{2,1,0:T(8,128)S(1)}, f32[9,32,128]{2,1,0:T(8,128)S(1)}, u32[]{:S(2)}, u32[]{:S(2)}) collective-permute-start(f32[9,32,128]{2,1,0:T(8,128)S(1)} %get-tuple-element.28), channel_id=1, source_target_pairs={{1,0},{2,1},{3,2},{5,4},{6,5},{7,6},{9,8},{10,9},{11,10},{13,12},{... | collective-permute-start | bytes 442376 | tf_op jit(solution)/shard_map/ppermute | solution.py:796
  35.8 18.8 %copy-start = (f32[32,16,8,128]{3,2,1,0:T(8,128)}, f32[32,16,8,128]{3,2,1,0:T(8,128)S(1)}, u32[]{:S(2)}) copy-start(f32[32,16,8,128]{3,2,1,0:T(8,128)S(1)} %get-tuple-element.23.refs_3_.refs_5_.refs_7_) | copy-start | bytes 6291460
  54.6 22.4 %copy-start.1 = (f32[32,16,8,128]{3,2,1,0:T(8,128)S(1)}, f32[32,16,8,128]{3,2,1,0:T(8,128)}, u32[]{:S(2)}) copy-start(f32[32,16,8,128]{3,2,1,0:T(8,128)} %copy-done) | copy-start | bytes 6291460
  59.9 35.0 %collective-permute-start.5 = (f32[4,2,16,8,128]{4,3,2,1,0:T(8,128)S(1)}, f32[4,2,16,8,128]{4,3,2,1,0:T(8,128)S(1)}, u32[]{:S(2)}, u32[]{:S(2)}) collective-permute-start(f32[4,2,16,8,128]{4,3,2,1,0:T(8,128)S(1)} %get-tuple-element.37.refs_1_), channel_id=1, source_target_pairs={{4,0},{8,4},{12,8},{16,12},{20,16},{24,20},{28,24},{5,1},{9,5},{13... | collective-permute-start | bytes 1572872 | tf_op jit(solution)/shard_map/ppermute | solution.py:796
  61.9 33.1 %collective-permute-start.4 = (f32[4,2,16,8,128]{4,3,2,1,0:T(8,128)S(1)}, f32[4,2,16,8,128]{4,3,2,1,0:T(8,128)S(1)}, u32[]{:S(2)}, u32[]{:S(2)}) collective-permute-start(f32[4,2,16,8,128]{4,3,2,1,0:T(8,128)S(1)} %get-tuple-element.38.refs_2_), channel_id=1, source_target_pairs={{0,4},{4,8},{8,12},{12,16},{16,20},{20,24},{24,28},{1,5},{5,9},{9,... | collective-permute-start | bytes 1572872 | tf_op jit(solution)/shard_map/ppermute | solution.py:796
  66.1 6.2 %collective-permute-start.6 = (f32[8,32,128]{2,1,0:T(8,128)S(1)}, f32[8,32,128]{2,1,0:T(8,128)S(1)}, u32[]{:S(2)}, u32[]{:S(2)}) collective-permute-start(f32[8,32,128]{2,1,0:T(8,128)S(1)} %get-tuple-element.39), channel_id=1, source_target_pairs={{0,1},{1,2},{2,3},{4,5},{5,6},{6,7},{8,9},{9,10},{10,11},{12,13},{... | collective-permute-start | bytes 393224 | tf_op jit(solution)/shard_map/ppermute | solution.py:796
  70.4 6.6 %collective-permute-start.7 = (f32[8,32,128]{2,1,0:T(8,128)S(1)}, f32[8,32,128]{2,1,0:T(8,128)S(1)}, u32[]{:S(2)}, u32[]{:S(2)}) collective-permute-start(f32[8,32,128]{2,1,0:T(8,128)S(1)} %get-tuple-element.40), channel_id=1, source_target_pairs={{1,0},{2,1},{3,2},{5,4},{6,5},{7,6},{9,8},{10,9},{11,10},{13,12},{... | collective-permute-start | bytes 393224 | tf_op jit(solution)/shard_map/ppermute | solution.py:796

commit v7 on v6

--- a/solution.py
+++ b/solution.py
@@ -14,8 +14,6 @@
 
 VMEM_LIMIT = 48 * 1024 * 1024
 PAIR = 2
-GROUP = 8
-GATHER = 4
 HIGHEST = lax.Precision.HIGHEST
 ANY = pl.BlockSpec(memory_space=pl.ANY)
 VMEM = pl.BlockSpec(memory_space=pltpu.VMEM)
@@ -138,7 +136,7 @@
     staged([functools.partial(job, range(t, t + PAIR)) for t in range(0, f.tiles, PAIR)])
 
 
-def slab_step(f, k, put):
+def slab_step(f, k, put, group_size=8):
     slab = k + 2
     lane = lax.broadcasted_iota(jnp.int32, (8, f.lanes), 1)
     top = f.lanes - 1
@@ -179,11 +177,11 @@
         return doubles[c, t]
 
     held = []
-    for t in range(GROUP):
+    for t in range(group_size):
         vertical(t)
-    for begin in range(0, f.tiles, GROUP):
-        group = range(begin, min(begin + GROUP, f.tiles))
-        for t in range(begin + GROUP, min(begin + 2 * GROUP, f.tiles)):
+    for begin in range(0, f.tiles, group_size):
+        group = range(begin, min(begin + group_size, f.tiles))
+        for t in range(begin + group_size, min(begin + 2 * group_size, f.tiles)):
             vertical(t)
         loaded = {}
         for t in group:
@@ -275,7 +273,7 @@
     q, uv, sz, fall, fx, lx, stage, in_sem, out_sem = refs[:9]
     kept = refs[9:11]
     comps, slabs, tiles = q.shape[1], q.shape[2], sz.shape[2]
-    chunk, flight = 8, 3
+    chunk, flight = (8, 3) if last else (4, 6)
     chunks = slabs // chunk
 
     def fetch(j, first, final):
@@ -336,15 +334,9 @@
         def put(c, t, value):
             stage[c, k, t] = value
 
-        slab_step(f, k, put)
+        slab_step(f, k, put, 16 if last else 4)
         if last:
-
-            @pl.when((k + 1) % GATHER == 0)
-            def _():
-                first = k + 1 - GATHER
-                source, target = pl.ds(first, GATHER), pl.ds(first + 2, GATHER)
-                start_sets([(lambda n: stage.at[:, source, :, n], lambda n: out.at[:, target, n])], out_sem)
-
+            start_sets([(lambda n: stage.at[:, k, :, n], lambda n: out.at[:, k + 2, n])], out_sem)
         else:
             start(stage.at[:, k], out.at[:, k + 2], out_sem)
         if not last:
@@ -609,25 +601,10 @@
     return jnp.sum(jnp.where(same, row, 0.0), axis=1, keepdims=True)
 
 
-def survey_kernel(
-    low_in, high_in, v_low, v_high, wind, state, velocity, low, high, stress, x_low, x_high, gathered, sems,
-):
+def stress_kernel(wind, stress, gathered):
     step, steps = pl.program_id(0), pl.num_programs(0)
-
-    @pl.when(step == 0)
-    def _():
-        for copy in x_copies(state, velocity, x_low, x_high, sems):
-            copy.start()
-
-    comps, part, rows, lanes = low_in.shape[0], wind.shape[1], wind.shape[2], wind.shape[3]
+    part, rows, lanes = wind.shape[1:]
     slabs = stress.shape[0]
-    for x in range(part):
-        for c in range(comps):
-            for r in range(2):
-                low[2 * c + r, x : x + 1, :] = low_in[c, x, r : r + 1, :]
-                high[2 * c + r, x : x + 1, :] = high_in[c, x, 6 + r : 7 + r, :]
-        low[2 * comps, x : x + 1, :] = v_low[0, x, 0:1, :]
-        high[2 * comps, x : x + 1, :] = v_high[0, x, 7:8, :]
     lane = lax.broadcasted_iota(jnp.int32, (rows, lanes), 1)
     weight = jnp.zeros((rows, lanes), jnp.float32)
     for level, value in enumerate(profile_weights):
@@ -653,11 +630,48 @@
         for level in range(1, LEVELS):
             total = total + gathered[pl.ds(level, slabs, stride=LEVELS), :]
         stress[...] = total
+
+
+def tile_stress(velocity):
+    _, slabs, rows, lanes = velocity.shape
+    part = 8
+    return pl.pallas_call(
+        stress_kernel,
+        grid=(slabs // part,),
+        out_shape=jax.ShapeDtypeStruct((slabs, lanes), jnp.float32),
+        in_specs=[pl.BlockSpec((2, part, rows, lanes), lambda i: (0, i, 0, 0))],
+        out_specs=pl.BlockSpec((slabs, lanes), lambda i: (0, 0)),
+        scratch_shapes=[pltpu.VMEM((rows, lanes), jnp.float32)],
+        compiler_params=params(),
+        cost_estimate=cost(10 * slabs * rows * lanes, 8 * slabs * rows * lanes),
+        name="tile_stress",
+    )(velocity)
+
+
+def pack_kernel(low_in, high_in, v_low, v_high, state, velocity, low, high, x_low, x_high, sems):
+    step, steps = pl.program_id(0), pl.num_programs(0)
+    comps, part = low_in.shape[:2]
+
+    @pl.when(step == 0)
+    def _():
+        for copy in x_copies(state, velocity, x_low, x_high, sems):
+            copy.start()
+
+    for x in range(part):
+        for c in range(comps):
+            for r in range(2):
+                low[2 * c + r, x : x + 1, :] = low_in[c, x, r : r + 1, :]
+                high[2 * c + r, x : x + 1, :] = high_in[c, x, 6 + r : 7 + r, :]
+        low[2 * comps, x : x + 1, :] = v_low[0, x, 0:1, :]
+        high[2 * comps, x : x + 1, :] = v_high[0, x, 7:8, :]
+
+    @pl.when(step == steps - 1)
+    def _():
         for copy in x_copies(state, velocity, x_low, x_high, sems):
             copy.wait()
 
 
-def survey(state, velocity):
+def pack(state, velocity):
     comps, slabs, rows, lanes = state.shape
     part = 8
     last = rows // 8 - 1
@@ -665,24 +679,23 @@
     packed_spec = pl.BlockSpec((2 * comps + 1, part, lanes), lambda i: (0, i, 0))
     x_packed = jax.ShapeDtypeStruct((2 * comps + 1, rows, lanes), jnp.float32)
     return pl.pallas_call(
-        survey_kernel,
+        pack_kernel,
         grid=(slabs // part,),
-        out_shape=(packed, packed, jax.ShapeDtypeStruct((slabs, lanes), jnp.float32), x_packed, x_packed),
+        out_shape=(packed, packed, x_packed, x_packed),
         in_specs=[
             pl.BlockSpec((comps, part, 8, lanes), lambda i: (0, i, 0, 0)),
             pl.BlockSpec((comps, part, 8, lanes), lambda i: (0, i, last, 0)),
             pl.BlockSpec((1, part, 8, lanes), lambda i: (1, i, 0, 0)),
             pl.BlockSpec((1, part, 8, lanes), lambda i: (1, i, last, 0)),
-            pl.BlockSpec((2, part, rows, lanes), lambda i: (0, i, 0, 0)),
             ANY,
             ANY,
         ],
-        out_specs=(packed_spec, packed_spec, pl.BlockSpec((slabs, lanes), lambda i: (0, 0)), ANY, ANY),
-        scratch_shapes=[pltpu.VMEM((rows, lanes), jnp.float32), pltpu.SemaphoreType.DMA((2, comps + 1))],
+        out_specs=(packed_spec, packed_spec, ANY, ANY),
+        scratch_shapes=[pltpu.SemaphoreType.DMA((2, comps + 1))],
         compiler_params=params(),
-        cost_estimate=cost(10 * slabs * rows * lanes, 10 * slabs * rows * lanes),
-        name="survey",
-    )(state, state, velocity, velocity, velocity, state, velocity)
+        cost_estimate=cost(1, 12 * (2 * comps + 1) * rows * lanes),
+        name="pack",
+    )(state, state, velocity, velocity, state, velocity)
 
 
 def census_kernel(stress, threshold, tile_owner, parcel_owner, count, share, copies):
@@ -801,7 +814,8 @@
     slabs = state.shape[1]
     me = lax.axis_index("gx").astype(jnp.int32).reshape(1)
 
-    low, high, stress, own_low, own_high = survey(state, velocity)
+    stress = tile_stress(velocity)
+    low, high, own_low, own_high = pack(state, velocity)
     copies = census(
         groups, stress, threshold, tile_owner[:, :, 0], parcel_owner[:, :, 0], parcel_count, parcel_share
     )

time: 100 us -> 102 us (1.020)
  blocking collectives: 10.5 us -> 0 us
  starting transfers between devices: 26.4 us -> 32.2 us
  local copies, waits for them, and re-layouts: 0.03 us -> 3.34 us
  waiting for transfers between devices: 5.02 us -> 7.27 us
    all_to_all x1 -> x0, blocking collectives: 10.5 us -> none  [shards(): lax.all_to_all(copies, 'gx', split_axis=0, concat_axis=0, tiled=True)]
    all_to_all x0 -> x1, starting transfers between devices: none -> 5.78 us  [shards(): lax.all_to_all(copies, 'gx', split_axis=0, concat_axis=0, tiled=True)]
    unnamed x14, local copies, waits for them, and re-layouts: 0.03 us -> 3.34 us
    all_to_all x0 -> x1, waiting for transfers between devices: none -> 2.24 us  [shards(): lax.all_to_all(copies, 'gx', split_axis=0, concat_axis=0, tiled=True)]
    pallas_call x1 -> x2, Pallas kernels: 4.38 us -> 6.23 us  [the longest x1 3.55 us: tile_stress(): pl.pallas_call(stress_kernel, grid=(slabs // part,), out_shape=jax.ShapeD...]
    pallas_call x2, Pallas kernels: 36.3 us -> 34.7 us  [interior(): pl.pallas_call(functools.partial(interior_kernel, last, groups, len(field...]
  transfers between devices with their start and end apart: 8 -> 9, of which waited for: 2 -> 3; matrix products, arithmetic and copies ran while one was open for 0% -> 0% of each run, Pallas kernels for 42% -> 43%
where the time goes in v7:
time: 102 us; the launch traced here: 101 us
  Pallas kernels  57.7 us (57%)
  starting transfers between devices  32.2 us (32%)
  waiting for transfers between devices  7.27 us (7%)
  local copies, waits for them, and re-layouts  3.34 us (3%)
    pallas_call x2, Pallas kernels, interior(): pl.pallas_call(functools.partial(interior_kernel, last, groups, len(field...  34.7 us
    ppermute x4, starting transfers between devices, exchange(): lax.ppermute(high, axis, forward)  18.5 us
    pallas_call x2, Pallas kernels, boundary(): pl.pallas_call(functools.partial(boundary_kernel, last, groups, slabs), o...  10.1 us
    ppermute x4, starting transfers between devices, exchange(): lax.ppermute(low, axis, backward)  7.99 us
    all_to_all x1, starting transfers between devices, shards(): lax.all_to_all(copies, 'gx', split_axis=0, concat_axis=0, tiled=True)  5.78 us
    ppermute x4, waiting for transfers between devices, exchange(): lax.ppermute(low, axis, backward)  5.01 us
    pallas_call x1, Pallas kernels, face_speeds(): pl.pallas_call(speeds_kernel, grid=(slabs // part,), out_shape=(jax.Shape...  4.44 us
    pallas_call x1, Pallas kernels, tile_stress(): pl.pallas_call(stress_kernel, grid=(slabs // part,), out_shape=jax.ShapeD...  3.55 us
  transfers between devices with their start and end apart: 9, of which 3 were waited for; matrix products, arithmetic and copies ran while one was open for 0% of the time, Pallas kernels for 43%

profile of v7, /device:TPU:3, one launch (start us, length us, event | category | flops | bytes accessed | tf_op | source)
XLA Modules:
  0.0 101.3 jit_solution(14168423308588220915)
XLA Ops:
  0.6 3.5 %tile_stress.1.stress = f32[32,128]{1,0:T(8,128)S(1)} custom-call(f32[3,32,128,128]{3,2,1,0:T(8,128)} %velocity.1), custom_call_target="tpu_custom_call" | custom-call | flops 5242880 | bytes 4194304 | tf_op jit(solution)/shard_map/tile_stress/pallas_call | solution.py:638
  4.2 0.0 copy-start.2
  4.2 0.7 copy-done.2
  4.9 0.0 copy-start.3
  4.9 0.7 copy-done.3
  5.6 0.0 copy-start.4
  5.6 0.7 copy-done.4
  6.2 0.0 copy-start.5
  6.2 0.7 copy-done.5
  6.9 0.0 copy-start.6
  6.9 0.7 copy-done.6
  7.5 0.9 census.1
  8.4 5.8 %all-to-all-start = ((f32[8,48,128]{2,1,0:T(8,128)}), f32[8,48,128]{2,1,0:T(8,128)S(1)}, u32[]{:S(2)}, u32[]{:S(2)}) async-start(f32[8,48,128]{2,1,0:T(8,128)} %census.1), calls=%async_computation | async-start | bytes 393216 | tf_op jit(solution)/shard_map/all_to_all | solution.py:829
  14.2 2.7 %pack.1 = (f32[9,32,128]{2,1,0:T(8,128)S(1)}, f32[9,32,128]{2,1,0:T(8,128)S(1)}, f32[9,128,128]{2,1,0:T(8,128)S(1)}, f32[9,128,128]{2,1,0:T(8,128)S(1)}) custom-call(f32[4,32,128,128]{3,2,1,0:T(8,128)} %state.1, f32[4,32,128,128]{3,2,1,0:T(8,128)} %state.1, f32[3,32,128,128]{3,2,1,0:T(8,128)} %velocity.1, f32[3,32,128,128]{3,2,1,0:T(8,128)} %velocity.1, ...), custom_call_target="tpu_custom_call" | custom-call | flops 1 | bytes 1769472 | tf_op jit(solution)/shard_map/pack/pallas_call | solution.py:681
  16.9 2.2 %all-to-all-done.gathered = f32[8,48,128]{2,1,0:T(8,128)S(1)} async-done(((f32[8,48,128]{2,1,0:T(8,128)}), f32[8,48,128]{2,1,0:T(8,128)S(1)}, u32[]{:S(2)}, u32[]{:S(2)}) %all-to-all-start) | async-done | bytes 196640 | tf_op jit(solution)/shard_map/all_to_all | solution.py:829
  19.1 3.1 %collective-permute-start.2 = (f32[9,128,128]{2,1,0:T(8,128)S(1)}, f32[9,128,128]{2,1,0:T(8,128)S(1)}, u32[]{:S(2)}, u32[]{:S(2)}) collective-permute-start(f32[9,128,128]{2,1,0:T(8,128)S(1)} %get-tuple-element.31), channel_id=1, source_target_pairs={{0,4},{4,8},{8,12},{12,16},{16,20},{20,24},{24,28},{1,5},{5,9},{9,... | collective-permute-start | bytes 1769480 | tf_op jit(solution)/shard_map/ppermute | solution.py:809
  22.2 2.2 %collective-permute-start.3 = (f32[9,128,128]{2,1,0:T(8,128)S(1)}, f32[9,128,128]{2,1,0:T(8,128)S(1)}, u32[]{:S(2)}, u32[]{:S(2)}) collective-permute-start(f32[9,128,128]{2,1,0:T(8,128)S(1)} %get-tuple-element.32), channel_id=1, source_target_pairs={{4,0},{8,4},{12,8},{16,12},{20,16},{24,20},{28,24},{5,1},{9,5},{13... | collective-permute-start | bytes 1769480 | tf_op jit(solution)/shard_map/ppermute | solution.py:809
  24.5 1.3 %settle.1 = (f32[1,128]{1,0:T(1,128)}, f32[16,8,128]{2,1,0:T(8,128)S(1)}, f32[9,32,128]{2,1,0:T(8,128)S(1)}, f32[9,32,128]{2,1,0:T(8,128)S(1)}) custom-call(s32[1]{0:T(128)} %bitcast.2.me, f32[8,48,128]{2,1,0:T(8,128)S(1)} %all-to-all-done.gathered, f32[9,32,128]{2,1,0:T(8,128)S(1)} %get-tuple-element.23.low_in, f32[9,32,128]{2,1,0:T(8,128)S(1)} %get-tuple-element.24.high_in), custom_call_target="tpu_custom_call" | custom-call | flops 1000000 | bytes 1000000 | tf_op jit(solution)/shard_map/settle/pallas_call | solution.py:785
  25.8 6.9 %collective-permute-start = (f32[9,32,128]{2,1,0:T(8,128)S(1)}, f32[9,32,128]{2,1,0:T(8,128)S(1)}, u32[]{:S(2)}, u32[]{:S(2)}) collective-permute-start(f32[9,32,128]{2,1,0:T(8,128)S(1)} %get-tuple-element.25), channel_id=1, source_target_pairs={{0,1},{1,2},{2,3},{4,5},{5,6},{6,7},{8,9},{9,10},{10,11},{12,13},{... | collective-permute-start | bytes 442376 | tf_op jit(solution)/shard_map/ppermute | solution.py:809
  32.7 1.9 %collective-permute-start.1 = (f32[9,32,128]{2,1,0:T(8,128)S(1)}, f32[9,32,128]{2,1,0:T(8,128)S(1)}, u32[]{:S(2)}, u32[]{:S(2)}) collective-permute-start(f32[9,32,128]{2,1,0:T(8,128)S(1)} %get-tuple-element.26), channel_id=1, source_target_pairs={{1,0},{2,1},{3,2},{5,4},{6,5},{7,6},{9,8},{10,9},{11,10},{13,12},{... | collective-permute-start | bytes 442376 | tf_op jit(solution)/shard_map/ppermute | solution.py:809
  34.6 4.4 %face_speeds.1 = (f32[32,16,8,128]{3,2,1,0:T(8,128)S(1)}, f32[32,16,8,128]{3,2,1,0:T(8,128)S(1)}) custom-call(f32[3,32,8,16,128]{4,3,2,1,0:T(8,128)} %bitcast.16), custom_call_target="tpu_custom_call" | custom-call | flops 4194304 | bytes 6291456 | tf_op jit(solution)/shard_map/face_speeds/pallas_call | solution.py:571
  39.1 0.0 copy-start
  39.1 0.0 collective-permute-done.refs_4_.refs_6_.refs_8_.refs_10_.refs_12_
  39.1 0.4 collective-permute-done.1.refs_5_.refs_7_.refs_9_.refs_11_.refs_13_
  39.5 17.2 %interior.2 = (f32[4,32,16,8,128]{4,3,2,1,0:T(8,128)}, f32[8,32,128]{2,1,0:T(8,128)S(1)}, f32[8,32,128]{2,1,0:T(8,128)S(1)}) custom-call(f32[4,32,8,16,128]{4,3,2,1,0:T(8,128)} %bitcast.21, f32[3,32,8,16,128]{4,3,2,1,0:T(8,128)} %bitcast.17, f32[32,16,8,128]{3,2,1,0:T(8,128)S(1)} %get-tuple-element.21.refs_2_.refs_4_.refs_6_, ...), custom_call_target="tpu_custom_call" | custom-call | flops 73400320 | bytes 23068672 | tf_op jit(solution)/shard_map/interior/pallas_call | solution.py:379
  56.7 0.0 copy-done
  56.7 0.0 collective-permute-done.2
  56.7 0.0 collective-permute-done.3
  56.7 0.0 copy-start.1
  56.7 5.4 %boundary.2 = (f32[4,2,16,8,128]{4,3,2,1,0:T(8,128)S(1)}, f32[4,2,16,8,128]{4,3,2,1,0:T(8,128)S(1)}, f32[8,32,128]{2,1,0:T(8,128)S(1)}, f32[8,32,128]{2,1,0:T(8,128)S(1)}) custom-call(f32[4,32,8,16,128]{4,3,2,1,0:T(8,128)} %bitcast.22, f32[9,8,16,128]{3,2,1,0:T(8,128)S(1)} %bitcast.8, f32[9,8,16,128]{3,2,1,0:T(8,128)S(1)} %bitcast.11, ...), custom_call_target="tpu_custom_call" | custom-call | flops 13107200 | bytes 6291456 | tf_op jit(solution)/shard_map/boundary/pallas_call | solution.py:527
  62.1 1.9 %collective-permute-start.5 = (f32[4,2,16,8,128]{4,3,2,1,0:T(8,128)S(1)}, f32[4,2,16,8,128]{4,3,2,1,0:T(8,128)S(1)}, u32[]{:S(2)}, u32[]{:S(2)}) collective-permute-start(f32[4,2,16,8,128]{4,3,2,1,0:T(8,128)S(1)} %get-tuple-element.35.refs_1_), channel_id=1, source_target_pairs={{4,0},{8,4},{12,8},{16,12},{20,16},{24,20},{28,24},{5,1},{9,5},{13... | collective-permute-start | bytes 1572872 | tf_op jit(solution)/shard_map/ppermute | solution.py:809
  64.0 4.3 %collective-permute-start.4 = (f32[4,2,16,8,128]{4,3,2,1,0:T(8,128)S(1)}, f32[4,2,16,8,128]{4,3,2,1,0:T(8,128)S(1)}, u32[]{:S(2)}, u32[]{:S(2)}) collective-permute-start(f32[4,2,16,8,128]{4,3,2,1,0:T(8,128)S(1)} %get-tuple-element.36.refs_2_), channel_id=1, source_target_pairs={{0,4},{4,8},{8,12},{12,16},{16,20},{20,24},{24,28},{1,5},{5,9},{9,... | collective-permute-start | bytes 1572872 | tf_op jit(solution)/shard_map/ppermute | solution.py:809
  68.3 4.2 %collective-permute-start.6 = (f32[8,32,128]{2,1,0:T(8,128)S(1)}, f32[8,32,128]{2,1,0:T(8,128)S(1)}, u32[]{:S(2)}, u32[]{:S(2)}) collective-permute-start(f32[8,32,128]{2,1,0:T(8,128)S(1)} %get-tuple-element.37), channel_id=1, source_target_pairs={{0,1},{1,2},{2,3},{4,5},{5,6},{6,7},{8,9},{9,10},{10,11},{12,13},{... | collective-permute-start | bytes 393224 | tf_op jit(solution)/shard_map/ppermute | solution.py:809
  72.5 1.9 %collective-permute-start.7 = (f32[8,32,128]{2,1,0:T(8,128)S(1)}, f32[8,32,128]{2,1,0:T(8,128)S(1)}, u32[]{:S(2)}, u32[]{:S(2)}) collective-permute-start(f32[8,32,128]{2,1,0:T(8,128)S(1)} %get-tuple-element.38), channel_id=1, source_target_pairs={{1,0},{2,1},{3,2},{5,4},{6,5},{7,6},{9,8},{10,9},{11,10},{13,12},{... | collective-permute-start | bytes 393224 | tf_op jit(solution)/shard_map/ppermute | solution.py:809
  74.5 0.0 collective-permute-done.6.refs_6_.refs_10_
  74.5 4.6 %collective-permute-done.7.refs_7_.refs_11_ = f32[8,32,128]{2,1,0:T(8,128)S(1)} collective-permute-done((f32[8,32,128]{2,1,0:T(8,128)S(1)}, f32[8,32,128]{2,1,0:T(8,128)S(1)}, u32[]{:S(2)}, u32[]{:S(2)}) %collective-permute-start.7) | collective-permute-done | bytes 131104 | tf_op jit(solution)/shard_map/ppermute | solution.py:809
  79.1 0.0 copy-done.1
  79.1 17.5 %interior.3.refs_14_ = f32[4,32,8,16,128]{4,3,2,1,0:T(8,128)} custom-call(f32[4,32,16,8,128]{4,3,2,1,0:T(8,128)} %get-tuple-element.28.refs_0_, f32[4,2,16,8,128]{4,3,2,1,0:T(8,128)S(1)} %get-tuple-element.35.refs_1_, f32[4,2,16,8,128]{4,3,2,1,0:T(8,128)S(1)} %get-tuple-element.36.refs_2_, f32[3,32,8,16,128]{4,3,2,1,0:T(8,128)} %bitcast.19, ...), custom_call_target="tpu_custom_call" | custom-call | flops 73400320 | bytes 23068672 | tf_op jit(solution)/shard_map/interior/pallas_call | solution.py:379
  96.6 0.0 collective-permute-done.5.refs_4_
  96.6 0.0 collective-permute-done.4.refs_3_
  96.6 4.7 %boundary.3 = f32[4,32,8,16,128]{4,3,2,1,0:T(8,128)} custom-call(f32[4,32,16,8,128]{4,3,2,1,0:T(8,128)} %get-tuple-element.28.refs_0_, f32[4,2,16,8,128]{4,3,2,1,0:T(8,128)S(1)} %get-tuple-element.35.refs_1_, f32[4,2,16,8,128]{4,3,2,1,0:T(8,128)S(1)} %get-tuple-element.36.refs_2_, ...), custom_call_target="tpu_custom_call", output_to_operand_aliasing={{}: (14, {})} | custom-call | flops 13107200 | bytes 6291456 | tf_op jit(solution)/shard_map/boundary/pallas_call | solution.py:527
Async XLA Ops:
  4.2 0.7 copy-start.2
  4.9 0.7 copy-start.3
  5.6 0.7 copy-start.4
  6.2 0.7 copy-start.5
  6.9 0.7 copy-start.6
  8.4 10.7 %all-to-all-start = ((f32[8,48,128]{2,1,0:T(8,128)}), f32[8,48,128]{2,1,0:T(8,128)S(1)}, u32[]{:S(2)}, u32[]{:S(2)}) async-start(f32[8,48,128]{2,1,0:T(8,128)} %census.1), calls=%async_computation | async-start | bytes 393216 | tf_op jit(solution)/shard_map/all_to_all | solution.py:829
  19.1 37.6 %collective-permute-start.2 = (f32[9,128,128]{2,1,0:T(8,128)S(1)}, f32[9,128,128]{2,1,0:T(8,128)S(1)}, u32[]{:S(2)}, u32[]{:S(2)}) collective-permute-start(f32[9,128,128]{2,1,0:T(8,128)S(1)} %get-tuple-element.31), channel_id=1, source_target_pairs={{0,4},{4,8},{8,12},{12,16},{16,20},{20,24},{24,28},{1,5},{5,9},{9,... | collective-permute-start | bytes 1769480 | tf_op jit(solution)/shard_map/ppermute | solution.py:809
  22.2 34.5 %collective-permute-start.3 = (f32[9,128,128]{2,1,0:T(8,128)S(1)}, f32[9,128,128]{2,1,0:T(8,128)S(1)}, u32[]{:S(2)}, u32[]{:S(2)}) collective-permute-start(f32[9,128,128]{2,1,0:T(8,128)S(1)} %get-tuple-element.32), channel_id=1, source_target_pairs={{4,0},{8,4},{12,8},{16,12},{20,16},{24,20},{28,24},{5,1},{9,5},{13... | collective-permute-start | bytes 1769480 | tf_op jit(solution)/shard_map/ppermute | solution.py:809
  25.8 13.3 %collective-permute-start = (f32[9,32,128]{2,1,0:T(8,128)S(1)}, f32[9,32,128]{2,1,0:T(8,128)S(1)}, u32[]{:S(2)}, u32[]{:S(2)}) collective-permute-start(f32[9,32,128]{2,1,0:T(8,128)S(1)} %get-tuple-element.25), channel_id=1, source_target_pairs={{0,1},{1,2},{2,3},{4,5},{5,6},{6,7},{8,9},{9,10},{10,11},{12,13},{... | collective-permute-start | bytes 442376 | tf_op jit(solution)/shard_map/ppermute | solution.py:809
  32.7 6.8 %collective-permute-start.1 = (f32[9,32,128]{2,1,0:T(8,128)S(1)}, f32[9,32,128]{2,1,0:T(8,128)S(1)}, u32[]{:S(2)}, u32[]{:S(2)}) collective-permute-start(f32[9,32,128]{2,1,0:T(8,128)S(1)} %get-tuple-element.26), channel_id=1, source_target_pairs={{1,0},{2,1},{3,2},{5,4},{6,5},{7,6},{9,8},{10,9},{11,10},{13,12},{... | collective-permute-start | bytes 442376 | tf_op jit(solution)/shard_map/ppermute | solution.py:809
  39.1 17.6 %copy-start = (f32[32,16,8,128]{3,2,1,0:T(8,128)}, f32[32,16,8,128]{3,2,1,0:T(8,128)S(1)}, u32[]{:S(2)}) copy-start(f32[32,16,8,128]{3,2,1,0:T(8,128)S(1)} %get-tuple-element.22.refs_3_.refs_5_.refs_7_) | copy-start | bytes 6291460
  56.7 22.4 %copy-start.1 = (f32[32,16,8,128]{3,2,1,0:T(8,128)S(1)}, f32[32,16,8,128]{3,2,1,0:T(8,128)}, u32[]{:S(2)}) copy-start(f32[32,16,8,128]{3,2,1,0:T(8,128)} %copy-done) | copy-start | bytes 6291460
  62.1 34.5 %collective-permute-start.5 = (f32[4,2,16,8,128]{4,3,2,1,0:T(8,128)S(1)}, f32[4,2,16,8,128]{4,3,2,1,0:T(8,128)S(1)}, u32[]{:S(2)}, u32[]{:S(2)}) collective-permute-start(f32[4,2,16,8,128]{4,3,2,1,0:T(8,128)S(1)} %get-tuple-element.35.refs_1_), channel_id=1, source_target_pairs={{4,0},{8,4},{12,8},{16,12},{20,16},{24,20},{28,24},{5,1},{9,5},{13... | collective-permute-start | bytes 1572872 | tf_op jit(solution)/shard_map/ppermute | solution.py:809
  64.0 32.6 %collective-permute-start.4 = (f32[4,2,16,8,128]{4,3,2,1,0:T(8,128)S(1)}, f32[4,2,16,8,128]{4,3,2,1,0:T(8,128)S(1)}, u32[]{:S(2)}, u32[]{:S(2)}) collective-permute-start(f32[4,2,16,8,128]{4,3,2,1,0:T(8,128)S(1)} %get-tuple-element.36.refs_2_), channel_id=1, source_target_pairs={{0,4},{4,8},{8,12},{12,16},{16,20},{20,24},{24,28},{1,5},{5,9},{9,... | collective-permute-start | bytes 1572872 | tf_op jit(solution)/shard_map/ppermute | solution.py:809
  68.3 6.2 %collective-permute-start.6 = (f32[8,32,128]{2,1,0:T(8,128)S(1)}, f32[8,32,128]{2,1,0:T(8,128)S(1)}, u32[]{:S(2)}, u32[]{:S(2)}) collective-permute-start(f32[8,32,128]{2,1,0:T(8,128)S(1)} %get-tuple-element.37), channel_id=1, source_target_pairs={{0,1},{1,2},{2,3},{4,5},{5,6},{6,7},{8,9},{9,10},{10,11},{12,13},{... | collective-permute-start | bytes 393224 | tf_op jit(solution)/shard_map/ppermute | solution.py:809
  72.5 6.6 %collective-permute-start.7 = (f32[8,32,128]{2,1,0:T(8,128)S(1)}, f32[8,32,128]{2,1,0:T(8,128)S(1)}, u32[]{:S(2)}, u32[]{:S(2)}) collective-permute-start(f32[8,32,128]{2,1,0:T(8,128)S(1)} %get-tuple-element.38), channel_id=1, source_target_pairs={{1,0},{2,1},{3,2},{5,4},{6,5},{7,6},{9,8},{10,9},{11,10},{13,12},{... | collective-permute-start | bytes 393224 | tf_op jit(solution)/shard_map/ppermute | solution.py:809

commit v8 on v7

--- a/solution.py
+++ b/solution.py
@@ -136,7 +136,7 @@
     staged([functools.partial(job, range(t, t + PAIR)) for t in range(0, f.tiles, PAIR)])
 
 
-def slab_step(f, k, put, group_size=8):
+def slab_step(f, k, put, group_size=4):
     slab = k + 2
     lane = lax.broadcasted_iota(jnp.int32, (8, f.lanes), 1)
     top = f.lanes - 1
@@ -334,7 +334,7 @@
         def put(c, t, value):
             stage[c, k, t] = value
 
-        slab_step(f, k, put, 16 if last else 4)
+        slab_step(f, k, put, 4 if last else 2)
         if last:
             start_sets([(lambda n: stage.at[:, k, :, n], lambda n: out.at[:, k + 2, n])], out_sem)
         else:
@@ -643,7 +643,7 @@
         out_specs=pl.BlockSpec((slabs, lanes), lambda i: (0, 0)),
         scratch_shapes=[pltpu.VMEM((rows, lanes), jnp.float32)],
         compiler_params=params(),
-        cost_estimate=cost(10 * slabs * rows * lanes, 8 * slabs * rows * lanes),
+        cost_estimate=cost(10 * slabs * rows * lanes, 80 * slabs * rows * lanes),
         name="tile_stress",
     )(velocity)
 

time: 102 us -> 101 us (level)
  transfers between devices with their start and end apart: 9 -> 9, of which waited for: 3 -> 3; matrix products, arithmetic and copies ran while one was open for 0% -> 0% of each run, Pallas kernels for 43% -> 42%
where the time goes in v8:
time: 101 us
  Pallas kernels  57 us (56%)
  starting transfers between devices  32.2 us (32%)
  waiting for transfers between devices  7.27 us (7%)
  local copies, waits for them, and re-layouts  3.34 us (3%)
    pallas_call x2, Pallas kernels, interior(): pl.pallas_call(functools.partial(interior_kernel, last, groups, len(field...  34.1 us
    ppermute x4, starting transfers between devices, exchange(): lax.ppermute(high, axis, forward)  18.5 us
    pallas_call x2, Pallas kernels, boundary(): pl.pallas_call(functools.partial(boundary_kernel, last, groups, slabs), o...  9.98 us
    ppermute x4, starting transfers between devices, exchange(): lax.ppermute(low, axis, backward)  7.99 us
    all_to_all x1, starting transfers between devices, shards(): lax.all_to_all(copies, 'gx', split_axis=0, concat_axis=0, tiled=True)  5.78 us
    ppermute x4, waiting for transfers between devices, exchange(): lax.ppermute(low, axis, backward)  5.01 us
    pallas_call x1, Pallas kernels, face_speeds(): pl.pallas_call(speeds_kernel, grid=(slabs // part,), out_shape=(jax.Shape...  4.44 us
    pallas_call x1, Pallas kernels, tile_stress(): pl.pallas_call(stress_kernel, grid=(slabs // part,), out_shape=jax.ShapeD...  3.55 us
  transfers between devices with their start and end apart: 9, of which 3 were waited for; matrix products, arithmetic and copies ran while one was open for 0% of the time, Pallas kernels for 42%

profile of v8, /device:TPU:3, one launch (start us, length us, event | category | flops | bytes accessed | tf_op | source)
XLA Modules:
  0.0 100.6 jit_solution(1218228338488256124)
XLA Ops:
  0.6 3.5 %tile_stress.1.stress = f32[32,128]{1,0:T(8,128)S(1)} custom-call(f32[3,32,128,128]{3,2,1,0:T(8,128)} %velocity.1), custom_call_target="tpu_custom_call" | custom-call | flops 5242880 | bytes 41943040 | tf_op jit(solution)/shard_map/tile_stress/pallas_call | solution.py:638
  4.2 0.0 copy-start.2
  4.2 0.7 copy-done.2
  4.9 0.0 copy-start.3
  4.9 0.7 copy-done.3
  5.6 0.0 copy-start.4
  5.6 0.7 copy-done.4
  6.2 0.0 copy-start.5
  6.2 0.7 copy-done.5
  6.9 0.0 copy-start.6
  6.9 0.7 copy-done.6
  7.5 0.9 census.1
  8.4 5.8 %all-to-all-start = ((f32[8,48,128]{2,1,0:T(8,128)}), f32[8,48,128]{2,1,0:T(8,128)S(1)}, u32[]{:S(2)}, u32[]{:S(2)}) async-start(f32[8,48,128]{2,1,0:T(8,128)} %census.1), calls=%async_computation | async-start | bytes 393216 | tf_op jit(solution)/shard_map/all_to_all | solution.py:829
  14.2 2.7 %pack.1 = (f32[9,32,128]{2,1,0:T(8,128)S(1)}, f32[9,32,128]{2,1,0:T(8,128)S(1)}, f32[9,128,128]{2,1,0:T(8,128)S(1)}, f32[9,128,128]{2,1,0:T(8,128)S(1)}) custom-call(f32[4,32,128,128]{3,2,1,0:T(8,128)} %state.1, f32[4,32,128,128]{3,2,1,0:T(8,128)} %state.1, f32[3,32,128,128]{3,2,1,0:T(8,128)} %velocity.1, f32[3,32,128,128]{3,2,1,0:T(8,128)} %velocity.1, ...), custom_call_target="tpu_custom_call" | custom-call | flops 1 | bytes 1769472 | tf_op jit(solution)/shard_map/pack/pallas_call | solution.py:681
  16.9 2.2 %all-to-all-done.gathered = f32[8,48,128]{2,1,0:T(8,128)S(1)} async-done(((f32[8,48,128]{2,1,0:T(8,128)}), f32[8,48,128]{2,1,0:T(8,128)S(1)}, u32[]{:S(2)}, u32[]{:S(2)}) %all-to-all-start) | async-done | bytes 196640 | tf_op jit(solution)/shard_map/all_to_all | solution.py:829
  19.1 3.1 %collective-permute-start.2 = (f32[9,128,128]{2,1,0:T(8,128)S(1)}, f32[9,128,128]{2,1,0:T(8,128)S(1)}, u32[]{:S(2)}, u32[]{:S(2)}) collective-permute-start(f32[9,128,128]{2,1,0:T(8,128)S(1)} %get-tuple-element.31), channel_id=1, source_target_pairs={{0,4},{4,8},{8,12},{12,16},{16,20},{20,24},{24,28},{1,5},{5,9},{9,... | collective-permute-start | bytes 1769480 | tf_op jit(solution)/shard_map/ppermute | solution.py:809
  22.2 2.2 %collective-permute-start.3 = (f32[9,128,128]{2,1,0:T(8,128)S(1)}, f32[9,128,128]{2,1,0:T(8,128)S(1)}, u32[]{:S(2)}, u32[]{:S(2)}) collective-permute-start(f32[9,128,128]{2,1,0:T(8,128)S(1)} %get-tuple-element.32), channel_id=1, source_target_pairs={{4,0},{8,4},{12,8},{16,12},{20,16},{24,20},{28,24},{5,1},{9,5},{13... | collective-permute-start | bytes 1769480 | tf_op jit(solution)/shard_map/ppermute | solution.py:809
  24.5 1.3 %settle.1 = (f32[1,128]{1,0:T(1,128)}, f32[16,8,128]{2,1,0:T(8,128)S(1)}, f32[9,32,128]{2,1,0:T(8,128)S(1)}, f32[9,32,128]{2,1,0:T(8,128)S(1)}) custom-call(s32[1]{0:T(128)} %bitcast.2.me, f32[8,48,128]{2,1,0:T(8,128)S(1)} %all-to-all-done.gathered, f32[9,32,128]{2,1,0:T(8,128)S(1)} %get-tuple-element.23.low_in, f32[9,32,128]{2,1,0:T(8,128)S(1)} %get-tuple-element.24.high_in), custom_call_target="tpu_custom_call" | custom-call | flops 1000000 | bytes 1000000 | tf_op jit(solution)/shard_map/settle/pallas_call | solution.py:785
  25.8 6.9 %collective-permute-start = (f32[9,32,128]{2,1,0:T(8,128)S(1)}, f32[9,32,128]{2,1,0:T(8,128)S(1)}, u32[]{:S(2)}, u32[]{:S(2)}) collective-permute-start(f32[9,32,128]{2,1,0:T(8,128)S(1)} %get-tuple-element.25), channel_id=1, source_target_pairs={{0,1},{1,2},{2,3},{4,5},{5,6},{6,7},{8,9},{9,10},{10,11},{12,13},{... | collective-permute-start | bytes 442376 | tf_op jit(solution)/shard_map/ppermute | solution.py:809
  32.7 1.9 %collective-permute-start.1 = (f32[9,32,128]{2,1,0:T(8,128)S(1)}, f32[9,32,128]{2,1,0:T(8,128)S(1)}, u32[]{:S(2)}, u32[]{:S(2)}) collective-permute-start(f32[9,32,128]{2,1,0:T(8,128)S(1)} %get-tuple-element.26), channel_id=1, source_target_pairs={{1,0},{2,1},{3,2},{5,4},{6,5},{7,6},{9,8},{10,9},{11,10},{13,12},{... | collective-permute-start | bytes 442376 | tf_op jit(solution)/shard_map/ppermute | solution.py:809
  34.6 4.4 %face_speeds.1 = (f32[32,16,8,128]{3,2,1,0:T(8,128)S(1)}, f32[32,16,8,128]{3,2,1,0:T(8,128)S(1)}) custom-call(f32[3,32,8,16,128]{4,3,2,1,0:T(8,128)} %bitcast.16), custom_call_target="tpu_custom_call" | custom-call | flops 4194304 | bytes 6291456 | tf_op jit(solution)/shard_map/face_speeds/pallas_call | solution.py:571
  39.1 0.0 copy-start
  39.1 0.0 collective-permute-done.refs_4_.refs_6_.refs_8_.refs_10_.refs_12_
  39.1 0.4 collective-permute-done.1.refs_5_.refs_7_.refs_9_.refs_11_.refs_13_
  39.5 17.6 %interior.2 = (f32[4,32,16,8,128]{4,3,2,1,0:T(8,128)}, f32[8,32,128]{2,1,0:T(8,128)S(1)}, f32[8,32,128]{2,1,0:T(8,128)S(1)}) custom-call(f32[4,32,8,16,128]{4,3,2,1,0:T(8,128)} %bitcast.21, f32[3,32,8,16,128]{4,3,2,1,0:T(8,128)} %bitcast.17, f32[32,16,8,128]{3,2,1,0:T(8,128)S(1)} %get-tuple-element.21.refs_2_.refs_4_.refs_6_, ...), custom_call_target="tpu_custom_call" | custom-call | flops 73400320 | bytes 23068672 | tf_op jit(solution)/shard_map/interior/pallas_call | solution.py:379
  57.1 0.0 copy-done
  57.1 0.0 collective-permute-done.2
  57.1 0.0 collective-permute-done.3
  57.1 0.0 copy-start.1
  57.1 5.3 %boundary.2 = (f32[4,2,16,8,128]{4,3,2,1,0:T(8,128)S(1)}, f32[4,2,16,8,128]{4,3,2,1,0:T(8,128)S(1)}, f32[8,32,128]{2,1,0:T(8,128)S(1)}, f32[8,32,128]{2,1,0:T(8,128)S(1)}) custom-call(f32[4,32,8,16,128]{4,3,2,1,0:T(8,128)} %bitcast.22, f32[9,8,16,128]{3,2,1,0:T(8,128)S(1)} %bitcast.8, f32[9,8,16,128]{3,2,1,0:T(8,128)S(1)} %bitcast.11, ...), custom_call_target="tpu_custom_call" | custom-call | flops 13107200 | bytes 6291456 | tf_op jit(solution)/shard_map/boundary/pallas_call | solution.py:527
  62.4 1.9 %collective-permute-start.5 = (f32[4,2,16,8,128]{4,3,2,1,0:T(8,128)S(1)}, f32[4,2,16,8,128]{4,3,2,1,0:T(8,128)S(1)}, u32[]{:S(2)}, u32[]{:S(2)}) collective-permute-start(f32[4,2,16,8,128]{4,3,2,1,0:T(8,128)S(1)} %get-tuple-element.35.refs_1_), channel_id=1, source_target_pairs={{4,0},{8,4},{12,8},{16,12},{20,16},{24,20},{28,24},{5,1},{9,5},{13... | collective-permute-start | bytes 1572872 | tf_op jit(solution)/shard_map/ppermute | solution.py:809
  64.3 4.3 %collective-permute-start.4 = (f32[4,2,16,8,128]{4,3,2,1,0:T(8,128)S(1)}, f32[4,2,16,8,128]{4,3,2,1,0:T(8,128)S(1)}, u32[]{:S(2)}, u32[]{:S(2)}) collective-permute-start(f32[4,2,16,8,128]{4,3,2,1,0:T(8,128)S(1)} %get-tuple-element.36.refs_2_), channel_id=1, source_target_pairs={{0,4},{4,8},{8,12},{12,16},{16,20},{20,24},{24,28},{1,5},{5,9},{9,... | collective-permute-start | bytes 1572872 | tf_op jit(solution)/shard_map/ppermute | solution.py:809
  68.6 4.2 %collective-permute-start.6 = (f32[8,32,128]{2,1,0:T(8,128)S(1)}, f32[8,32,128]{2,1,0:T(8,128)S(1)}, u32[]{:S(2)}, u32[]{:S(2)}) collective-permute-start(f32[8,32,128]{2,1,0:T(8,128)S(1)} %get-tuple-element.37), channel_id=1, source_target_pairs={{0,1},{1,2},{2,3},{4,5},{5,6},{6,7},{8,9},{9,10},{10,11},{12,13},{... | collective-permute-start | bytes 393224 | tf_op jit(solution)/shard_map/ppermute | solution.py:809
  72.8 1.9 %collective-permute-start.7 = (f32[8,32,128]{2,1,0:T(8,128)S(1)}, f32[8,32,128]{2,1,0:T(8,128)S(1)}, u32[]{:S(2)}, u32[]{:S(2)}) collective-permute-start(f32[8,32,128]{2,1,0:T(8,128)S(1)} %get-tuple-element.38), channel_id=1, source_target_pairs={{1,0},{2,1},{3,2},{5,4},{6,5},{7,6},{9,8},{10,9},{11,10},{13,12},{... | collective-permute-start | bytes 393224 | tf_op jit(solution)/shard_map/ppermute | solution.py:809
  74.8 0.0 collective-permute-done.6.refs_6_.refs_10_
  74.8 4.6 %collective-permute-done.7.refs_7_.refs_11_ = f32[8,32,128]{2,1,0:T(8,128)S(1)} collective-permute-done((f32[8,32,128]{2,1,0:T(8,128)S(1)}, f32[8,32,128]{2,1,0:T(8,128)S(1)}, u32[]{:S(2)}, u32[]{:S(2)}) %collective-permute-start.7) | collective-permute-done | bytes 131104 | tf_op jit(solution)/shard_map/ppermute | solution.py:809
  79.4 0.0 copy-done.1
  79.4 16.5 %interior.3.refs_14_ = f32[4,32,8,16,128]{4,3,2,1,0:T(8,128)} custom-call(f32[4,32,16,8,128]{4,3,2,1,0:T(8,128)} %get-tuple-element.28.refs_0_, f32[4,2,16,8,128]{4,3,2,1,0:T(8,128)S(1)} %get-tuple-element.35.refs_1_, f32[4,2,16,8,128]{4,3,2,1,0:T(8,128)S(1)} %get-tuple-element.36.refs_2_, f32[3,32,8,16,128]{4,3,2,1,0:T(8,128)} %bitcast.19, ...), custom_call_target="tpu_custom_call" | custom-call | flops 73400320 | bytes 23068672 | tf_op jit(solution)/shard_map/interior/pallas_call | solution.py:379
  95.9 0.0 collective-permute-done.5.refs_4_
  95.9 0.0 collective-permute-done.4.refs_3_
  95.9 4.7 %boundary.3 = f32[4,32,8,16,128]{4,3,2,1,0:T(8,128)} custom-call(f32[4,32,16,8,128]{4,3,2,1,0:T(8,128)} %get-tuple-element.28.refs_0_, f32[4,2,16,8,128]{4,3,2,1,0:T(8,128)S(1)} %get-tuple-element.35.refs_1_, f32[4,2,16,8,128]{4,3,2,1,0:T(8,128)S(1)} %get-tuple-element.36.refs_2_, ...), custom_call_target="tpu_custom_call", output_to_operand_aliasing={{}: (14, {})} | custom-call | flops 13107200 | bytes 6291456 | tf_op jit(solution)/shard_map/boundary/pallas_call | solution.py:527
Async XLA Ops:
  4.2 0.7 copy-start.2
  4.9 0.7 copy-start.3
  5.6 0.7 copy-start.4
  6.2 0.7 copy-start.5
  6.9 0.7 copy-start.6
  8.4 10.7 %all-to-all-start = ((f32[8,48,128]{2,1,0:T(8,128)}), f32[8,48,128]{2,1,0:T(8,128)S(1)}, u32[]{:S(2)}, u32[]{:S(2)}) async-start(f32[8,48,128]{2,1,0:T(8,128)} %census.1), calls=%async_computation | async-start | bytes 393216 | tf_op jit(solution)/shard_map/all_to_all | solution.py:829
  19.1 37.9 %collective-permute-start.2 = (f32[9,128,128]{2,1,0:T(8,128)S(1)}, f32[9,128,128]{2,1,0:T(8,128)S(1)}, u32[]{:S(2)}, u32[]{:S(2)}) collective-permute-start(f32[9,128,128]{2,1,0:T(8,128)S(1)} %get-tuple-element.31), channel_id=1, source_target_pairs={{0,4},{4,8},{8,12},{12,16},{16,20},{20,24},{24,28},{1,5},{5,9},{9,... | collective-permute-start | bytes 1769480 | tf_op jit(solution)/shard_map/ppermute | solution.py:809
  22.2 34.9 %collective-permute-start.3 = (f32[9,128,128]{2,1,0:T(8,128)S(1)}, f32[9,128,128]{2,1,0:T(8,128)S(1)}, u32[]{:S(2)}, u32[]{:S(2)}) collective-permute-start(f32[9,128,128]{2,1,0:T(8,128)S(1)} %get-tuple-element.32), channel_id=1, source_target_pairs={{4,0},{8,4},{12,8},{16,12},{20,16},{24,20},{28,24},{5,1},{9,5},{13... | collective-permute-start | bytes 1769480 | tf_op jit(solution)/shard_map/ppermute | solution.py:809
  25.8 13.3 %collective-permute-start = (f32[9,32,128]{2,1,0:T(8,128)S(1)}, f32[9,32,128]{2,1,0:T(8,128)S(1)}, u32[]{:S(2)}, u32[]{:S(2)}) collective-permute-start(f32[9,32,128]{2,1,0:T(8,128)S(1)} %get-tuple-element.25), channel_id=1, source_target_pairs={{0,1},{1,2},{2,3},{4,5},{5,6},{6,7},{8,9},{9,10},{10,11},{12,13},{... | collective-permute-start | bytes 442376 | tf_op jit(solution)/shard_map/ppermute | solution.py:809
  32.7 6.8 %collective-permute-start.1 = (f32[9,32,128]{2,1,0:T(8,128)S(1)}, f32[9,32,128]{2,1,0:T(8,128)S(1)}, u32[]{:S(2)}, u32[]{:S(2)}) collective-permute-start(f32[9,32,128]{2,1,0:T(8,128)S(1)} %get-tuple-element.26), channel_id=1, source_target_pairs={{1,0},{2,1},{3,2},{5,4},{6,5},{7,6},{9,8},{10,9},{11,10},{13,12},{... | collective-permute-start | bytes 442376 | tf_op jit(solution)/shard_map/ppermute | solution.py:809
  39.1 18.0 %copy-start = (f32[32,16,8,128]{3,2,1,0:T(8,128)}, f32[32,16,8,128]{3,2,1,0:T(8,128)S(1)}, u32[]{:S(2)}) copy-start(f32[32,16,8,128]{3,2,1,0:T(8,128)S(1)} %get-tuple-element.22.refs_3_.refs_5_.refs_7_) | copy-start | bytes 6291460
  57.1 22.3 %copy-start.1 = (f32[32,16,8,128]{3,2,1,0:T(8,128)S(1)}, f32[32,16,8,128]{3,2,1,0:T(8,128)}, u32[]{:S(2)}) copy-start(f32[32,16,8,128]{3,2,1,0:T(8,128)} %copy-done) | copy-start | bytes 6291460
  62.4 33.5 %collective-permute-start.5 = (f32[4,2,16,8,128]{4,3,2,1,0:T(8,128)S(1)}, f32[4,2,16,8,128]{4,3,2,1,0:T(8,128)S(1)}, u32[]{:S(2)}, u32[]{:S(2)}) collective-permute-start(f32[4,2,16,8,128]{4,3,2,1,0:T(8,128)S(1)} %get-tuple-element.35.refs_1_), channel_id=1, source_target_pairs={{4,0},{8,4},{12,8},{16,12},{20,16},{24,20},{28,24},{5,1},{9,5},{13... | collective-permute-start | bytes 1572872 | tf_op jit(solution)/shard_map/ppermute | solution.py:809
  64.3 31.6 %collective-permute-start.4 = (f32[4,2,16,8,128]{4,3,2,1,0:T(8,128)S(1)}, f32[4,2,16,8,128]{4,3,2,1,0:T(8,128)S(1)}, u32[]{:S(2)}, u32[]{:S(2)}) collective-permute-start(f32[4,2,16,8,128]{4,3,2,1,0:T(8,128)S(1)} %get-tuple-element.36.refs_2_), channel_id=1, source_target_pairs={{0,4},{4,8},{8,12},{12,16},{16,20},{20,24},{24,28},{1,5},{5,9},{9,... | collective-permute-start | bytes 1572872 | tf_op jit(solution)/shard_map/ppermute | solution.py:809
  68.6 6.2 %collective-permute-start.6 = (f32[8,32,128]{2,1,0:T(8,128)S(1)}, f32[8,32,128]{2,1,0:T(8,128)S(1)}, u32[]{:S(2)}, u32[]{:S(2)}) collective-permute-start(f32[8,32,128]{2,1,0:T(8,128)S(1)} %get-tuple-element.37), channel_id=1, source_target_pairs={{0,1},{1,2},{2,3},{4,5},{5,6},{6,7},{8,9},{9,10},{10,11},{12,13},{... | collective-permute-start | bytes 393224 | tf_op jit(solution)/shard_map/ppermute | solution.py:809
  72.8 6.6 %collective-permute-start.7 = (f32[8,32,128]{2,1,0:T(8,128)S(1)}, f32[8,32,128]{2,1,0:T(8,128)S(1)}, u32[]{:S(2)}, u32[]{:S(2)}) collective-permute-start(f32[8,32,128]{2,1,0:T(8,128)S(1)} %get-tuple-element.38), channel_id=1, source_target_pairs={{1,0},{2,1},{3,2},{5,4},{6,5},{7,6},{9,8},{10,9},{11,10},{13,12},{... | collective-permute-start | bytes 393224 | tf_op jit(solution)/shard_map/ppermute | solution.py:809

commit v9 on v8

--- a/solution.py
+++ b/solution.py
@@ -334,7 +334,7 @@
         def put(c, t, value):
             stage[c, k, t] = value
 
-        slab_step(f, k, put, 4 if last else 2)
+        slab_step(f, k, put)
         if last:
             start_sets([(lambda n: stage.at[:, k, :, n], lambda n: out.at[:, k + 2, n])], out_sem)
         else:
@@ -601,10 +601,16 @@
     return jnp.sum(jnp.where(same, row, 0.0), axis=1, keepdims=True)
 
 
-def stress_kernel(wind, stress, gathered):
+def stress_kernel(wind, state, velocity, stress, x_low, x_high, gathered, sems):
     step, steps = pl.program_id(0), pl.num_programs(0)
     part, rows, lanes = wind.shape[1:]
     slabs = stress.shape[0]
+
+    @pl.when(step == 0)
+    def _():
+        for copy in x_copies(state, velocity, x_low, x_high, sems):
+            copy.start()
+
     lane = lax.broadcasted_iota(jnp.int32, (rows, lanes), 1)
     weight = jnp.zeros((rows, lanes), jnp.float32)
     for level, value in enumerate(profile_weights):
@@ -630,32 +636,29 @@
         for level in range(1, LEVELS):
             total = total + gathered[pl.ds(level, slabs, stride=LEVELS), :]
         stress[...] = total
-
-
-def tile_stress(velocity):
-    _, slabs, rows, lanes = velocity.shape
+        for copy in x_copies(state, velocity, x_low, x_high, sems):
+            copy.wait()
+
+
+def tile_stress(state, velocity):
+    comps, slabs, rows, lanes = state.shape
+    x_packed = jax.ShapeDtypeStruct((2 * comps + 1, rows, lanes), jnp.float32)
     part = 8
     return pl.pallas_call(
         stress_kernel,
         grid=(slabs // part,),
-        out_shape=jax.ShapeDtypeStruct((slabs, lanes), jnp.float32),
-        in_specs=[pl.BlockSpec((2, part, rows, lanes), lambda i: (0, i, 0, 0))],
-        out_specs=pl.BlockSpec((slabs, lanes), lambda i: (0, 0)),
-        scratch_shapes=[pltpu.VMEM((rows, lanes), jnp.float32)],
+        out_shape=(jax.ShapeDtypeStruct((slabs, lanes), jnp.float32), x_packed, x_packed),
+        in_specs=[pl.BlockSpec((2, part, rows, lanes), lambda i: (0, i, 0, 0)), ANY, ANY],
+        out_specs=(pl.BlockSpec((slabs, lanes), lambda i: (0, 0)), ANY, ANY),
+        scratch_shapes=[pltpu.VMEM((rows, lanes), jnp.float32), pltpu.SemaphoreType.DMA((2, comps + 1))],
         compiler_params=params(),
-        cost_estimate=cost(10 * slabs * rows * lanes, 80 * slabs * rows * lanes),
+        cost_estimate=cost(10 * slabs * rows * lanes, 8 * slabs * rows * lanes),
         name="tile_stress",
-    )(velocity)
-
-
-def pack_kernel(low_in, high_in, v_low, v_high, state, velocity, low, high, x_low, x_high, sems):
-    step, steps = pl.program_id(0), pl.num_programs(0)
+    )(velocity, state, velocity)
+
+
+def pack_kernel(low_in, high_in, v_low, v_high, low, high):
     comps, part = low_in.shape[:2]
-
-    @pl.when(step == 0)
-    def _():
-        for copy in x_copies(state, velocity, x_low, x_high, sems):
-            copy.start()
 
     for x in range(part):
         for c in range(comps):
@@ -665,11 +668,6 @@
         low[2 * comps, x : x + 1, :] = v_low[0, x, 0:1, :]
         high[2 * comps, x : x + 1, :] = v_high[0, x, 7:8, :]
 
-    @pl.when(step == steps - 1)
-    def _():
-        for copy in x_copies(state, velocity, x_low, x_high, sems):
-            copy.wait()
-
 
 def pack(state, velocity):
     comps, slabs, rows, lanes = state.shape
@@ -677,25 +675,21 @@
     last = rows // 8 - 1
     packed = jax.ShapeDtypeStruct((2 * comps + 1, slabs, lanes), jnp.float32)
     packed_spec = pl.BlockSpec((2 * comps + 1, part, lanes), lambda i: (0, i, 0))
-    x_packed = jax.ShapeDtypeStruct((2 * comps + 1, rows, lanes), jnp.float32)
     return pl.pallas_call(
         pack_kernel,
         grid=(slabs // part,),
-        out_shape=(packed, packed, x_packed, x_packed),
+        out_shape=(packed, packed),
         in_specs=[
             pl.BlockSpec((comps, part, 8, lanes), lambda i: (0, i, 0, 0)),
             pl.BlockSpec((comps, part, 8, lanes), lambda i: (0, i, last, 0)),
             pl.BlockSpec((1, part, 8, lanes), lambda i: (1, i, 0, 0)),
             pl.BlockSpec((1, part, 8, lanes), lambda i: (1, i, last, 0)),
-            ANY,
-            ANY,
         ],
-        out_specs=(packed_spec, packed_spec, ANY, ANY),
-        scratch_shapes=[pltpu.SemaphoreType.DMA((2, comps + 1))],
+        out_specs=(packed_spec, packed_spec),
         compiler_params=params(),
         cost_estimate=cost(1, 12 * (2 * comps + 1) * rows * lanes),
         name="pack",
-    )(state, state, velocity, velocity, state, velocity)
+    )(state, state, velocity, velocity)
 
 
 def census_kernel(stress, threshold, tile_owner, parcel_owner, count, share, copies):
@@ -814,8 +808,8 @@
     slabs = state.shape[1]
     me = lax.axis_index("gx").astype(jnp.int32).reshape(1)
 
-    stress = tile_stress(velocity)
-    low, high, own_low, own_high = pack(state, velocity)
+    stress, own_low, own_high = tile_stress(state, velocity)
+    low, high = pack(state, velocity)
     copies = census(
         groups, stress, threshold, tile_owner[:, :, 0], parcel_owner[:, :, 0], parcel_count, parcel_share
     )

time: 101 us -> 99.2 us (0.982)
  blocking collectives: 0 us -> 10.5 us
  starting transfers between devices: 32.2 us -> 26.4 us
  local copies, waits for them, and re-layouts: 3.34 us -> 0.03 us
  waiting for transfers between devices: 7.27 us -> 5.02 us
  Pallas kernels: 57 us -> 55.8 us
    all_to_all x0 -> x1, blocking collectives: none -> 10.5 us  [shards(): lax.all_to_all(copies, 'gx', split_axis=0, concat_axis=0, tiled=True)]
    all_to_all x1 -> x0, starting transfers between devices: 5.78 us -> none  [shards(): lax.all_to_all(copies, 'gx', split_axis=0, concat_axis=0, tiled=True)]
    unnamed x14, local copies, waits for them, and re-layouts: 3.34 us -> 0.03 us
    all_to_all x1 -> x0, waiting for transfers between devices: 2.24 us -> none  [shards(): lax.all_to_all(copies, 'gx', split_axis=0, concat_axis=0, tiled=True)]
  transfers between devices with their start and end apart: 9 -> 8, of which waited for: 3 -> 2; matrix products, arithmetic and copies ran while one was open for 0% -> 0% of each run, Pallas kernels for 42% -> 42%
where the time goes in v9:
time: 99.2 us; the launch traced here: 98.7 us
  Pallas kernels  55.8 us (56%)
  starting transfers between devices  26.4 us (27%)
  blocking collectives  10.5 us (11%)
  waiting for transfers between devices  5.02 us (5%)
    pallas_call x2, Pallas kernels, interior(): pl.pallas_call(functools.partial(interior_kernel, last, groups, len(field...  33.7 us
    ppermute x4, starting transfers between devices, exchange(): lax.ppermute(high, axis, forward)  18.5 us
    all_to_all x1, blocking collectives, shards(): lax.all_to_all(copies, 'gx', split_axis=0, concat_axis=0, tiled=True)  10.5 us
    pallas_call x2, Pallas kernels, boundary(): pl.pallas_call(functools.partial(boundary_kernel, last, groups, slabs), o...  9.98 us
    ppermute x4, starting transfers between devices, exchange(): lax.ppermute(low, axis, backward)  7.99 us
    ppermute x4, waiting for transfers between devices, exchange(): lax.ppermute(low, axis, backward)  5.01 us
    pallas_call x1, Pallas kernels, face_speeds(): pl.pallas_call(speeds_kernel, grid=(slabs // part,), out_shape=(jax.Shape...  4.44 us
    pallas_call x1, Pallas kernels, tile_stress(): pl.pallas_call(stress_kernel, grid=(slabs // part,), out_shape=(jax.Shape...  3.81 us
  transfers between devices with their start and end apart: 8, of which 2 were waited for; matrix products, arithmetic and copies ran while one was open for 0% of the time, Pallas kernels for 42%

profile of v9, /device:TPU:3, one launch (start us, length us, event | category | flops | bytes accessed | tf_op | source)
XLA Modules:
  0.0 98.7 jit_solution(13059127549952689312)
XLA Ops:
  0.6 0.0 copy-start.2
  0.6 0.0 copy-start.6
  0.7 0.0 copy-start.5
  0.7 0.0 copy-start.4
  0.7 0.0 copy-start.3
  0.7 3.8 %tile_stress.1 = (f32[32,128]{1,0:T(8,128)S(1)}, f32[9,128,128]{2,1,0:T(8,128)S(1)}, f32[9,128,128]{2,1,0:T(8,128)S(1)}) custom-call(f32[3,32,128,128]{3,2,1,0:T(8,128)} %v_high.1, f32[4,32,128,128]{3,2,1,0:T(8,128)} %high_in.1, f32[3,32,128,128]{3,2,1,0:T(8,128)} %v_high.1), custom_call_target="tpu_custom_call" | custom-call | flops 5242880 | bytes 4194304 | tf_op jit(solution)/shard_map/tile_stress/pallas_call | solution.py:647
  4.5 0.0 copy-done.2
  4.5 0.0 copy-done.6
  4.5 0.0 copy-done.5
  4.5 0.0 copy-done.4
  4.5 0.0 copy-done.3
  4.5 0.2 census.1
  4.8 10.5 %all_to_all.5.gathered = f32[8,48,128]{2,1,0:T(8,128)S(1)} all-to-all(f32[8,48,128]{2,1,0:T(8,128)S(1)} %census.1), channel_id=1, replica_groups=mesh['gx'=8,'gy'=4] {'gx'}, dimensions={0} | all-to-all | bytes 393216 | tf_op jit(solution)/shard_map/all_to_all | solution.py:823
  15.3 3.1 %collective-permute-start.2 = (f32[9,128,128]{2,1,0:T(8,128)S(1)}, f32[9,128,128]{2,1,0:T(8,128)S(1)}, u32[]{:S(2)}, u32[]{:S(2)}) collective-permute-start(f32[9,128,128]{2,1,0:T(8,128)S(1)} %get-tuple-element.33), channel_id=1, source_target_pairs={{0,4},{4,8},{8,12},{12,16},{16,20},{20,24},{24,28},{1,5},{5,9},{9,... | collective-permute-start | bytes 1769480 | tf_op jit(solution)/shard_map/ppermute | solution.py:803
  18.3 2.2 %collective-permute-start.3 = (f32[9,128,128]{2,1,0:T(8,128)S(1)}, f32[9,128,128]{2,1,0:T(8,128)S(1)}, u32[]{:S(2)}, u32[]{:S(2)}) collective-permute-start(f32[9,128,128]{2,1,0:T(8,128)S(1)} %get-tuple-element.34), channel_id=1, source_target_pairs={{4,0},{8,4},{12,8},{16,12},{20,16},{24,20},{28,24},{5,1},{9,5},{13... | collective-permute-start | bytes 1769480 | tf_op jit(solution)/shard_map/ppermute | solution.py:803
  20.6 2.3 %pack.1 = (f32[9,32,128]{2,1,0:T(8,128)S(1)}, f32[9,32,128]{2,1,0:T(8,128)S(1)}) custom-call(f32[4,32,128,128]{3,2,1,0:T(8,128)} %high_in.1, f32[4,32,128,128]{3,2,1,0:T(8,128)} %high_in.1, f32[3,32,128,128]{3,2,1,0:T(8,128)} %v_high.1, f32[3,32,128,128]{3,2,1,0:T(8,128)} %v_high.1), custom_call_target="tpu_custom_call" | custom-call | flops 1 | bytes 1769472 | tf_op jit(solution)/shard_map/pack/pallas_call | solution.py:678
  22.9 1.3 %settle.1 = (f32[1,128]{1,0:T(1,128)}, f32[16,8,128]{2,1,0:T(8,128)S(1)}, f32[9,32,128]{2,1,0:T(8,128)S(1)}, f32[9,32,128]{2,1,0:T(8,128)S(1)}) custom-call(s32[1]{0:T(128)} %bitcast.2.me, f32[8,48,128]{2,1,0:T(8,128)S(1)} %all_to_all.5.gathered, f32[9,32,128]{2,1,0:T(8,128)S(1)} %get-tuple-element.25.low_in, f32[9,32,128]{2,1,0:T(8,128)S(1)} %get-tuple-element.26.high_in), custom_call_target="tpu_custom_call" | custom-call | flops 1000000 | bytes 1000000 | tf_op jit(solution)/shard_map/settle/pallas_call | solution.py:779
  24.3 6.9 %collective-permute-start = (f32[9,32,128]{2,1,0:T(8,128)S(1)}, f32[9,32,128]{2,1,0:T(8,128)S(1)}, u32[]{:S(2)}, u32[]{:S(2)}) collective-permute-start(f32[9,32,128]{2,1,0:T(8,128)S(1)} %get-tuple-element.27), channel_id=1, source_target_pairs={{0,1},{1,2},{2,3},{4,5},{5,6},{6,7},{8,9},{9,10},{10,11},{12,13},{... | collective-permute-start | bytes 442376 | tf_op jit(solution)/shard_map/ppermute | solution.py:803
  31.2 1.9 %collective-permute-start.1 = (f32[9,32,128]{2,1,0:T(8,128)S(1)}, f32[9,32,128]{2,1,0:T(8,128)S(1)}, u32[]{:S(2)}, u32[]{:S(2)}) collective-permute-start(f32[9,32,128]{2,1,0:T(8,128)S(1)} %get-tuple-element.28), channel_id=1, source_target_pairs={{1,0},{2,1},{3,2},{5,4},{6,5},{7,6},{9,8},{10,9},{11,10},{13,12},{... | collective-permute-start | bytes 442376 | tf_op jit(solution)/shard_map/ppermute | solution.py:803
  33.1 4.4 %face_speeds.1 = (f32[32,16,8,128]{3,2,1,0:T(8,128)S(1)}, f32[32,16,8,128]{3,2,1,0:T(8,128)S(1)}) custom-call(f32[3,32,8,16,128]{4,3,2,1,0:T(8,128)} %bitcast.16), custom_call_target="tpu_custom_call" | custom-call | flops 4194304 | bytes 6291456 | tf_op jit(solution)/shard_map/face_speeds/pallas_call | solution.py:571
  37.5 0.0 copy-start
  37.5 0.0 collective-permute-done.refs_4_.refs_6_.refs_8_.refs_10_.refs_12_
  37.6 0.4 collective-permute-done.1.refs_5_.refs_7_.refs_9_.refs_11_.refs_13_
  37.9 17.2 %interior.2 = (f32[4,32,16,8,128]{4,3,2,1,0:T(8,128)}, f32[8,32,128]{2,1,0:T(8,128)S(1)}, f32[8,32,128]{2,1,0:T(8,128)S(1)}) custom-call(f32[4,32,8,16,128]{4,3,2,1,0:T(8,128)} %bitcast.21, f32[3,32,8,16,128]{4,3,2,1,0:T(8,128)} %bitcast.17, f32[32,16,8,128]{3,2,1,0:T(8,128)S(1)} %get-tuple-element.22.refs_2_.refs_4_.refs_6_, ...), custom_call_target="tpu_custom_call" | custom-call | flops 73400320 | bytes 23068672 | tf_op jit(solution)/shard_map/interior/pallas_call | solution.py:379
  55.1 0.0 copy-done
  55.2 0.0 collective-permute-done.2
  55.2 0.0 collective-permute-done.3
  55.2 0.0 copy-start.1
  55.2 5.3 %boundary.2 = (f32[4,2,16,8,128]{4,3,2,1,0:T(8,128)S(1)}, f32[4,2,16,8,128]{4,3,2,1,0:T(8,128)S(1)}, f32[8,32,128]{2,1,0:T(8,128)S(1)}, f32[8,32,128]{2,1,0:T(8,128)S(1)}) custom-call(f32[4,32,8,16,128]{4,3,2,1,0:T(8,128)} %bitcast.22, f32[9,8,16,128]{3,2,1,0:T(8,128)S(1)} %bitcast.8, f32[9,8,16,128]{3,2,1,0:T(8,128)S(1)} %bitcast.11, ...), custom_call_target="tpu_custom_call" | custom-call | flops 13107200 | bytes 6291456 | tf_op jit(solution)/shard_map/boundary/pallas_call | solution.py:527
  60.5 1.9 %collective-permute-start.5 = (f32[4,2,16,8,128]{4,3,2,1,0:T(8,128)S(1)}, f32[4,2,16,8,128]{4,3,2,1,0:T(8,128)S(1)}, u32[]{:S(2)}, u32[]{:S(2)}) collective-permute-start(f32[4,2,16,8,128]{4,3,2,1,0:T(8,128)S(1)} %get-tuple-element.37.refs_1_), channel_id=1, source_target_pairs={{4,0},{8,4},{12,8},{16,12},{20,16},{24,20},{28,24},{5,1},{9,5},{13... | collective-permute-start | bytes 1572872 | tf_op jit(solution)/shard_map/ppermute | solution.py:803
  62.4 4.3 %collective-permute-start.4 = (f32[4,2,16,8,128]{4,3,2,1,0:T(8,128)S(1)}, f32[4,2,16,8,128]{4,3,2,1,0:T(8,128)S(1)}, u32[]{:S(2)}, u32[]{:S(2)}) collective-permute-start(f32[4,2,16,8,128]{4,3,2,1,0:T(8,128)S(1)} %get-tuple-element.38.refs_2_), channel_id=1, source_target_pairs={{0,4},{4,8},{8,12},{12,16},{16,20},{20,24},{24,28},{1,5},{5,9},{9,... | collective-permute-start | bytes 1572872 | tf_op jit(solution)/shard_map/ppermute | solution.py:803
  66.7 4.2 %collective-permute-start.6 = (f32[8,32,128]{2,1,0:T(8,128)S(1)}, f32[8,32,128]{2,1,0:T(8,128)S(1)}, u32[]{:S(2)}, u32[]{:S(2)}) collective-permute-start(f32[8,32,128]{2,1,0:T(8,128)S(1)} %get-tuple-element.39), channel_id=1, source_target_pairs={{0,1},{1,2},{2,3},{4,5},{5,6},{6,7},{8,9},{9,10},{10,11},{12,13},{... | collective-permute-start | bytes 393224 | tf_op jit(solution)/shard_map/ppermute | solution.py:803
  70.9 1.9 %collective-permute-start.7 = (f32[8,32,128]{2,1,0:T(8,128)S(1)}, f32[8,32,128]{2,1,0:T(8,128)S(1)}, u32[]{:S(2)}, u32[]{:S(2)}) collective-permute-start(f32[8,32,128]{2,1,0:T(8,128)S(1)} %get-tuple-element.40), channel_id=1, source_target_pairs={{1,0},{2,1},{3,2},{5,4},{6,5},{7,6},{9,8},{10,9},{11,10},{13,12},{... | collective-permute-start | bytes 393224 | tf_op jit(solution)/shard_map/ppermute | solution.py:803
  72.9 0.0 collective-permute-done.6.refs_6_.refs_10_
  72.9 4.6 %collective-permute-done.7.refs_7_.refs_11_ = f32[8,32,128]{2,1,0:T(8,128)S(1)} collective-permute-done((f32[8,32,128]{2,1,0:T(8,128)S(1)}, f32[8,32,128]{2,1,0:T(8,128)S(1)}, u32[]{:S(2)}, u32[]{:S(2)}) %collective-permute-start.7) | collective-permute-done | bytes 131104 | tf_op jit(solution)/shard_map/ppermute | solution.py:803
  77.5 0.0 copy-done.1
  77.5 16.5 %interior.3.refs_14_ = f32[4,32,8,16,128]{4,3,2,1,0:T(8,128)} custom-call(f32[4,32,16,8,128]{4,3,2,1,0:T(8,128)} %get-tuple-element.30.refs_0_, f32[4,2,16,8,128]{4,3,2,1,0:T(8,128)S(1)} %get-tuple-element.37.refs_1_, f32[4,2,16,8,128]{4,3,2,1,0:T(8,128)S(1)} %get-tuple-element.38.refs_2_, f32[3,32,8,16,128]{4,3,2,1,0:T(8,128)} %bitcast.19, ...), custom_call_target="tpu_custom_call" | custom-call | flops 73400320 | bytes 23068672 | tf_op jit(solution)/shard_map/interior/pallas_call | solution.py:379
  94.0 0.0 collective-permute-done.5.refs_4_
  94.0 0.0 collective-permute-done.4.refs_3_
  94.0 4.7 %boundary.3 = f32[4,32,8,16,128]{4,3,2,1,0:T(8,128)} custom-call(f32[4,32,16,8,128]{4,3,2,1,0:T(8,128)} %get-tuple-element.30.refs_0_, f32[4,2,16,8,128]{4,3,2,1,0:T(8,128)S(1)} %get-tuple-element.37.refs_1_, f32[4,2,16,8,128]{4,3,2,1,0:T(8,128)S(1)} %get-tuple-element.38.refs_2_, ...), custom_call_target="tpu_custom_call", output_to_operand_aliasing={{}: (14, {})} | custom-call | flops 13107200 | bytes 6291456 | tf_op jit(solution)/shard_map/boundary/pallas_call | solution.py:527
Async XLA Ops:
  0.6 3.9 %copy-start.2 = (f32[1,32,128]{2,1,0:T(8,128)S(1)}, f32[1,32,128]{2,1,0:T(8,128)}, u32[]{:S(2)}) copy-start(f32[1,32,128]{2,1,0:T(8,128)} %share.1) | copy-start | bytes 49156
  0.6 3.9 %copy-start.6 = (s32[1,32]{1,0:T(1,128)S(1)}, s32[1,32]{1,0:T(1,128)}, u32[]{:S(2)}) copy-start(s32[1,32]{1,0:T(1,128)} %count.1) | copy-start | bytes 388
  0.7 3.9 %copy-start.5 = (s32[1,32,1]{1,2,0:T(1,128)S(1)}, s32[1,32,1]{1,2,0:T(1,128)}, u32[]{:S(2)}) copy-start(s32[1,32,1]{1,2,0:T(1,128)} %param.11) | copy-start | bytes 388
  0.7 3.9 %copy-start.4 = (s32[1,32,1]{1,2,0:T(1,128)S(1)}, s32[1,32,1]{1,2,0:T(1,128)}, u32[]{:S(2)}) copy-start(s32[1,32,1]{1,2,0:T(1,128)} %param.10) | copy-start | bytes 388
  0.7 3.9 %copy-start.3 = (f32[1,128]{1,0:T(1,128)S(1)}, f32[1,128]{1,0:T(1,128)}, u32[]{:S(2)}) copy-start(f32[1,128]{1,0:T(1,128)} %threshold.1) | copy-start | bytes 1540
  15.3 39.9 %collective-permute-start.2 = (f32[9,128,128]{2,1,0:T(8,128)S(1)}, f32[9,128,128]{2,1,0:T(8,128)S(1)}, u32[]{:S(2)}, u32[]{:S(2)}) collective-permute-start(f32[9,128,128]{2,1,0:T(8,128)S(1)} %get-tuple-element.33), channel_id=1, source_target_pairs={{0,4},{4,8},{8,12},{12,16},{16,20},{20,24},{24,28},{1,5},{5,9},{9,... | collective-permute-start | bytes 1769480 | tf_op jit(solution)/shard_map/ppermute | solution.py:803
  18.3 36.8 %collective-permute-start.3 = (f32[9,128,128]{2,1,0:T(8,128)S(1)}, f32[9,128,128]{2,1,0:T(8,128)S(1)}, u32[]{:S(2)}, u32[]{:S(2)}) collective-permute-start(f32[9,128,128]{2,1,0:T(8,128)S(1)} %get-tuple-element.34), channel_id=1, source_target_pairs={{4,0},{8,4},{12,8},{16,12},{20,16},{24,20},{28,24},{5,1},{9,5},{13... | collective-permute-start | bytes 1769480 | tf_op jit(solution)/shard_map/ppermute | solution.py:803
  24.3 13.3 %collective-permute-start = (f32[9,32,128]{2,1,0:T(8,128)S(1)}, f32[9,32,128]{2,1,0:T(8,128)S(1)}, u32[]{:S(2)}, u32[]{:S(2)}) collective-permute-start(f32[9,32,128]{2,1,0:T(8,128)S(1)} %get-tuple-element.27), channel_id=1, source_target_pairs={{0,1},{1,2},{2,3},{4,5},{5,6},{6,7},{8,9},{9,10},{10,11},{12,13},{... | collective-permute-start | bytes 442376 | tf_op jit(solution)/shard_map/ppermute | solution.py:803
  31.2 6.8 %collective-permute-start.1 = (f32[9,32,128]{2,1,0:T(8,128)S(1)}, f32[9,32,128]{2,1,0:T(8,128)S(1)}, u32[]{:S(2)}, u32[]{:S(2)}) collective-permute-start(f32[9,32,128]{2,1,0:T(8,128)S(1)} %get-tuple-element.28), channel_id=1, source_target_pairs={{1,0},{2,1},{3,2},{5,4},{6,5},{7,6},{9,8},{10,9},{11,10},{13,12},{... | collective-permute-start | bytes 442376 | tf_op jit(solution)/shard_map/ppermute | solution.py:803
  37.5 17.6 %copy-start = (f32[32,16,8,128]{3,2,1,0:T(8,128)}, f32[32,16,8,128]{3,2,1,0:T(8,128)S(1)}, u32[]{:S(2)}) copy-start(f32[32,16,8,128]{3,2,1,0:T(8,128)S(1)} %get-tuple-element.23.refs_3_.refs_5_.refs_7_) | copy-start | bytes 6291460
  55.2 22.3 %copy-start.1 = (f32[32,16,8,128]{3,2,1,0:T(8,128)S(1)}, f32[32,16,8,128]{3,2,1,0:T(8,128)}, u32[]{:S(2)}) copy-start(f32[32,16,8,128]{3,2,1,0:T(8,128)} %copy-done) | copy-start | bytes 6291460
  60.5 33.5 %collective-permute-start.5 = (f32[4,2,16,8,128]{4,3,2,1,0:T(8,128)S(1)}, f32[4,2,16,8,128]{4,3,2,1,0:T(8,128)S(1)}, u32[]{:S(2)}, u32[]{:S(2)}) collective-permute-start(f32[4,2,16,8,128]{4,3,2,1,0:T(8,128)S(1)} %get-tuple-element.37.refs_1_), channel_id=1, source_target_pairs={{4,0},{8,4},{12,8},{16,12},{20,16},{24,20},{28,24},{5,1},{9,5},{13... | collective-permute-start | bytes 1572872 | tf_op jit(solution)/shard_map/ppermute | solution.py:803
  62.4 31.6 %collective-permute-start.4 = (f32[4,2,16,8,128]{4,3,2,1,0:T(8,128)S(1)}, f32[4,2,16,8,128]{4,3,2,1,0:T(8,128)S(1)}, u32[]{:S(2)}, u32[]{:S(2)}) collective-permute-start(f32[4,2,16,8,128]{4,3,2,1,0:T(8,128)S(1)} %get-tuple-element.38.refs_2_), channel_id=1, source_target_pairs={{0,4},{4,8},{8,12},{12,16},{16,20},{20,24},{24,28},{1,5},{5,9},{9,... | collective-permute-start | bytes 1572872 | tf_op jit(solution)/shard_map/ppermute | solution.py:803
  66.7 6.2 %collective-permute-start.6 = (f32[8,32,128]{2,1,0:T(8,128)S(1)}, f32[8,32,128]{2,1,0:T(8,128)S(1)}, u32[]{:S(2)}, u32[]{:S(2)}) collective-permute-start(f32[8,32,128]{2,1,0:T(8,128)S(1)} %get-tuple-element.39), channel_id=1, source_target_pairs={{0,1},{1,2},{2,3},{4,5},{5,6},{6,7},{8,9},{9,10},{10,11},{12,13},{... | collective-permute-start | bytes 393224 | tf_op jit(solution)/shard_map/ppermute | solution.py:803
  70.9 6.6 %collective-permute-start.7 = (f32[8,32,128]{2,1,0:T(8,128)S(1)}, f32[8,32,128]{2,1,0:T(8,128)S(1)}, u32[]{:S(2)}, u32[]{:S(2)}) collective-permute-start(f32[8,32,128]{2,1,0:T(8,128)S(1)} %get-tuple-element.40), channel_id=1, source_target_pairs={{1,0},{2,1},{3,2},{5,4},{6,5},{7,6},{9,8},{10,9},{11,10},{13,12},{... | collective-permute-start | bytes 393224 | tf_op jit(solution)/shard_map/ppermute | solution.py:803

commit v10 on v6

--- a/solution.py
+++ b/solution.py
@@ -14,8 +14,6 @@
 
 VMEM_LIMIT = 48 * 1024 * 1024
 PAIR = 2
-GROUP = 8
-GATHER = 4
 HIGHEST = lax.Precision.HIGHEST
 ANY = pl.BlockSpec(memory_space=pl.ANY)
 VMEM = pl.BlockSpec(memory_space=pltpu.VMEM)
@@ -138,7 +136,7 @@
     staged([functools.partial(job, range(t, t + PAIR)) for t in range(0, f.tiles, PAIR)])
 
 
-def slab_step(f, k, put):
+def slab_step(f, k, put, group_size=4):
     slab = k + 2
     lane = lax.broadcasted_iota(jnp.int32, (8, f.lanes), 1)
     top = f.lanes - 1
@@ -179,11 +177,11 @@
         return doubles[c, t]
 
     held = []
-    for t in range(GROUP):
+    for t in range(group_size):
         vertical(t)
-    for begin in range(0, f.tiles, GROUP):
-        group = range(begin, min(begin + GROUP, f.tiles))
-        for t in range(begin + GROUP, min(begin + 2 * GROUP, f.tiles)):
+    for begin in range(0, f.tiles, group_size):
+        group = range(begin, min(begin + group_size, f.tiles))
+        for t in range(begin + group_size, min(begin + 2 * group_size, f.tiles)):
             vertical(t)
         loaded = {}
         for t in group:
@@ -275,7 +273,7 @@
     q, uv, sz, fall, fx, lx, stage, in_sem, out_sem = refs[:9]
     kept = refs[9:11]
     comps, slabs, tiles = q.shape[1], q.shape[2], sz.shape[2]
-    chunk, flight = 8, 3
+    chunk, flight = (8, 3) if last else (4, 6)
     chunks = slabs // chunk
 
     def fetch(j, first, final):
@@ -338,13 +336,7 @@
 
         slab_step(f, k, put)
         if last:
-
-            @pl.when((k + 1) % GATHER == 0)
-            def _():
-                first = k + 1 - GATHER
-                source, target = pl.ds(first, GATHER), pl.ds(first + 2, GATHER)
-                start_sets([(lambda n: stage.at[:, source, :, n], lambda n: out.at[:, target, n])], out_sem)
-
+            start_sets([(lambda n: stage.at[:, k, :, n], lambda n: out.at[:, k + 2, n])], out_sem)
         else:
             start(stage.at[:, k], out.at[:, k + 2], out_sem)
         if not last:

time: 100 us -> 97.4 us (0.974)
  Pallas kernels: 56.8 us -> 54.1 us
    pallas_call x2, Pallas kernels: 36.3 us -> 33.7 us  [interior(): pl.pallas_call(functools.partial(interior_kernel, last, groups, len(field...]
  transfers between devices with their start and end apart: 8 -> 8, of which waited for: 2 -> 2; matrix products, arithmetic and copies ran while one was open for 0% -> 0% of each run, Pallas kernels for 42% -> 41%
where the time goes in v10:
time: 97.4 us; the launch traced here: 97 us
  Pallas kernels  54.1 us (56%)
  starting transfers between devices  26.4 us (27%)
  blocking collectives  10.5 us (11%)
  waiting for transfers between devices  5.02 us (5%)
    pallas_call x2, Pallas kernels, interior(): pl.pallas_call(functools.partial(interior_kernel, last, groups, len(field...  33.7 us
    ppermute x4, starting transfers between devices, exchange(): lax.ppermute(high, axis, forward)  18.5 us
    all_to_all x1, blocking collectives, shards(): lax.all_to_all(copies, 'gx', split_axis=0, concat_axis=0, tiled=True)  10.5 us
    pallas_call x2, Pallas kernels, boundary(): pl.pallas_call(functools.partial(boundary_kernel, last, groups, slabs), o...  9.98 us
    ppermute x4, starting transfers between devices, exchange(): lax.ppermute(low, axis, backward)  7.99 us
    ppermute x4, waiting for transfers between devices, exchange(): lax.ppermute(low, axis, backward)  5.01 us
    pallas_call x1, Pallas kernels, face_speeds(): pl.pallas_call(speeds_kernel, grid=(slabs // part,), out_shape=(jax.Shape...  4.44 us
    pallas_call x1, Pallas kernels, survey(): pl.pallas_call(survey_kernel, grid=(slabs // part,), out_shape=(packed, p...  4.38 us
  transfers between devices with their start and end apart: 8, of which 2 were waited for; matrix products, arithmetic and copies ran while one was open for 0% of the time, Pallas kernels for 41%

profile of v10, /device:TPU:3, one launch (start us, length us, event | category | flops | bytes accessed | tf_op | source)
XLA Modules:
  0.0 97.0 jit_solution(1345243442571079383)
XLA Ops:
  0.6 0.0 copy-start.2
  0.6 0.0 copy-start.6
  0.7 0.0 copy-start.5
  0.7 0.0 copy-start.4
  0.7 0.0 copy-start.3
  0.7 4.4 %survey.1 = (f32[9,32,128]{2,1,0:T(8,128)S(1)}, f32[9,32,128]{2,1,0:T(8,128)S(1)}, f32[32,128]{1,0:T(8,128)S(1)}, f32[9,128,128]{2,1,0:T(8,128)S(1)}, f32[9,128,128]{2,1,0:T(8,128)S(1)}) custom-call(f32[4,32,128,128]{3,2,1,0:T(8,128)} %state.1, f32[4,32,128,128]{3,2,1,0:T(8,128)} %state.1, f32[3,32,128,128]{3,2,1,0:T(8,128)} %velocity.1, ...), custom_call_target="tpu_custom_call" | custom-call | flops 5242880 | bytes 5242880 | tf_op jit(solution)/shard_map/survey/pallas_call | solution.py:659
  5.1 0.0 copy-done.2
  5.1 0.0 copy-done.6
  5.1 0.0 copy-done.5
  5.1 0.0 copy-done.4
  5.1 0.0 copy-done.3
  5.1 0.2 census.1
  5.3 10.5 %all_to_all.5.gathered = f32[8,48,128]{2,1,0:T(8,128)S(1)} all-to-all(f32[8,48,128]{2,1,0:T(8,128)S(1)} %census.1), channel_id=1, replica_groups=mesh['gx'=8,'gy'=4] {'gx'}, dimensions={0} | all-to-all | bytes 393216 | tf_op jit(solution)/shard_map/all_to_all | solution.py:807
  15.8 3.1 %collective-permute-start.2 = (f32[9,128,128]{2,1,0:T(8,128)S(1)}, f32[9,128,128]{2,1,0:T(8,128)S(1)}, u32[]{:S(2)}, u32[]{:S(2)}) collective-permute-start(f32[9,128,128]{2,1,0:T(8,128)S(1)} %get-tuple-element.33), channel_id=1, source_target_pairs={{0,4},{4,8},{8,12},{12,16},{16,20},{20,24},{24,28},{1,5},{5,9},{9,... | collective-permute-start | bytes 1769480 | tf_op jit(solution)/shard_map/ppermute | solution.py:788
  18.9 2.2 %collective-permute-start.3 = (f32[9,128,128]{2,1,0:T(8,128)S(1)}, f32[9,128,128]{2,1,0:T(8,128)S(1)}, u32[]{:S(2)}, u32[]{:S(2)}) collective-permute-start(f32[9,128,128]{2,1,0:T(8,128)S(1)} %get-tuple-element.34), channel_id=1, source_target_pairs={{4,0},{8,4},{12,8},{16,12},{20,16},{24,20},{28,24},{5,1},{9,5},{13... | collective-permute-start | bytes 1769480 | tf_op jit(solution)/shard_map/ppermute | solution.py:788
  21.2 1.3 %settle.1 = (f32[1,128]{1,0:T(1,128)}, f32[16,8,128]{2,1,0:T(8,128)S(1)}, f32[9,32,128]{2,1,0:T(8,128)S(1)}, f32[9,32,128]{2,1,0:T(8,128)S(1)}) custom-call(s32[1]{0:T(128)} %bitcast.2.me, f32[8,48,128]{2,1,0:T(8,128)S(1)} %all_to_all.5.gathered, f32[9,32,128]{2,1,0:T(8,128)S(1)} %get-tuple-element.25.low_in, f32[9,32,128]{2,1,0:T(8,128)S(1)} %get-tuple-element.26.high_in), custom_call_target="tpu_custom_call" | custom-call | flops 1000000 | bytes 1000000 | tf_op jit(solution)/shard_map/settle/pallas_call | solution.py:764
  22.5 6.9 %collective-permute-start = (f32[9,32,128]{2,1,0:T(8,128)S(1)}, f32[9,32,128]{2,1,0:T(8,128)S(1)}, u32[]{:S(2)}, u32[]{:S(2)}) collective-permute-start(f32[9,32,128]{2,1,0:T(8,128)S(1)} %get-tuple-element.27), channel_id=1, source_target_pairs={{0,1},{1,2},{2,3},{4,5},{5,6},{6,7},{8,9},{9,10},{10,11},{12,13},{... | collective-permute-start | bytes 442376 | tf_op jit(solution)/shard_map/ppermute | solution.py:788
  29.4 1.9 %collective-permute-start.1 = (f32[9,32,128]{2,1,0:T(8,128)S(1)}, f32[9,32,128]{2,1,0:T(8,128)S(1)}, u32[]{:S(2)}, u32[]{:S(2)}) collective-permute-start(f32[9,32,128]{2,1,0:T(8,128)S(1)} %get-tuple-element.28), channel_id=1, source_target_pairs={{1,0},{2,1},{3,2},{5,4},{6,5},{7,6},{9,8},{10,9},{11,10},{13,12},{... | collective-permute-start | bytes 442376 | tf_op jit(solution)/shard_map/ppermute | solution.py:788
  31.3 4.4 %face_speeds.1 = (f32[32,16,8,128]{3,2,1,0:T(8,128)S(1)}, f32[32,16,8,128]{3,2,1,0:T(8,128)S(1)}) custom-call(f32[3,32,8,16,128]{4,3,2,1,0:T(8,128)} %bitcast.16), custom_call_target="tpu_custom_call" | custom-call | flops 4194304 | bytes 6291456 | tf_op jit(solution)/shard_map/face_speeds/pallas_call | solution.py:571
  35.8 0.0 copy-start
  35.8 0.0 collective-permute-done.refs_4_.refs_6_.refs_8_.refs_10_.refs_12_
  35.8 0.4 collective-permute-done.1.refs_5_.refs_7_.refs_9_.refs_11_.refs_13_
  36.2 17.2 %interior.2 = (f32[4,32,16,8,128]{4,3,2,1,0:T(8,128)}, f32[8,32,128]{2,1,0:T(8,128)S(1)}, f32[8,32,128]{2,1,0:T(8,128)S(1)}) custom-call(f32[4,32,8,16,128]{4,3,2,1,0:T(8,128)} %bitcast.21, f32[3,32,8,16,128]{4,3,2,1,0:T(8,128)} %bitcast.17, f32[32,16,8,128]{3,2,1,0:T(8,128)S(1)} %get-tuple-element.22.refs_2_.refs_4_.refs_6_, ...), custom_call_target="tpu_custom_call" | custom-call | flops 73400320 | bytes 23068672 | tf_op jit(solution)/shard_map/interior/pallas_call | solution.py:379
  53.4 0.0 copy-done
  53.4 0.0 collective-permute-done.2
  53.4 0.0 collective-permute-done.3
  53.4 0.0 copy-start.1
  53.4 5.3 %boundary.2 = (f32[4,2,16,8,128]{4,3,2,1,0:T(8,128)S(1)}, f32[4,2,16,8,128]{4,3,2,1,0:T(8,128)S(1)}, f32[8,32,128]{2,1,0:T(8,128)S(1)}, f32[8,32,128]{2,1,0:T(8,128)S(1)}) custom-call(f32[4,32,8,16,128]{4,3,2,1,0:T(8,128)} %bitcast.22, f32[9,8,16,128]{3,2,1,0:T(8,128)S(1)} %bitcast.8, f32[9,8,16,128]{3,2,1,0:T(8,128)S(1)} %bitcast.11, ...), custom_call_target="tpu_custom_call" | custom-call | flops 13107200 | bytes 6291456 | tf_op jit(solution)/shard_map/boundary/pallas_call | solution.py:527
  58.7 1.9 %collective-permute-start.5 = (f32[4,2,16,8,128]{4,3,2,1,0:T(8,128)S(1)}, f32[4,2,16,8,128]{4,3,2,1,0:T(8,128)S(1)}, u32[]{:S(2)}, u32[]{:S(2)}) collective-permute-start(f32[4,2,16,8,128]{4,3,2,1,0:T(8,128)S(1)} %get-tuple-element.37.refs_1_), channel_id=1, source_target_pairs={{4,0},{8,4},{12,8},{16,12},{20,16},{24,20},{28,24},{5,1},{9,5},{13... | collective-permute-start | bytes 1572872 | tf_op jit(solution)/shard_map/ppermute | solution.py:788
  60.7 4.3 %collective-permute-start.4 = (f32[4,2,16,8,128]{4,3,2,1,0:T(8,128)S(1)}, f32[4,2,16,8,128]{4,3,2,1,0:T(8,128)S(1)}, u32[]{:S(2)}, u32[]{:S(2)}) collective-permute-start(f32[4,2,16,8,128]{4,3,2,1,0:T(8,128)S(1)} %get-tuple-element.38.refs_2_), channel_id=1, source_target_pairs={{0,4},{4,8},{8,12},{12,16},{16,20},{20,24},{24,28},{1,5},{5,9},{9,... | collective-permute-start | bytes 1572872 | tf_op jit(solution)/shard_map/ppermute | solution.py:788
  64.9 4.2 %collective-permute-start.6 = (f32[8,32,128]{2,1,0:T(8,128)S(1)}, f32[8,32,128]{2,1,0:T(8,128)S(1)}, u32[]{:S(2)}, u32[]{:S(2)}) collective-permute-start(f32[8,32,128]{2,1,0:T(8,128)S(1)} %get-tuple-element.39), channel_id=1, source_target_pairs={{0,1},{1,2},{2,3},{4,5},{5,6},{6,7},{8,9},{9,10},{10,11},{12,13},{... | collective-permute-start | bytes 393224 | tf_op jit(solution)/shard_map/ppermute | solution.py:788
  69.2 1.9 %collective-permute-start.7 = (f32[8,32,128]{2,1,0:T(8,128)S(1)}, f32[8,32,128]{2,1,0:T(8,128)S(1)}, u32[]{:S(2)}, u32[]{:S(2)}) collective-permute-start(f32[8,32,128]{2,1,0:T(8,128)S(1)} %get-tuple-element.40), channel_id=1, source_target_pairs={{1,0},{2,1},{3,2},{5,4},{6,5},{7,6},{9,8},{10,9},{11,10},{13,12},{... | collective-permute-start | bytes 393224 | tf_op jit(solution)/shard_map/ppermute | solution.py:788
  71.1 0.0 collective-permute-done.6.refs_6_.refs_10_
  71.1 4.6 %collective-permute-done.7.refs_7_.refs_11_ = f32[8,32,128]{2,1,0:T(8,128)S(1)} collective-permute-done((f32[8,32,128]{2,1,0:T(8,128)S(1)}, f32[8,32,128]{2,1,0:T(8,128)S(1)}, u32[]{:S(2)}, u32[]{:S(2)}) %collective-permute-start.7) | collective-permute-done | bytes 131104 | tf_op jit(solution)/shard_map/ppermute | solution.py:788
  75.8 0.0 copy-done.1
  75.8 16.5 %interior.3.refs_14_ = f32[4,32,8,16,128]{4,3,2,1,0:T(8,128)} custom-call(f32[4,32,16,8,128]{4,3,2,1,0:T(8,128)} %get-tuple-element.30.refs_0_, f32[4,2,16,8,128]{4,3,2,1,0:T(8,128)S(1)} %get-tuple-element.37.refs_1_, f32[4,2,16,8,128]{4,3,2,1,0:T(8,128)S(1)} %get-tuple-element.38.refs_2_, f32[3,32,8,16,128]{4,3,2,1,0:T(8,128)} %bitcast.19, ...), custom_call_target="tpu_custom_call" | custom-call | flops 73400320 | bytes 23068672 | tf_op jit(solution)/shard_map/interior/pallas_call | solution.py:379
  92.3 0.0 collective-permute-done.5.refs_4_
  92.3 0.0 collective-permute-done.4.refs_3_
  92.3 4.7 %boundary.3 = f32[4,32,8,16,128]{4,3,2,1,0:T(8,128)} custom-call(f32[4,32,16,8,128]{4,3,2,1,0:T(8,128)} %get-tuple-element.30.refs_0_, f32[4,2,16,8,128]{4,3,2,1,0:T(8,128)S(1)} %get-tuple-element.37.refs_1_, f32[4,2,16,8,128]{4,3,2,1,0:T(8,128)S(1)} %get-tuple-element.38.refs_2_, ...), custom_call_target="tpu_custom_call", output_to_operand_aliasing={{}: (14, {})} | custom-call | flops 13107200 | bytes 6291456 | tf_op jit(solution)/shard_map/boundary/pallas_call | solution.py:527
Async XLA Ops:
  0.6 4.4 %copy-start.2 = (f32[1,32,128]{2,1,0:T(8,128)S(1)}, f32[1,32,128]{2,1,0:T(8,128)}, u32[]{:S(2)}) copy-start(f32[1,32,128]{2,1,0:T(8,128)} %share.1) | copy-start | bytes 49156
  0.6 4.4 %copy-start.6 = (s32[1,32]{1,0:T(1,128)S(1)}, s32[1,32]{1,0:T(1,128)}, u32[]{:S(2)}) copy-start(s32[1,32]{1,0:T(1,128)} %count.1) | copy-start | bytes 388
  0.7 4.4 %copy-start.5 = (s32[1,32,1]{1,2,0:T(1,128)S(1)}, s32[1,32,1]{1,2,0:T(1,128)}, u32[]{:S(2)}) copy-start(s32[1,32,1]{1,2,0:T(1,128)} %param.11) | copy-start | bytes 388
  0.7 4.4 %copy-start.4 = (s32[1,32,1]{1,2,0:T(1,128)S(1)}, s32[1,32,1]{1,2,0:T(1,128)}, u32[]{:S(2)}) copy-start(s32[1,32,1]{1,2,0:T(1,128)} %param.10) | copy-start | bytes 388
  0.7 4.4 %copy-start.3 = (f32[1,128]{1,0:T(1,128)S(1)}, f32[1,128]{1,0:T(1,128)}, u32[]{:S(2)}) copy-start(f32[1,128]{1,0:T(1,128)} %threshold.1) | copy-start | bytes 1540
  15.8 37.6 %collective-permute-start.2 = (f32[9,128,128]{2,1,0:T(8,128)S(1)}, f32[9,128,128]{2,1,0:T(8,128)S(1)}, u32[]{:S(2)}, u32[]{:S(2)}) collective-permute-start(f32[9,128,128]{2,1,0:T(8,128)S(1)} %get-tuple-element.33), channel_id=1, source_target_pairs={{0,4},{4,8},{8,12},{12,16},{16,20},{20,24},{24,28},{1,5},{5,9},{9,... | collective-permute-start | bytes 1769480 | tf_op jit(solution)/shard_map/ppermute | solution.py:788
  18.9 34.5 %collective-permute-start.3 = (f32[9,128,128]{2,1,0:T(8,128)S(1)}, f32[9,128,128]{2,1,0:T(8,128)S(1)}, u32[]{:S(2)}, u32[]{:S(2)}) collective-permute-start(f32[9,128,128]{2,1,0:T(8,128)S(1)} %get-tuple-element.34), channel_id=1, source_target_pairs={{4,0},{8,4},{12,8},{16,12},{20,16},{24,20},{28,24},{5,1},{9,5},{13... | collective-permute-start | bytes 1769480 | tf_op jit(solution)/shard_map/ppermute | solution.py:788
  22.5 13.3 %collective-permute-start = (f32[9,32,128]{2,1,0:T(8,128)S(1)}, f32[9,32,128]{2,1,0:T(8,128)S(1)}, u32[]{:S(2)}, u32[]{:S(2)}) collective-permute-start(f32[9,32,128]{2,1,0:T(8,128)S(1)} %get-tuple-element.27), channel_id=1, source_target_pairs={{0,1},{1,2},{2,3},{4,5},{5,6},{6,7},{8,9},{9,10},{10,11},{12,13},{... | collective-permute-start | bytes 442376 | tf_op jit(solution)/shard_map/ppermute | solution.py:788
  29.4 6.8 %collective-permute-start.1 = (f32[9,32,128]{2,1,0:T(8,128)S(1)}, f32[9,32,128]{2,1,0:T(8,128)S(1)}, u32[]{:S(2)}, u32[]{:S(2)}) collective-permute-start(f32[9,32,128]{2,1,0:T(8,128)S(1)} %get-tuple-element.28), channel_id=1, source_target_pairs={{1,0},{2,1},{3,2},{5,4},{6,5},{7,6},{9,8},{10,9},{11,10},{13,12},{... | collective-permute-start | bytes 442376 | tf_op jit(solution)/shard_map/ppermute | solution.py:788
  35.8 17.6 %copy-start = (f32[32,16,8,128]{3,2,1,0:T(8,128)}, f32[32,16,8,128]{3,2,1,0:T(8,128)S(1)}, u32[]{:S(2)}) copy-start(f32[32,16,8,128]{3,2,1,0:T(8,128)S(1)} %get-tuple-element.23.refs_3_.refs_5_.refs_7_) | copy-start | bytes 6291460
  53.4 22.3 %copy-start.1 = (f32[32,16,8,128]{3,2,1,0:T(8,128)S(1)}, f32[32,16,8,128]{3,2,1,0:T(8,128)}, u32[]{:S(2)}) copy-start(f32[32,16,8,128]{3,2,1,0:T(8,128)} %copy-done) | copy-start | bytes 6291460
  58.7 33.5 %collective-permute-start.5 = (f32[4,2,16,8,128]{4,3,2,1,0:T(8,128)S(1)}, f32[4,2,16,8,128]{4,3,2,1,0:T(8,128)S(1)}, u32[]{:S(2)}, u32[]{:S(2)}) collective-permute-start(f32[4,2,16,8,128]{4,3,2,1,0:T(8,128)S(1)} %get-tuple-element.37.refs_1_), channel_id=1, source_target_pairs={{4,0},{8,4},{12,8},{16,12},{20,16},{24,20},{28,24},{5,1},{9,5},{13... | collective-permute-start | bytes 1572872 | tf_op jit(solution)/shard_map/ppermute | solution.py:788
  60.7 31.6 %collective-permute-start.4 = (f32[4,2,16,8,128]{4,3,2,1,0:T(8,128)S(1)}, f32[4,2,16,8,128]{4,3,2,1,0:T(8,128)S(1)}, u32[]{:S(2)}, u32[]{:S(2)}) collective-permute-start(f32[4,2,16,8,128]{4,3,2,1,0:T(8,128)S(1)} %get-tuple-element.38.refs_2_), channel_id=1, source_target_pairs={{0,4},{4,8},{8,12},{12,16},{16,20},{20,24},{24,28},{1,5},{5,9},{9,... | collective-permute-start | bytes 1572872 | tf_op jit(solution)/shard_map/ppermute | solution.py:788
  64.9 6.2 %collective-permute-start.6 = (f32[8,32,128]{2,1,0:T(8,128)S(1)}, f32[8,32,128]{2,1,0:T(8,128)S(1)}, u32[]{:S(2)}, u32[]{:S(2)}) collective-permute-start(f32[8,32,128]{2,1,0:T(8,128)S(1)} %get-tuple-element.39), channel_id=1, source_target_pairs={{0,1},{1,2},{2,3},{4,5},{5,6},{6,7},{8,9},{9,10},{10,11},{12,13},{... | collective-permute-start | bytes 393224 | tf_op jit(solution)/shard_map/ppermute | solution.py:788
  69.2 6.6 %collective-permute-start.7 = (f32[8,32,128]{2,1,0:T(8,128)S(1)}, f32[8,32,128]{2,1,0:T(8,128)S(1)}, u32[]{:S(2)}, u32[]{:S(2)}) collective-permute-start(f32[8,32,128]{2,1,0:T(8,128)S(1)} %get-tuple-element.40), channel_id=1, source_target_pairs={{1,0},{2,1},{3,2},{5,4},{6,5},{7,6},{9,8},{10,9},{11,10},{13,12},{... | collective-permute-start | bytes 393224 | tf_op jit(solution)/shard_map/ppermute | solution.py:788
